TPU v7x, 32 devices: a whole 2x2x4 slice. The times are simulated.
32 devices in a mesh: row: 4 (over y, x), col: 8 (over z, core).
Axes of the slice: x: 2, y: 2, z: 4, core: 2. Of those that a mesh axis runs over, the one named last changes fastest.
Arguments:
- tile_counts: int32 [4, 8, 160, 128, 128], P('row', 'col'), may hold values from 0 to 1536, as said below
- tile_rows: int32 [4, 8, 160], P('row', 'col'), may hold values from 0 to 255, as said below
- tile_cols: int32 [4, 8, 160], P('row', 'col'), may hold values from 0 to 127
- panel: bfloat16 [131072, 128], P(('col', 'row')), may hold values from -0.059814453 to 0.059814453
Outputs:
- word_panel: float32 [131072, 128], P(('row', 'col'))
- context_panel: float32 [131072, 128], P(('col', 'row'))
Inputs may be any that keep to these rules, and one draw needn't show every extreme that they name: `tile_counts`: on each device the occupied tiles come first: every slot at or after that device's number of occupied tiles holds only zeros, and some device has all 160 slots occupied. On each device the pairs (tile_rows, tile_cols) of the slots are distinct.
All inputs are finite; a program needn't handle non-finite values.
Results may differ from a plain program's by a relative error of at most 0.0029.
Values may be sent and summed in bfloat16 or wider, within the bound.
No kernel may reach another device: no remote copies, remote signals or barrier semaphores. Data moves between devices by JAX's collectives and lax.ppermute only.
A program may use at most 128 MiB of HBM per device.

v0:
```python
import math

import jax
import jax.numpy as jnp
from jax import lax
from jax.sharding import PartitionSpec as P

VOCAB = 131072
NEG_SAMPLES = 15


def ppmi_tiles(counts, word_rows, context_cols, row_totals, context_powers, log_scale):
    counts_float = counts.astype(jnp.float32)
    word_log = jnp.log(jnp.maximum(row_totals[word_rows], 1.0))
    context_log = jnp.log(jnp.maximum(context_powers[context_cols], 1.0))
    pointwise = (
        jnp.log(jnp.maximum(counts_float, 1.0))
        + log_scale
        - word_log[:, :, None]
        - context_log[:, None, :]
    )
    return jnp.where(counts > 0, jnp.maximum(pointwise, 0.0), 0.0).astype(jnp.bfloat16)


def shards(tile_counts, tile_rows, tile_cols, panel):
    counts = tile_counts[0, 0]
    word_rows = tile_rows[0, 0]
    context_cols = tile_cols[0, 0]
    tile_size = counts.shape[-1]
    panel_width = panel.shape[-1]
    band_rows = VOCAB // (tile_size * lax.axis_size("row"))
    panel_band = lax.all_gather(panel, "row", axis=0, tiled=True)
    band_cols = panel_band.shape[0] // tile_size
    word_part = jax.ops.segment_sum(
        jnp.sum(counts, axis=2).astype(jnp.float32), word_rows, num_segments=band_rows
    )
    context_part = jax.ops.segment_sum(
        jnp.sum(counts, axis=1).astype(jnp.float32), context_cols, num_segments=band_cols
    )
    context_totals = lax.psum(context_part, "row")
    context_powers = context_totals**0.75
    band_power = jnp.sum(context_powers)
    row_totals = lax.psum(word_part, "col")
    total_power = lax.psum(band_power, "col")
    log_scale = jnp.log(total_power) - math.log(NEG_SAMPLES)
    tiles = ppmi_tiles(counts, word_rows, context_cols, row_totals, context_powers, log_scale)
    picked = panel_band.reshape(band_cols, tile_size, panel_width)[context_cols]
    product = jnp.einsum("nij,njk->nik", tiles, picked, preferred_element_type=jnp.float32)
    word_partial = jax.ops.segment_sum(product, word_rows, num_segments=band_rows)
    word_partial = word_partial.reshape(band_rows * tile_size, panel_width)
    word_share = lax.psum_scatter(word_partial, "col", scatter_dimension=0, tiled=True)
    word_rounded = lax.all_gather(word_share.astype(jnp.bfloat16), "col", axis=0, tiled=True)
    word_picked = word_rounded.reshape(band_rows, tile_size, panel_width)[word_rows]
    context_product = jnp.einsum(
        "nji,njk->nik", tiles, word_picked, preferred_element_type=jnp.float32
    )
    context_partial = jax.ops.segment_sum(context_product, context_cols, num_segments=band_cols)
    context_partial = context_partial.reshape(band_cols * tile_size, panel_width)
    context_share = (
        lax.psum_scatter(context_partial, "row", scatter_dimension=0, tiled=True) / tile_size
    )
    return (word_share, context_share)


def solution(mesh):
    in_specs = (
        P("row", "col", None, None, None),
        P("row", "col", None),
        P("row", "col", None),
        P(("col", "row"), None),
    )
    out_specs = (P(("row", "col"), None), P(("col", "row"), None))
    return jax.shard_map(shards, mesh=mesh, in_specs=in_specs, out_specs=out_specs, check_vma=False)
```

profile of v0, /device:TPU:0, one launch (start us, length us, event | category | flops | bytes accessed | tf_op | source)
XLA Modules:
  0.0 645.1 jit_solution(5155534995468058630)
XLA Ops:
  7.2 0.0 copy-start.1
  7.2 0.0 copy-start
  7.2 0.0 all-reduce.3.cloned.1.call-start
  7.2 6.8 %fusion.15 = (s32[160,128]{1,0:T(8,128)S(1)}, s32[160,128]{1,0:T(8,128)S(1)}) fusion(s32[1,1,160,128,128]{4,3,2,1,0:T(8,128)} %param.4), kind=kLoop, calls=%fused_computation.30 | loop fusion | flops 5201920 | bytes 10649600 | tf_op jit(solution)/shard_map/reduce_sum | solution.py:35
  14.0 0.0 copy-done.1
  14.0 1.7 scatter_custom_fusion
  15.7 0.0 all-reduce.3.cloned.1.call-update
  15.7 0.0 all-reduce.5.cloned.1.call-start
  15.8 0.0 copy-done
  15.8 1.7 scatter_custom_fusion.1
  17.5 0.0 all-reduce.5.cloned.1.call-update
  17.6 0.0 all-gather.3.cloned.1.call-start
  17.6 0.7 all-gather.3.cloned.1.call-update
  18.3 0.0 reduce-scatter.3.cloned.1.call-start
  18.4 41.7 %all-reduce.3.cloned.1.call-done = f32[128,128]{1,0:T(8,128)} async-done(((f32[128,128]{1,0:T(8,128)}), f32[128,128]{1,0:T(8,128)}) %all-reduce.3.cloned.1.call-update) | async-done | bytes 65552 | tf_op jit(solution)/shard_map/psum | solution.py:40
  60.1 1.5 fusion.10
  61.5 16.6 %psum.22 = f32[]{:T(128)} all-reduce(f32[]{:T(128)} %get-tuple-element.4), channel_id=1, replica_groups=mesh['row'=4,'col'=8] {'col'}, use_global_device_ids=true, to_apply=%region_4.0 | all-reduce | flops 1 | bytes 8 | tf_op jit(solution)/shard_map/psum | solution.py:44
  78.8 0.7 gather_fusion.1
  79.5 37.8 %all-reduce.5.cloned.1.call-done = f32[256,128]{1,0:T(8,128)} async-done(((f32[256,128]{1,0:T(8,128)}), f32[256,128]{1,0:T(8,128)}) %all-reduce.5.cloned.1.call-update) | async-done | bytes 131088 | tf_op jit(solution)/shard_map/psum | solution.py:43
  117.3 1.6 gather_fusion
  118.9 52.0 %all-gather.3.cloned.1.call-done = bf16[16384,128]{1,0:T(8,128)(2,1)} async-done(((bf16[4096,128]{1,0:T(8,128)(2,1)}), bf16[16384,128]{1,0:T(8,128)(2,1)}) %all-gather.3.cloned.1.call-update) | async-done | bytes 4194320 | tf_op jit(solution)/shard_map/all_gather | solution.py:32
  170.9 9.9 %gather_fusion.2 = bf16[160,128,128]{2,1,0:T(8,128)(2,1)} fusion(bf16[128,128,128]{2,1,0:T(8,128)(2,1)} %bitcast.32, s32[1024]{0:T(1024)S(1)} %pad_clamp_fusion), kind=kCustom, calls=%fused_computation.2 | custom fusion | bytes 10486400 | tf_op jit(solution)/shard_map/gather | solution.py:47
  180.8 12.9 %fusion.13 = f32[160,128,128]{2,1,0:T(8,128)} fusion(bf16[160,128,128]{2,1,0:T(8,128)(2,1)} %gather_fusion.2, s32[1,1,160,128,128]{4,3,2,1,0:T(8,128)} %param.4, f32[160,128]{1,0:T(8,128)S(1)} %maximum_log_fusion, f32[160,128]{1,0:T(8,128)S(1)} %maximum_log_fusion.1, f32[]{:T(128)S(6)} %sub.19), kind=kOutput, calls=%fused_computation.29 | convolution fusion | flops 694681600 | bytes 26378244 | tf_op jit(solution)/shard_map/nij,njk->nik/dot_general | solution.py:48
  193.6 7.8 %broadcast_in_dim.10 = f32[256,128,128]{2,1,0:T(8,128)} broadcast(f32[]{:T(128)} %constant.8.clone.1), dimensions={} | broadcast | bytes 16777220 | tf_op jit(solution)/shard_map/broadcast_in_dim | solution.py:49
  201.5 33.2 %scatter_fusion = f32[256,128,128]{2,1,0:T(8,128)} fusion(f32[256,128,128]{2,1,0:T(8,128)} %broadcast_in_dim.10, s32[160]{0:T(256)S(1)} %bitcast.35, f32[160,128,128]{2,1,0:T(8,128)} %fusion.13), kind=kCustom, calls=%fused_computation.6 | custom fusion | flops 2621440 | bytes 31457920 | tf_op jit(solution)/shard_map/scatter-add | solution.py:49
  234.7 0.0 reduce-scatter.3.cloned.1.call-update
  234.7 0.0 all-gather.5.cloned.1.call-start
  234.8 168.3 %reduce-scatter.3.cloned.1.call-done = f32[4096,128]{1,0:T(8,128)} async-done(((f32[32768,128]{1,0:T(8,128)}), f32[4096,128]{1,0:T(8,128)}) %reduce-scatter.3.cloned.1.call-update) | async-done | bytes 2097168 | tf_op jit(solution)/shard_map/reduce_scatter | solution.py:51
  403.1 2.7 convert_element_type.20
  405.8 0.0 all-gather.5.cloned.1.call-update
  405.8 0.2 reduce-scatter.5.cloned.1.call-start
  406.0 80.3 %all-gather.5.cloned.1.call-done = bf16[32768,128]{1,0:T(8,128)(2,1)} async-done(((bf16[4096,128]{1,0:T(8,128)(2,1)}), bf16[32768,128]{1,0:T(8,128)(2,1)}) %all-gather.5.cloned.1.call-update) | async-done | bytes 8388624 | tf_op jit(solution)/shard_map/all_gather | solution.py:52
  486.4 11.1 %gather_fusion.3 = bf16[160,128,128]{2,1,0:T(8,128)(2,1)} fusion(bf16[256,128,128]{2,1,0:T(8,128)(2,1)} %bitcast.33, s32[1024]{0:T(1024)S(1)} %pad_clamp_fusion.1), kind=kCustom, calls=%fused_computation.3 | custom fusion | bytes 10486400 | tf_op jit(solution)/shard_map/gather | solution.py:53
  497.5 15.1 %fusion.11 = f32[160,128,128]{2,1,0:T(8,128)} fusion(bf16[160,128,128]{2,1,0:T(8,128)(2,1)} %gather_fusion.3, s32[1,1,160,128,128]{4,3,2,1,0:T(8,128)} %param.4, f32[160,128]{1,0:T(8,128)S(1)} %maximum_log_fusion, f32[160,128]{1,0:T(8,128)S(1)} %maximum_log_fusion.1, f32[]{:T(128)S(6)} %sub.19), kind=kOutput, calls=%fused_computation.28 | convolution fusion | flops 694681600 | bytes 26378244 | tf_op jit(solution)/shard_map/nji,njk->nik/dot_general | solution.py:54
  512.6 4.4 broadcast_in_dim.23
  517.0 33.3 %scatter_fusion.1 = f32[128,128,128]{2,1,0:T(8,128)} fusion(f32[128,128,128]{2,1,0:T(8,128)} %broadcast_in_dim.23, s32[160]{0:T(256)S(1)} %bitcast.37, f32[160,128,128]{2,1,0:T(8,128)} %fusion.11), kind=kCustom, calls=%fused_computation.7 | custom fusion | flops 2621440 | bytes 31457920 | tf_op jit(solution)/shard_map/scatter-add | solution.py:57
  550.3 0.0 reduce-scatter.5.cloned.1.call-update
  550.3 84.9 %reduce-scatter.5.cloned.1.call-done = f32[4096,128]{1,0:T(8,128)} async-done(((f32[16384,128]{1,0:T(8,128)}), f32[4096,128]{1,0:T(8,128)}) %reduce-scatter.5.cloned.1.call-update) | async-done | bytes 2097168 | tf_op jit(solution)/shard_map/reduce_scatter | solution.py:60
  635.2 3.0 broadcast_multiply_fusion
  (6 shorter events, 0.1 us)
Async XLA Ops:
  7.2 6.8 %copy-start.1 = (s32[1,1,160]{2,1,0:T(1,128)S(1)}, s32[1,1,160]{2,1,0:T(1,128)}, u32[]{:S(2)}) copy-start(s32[1,1,160]{2,1,0:T(1,128)} %param.6) | copy-start | bytes 1924
  7.2 8.6 %copy-start = (s32[1,1,160]{2,1,0:T(1,128)S(1)}, s32[1,1,160]{2,1,0:T(1,128)}, u32[]{:S(2)}) copy-start(s32[1,1,160]{2,1,0:T(1,128)} %param.5) | copy-start | bytes 1924
  7.2 52.9 %all-reduce.3.cloned.1.call-start = ((), (), s32[]{:S(2)}) async-start(), calls=%async_computation.2 | async-start | bytes 131072 | tf_op jit(solution)/shard_map/psum | solution.py:40
  15.7 101.6 %all-reduce.5.cloned.1.call-start = ((), (), s32[]{:S(2)}) async-start(), calls=%async_computation.3 | async-start | bytes 262144 | tf_op jit(solution)/shard_map/psum | solution.py:43
  17.6 153.3 %all-gather.3.cloned.1.call-start = ((), (), s32[]{:S(2)}) async-start(), calls=%async_computation.4 | async-start | bytes 5242880 | tf_op jit(solution)/shard_map/all_gather | solution.py:32
  18.3 384.8 %reduce-scatter.3.cloned.1.call-start = ((), (), s32[]{:S(2)}) async-start(), calls=%async_computation.5 | async-start | bytes 18874368 | tf_op jit(solution)/shard_map/reduce_scatter | solution.py:51
  234.7 251.7 %all-gather.5.cloned.1.call-start = ((), (), s32[]{:S(2)}) async-start(), calls=%async_computation.6 | async-start | bytes 9437184 | tf_op jit(solution)/shard_map/all_gather | solution.py:52
  405.8 229.4 %reduce-scatter.5.cloned.1.call-start = ((), (), s32[]{:S(2)}) async-start(), calls=%async_computation.7 | async-start | bytes 10485760 | tf_op jit(solution)/shard_map/reduce_scatter | solution.py:60
Sparse Core Ops, SparseCore 0:
  15.9 44.1 all-reduce.2
  63.0 54.1 all-reduce.4
  119.1 51.6 all-gather.2
  234.8 168.2 reduce-scatter.2
  405.9 80.4 all-gather.4
  550.5 84.7 reduce-scatter.4
where the time goes:
time: 646 us; the launch traced here: 645 us
  waiting for transfers between devices  466 us (72%)
  other arithmetic  84 us (13%)
  local copies, waits for them, and re-layouts  35.5 us (5%)
  matrix products  27.9 us (4%)
  blocking collectives  16.6 us (3%)
  between operations  14.9 us (2%)
    reduce_scatter x1, waiting for transfers between devices, shards(): lax.psum_scatter(word_partial, 'col', scatter_dimension=0, tiled=True)  168 us
    reduce_scatter x1, waiting for transfers between devices, shards(): lax.psum_scatter(context_partial, 'row', scatter_dimension=0, tiled=True)  84.9 us
    all_gather x1, waiting for transfers between devices, shards(): lax.all_gather(word_share.astype(jnp.bfloat16), 'col', axis=0, tiled=True)  80.3 us
    all_gather x1, waiting for transfers between devices, shards(): panel_band = lax.all_gather(panel, 'row', axis=0, tiled=True)  52 us
    psum x1, waiting for transfers between devices, shards(): context_totals = lax.psum(context_part, 'row')  41.7 us
    psum x1, waiting for transfers between devices, shards(): row_totals = lax.psum(word_part, 'col')  37.8 us
    scatter-add x1, other arithmetic, shards(): jax.ops.segment_sum(context_product, context_cols, num_segments=band_cols)  33.3 us
    scatter-add x1, other arithmetic, shards(): jax.ops.segment_sum(product, word_rows, num_segments=band_rows)  33.2 us
  transfers between devices with their start and end apart: 6, of which 6 were waited for; matrix products, arithmetic and copies ran while one was open for 1% of the time, Pallas kernels for 0%

commit v1 on v0

v1 whole, which is shorter than its diff:
```python
import functools
import math

import jax
import jax.numpy as jnp
from jax import lax
from jax.experimental import pallas as pl
from jax.experimental.pallas import tpu as pltpu
from jax.sharding import PartitionSpec as P

NEG_SAMPLES = 15
CHUNKS = 2
VMEM = 48 * 2**20
F32 = jnp.float32
BF16 = jnp.bfloat16


def params(**kwargs):
    return pltpu.CompilerParams(vmem_limit_bytes=VMEM, **kwargs)


def whole(shape):
    return pl.BlockSpec(shape, lambda *_: (0,) * len(shape))


ANY = pl.BlockSpec(memory_space=pl.ANY)


def cost(flops, moved):
    return pl.CostEstimate(flops=flops, bytes_accessed=moved, transcendentals=0)


def count_sums(counts, rows, cols, band_rows, band_cols):
    slots, tile, _ = counts.shape
    step = math.gcd(slots, 16)

    def kernel(rows_ref, cols_ref, counts_ref, word_ref, context_ref):
        at = pl.program_id(0)

        @pl.when(at == 0)
        def _():
            word_ref[...] = jnp.zeros_like(word_ref)
            context_ref[...] = jnp.zeros_like(context_ref)

        weights = jnp.concatenate(
            [jnp.full((8, tile), 32.0, BF16), jnp.ones((8, tile), BF16)], axis=1
        )
        for n in range(step):
            tile_counts = counts_ref[n]
            high = (tile_counts >> 5).astype(F32).astype(BF16)
            low = (tile_counts & 31).astype(F32).astype(BF16)
            context = jnp.dot(
                weights, jnp.concatenate([high, low], axis=0), preferred_element_type=F32
            )
            word = lax.dot_general(
                weights,
                jnp.concatenate([high, low], axis=1),
                (((1,), (1,)), ((), ())),
                preferred_element_type=F32,
            )
            row, col = rows_ref[at * step + n], cols_ref[at * step + n]
            word_ref[pl.ds(row, 1), :] += word[:1]
            context_ref[pl.ds(col, 1), :] += context[:1]

    return pl.pallas_call(
        kernel,
        grid_spec=pltpu.PrefetchScalarGridSpec(
            num_scalar_prefetch=2,
            grid=(slots // step,),
            in_specs=[pl.BlockSpec((step, tile, tile), lambda n, *_: (n, 0, 0))],
            out_specs=[whole((band_rows, tile)), whole((band_cols, tile))],
        ),
        out_shape=[
            jax.ShapeDtypeStruct((band_rows, tile), F32),
            jax.ShapeDtypeStruct((band_cols, tile), F32),
        ],
        compiler_params=params(),
        cost_estimate=cost(0, 4 * counts.size),
        name="count_sums",
    )(rows, cols, counts)


def smoothed(word_part, context_a, context_b):
    band_rows, tile = word_part.shape
    band_cols = context_a.shape[0]

    def kernel(word_ref, a_ref, b_ref, bundle_ref, log_ref):
        total = a_ref[...] + b_ref[...]
        root = jnp.sqrt(total)
        powers = root * jnp.sqrt(root)
        bundle_ref[:band_rows, :] = word_ref[...]
        bundle_ref[band_rows:, :] = jnp.sum(powers.reshape(band_cols // 8, 8, tile), axis=0)
        log_ref[...] = jnp.maximum(0.75 * jnp.log(total), 0.0)

    return pl.pallas_call(
        kernel,
        out_shape=[
            jax.ShapeDtypeStruct((band_rows + 8, tile), F32),
            jax.ShapeDtypeStruct((band_cols, tile), F32),
        ],
        compiler_params=params(),
        name="smoothed",
    )(word_part, context_a, context_b)


def ppmi(counts, rows, cols, bundle_a, bundle_b, context_log):
    slots, tile, _ = counts.shape
    band_rows = bundle_a.shape[0] - 8
    step = math.gcd(slots, 16)

    def kernel(rows_ref, cols_ref, counts_ref, a_ref, b_ref, log_ref, out_ref, word_log, shift):
        at = pl.program_id(0)

        @pl.when(at == 0)
        def _():
            totals = a_ref[:band_rows, :] + b_ref[:band_rows, :]
            word_log[...] = jnp.log(jnp.maximum(totals, 1.0))
            power = jnp.sum(a_ref[band_rows:, :] + b_ref[band_rows:, :], axis=0, keepdims=True)
            power = jnp.sum(power, axis=1, keepdims=True)
            shift[...] = (jnp.log(power) - math.log(NEG_SAMPLES)) - log_ref[...]

        for n in range(step):
            row, col = rows_ref[at * step + n], cols_ref[at * step + n]
            word = jnp.broadcast_to(word_log[pl.ds(row, 1), :], (tile, tile)).T
            logs = jnp.log(counts_ref[n].astype(F32))
            pointwise = logs + (shift[pl.ds(col, 1), :] - word)
            out_ref[n] = jnp.maximum(pointwise, 0.0).astype(BF16)

    return pl.pallas_call(
        kernel,
        grid_spec=pltpu.PrefetchScalarGridSpec(
            num_scalar_prefetch=2,
            grid=(slots // step,),
            in_specs=[
                pl.BlockSpec((step, tile, tile), lambda n, *_: (n, 0, 0)),
                whole(bundle_a.shape),
                whole(bundle_a.shape),
                whole(context_log.shape),
            ],
            out_specs=pl.BlockSpec((step, tile, tile), lambda n, *_: (n, 0, 0)),
            scratch_shapes=[
                pltpu.VMEM((band_rows, tile), F32),
                pltpu.VMEM(context_log.shape, F32),
            ],
        ),
        out_shape=jax.ShapeDtypeStruct(counts.shape, BF16),
        compiler_params=params(),
        cost_estimate=cost(0, 6 * counts.size),
        name="ppmi",
    )(rows, cols, counts, bundle_a, bundle_b, context_log)


def turn_panel(panel, tile):
    blocks, width = panel.shape[0] // tile, panel.shape[1]
    part = width // CHUNKS

    def kernel(in_ref, *out_refs):
        for n in range(blocks):
            turned = in_ref[n * tile : (n + 1) * tile, :].astype(F32).T.astype(BF16)
            for chunk, out_ref in enumerate(out_refs):
                out_ref[n] = turned[chunk * part : (chunk + 1) * part]

    return pl.pallas_call(
        kernel,
        out_shape=[jax.ShapeDtypeStruct((blocks, part, tile), BF16)] * CHUNKS,
        compiler_params=params(),
        name="turn_panel",
    )(panel)


def word_products(tiles, place, rows, cols, blocks, chips):
    slots, tile, _ = tiles.shape
    share, part, _ = blocks[0].shape
    slot_count, block_rows = 2 * chips - 1, place["block_rows"]
    step = math.gcd(slots, 32)
    grid = slots // step
    n_in = len(blocks)

    def kernel(rows_ref, cols_ref, valid_ref, tiles_ref, *refs):
        block_refs, outs = refs[:n_in], refs[n_in : n_in + slot_count]
        acc, band, sems = refs[n_in + slot_count :]
        at = pl.program_id(0)

        @pl.when(at == 0)
        def _():
            copies = [
                pltpu.make_async_copy(ref, band.at[pl.ds(n * share, share)], sems.at[n])
                for n, ref in enumerate(block_refs)
            ]
            for copy in copies:
                copy.start()
            for slot in range(slot_count):

                @pl.when(valid_ref[slot] == 1)
                def _():
                    acc[slot * block_rows : (slot + 1) * block_rows] = jnp.zeros(
                        (block_rows, part, tile), F32
                    )

            for copy in copies:
                copy.wait()

        for n in range(step):
            row, col = rows_ref[at * step + n], cols_ref[at * step + n]
            acc[row] += lax.dot_general(
                band[col], tiles_ref[n], (((1,), (1,)), ((), ())), preferred_element_type=F32
            )

        @pl.when(at == grid - 1)
        def _():
            for slot, out in enumerate(outs):

                @pl.when(valid_ref[slot] == 1)
                def _():
                    out[...] = acc[slot * block_rows : (slot + 1) * block_rows].astype(out.dtype)

    shape = (block_rows, part, tile)
    types = [BF16] * (chips - 1) + [F32] * chips
    outs = pl.pallas_call(
        kernel,
        grid_spec=pltpu.PrefetchScalarGridSpec(
            num_scalar_prefetch=3,
            grid=(grid,),
            in_specs=[pl.BlockSpec((step, tile, tile), lambda n, *_: (n, 0, 0))] + [ANY] * n_in,
            out_specs=[whole(shape)] * slot_count,
            scratch_shapes=[
                pltpu.VMEM((slot_count * block_rows, part, tile), F32),
                pltpu.VMEM((n_in * share, part, tile), BF16),
                pltpu.SemaphoreType.DMA((n_in,)),
            ],
        ),
        out_shape=[jax.ShapeDtypeStruct(shape, kind) for kind in types],
        compiler_params=params(),
        cost_estimate=cost(2 * slots * part * tile * tile, 2 * tiles.size + 4 * 2**20),
        name="word_products",
    )(rows, cols, place["valid"], tiles, *blocks)
    given = {distance: outs[chips - 1 - distance] for distance in range(1, chips)}
    kept = {distance: outs[chips - 1 + distance] for distance in range(1, chips)}
    return given, outs[chips - 1], kept


def context_products(tiles, place, rows, cols, blocks, band_cols):
    slots, tile, _ = tiles.shape
    block_rows, part, _ = blocks[0].shape
    slot_count = len(blocks)
    step = math.gcd(slots, 32)
    grid = slots // step
    half = band_cols // 2

    def kernel(rows_ref, cols_ref, valid_ref, tiles_ref, *refs):
        block_refs, (send, keep) = refs[:slot_count], refs[slot_count : slot_count + 2]
        acc, band, sems = refs[slot_count + 2 :]
        at = pl.program_id(0)

        @pl.when(at == 0)
        def _():
            for begin in (True, False):
                for slot, ref in enumerate(block_refs):

                    @pl.when(valid_ref[slot] == 1)
                    def _():
                        copy = pltpu.make_async_copy(
                            ref, band.at[pl.ds(slot * block_rows, block_rows)], sems.at[slot]
                        )
                        if begin:
                            copy.start()
                        else:
                            copy.wait()

                if begin:
                    acc[...] = jnp.zeros_like(acc)

        for n in range(step):
            row, col = rows_ref[at * step + n], cols_ref[at * step + n]
            acc[col] += jnp.dot(band[row], tiles_ref[n], preferred_element_type=F32)

        @pl.when(at == grid - 1)
        def _():
            send[...] = acc[half:].astype(BF16)
            keep[...] = acc[:half]

    shape = (half, part, tile)
    return pl.pallas_call(
        kernel,
        grid_spec=pltpu.PrefetchScalarGridSpec(
            num_scalar_prefetch=3,
            grid=(grid,),
            in_specs=[pl.BlockSpec((step, tile, tile), lambda n, *_: (n, 0, 0))]
            + [ANY] * slot_count,
            out_specs=[whole(shape)] * 2,
            scratch_shapes=[
                pltpu.VMEM((band_cols, part, tile), F32),
                pltpu.VMEM((slot_count * block_rows, part, tile), BF16),
                pltpu.SemaphoreType.DMA((slot_count,)),
            ],
        ),
        out_shape=[jax.ShapeDtypeStruct(shape, BF16), jax.ShapeDtypeStruct(shape, F32)],
        compiler_params=params(),
        cost_estimate=cost(2 * slots * part * tile * tile, 2 * tiles.size + 4 * 2**20),
        name="context_products",
    )(rows, cols, place["valid"], tiles, *blocks)


def turn_back(chunks, scale):
    blocks, part, tile = chunks[0][0].shape
    terms = [term for chunk in chunks for term in chunk]
    width = part * len(chunks)
    step = math.gcd(blocks, 8)

    def kernel(*refs):
        out_ref, reads = refs[-1], list(refs[:-1])
        for n in range(step):
            pieces, at = [], 0
            for chunk in chunks:
                pieces.append(sum(ref[n].astype(F32) for ref in reads[at : at + len(chunk)]))
                at += len(chunk)
            out_ref[n * tile : (n + 1) * tile, :] = jnp.concatenate(pieces, axis=0).T * scale

    return pl.pallas_call(
        kernel,
        grid=(blocks // step,),
        in_specs=[pl.BlockSpec((step, part, tile), lambda n: (n, 0, 0))] * len(terms),
        out_specs=pl.BlockSpec((step * tile, width), lambda n: (n, 0)),
        out_shape=jax.ShapeDtypeStruct((blocks * tile, width), F32),
        compiler_params=params(),
        cost_estimate=cost(0, 8 * blocks * tile * width),
        name="turn_back",
    )(*terms)


def shards(n_row, n_col, tile_counts, tile_rows, tile_cols, panel):
    counts, rows, cols = tile_counts[0, 0], tile_rows[0, 0], tile_cols[0, 0]
    tile = counts.shape[-1]
    share = panel.shape[0] // tile
    band_rows, band_cols = share * n_col, share * n_row
    chips, bits = n_col // 2, n_row.bit_length() - 1
    block_rows = 2 * share
    my_row, my_col = lax.axis_index("row"), lax.axis_index("col")
    chip, core = my_col // 2, my_col % 2

    def row_swap(x, step):
        pairs = []
        for r in range(n_row):
            for c in range(n_col):
                bit = step if c % 2 == 0 else bits - 1 - step
                pairs.append((r * n_col + c, (r ^ (1 << bit)) * n_col + c))
        return lax.ppermute(x, ("row", "col"), pairs)

    def core_swap(x, keep=lambda c, z: True):
        return lax.ppermute(
            x, "col", [(i, i ^ 1) for i in range(n_col) if keep(i % 2, i // 2)]
        )

    def along(x, keep):
        pairs = []
        for z in range(chips - 1):
            if keep(z):
                pairs.append((2 * z, 2 * z + 2))
                pairs.append((2 * (chips - 1 - z) + 1, 2 * (chips - 2 - z) + 1))
        return lax.ppermute(x, "col", pairs)

    distance = (rows // block_rows - chip) * jnp.where(core == 0, 1, -1)
    row_place = (distance + chips - 1) * block_rows + rows % block_rows
    slot_chip = (jnp.arange(2 * chips - 1) - (chips - 1)) * jnp.where(core == 0, 1, -1) + chip
    place = {
        "block_rows": block_rows,
        "valid": ((slot_chip >= 0) & (slot_chip < chips)).astype(jnp.int32),
    }
    differ = (cols // share) ^ my_row
    turned = sum(((differ >> b) & 1) << (bits - 1 - b) for b in range(bits))
    col_place = jnp.where(core == 0, turned, differ) * share + cols % share

    panel_parts = turn_panel(panel, tile)
    panel_blocks = []
    for part in panel_parts:
        blocks = {0: part}
        for step in range(bits):
            blocks.update(
                {
                    at | (1 << (bits - 1 - step)): row_swap(block, step)
                    for at, block in list(blocks.items())
                }
            )
        panel_blocks.append([blocks[at] for at in range(n_row)])

    word_part, context = count_sums(counts, rows, cols, band_rows, band_cols)
    for step in range(bits - 1):
        context = context + row_swap(context, step)
    bundle, context_log = smoothed(word_part, context, row_swap(context, bits - 1))
    bundle = bundle + core_swap(bundle)
    other = None
    for step in range(chips.bit_length() - 1):
        if other is not None:
            bundle = bundle + other
        other = lax.ppermute(bundle, "col", [(i, i ^ (2 << step)) for i in range(n_col)])
    tiles = ppmi(counts, rows, cols, bundle, other, context_log)

    word_chunks, context_chunks = [], []
    for chunk in range(CHUNKS):
        given, mine, kept = word_products(
            tiles, place, row_place, col_place, panel_blocks[chunk], chips
        )
        got = None
        for step in range(1, chips):
            far = chips - step
            passed = core_swap(
                given[far], lambda c, z, far=far: z >= far if c == 0 else z < chips - far
            )
            total = kept[far] + passed.astype(F32)
            if got is not None:
                total = total + got.astype(F32)
            got = along(total.astype(BF16), lambda z, step=step: z <= step - 1)
        mine = mine + got.astype(F32)
        mine = mine + core_swap(mine)
        word_chunks.append([lax.dynamic_slice_in_dim(mine, core * share, share)])
        rounded = mine.astype(BF16)
        near, swapped, block = [], [], rounded
        for step in range(1, chips):
            block = along(block, lambda z, step=step: z >= step - 1)
            near.append(block)
            swapped.append(core_swap(block))
        blocks = near[::-1] + [rounded] + swapped
        send, keep = context_products(tiles, place, row_place, col_place, blocks, band_cols)
        for step in range(bits):
            got = row_swap(send, step)
            if step < bits - 1:
                keep = keep + got.astype(F32)
                half = keep.shape[0] // 2
                send, keep = keep[half:].astype(BF16), keep[:half]
        context_chunks.append([keep, got])
    return turn_back(word_chunks, 1.0), turn_back(context_chunks, 1.0 / tile)


def solution(mesh):
    in_specs = (
        P("row", "col", None, None, None),
        P("row", "col", None),
        P("row", "col", None),
        P(("col", "row"), None),
    )
    out_specs = (P(("row", "col"), None), P(("col", "row"), None))
    body = functools.partial(shards, mesh.shape["row"], mesh.shape["col"])
    return jax.shard_map(body, mesh=mesh, in_specs=in_specs, out_specs=out_specs, check_vma=False)
```

time: 646 us -> 287 us (0.44)
  waiting for transfers between devices: 466 us -> 89.3 us
  starting transfers between devices: 0.42 us -> 105 us
  other arithmetic: 84 us -> 7.79 us
  Pallas kernels: 0 us -> 66.1 us
  matrix products: 27.9 us -> 0 us
  local copies, waits for them, and re-layouts: 35.5 us -> 16 us
  blocking collectives: 16.6 us -> 0 us
  between operations: 14.9 us -> 1.21 us
    reduce_scatter x2 -> x0, waiting for transfers between devices: 253 us -> none  [the longest x1 168 us: shards(): lax.psum_scatter(word_partial, 'col', scatter_dimension=0, tiled=True)]
    all_gather x2 -> x0, waiting for transfers between devices: 132 us -> none  [the longest x1 80.3 us: shards(): lax.all_gather(word_share.astype(jnp.bfloat16), 'col', axis=0, tiled=True)]
    ppermute x0 -> x41, starting transfers between devices: none -> 105 us  [the longest x15 50.9 us: core_swap(): lax.ppermute(x, 'col', [(i, i ^ 1) for i in range(n_col) if keep(i % 2, i...]
    ppermute x0 -> x41, waiting for transfers between devices: none -> 89.3 us  [the longest x12 59.5 us: along(): return lax.ppermute(x, 'col', pairs)]
    psum x2 -> x0, waiting for transfers between devices: 79.4 us -> none  [the longest x1 41.7 us: shards(): context_totals = lax.psum(context_part, 'row')]
    scatter-add x4 -> x0, other arithmetic: 70 us -> none  [the longest x1 33.3 us: shards(): jax.ops.segment_sum(context_product, context_cols, num_segments=band_cols)]
    pallas_call x0 -> x10, Pallas kernels: none -> 66.1 us  [the longest x2 23.3 us: word_products(): pl.pallas_call(kernel, grid_spec=pltpu.PrefetchScalarGridSpec(num_scalar_...]
    dot_general x2 -> x0, matrix products: 27.9 us -> none  [the longest x1 15.1 us: shards(): jnp.einsum('nji,njk->nik', tiles, word_picked, preferred_element_type=jnp...]
  transfers between devices with their start and end apart: 6 -> 41, of which waited for: 6 -> 15; matrix products, arithmetic and copies ran while one was open for 1% -> 4% of each run, Pallas kernels for 0% -> 22%
where the time goes in v1:
time: 287 us; the launch traced here: 286 us
  starting transfers between devices  105 us (37%)
  waiting for transfers between devices  89.3 us (31%)
  Pallas kernels  66.1 us (23%)
  local copies, waits for them, and re-layouts  16 us (6%)
  other arithmetic  7.79 us (3%)
    ppermute x12, waiting for transfers between devices, along(): return lax.ppermute(x, 'col', pairs)  59.5 us
    ppermute x15, starting transfers between devices, core_swap(): lax.ppermute(x, 'col', [(i, i ^ 1) for i in range(n_col) if keep(i % 2, i...  50.9 us
    ppermute x12, starting transfers between devices, along(): return lax.ppermute(x, 'col', pairs)  31.8 us
    ppermute x12, waiting for transfers between devices, row_swap(): return lax.ppermute(x, ('row', 'col'), pairs)  23.4 us
    pallas_call x2, Pallas kernels, word_products(): pl.pallas_call(kernel, grid_spec=pltpu.PrefetchScalarGridSpec(num_scalar_...  23.3 us
    pallas_call x2, Pallas kernels, context_products(): pl.pallas_call(kernel, grid_spec=pltpu.PrefetchScalarGridSpec(num_scalar_...  18.3 us
    ppermute x12, starting transfers between devices, row_swap(): return lax.ppermute(x, ('row', 'col'), pairs)  17.8 us
    unnamed x50, local copies, waits for them, and re-layouts  12.5 us
  transfers between devices with their start and end apart: 41, of which 15 were waited for; matrix products, arithmetic and copies ran while one was open for 4% of the time, Pallas kernels for 22%

profile of v1, /device:TPU:0, one launch (start us, length us, event | category | flops | bytes accessed | tf_op | source)
XLA Modules:
  0.0 285.8 jit_solution(17678859636151571822)
XLA Ops:
  0.6 1.2 copy-done.1
  2.2 3.0 %collective-permute-start.6 = (bf16[32,64,128]{2,1,0:T(8,128)(2,1)S(1)}, bf16[32,64,128]{2,1,0:T(8,128)(2,1)S(1)}, u32[]{:S(2)}, u32[]{:S(2)}) collective-permute-start(bf16[32,64,128]{2,1,0:T(8,128)(2,1)S(1)} %get-tuple-element.30.refs_0_), channel_id=1, source_target_pairs={{0,8},{1,17},{2,10},{3,19},{4,12},{5,21},{6,14},{7,23},{8,0},{9,25... | collective-permute-start | bytes 1572872 | tf_op jit(solution)/shard_map/ppermute | solution.py:347
  6.6 10.3 %count_sums.1 = (f32[256,128]{1,0:T(8,128)S(1)}, f32[128,128]{1,0:T(8,128)S(1)}) custom-call(s32[160]{0:T(256)S(1)} %bitcast.3, s32[160]{0:T(256)S(1)} %bitcast.6, s32[160,128,128]{2,1,0:T(8,128)} %bitcast.9), custom_call_target="tpu_custom_call" | custom-call | bytes 10485760 | tf_op jit(solution)/shard_map/count_sums/pallas_call | solution.py:65
  17.0 2.0 collective-permute-start
  19.0 2.3 collective-permute-done
  21.3 2.0 collective-permute-start.1
  23.4 2.3 collective-permute-done.1.b_ref
  25.8 2.0 collective-permute-start.5
  28.0 2.1 collective-permute-start.3
  30.0 1.5 collective-permute-start.15
  31.5 2.1 collective-permute-done.3
  33.7 2.8 collective-permute-start.4
  36.5 1.5 collective-permute-start.17
  38.0 4.3 %collective-permute-done.4.b_ref = f32[264,128]{1,0:T(8,128)S(1)} collective-permute-done((f32[264,128]{1,0:T(8,128)S(1)}, f32[264,128]{1,0:T(8,128)S(1)}, u32[]{:S(2)}, u32[]{:S(2)}) %collective-permute-start.4) | collective-permute-done | bytes 135200 | tf_op jit(solution)/shard_map/ppermute | solution.py:395
  42.3 9.2 %ppmi.1.tiles_ref = bf16[160,128,128]{2,1,0:T(8,128)(2,1)S(1)} custom-call(s32[160]{0:T(256)S(1)} %bitcast.5, s32[160]{0:T(256)S(1)} %bitcast.8, s32[160,128,128]{2,1,0:T(8,128)} %bitcast.10, f32[264,128]{1,0:T(8,128)S(1)} %add.109.a_ref, f32[264,128]{1,0:T(8,128)S(1)} %collective-permute-done.4.b_ref, f32[128,128]{1,0:T(8,128)S(1)} %get-tuple-element.29.log_ref), custom_call_target="tpu_custom_call" | custom-call | bytes 15728640 | tf_op jit(solution)/shard_map/ppmi/pallas_call | solution.py:129
  51.6 2.3 copy-done
  53.9 11.9 %word_products.2 = (bf16[64,64,128]{2,1,0:T(8,128)(2,1)S(1)}, bf16[64,64,128]{2,1,0:T(8,128)(2,1)S(1)}, bf16[64,64,128]{2,1,0:T(8,128)(2,1)S(1)}, f32[64,64,128]...) custom-call(s32[160]{0:T(256)S(1)} %get-tuple-element.54.rows_ref, ...), custom_call_target="tpu_custom_call" | custom-call | flops 335544320 | bytes 9437184 | tf_op jit(solution)/shard_map/word_products/pallas_call | solution.py:219
  65.9 1.4 collective-permute-start.10
  67.3 11.4 %word_products.3 = (bf16[64,64,128]{2,1,0:T(8,128)(2,1)S(1)}, bf16[64,64,128]{2,1,0:T(8,128)(2,1)S(1)}, bf16[64,64,128]{2,1,0:T(8,128)(2,1)S(1)}, f32[64,64,128]...) custom-call(s32[160]{0:T(256)S(1)} %get-tuple-element.54.rows_ref, ...), custom_call_target="tpu_custom_call" | custom-call | flops 335544320 | bytes 9437184 | tf_op jit(solution)/shard_map/word_products/pallas_call | solution.py:219
  78.7 1.3 collective-permute-start.20
  80.0 1.3 collective-permute-start.9
  81.7 1.5 collective-permute-start.11
  83.2 1.3 collective-permute-start.19
  84.8 1.5 collective-permute-start.21
  86.3 1.3 collective-permute-start.8
  87.7 7.7 %collective-permute-done.11 = bf16[64,64,128]{2,1,0:T(8,128)(2,1)S(1)} collective-permute-done((bf16[64,64,128]{2,1,0:T(8,128)(2,1)S(1)}, bf16[64,64,128]{2,1,0:T(8,128)(2,1)S(1)}, u32[]{:S(2)}, u32[]{:S(2)}) %collective-permute-start.11) | collective-permute-done | bytes 1048608 | tf_op jit(solution)/shard_map/ppermute | solution.py:360
  95.9 4.6 %collective-permute-start.12 = (bf16[64,64,128]{2,1,0:T(8,128)(2,1)S(1)}, bf16[64,64,128]{2,1,0:T(8,128)(2,1)S(1)}, u32[]{:S(2)}, u32[]{:S(2)}) collective-permute-start(bf16[64,64,128]{2,1,0:T(8,128)(2,1)S(1)} %add_convert_fusion.4), channel_id=1, source_target_pairs={{0,2},{7,5},{2,4},{5,3},{8,10},{15,13},{10,12},{13,11},{16,18},{23... | collective-permute-start | bytes 3145736 | tf_op jit(solution)/shard_map/ppermute | solution.py:360
  100.5 1.3 collective-permute-start.18
  101.8 4.8 %collective-permute-done.21 = bf16[64,64,128]{2,1,0:T(8,128)(2,1)S(1)} collective-permute-done((bf16[64,64,128]{2,1,0:T(8,128)(2,1)S(1)}, bf16[64,64,128]{2,1,0:T(8,128)(2,1)S(1)}, u32[]{:S(2)}, u32[]{:S(2)}) %collective-permute-start.21) | collective-permute-done | bytes 1048608 | tf_op jit(solution)/shard_map/ppermute | solution.py:360
  107.2 4.6 %collective-permute-start.22 = (bf16[64,64,128]{2,1,0:T(8,128)(2,1)S(1)}, bf16[64,64,128]{2,1,0:T(8,128)(2,1)S(1)}, u32[]{:S(2)}, u32[]{:S(2)}) collective-permute-start(bf16[64,64,128]{2,1,0:T(8,128)(2,1)S(1)} %add_convert_fusion.1), channel_id=1, source_target_pairs={{0,2},{7,5},{2,4},{5,3},{8,10},{15,13},{10,12},{13,11},{16,18},{23... | collective-permute-start | bytes 3145736 | tf_op jit(solution)/shard_map/ppermute | solution.py:360
  111.8 6.1 %collective-permute-done.12 = bf16[64,64,128]{2,1,0:T(8,128)(2,1)S(1)} collective-permute-done((bf16[64,64,128]{2,1,0:T(8,128)(2,1)S(1)}, bf16[64,64,128]{2,1,0:T(8,128)(2,1)S(1)}, u32[]{:S(2)}, u32[]{:S(2)}) %collective-permute-start.12) | collective-permute-done | bytes 1048608 | tf_op jit(solution)/shard_map/ppermute | solution.py:360
  118.4 4.8 %collective-permute-start.13 = (bf16[64,64,128]{2,1,0:T(8,128)(2,1)S(1)}, bf16[64,64,128]{2,1,0:T(8,128)(2,1)S(1)}, u32[]{:S(2)}, u32[]{:S(2)}) collective-permute-start(bf16[64,64,128]{2,1,0:T(8,128)(2,1)S(1)} %add_convert_fusion.3), channel_id=1, source_target_pairs={{0,2},{7,5},{2,4},{5,3},{4,6},{3,1},{8,10},{15,13},{10,12},{13,11}... | collective-permute-start | bytes 3145736 | tf_op jit(solution)/shard_map/ppermute | solution.py:360
  123.2 5.9 %collective-permute-done.22 = bf16[64,64,128]{2,1,0:T(8,128)(2,1)S(1)} collective-permute-done((bf16[64,64,128]{2,1,0:T(8,128)(2,1)S(1)}, bf16[64,64,128]{2,1,0:T(8,128)(2,1)S(1)}, u32[]{:S(2)}, u32[]{:S(2)}) %collective-permute-start.22) | collective-permute-done | bytes 1048608 | tf_op jit(solution)/shard_map/ppermute | solution.py:360
  129.6 4.6 %collective-permute-start.23 = (bf16[64,64,128]{2,1,0:T(8,128)(2,1)S(1)}, bf16[64,64,128]{2,1,0:T(8,128)(2,1)S(1)}, u32[]{:S(2)}, u32[]{:S(2)}) collective-permute-start(bf16[64,64,128]{2,1,0:T(8,128)(2,1)S(1)} %add_convert_fusion), channel_id=1, source_target_pairs={{0,2},{7,5},{2,4},{5,3},{4,6},{3,1},{8,10},{15,13},{10,12},{13,11}... | collective-permute-start | bytes 3145736 | tf_op jit(solution)/shard_map/ppermute | solution.py:360
  134.2 6.1 %collective-permute-done.13 = bf16[64,64,128]{2,1,0:T(8,128)(2,1)S(1)} collective-permute-done((bf16[64,64,128]{2,1,0:T(8,128)(2,1)S(1)}, bf16[64,64,128]{2,1,0:T(8,128)(2,1)S(1)}, u32[]{:S(2)}, u32[]{:S(2)}) %collective-permute-start.13) | collective-permute-done | bytes 1048608 | tf_op jit(solution)/shard_map/ppermute | solution.py:360
  140.7 10.8 %collective-permute-done.23 = bf16[64,64,128]{2,1,0:T(8,128)(2,1)S(1)} collective-permute-done((bf16[64,64,128]{2,1,0:T(8,128)(2,1)S(1)}, bf16[64,64,128]{2,1,0:T(8,128)(2,1)S(1)}, u32[]{:S(2)}, u32[]{:S(2)}) %collective-permute-start.23) | collective-permute-done | bytes 1048608 | tf_op jit(solution)/shard_map/ppermute | solution.py:360
  152.1 1.8 fusion.3
  153.9 4.4 %collective-permute-start.25 = (bf16[64,64,128]{2,1,0:T(8,128)(2,1)S(1)}, bf16[64,64,128]{2,1,0:T(8,128)(2,1)S(1)}, u32[]{:S(2)}, u32[]{:S(2)}) collective-permute-start(bf16[64,64,128]{2,1,0:T(8,128)(2,1)S(1)} %get-tuple-element.52.refs_3_), channel_id=1, source_target_pairs={{0,2},{7,5},{2,4},{5,3},{4,6},{3,1},{8,10},{15,13},{10,12},{13,11}... | collective-permute-start | bytes 3145736 | tf_op jit(solution)/shard_map/ppermute | solution.py:360
  158.4 1.8 fusion.2
  160.2 3.0 %collective-permute-start.33 = (bf16[64,64,128]{2,1,0:T(8,128)(2,1)S(1)}, bf16[64,64,128]{2,1,0:T(8,128)(2,1)S(1)}, u32[]{:S(2)}, u32[]{:S(2)}) collective-permute-start(bf16[64,64,128]{2,1,0:T(8,128)(2,1)S(1)} %get-tuple-element.50.refs_3_), channel_id=1, source_target_pairs={{0,2},{7,5},{2,4},{5,3},{4,6},{3,1},{8,10},{15,13},{10,12},{13,11}... | collective-permute-start | bytes 3145736 | tf_op jit(solution)/shard_map/ppermute | solution.py:360
  163.2 7.4 %collective-permute-done.25.refs_2_ = bf16[64,64,128]{2,1,0:T(8,128)(2,1)S(1)} collective-permute-done((bf16[64,64,128]{2,1,0:T(8,128)(2,1)S(1)}, bf16[64,64,128]{2,1,0:T(8,128)(2,1)S(1)}, u32[]{:S(2)}, u32[]{:S(2)}) %collective-permute-start.25) | collective-permute-done | bytes 1048608 | tf_op jit(solution)/shard_map/ppermute | solution.py:360
  171.3 10.5 %collective-permute-done.33.refs_2_ = bf16[64,64,128]{2,1,0:T(8,128)(2,1)S(1)} collective-permute-done((bf16[64,64,128]{2,1,0:T(8,128)(2,1)S(1)}, bf16[64,64,128]{2,1,0:T(8,128)(2,1)S(1)}, u32[]{:S(2)}, u32[]{:S(2)}) %collective-permute-start.33) | collective-permute-done | bytes 1048608 | tf_op jit(solution)/shard_map/ppermute | solution.py:360
  183.3 11.2 %collective-permute-start.28 = (bf16[64,64,128]{2,1,0:T(8,128)(2,1)S(1)}, bf16[64,64,128]{2,1,0:T(8,128)(2,1)S(1)}, u32[]{:S(2)}, u32[]{:S(2)}) collective-permute-start(bf16[64,64,128]{2,1,0:T(8,128)(2,1)S(1)} %collective-permute-done.25.refs_2_), channel_id=1, source_target_pairs={{0,1},{1,0},{2,3},{3,2},{4,5},{5,4},{6,7},{7,6},{8,9},{9,8},{10,11... | collective-permute-start | bytes 3145736 | tf_op jit(solution)/shard_map/ppermute | solution.py:350
  195.3 10.5 %collective-permute-start.29 = (bf16[64,64,128]{2,1,0:T(8,128)(2,1)S(1)}, bf16[64,64,128]{2,1,0:T(8,128)(2,1)S(1)}, u32[]{:S(2)}, u32[]{:S(2)}) collective-permute-start(bf16[64,64,128]{2,1,0:T(8,128)(2,1)S(1)} %collective-permute-done.26.refs_1_), channel_id=1, source_target_pairs={{0,1},{1,0},{2,3},{3,2},{4,5},{5,4},{6,7},{7,6},{8,9},{9,8},{10,11... | collective-permute-start | bytes 3145736 | tf_op jit(solution)/shard_map/ppermute | solution.py:350
  205.8 9.9 %collective-permute-start.30 = (bf16[64,64,128]{2,1,0:T(8,128)(2,1)S(1)}, bf16[64,64,128]{2,1,0:T(8,128)(2,1)S(1)}, u32[]{:S(2)}, u32[]{:S(2)}) collective-permute-start(bf16[64,64,128]{2,1,0:T(8,128)(2,1)S(1)} %collective-permute-done.27.refs_0_), channel_id=1, source_target_pairs={{0,1},{1,0},{2,3},{3,2},{4,5},{5,4},{6,7},{7,6},{8,9},{9,8},{10,11... | collective-permute-start | bytes 3145736 | tf_op jit(solution)/shard_map/ppermute | solution.py:350
  216.2 10.7 %collective-permute-start.38 = (bf16[64,64,128]{2,1,0:T(8,128)(2,1)S(1)}, bf16[64,64,128]{2,1,0:T(8,128)(2,1)S(1)}, u32[]{:S(2)}, u32[]{:S(2)}) collective-permute-start(bf16[64,64,128]{2,1,0:T(8,128)(2,1)S(1)} %collective-permute-done.35.refs_0_), channel_id=1, source_target_pairs={{0,1},{1,0},{2,3},{3,2},{4,5},{5,4},{6,7},{7,6},{8,9},{9,8},{10,11... | collective-permute-start | bytes 3145736 | tf_op jit(solution)/shard_map/ppermute | solution.py:350
  226.9 0.9 copy-done.23
  227.8 1.0 copy-done.24
  228.8 9.2 %context_products.2 = (bf16[64,64,128]{2,1,0:T(8,128)(2,1)S(1)}, f32[64,64,128]{2,1,0:T(8,128)}) custom-call(s32[160]{0:T(256)S(1)} %get-tuple-element.54.rows_ref, s32[160]{0:T(256)S(1)} %get-tuple-element.55.cols_ref, s32[7]{0:T(128)S(1)} %and_convert_fusion.valid_ref, bf16[160,128,128]{2,1,0:T(8,128)(2,1)} %copy-done, ...), custom_call_target="tpu_custom_call" | custom-call | flops 335544320 | bytes 9437184 | tf_op jit(solution)/shard_map/context_products/pallas_call | solution.py:283
  238.0 1.5 collective-permute-start.31
  239.5 1.0 copy-done.19
  240.8 1.0 copy-done.22
  241.9 9.2 %context_products.3 = (bf16[64,64,128]{2,1,0:T(8,128)(2,1)S(1)}, f32[64,64,128]{2,1,0:T(8,128)}) custom-call(s32[160]{0:T(256)S(1)} %get-tuple-element.54.rows_ref, s32[160]{0:T(256)S(1)} %get-tuple-element.55.cols_ref, s32[7]{0:T(128)S(1)} %and_convert_fusion.valid_ref, bf16[160,128,128]{2,1,0:T(8,128)(2,1)} %copy-done, ...), custom_call_target="tpu_custom_call" | custom-call | flops 335544320 | bytes 9437184 | tf_op jit(solution)/shard_map/context_products/pallas_call | solution.py:283
  251.7 1.1 collective-permute-done.31
  253.2 0.9 slice.25
  254.1 1.5 collective-permute-start.32
  255.6 16.1 %collective-permute-done.39 = bf16[64,64,128]{2,1,0:T(8,128)(2,1)S(1)} collective-permute-done((bf16[64,64,128]{2,1,0:T(8,128)(2,1)S(1)}, bf16[64,64,128]{2,1,0:T(8,128)(2,1)S(1)}, u32[]{:S(2)}, u32[]{:S(2)}) %collective-permute-start.39) | collective-permute-done | bytes 1048608 | tf_op jit(solution)/shard_map/ppermute | solution.py:347
  272.0 1.3 copy-done.6
  274.2 1.9 collective-permute-start.40
  276.1 1.5 constant_dynamic-slice_fusion.1.refs_0_
  278.1 2.2 turn_back.2
  280.4 1.5 copy-done.7
  282.0 1.6 collective-permute-done.40.refs_3_
  283.6 2.2 turn_back.3
  (101 shorter events, 12.4 us)
Async XLA Ops:
  0.6 1.2 copy-start.1
  2.2 25.6 %collective-permute-start.6 = (bf16[32,64,128]{2,1,0:T(8,128)(2,1)S(1)}, bf16[32,64,128]{2,1,0:T(8,128)(2,1)S(1)}, u32[]{:S(2)}, u32[]{:S(2)}) collective-permute-start(bf16[32,64,128]{2,1,0:T(8,128)(2,1)S(1)} %get-tuple-element.30.refs_0_), channel_id=1, source_target_pairs={{0,8},{1,17},{2,10},{3,19},{4,12},{5,21},{6,14},{7,23},{8,0},{9,25... | collective-permute-start | bytes 1572872 | tf_op jit(solution)/shard_map/ppermute | solution.py:347
  5.2 31.3 %collective-permute-start.16 = (bf16[32,64,128]{2,1,0:T(8,128)(2,1)S(1)}, bf16[32,64,128]{2,1,0:T(8,128)(2,1)S(1)}, u32[]{:S(2)}, u32[]{:S(2)}) collective-permute-start(bf16[32,64,128]{2,1,0:T(8,128)(2,1)S(1)} %get-tuple-element.38.refs_0_), channel_id=1, source_target_pairs={{0,8},{1,17},{2,10},{3,19},{4,12},{5,21},{6,14},{7,23},{8,0},{9,25... | collective-permute-start | bytes 1572872 | tf_op jit(solution)/shard_map/ppermute | solution.py:347
  6.6 31.4 %copy-start.3 = (s32[1,1,160]{2,1,0:T(1,128)S(1)}, s32[1,1,160]{2,1,0:T(1,128)}, u32[]{:S(2)}) copy-start(s32[1,1,160]{2,1,0:T(1,128)} %param.5) | copy-start | bytes 1924
  6.6 31.4 %copy-start.5 = (s32[1,1,160]{2,1,0:T(1,128)S(1)}, s32[1,1,160]{2,1,0:T(1,128)}, u32[]{:S(2)}) copy-start(s32[1,1,160]{2,1,0:T(1,128)} %param.6) | copy-start | bytes 1924
  17.0 4.3 %collective-permute-start = (f32[128,128]{1,0:T(8,128)S(1)}, f32[128,128]{1,0:T(8,128)S(1)}, u32[]{:S(2)}, u32[]{:S(2)}) collective-permute-start(f32[128,128]{1,0:T(8,128)S(1)} %get-tuple-element.27), channel_id=1, source_target_pairs={{0,8},{1,17},{2,10},{3,19},{4,12},{5,21},{6,14},{7,23},{8,0},{9,25... | collective-permute-start | bytes 196616 | tf_op jit(solution)/shard_map/ppermute | solution.py:347
  21.3 4.3 %collective-permute-start.1 = (f32[128,128]{1,0:T(8,128)S(1)}, f32[128,128]{1,0:T(8,128)S(1)}, u32[]{:S(2)}, u32[]{:S(2)}) collective-permute-start(f32[128,128]{1,0:T(8,128)S(1)} %add.107.a_ref), channel_id=1, source_target_pairs={{0,16},{1,9},{2,18},{3,11},{4,20},{5,13},{6,22},{7,15},{8,24},{9,1... | collective-permute-start | bytes 196616 | tf_op jit(solution)/shard_map/ppermute | solution.py:347
  25.7 2.2 collective-permute-start.2
  25.8 28.1 %collective-permute-start.5 = (bf16[32,64,128]{2,1,0:T(8,128)(2,1)S(1)}, bf16[32,64,128]{2,1,0:T(8,128)(2,1)S(1)}, u32[]{:S(2)}, u32[]{:S(2)}) collective-permute-start(bf16[32,64,128]{2,1,0:T(8,128)(2,1)S(1)} %get-tuple-element.30.refs_0_), channel_id=1, source_target_pairs={{0,16},{1,9},{2,18},{3,11},{4,20},{5,13},{6,22},{7,15},{8,24},{9,1... | collective-permute-start | bytes 1572872 | tf_op jit(solution)/shard_map/ppermute | solution.py:347
  27.8 26.1 %collective-permute-start.7 = (bf16[32,64,128]{2,1,0:T(8,128)(2,1)S(1)}, bf16[32,64,128]{2,1,0:T(8,128)(2,1)}, u32[]{:S(2)}, u32[]{:S(2)}) collective-permute-start(bf16[32,64,128]{2,1,0:T(8,128)(2,1)S(1)} %collective-permute-done.6.refs_2_), channel_id=1, source_target_pairs={{0,16},{1,9},{2,18},{3,11},{4,20},{5,13},{6,22},{7,15},{8,24},{9,1... | collective-permute-start | bytes 1572872 | tf_op jit(solution)/shard_map/ppermute | solution.py:347
  28.0 5.7 %collective-permute-start.3 = (f32[264,128]{1,0:T(8,128)S(1)}, f32[264,128]{1,0:T(8,128)S(1)}, u32[]{:S(2)}, u32[]{:S(2)}) collective-permute-start(f32[264,128]{1,0:T(8,128)S(1)} %add.108), channel_id=1, source_target_pairs={{0,2},{1,3},{2,0},{3,1},{4,6},{5,7},{6,4},{7,5},{8,10},{9,11},{10,... | collective-permute-start | bytes 405512 | tf_op jit(solution)/shard_map/ppermute | solution.py:395
  30.0 37.3 %collective-permute-start.15 = (bf16[32,64,128]{2,1,0:T(8,128)(2,1)S(1)}, bf16[32,64,128]{2,1,0:T(8,128)(2,1)S(1)}, u32[]{:S(2)}, u32[]{:S(2)}) collective-permute-start(bf16[32,64,128]{2,1,0:T(8,128)(2,1)S(1)} %get-tuple-element.38.refs_0_), channel_id=1, source_target_pairs={{0,16},{1,9},{2,18},{3,11},{4,20},{5,13},{6,22},{7,15},{8,24},{9,1... | collective-permute-start | bytes 1572872 | tf_op jit(solution)/shard_map/ppermute | solution.py:347
  33.7 8.7 %collective-permute-start.4 = (f32[264,128]{1,0:T(8,128)S(1)}, f32[264,128]{1,0:T(8,128)S(1)}, u32[]{:S(2)}, u32[]{:S(2)}) collective-permute-start(f32[264,128]{1,0:T(8,128)S(1)} %add.109.a_ref), channel_id=1, source_target_pairs={{0,4},{1,5},{2,6},{3,7},{4,0},{5,1},{6,2},{7,3},{8,12},{9,13},{10,... | collective-permute-start | bytes 405512 | tf_op jit(solution)/shard_map/ppermute | solution.py:395
  36.5 30.8 %collective-permute-start.17 = (bf16[32,64,128]{2,1,0:T(8,128)(2,1)S(1)}, bf16[32,64,128]{2,1,0:T(8,128)(2,1)S(1)}, u32[]{:S(2)}, u32[]{:S(2)}) collective-permute-start(bf16[32,64,128]{2,1,0:T(8,128)(2,1)S(1)} %collective-permute-done.16.refs_2_), channel_id=1, source_target_pairs={{0,16},{1,9},{2,18},{3,11},{4,20},{5,13},{6,22},{7,15},{8,24},{9,1... | collective-permute-start | bytes 1572872 | tf_op jit(solution)/shard_map/ppermute | solution.py:347
  51.6 2.3 copy-start
  65.9 15.5 %copy-start.15 = (f32[64,64,128]{2,1,0:T(8,128)S(1)}, f32[64,64,128]{2,1,0:T(8,128)}, u32[]{:S(2)}) copy-start(f32[64,64,128]{2,1,0:T(8,128)} %get-tuple-element.36) | copy-start | bytes 6291460
  65.9 15.4 %collective-permute-start.10 = (bf16[64,64,128]{2,1,0:T(8,128)(2,1)S(1)}, bf16[64,64,128]{2,1,0:T(8,128)(2,1)S(1)}, u32[]{:S(2)}, u32[]{:S(2)}) collective-permute-start(bf16[64,64,128]{2,1,0:T(8,128)(2,1)S(1)} %get-tuple-element.37), channel_id=1, source_target_pairs={{1,0},{6,7},{9,8},{14,15},{17,16},{22,23},{25,24},{30,31}} | collective-permute-start | bytes 3145736 | tf_op jit(solution)/shard_map/ppermute | solution.py:350
  78.7 5.8 %collective-permute-start.20 = (bf16[64,64,128]{2,1,0:T(8,128)(2,1)S(1)}, bf16[64,64,128]{2,1,0:T(8,128)(2,1)S(1)}, u32[]{:S(2)}, u32[]{:S(2)}) collective-permute-start(bf16[64,64,128]{2,1,0:T(8,128)(2,1)S(1)} %get-tuple-element.45), channel_id=1, source_target_pairs={{1,0},{6,7},{9,8},{14,15},{17,16},{22,23},{25,24},{30,31}} | collective-permute-start | bytes 3145736 | tf_op jit(solution)/shard_map/ppermute | solution.py:350
  80.0 7.6 %collective-permute-start.9 = (bf16[64,64,128]{2,1,0:T(8,128)(2,1)S(1)}, bf16[64,64,128]{2,1,0:T(8,128)(2,1)S(1)}, u32[]{:S(2)}, u32[]{:S(2)}) collective-permute-start(bf16[64,64,128]{2,1,0:T(8,128)(2,1)S(1)} %get-tuple-element.35), channel_id=1, source_target_pairs={{1,0},{3,2},{4,5},{6,7},{9,8},{11,10},{12,13},{14,15},{17,16},{19,... | collective-permute-start | bytes 3145736 | tf_op jit(solution)/shard_map/ppermute | solution.py:350
  81.3 3.2 %copy-start.17 = (f32[64,64,128]{2,1,0:T(8,128)S(1)}, f32[64,64,128]{2,1,0:T(8,128)}, u32[]{:S(2)}) copy-start(f32[64,64,128]{2,1,0:T(8,128)} %get-tuple-element.44) | copy-start | bytes 6291460
  81.7 13.7 %collective-permute-start.11 = (bf16[64,64,128]{2,1,0:T(8,128)(2,1)S(1)}, bf16[64,64,128]{2,1,0:T(8,128)(2,1)S(1)}, u32[]{:S(2)}, u32[]{:S(2)}) collective-permute-start(bf16[64,64,128]{2,1,0:T(8,128)(2,1)S(1)} %add_convert_fusion.5), channel_id=1, source_target_pairs={{0,2},{7,5},{8,10},{15,13},{16,18},{23,21},{24,26},{31,29}} | collective-permute-start | bytes 3145736 | tf_op jit(solution)/shard_map/ppermute | solution.py:360
  83.2 18.7 %collective-permute-start.19 = (bf16[64,64,128]{2,1,0:T(8,128)(2,1)S(1)}, bf16[64,64,128]{2,1,0:T(8,128)(2,1)S(1)}, u32[]{:S(2)}, u32[]{:S(2)}) collective-permute-start(bf16[64,64,128]{2,1,0:T(8,128)(2,1)S(1)} %get-tuple-element.43), channel_id=1, source_target_pairs={{1,0},{3,2},{4,5},{6,7},{9,8},{11,10},{12,13},{14,15},{17,16},{19,... | collective-permute-start | bytes 3145736 | tf_op jit(solution)/shard_map/ppermute | solution.py:350
  84.5 10.9 %copy-start.13 = (f32[64,64,128]{2,1,0:T(8,128)S(1)}, f32[64,64,128]{2,1,0:T(8,128)}, u32[]{:S(2)}) copy-start(f32[64,64,128]{2,1,0:T(8,128)} %get-tuple-element.34) | copy-start | bytes 6291460
  84.8 21.8 %collective-permute-start.21 = (bf16[64,64,128]{2,1,0:T(8,128)(2,1)S(1)}, bf16[64,64,128]{2,1,0:T(8,128)(2,1)S(1)}, u32[]{:S(2)}, u32[]{:S(2)}) collective-permute-start(bf16[64,64,128]{2,1,0:T(8,128)(2,1)S(1)} %add_convert_fusion.2), channel_id=1, source_target_pairs={{0,2},{7,5},{8,10},{15,13},{16,18},{23,21},{24,26},{31,29}} | collective-permute-start | bytes 3145736 | tf_op jit(solution)/shard_map/ppermute | solution.py:360
  86.3 25.4 %collective-permute-start.8 = (bf16[64,64,128]{2,1,0:T(8,128)(2,1)S(1)}, bf16[64,64,128]{2,1,0:T(8,128)(2,1)S(1)}, u32[]{:S(2)}, u32[]{:S(2)}) collective-permute-start(bf16[64,64,128]{2,1,0:T(8,128)(2,1)S(1)} %get-tuple-element.33), channel_id=1, source_target_pairs={{1,0},{2,3},{3,2},{4,5},{5,4},{6,7},{9,8},{10,11},{11,10},{12,13},... | collective-permute-start | bytes 3145736 | tf_op jit(solution)/shard_map/ppermute | solution.py:350
  95.4 11.2 %copy-start.14 = (f32[64,64,128]{2,1,0:T(8,128)S(1)}, f32[64,64,128]{2,1,0:T(8,128)}, u32[]{:S(2)}) copy-start(f32[64,64,128]{2,1,0:T(8,128)} %get-tuple-element.42) | copy-start | bytes 6291460
  95.9 21.9 %collective-permute-start.12 = (bf16[64,64,128]{2,1,0:T(8,128)(2,1)S(1)}, bf16[64,64,128]{2,1,0:T(8,128)(2,1)S(1)}, u32[]{:S(2)}, u32[]{:S(2)}) collective-permute-start(bf16[64,64,128]{2,1,0:T(8,128)(2,1)S(1)} %add_convert_fusion.4), channel_id=1, source_target_pairs={{0,2},{7,5},{2,4},{5,3},{8,10},{15,13},{10,12},{13,11},{16,18},{23... | collective-permute-start | bytes 3145736 | tf_op jit(solution)/shard_map/ppermute | solution.py:360
  100.5 22.6 %collective-permute-start.18 = (bf16[64,64,128]{2,1,0:T(8,128)(2,1)S(1)}, bf16[64,64,128]{2,1,0:T(8,128)(2,1)S(1)}, u32[]{:S(2)}, u32[]{:S(2)}) collective-permute-start(bf16[64,64,128]{2,1,0:T(8,128)(2,1)S(1)} %get-tuple-element.41), channel_id=1, source_target_pairs={{1,0},{2,3},{3,2},{4,5},{5,4},{6,7},{9,8},{10,11},{11,10},{12,13},... | collective-permute-start | bytes 3145736 | tf_op jit(solution)/shard_map/ppermute | solution.py:350
  106.6 11.2 %copy-start.11 = (f32[64,64,128]{2,1,0:T(8,128)S(1)}, f32[64,64,128]{2,1,0:T(8,128)}, u32[]{:S(2)}) copy-start(f32[64,64,128]{2,1,0:T(8,128)} %get-tuple-element.32) | copy-start | bytes 6291460
  107.2 22.0 %collective-permute-start.22 = (bf16[64,64,128]{2,1,0:T(8,128)(2,1)S(1)}, bf16[64,64,128]{2,1,0:T(8,128)(2,1)S(1)}, u32[]{:S(2)}, u32[]{:S(2)}) collective-permute-start(bf16[64,64,128]{2,1,0:T(8,128)(2,1)S(1)} %add_convert_fusion.1), channel_id=1, source_target_pairs={{0,2},{7,5},{2,4},{5,3},{8,10},{15,13},{10,12},{13,11},{16,18},{23... | collective-permute-start | bytes 3145736 | tf_op jit(solution)/shard_map/ppermute | solution.py:360
  117.9 11.2 %copy-start.12 = (f32[64,64,128]{2,1,0:T(8,128)S(1)}, f32[64,64,128]{2,1,0:T(8,128)}, u32[]{:S(2)}) copy-start(f32[64,64,128]{2,1,0:T(8,128)} %get-tuple-element.40) | copy-start | bytes 6291460
  118.4 21.9 %collective-permute-start.13 = (bf16[64,64,128]{2,1,0:T(8,128)(2,1)S(1)}, bf16[64,64,128]{2,1,0:T(8,128)(2,1)S(1)}, u32[]{:S(2)}, u32[]{:S(2)}) collective-permute-start(bf16[64,64,128]{2,1,0:T(8,128)(2,1)S(1)} %add_convert_fusion.3), channel_id=1, source_target_pairs={{0,2},{7,5},{2,4},{5,3},{4,6},{3,1},{8,10},{15,13},{10,12},{13,11}... | collective-permute-start | bytes 3145736 | tf_op jit(solution)/shard_map/ppermute | solution.py:360
  129.1 11.2 %copy-start.9 = (f32[64,64,128]{2,1,0:T(8,128)S(1)}, f32[64,64,128]{2,1,0:T(8,128)}, u32[]{:S(2)}) copy-start(f32[64,64,128]{2,1,0:T(8,128)} %get-tuple-element.31) | copy-start | bytes 6291460
  129.6 22.0 %collective-permute-start.23 = (bf16[64,64,128]{2,1,0:T(8,128)(2,1)S(1)}, bf16[64,64,128]{2,1,0:T(8,128)(2,1)S(1)}, u32[]{:S(2)}, u32[]{:S(2)}) collective-permute-start(bf16[64,64,128]{2,1,0:T(8,128)(2,1)S(1)} %add_convert_fusion), channel_id=1, source_target_pairs={{0,2},{7,5},{2,4},{5,3},{4,6},{3,1},{8,10},{15,13},{10,12},{13,11}... | collective-permute-start | bytes 3145736 | tf_op jit(solution)/shard_map/ppermute | solution.py:360
  140.3 11.2 %copy-start.10 = (f32[64,64,128]{2,1,0:T(8,128)S(1)}, f32[64,64,128]{2,1,0:T(8,128)}, u32[]{:S(2)}) copy-start(f32[64,64,128]{2,1,0:T(8,128)} %get-tuple-element.39) | copy-start | bytes 6291460
  140.7 11.5 %collective-permute-start.14 = (f32[64,64,128]{2,1,0:T(8,128)S(1)}, f32[64,64,128]{2,1,0:T(8,128)S(1)}, u32[]{:S(2)}, u32[]{:S(2)}) collective-permute-start(f32[64,64,128]{2,1,0:T(8,128)S(1)} %convert_add_fusion.3), channel_id=1, source_target_pairs={{0,1},{1,0},{2,3},{3,2},{4,5},{5,4},{6,7},{7,6},{8,9},{9,8},{10,11... | collective-permute-start | bytes 6291464 | tf_op jit(solution)/shard_map/ppermute | solution.py:350
  152.0 6.3 %collective-permute-start.24 = (f32[64,64,128]{2,1,0:T(8,128)S(1)}, f32[64,64,128]{2,1,0:T(8,128)S(1)}, u32[]{:S(2)}, u32[]{:S(2)}) collective-permute-start(f32[64,64,128]{2,1,0:T(8,128)S(1)} %convert_add_fusion.2), channel_id=1, source_target_pairs={{0,1},{1,0},{2,3},{3,2},{4,5},{5,4},{6,7},{7,6},{8,9},{9,8},{10,11... | collective-permute-start | bytes 6291464 | tf_op jit(solution)/shard_map/ppermute | solution.py:350
  153.9 16.7 %collective-permute-start.25 = (bf16[64,64,128]{2,1,0:T(8,128)(2,1)S(1)}, bf16[64,64,128]{2,1,0:T(8,128)(2,1)S(1)}, u32[]{:S(2)}, u32[]{:S(2)}) collective-permute-start(bf16[64,64,128]{2,1,0:T(8,128)(2,1)S(1)} %get-tuple-element.52.refs_3_), channel_id=1, source_target_pairs={{0,2},{7,5},{2,4},{5,3},{4,6},{3,1},{8,10},{15,13},{10,12},{13,11}... | collective-permute-start | bytes 3145736 | tf_op jit(solution)/shard_map/ppermute | solution.py:360
  160.2 21.7 %collective-permute-start.33 = (bf16[64,64,128]{2,1,0:T(8,128)(2,1)S(1)}, bf16[64,64,128]{2,1,0:T(8,128)(2,1)S(1)}, u32[]{:S(2)}, u32[]{:S(2)}) collective-permute-start(bf16[64,64,128]{2,1,0:T(8,128)(2,1)S(1)} %get-tuple-element.50.refs_3_), channel_id=1, source_target_pairs={{0,2},{7,5},{2,4},{5,3},{4,6},{3,1},{8,10},{15,13},{10,12},{13,11}... | collective-permute-start | bytes 3145736 | tf_op jit(solution)/shard_map/ppermute | solution.py:360
  170.6 12.0 %collective-permute-start.26 = (bf16[64,64,128]{2,1,0:T(8,128)(2,1)S(1)}, bf16[64,64,128]{2,1,0:T(8,128)(2,1)S(1)}, u32[]{:S(2)}, u32[]{:S(2)}) collective-permute-start(bf16[64,64,128]{2,1,0:T(8,128)(2,1)S(1)} %collective-permute-done.25.refs_2_), channel_id=1, source_target_pairs={{2,4},{5,3},{4,6},{3,1},{10,12},{13,11},{12,14},{11,9},{18,20},{21... | collective-permute-start | bytes 3145736 | tf_op jit(solution)/shard_map/ppermute | solution.py:360
  181.9 12.7 %collective-permute-start.34 = (bf16[64,64,128]{2,1,0:T(8,128)(2,1)S(1)}, bf16[64,64,128]{2,1,0:T(8,128)(2,1)S(1)}, u32[]{:S(2)}, u32[]{:S(2)}) collective-permute-start(bf16[64,64,128]{2,1,0:T(8,128)(2,1)S(1)} %collective-permute-done.33.refs_2_), channel_id=1, source_target_pairs={{2,4},{5,3},{4,6},{3,1},{10,12},{13,11},{12,14},{11,9},{18,20},{21... | collective-permute-start | bytes 3145736 | tf_op jit(solution)/shard_map/ppermute | solution.py:360
  182.6 23.2 %collective-permute-start.27 = (bf16[64,64,128]{2,1,0:T(8,128)(2,1)S(1)}, bf16[64,64,128]{2,1,0:T(8,128)(2,1)S(1)}, u32[]{:S(2)}, u32[]{:S(2)}) collective-permute-start(bf16[64,64,128]{2,1,0:T(8,128)(2,1)S(1)} %collective-permute-done.26.refs_1_), channel_id=1, source_target_pairs={{4,6},{3,1},{12,14},{11,9},{20,22},{19,17},{28,30},{27,25}} | collective-permute-start | bytes 3145736 | tf_op jit(solution)/shard_map/ppermute | solution.py:360
  183.3 32.3 %collective-permute-start.28 = (bf16[64,64,128]{2,1,0:T(8,128)(2,1)S(1)}, bf16[64,64,128]{2,1,0:T(8,128)(2,1)S(1)}, u32[]{:S(2)}, u32[]{:S(2)}) collective-permute-start(bf16[64,64,128]{2,1,0:T(8,128)(2,1)S(1)} %collective-permute-done.25.refs_2_), channel_id=1, source_target_pairs={{0,1},{1,0},{2,3},{3,2},{4,5},{5,4},{6,7},{7,6},{8,9},{9,8},{10,11... | collective-permute-start | bytes 3145736 | tf_op jit(solution)/shard_map/ppermute | solution.py:350
  194.5 21.6 %collective-permute-start.35 = (bf16[64,64,128]{2,1,0:T(8,128)(2,1)S(1)}, bf16[64,64,128]{2,1,0:T(8,128)(2,1)S(1)}, u32[]{:S(2)}, u32[]{:S(2)}) collective-permute-start(bf16[64,64,128]{2,1,0:T(8,128)(2,1)S(1)} %collective-permute-done.34.refs_1_), channel_id=1, source_target_pairs={{4,6},{3,1},{12,14},{11,9},{20,22},{19,17},{28,30},{27,25}} | collective-permute-start | bytes 3145736 | tf_op jit(solution)/shard_map/ppermute | solution.py:360
  195.3 31.6 %collective-permute-start.29 = (bf16[64,64,128]{2,1,0:T(8,128)(2,1)S(1)}, bf16[64,64,128]{2,1,0:T(8,128)(2,1)S(1)}, u32[]{:S(2)}, u32[]{:S(2)}) collective-permute-start(bf16[64,64,128]{2,1,0:T(8,128)(2,1)S(1)} %collective-permute-done.26.refs_1_), channel_id=1, source_target_pairs={{0,1},{1,0},{2,3},{3,2},{4,5},{5,4},{6,7},{7,6},{8,9},{9,8},{10,11... | collective-permute-start | bytes 3145736 | tf_op jit(solution)/shard_map/ppermute | solution.py:350
  205.8 21.1 %collective-permute-start.30 = (bf16[64,64,128]{2,1,0:T(8,128)(2,1)S(1)}, bf16[64,64,128]{2,1,0:T(8,128)(2,1)S(1)}, u32[]{:S(2)}, u32[]{:S(2)}) collective-permute-start(bf16[64,64,128]{2,1,0:T(8,128)(2,1)S(1)} %collective-permute-done.27.refs_0_), channel_id=1, source_target_pairs={{0,1},{1,0},{2,3},{3,2},{4,5},{5,4},{6,7},{7,6},{8,9},{9,8},{10,11... | collective-permute-start | bytes 3145736 | tf_op jit(solution)/shard_map/ppermute | solution.py:350
  215.6 23.9 %collective-permute-start.36 = (bf16[64,64,128]{2,1,0:T(8,128)(2,1)S(1)}, bf16[64,64,128]{2,1,0:T(8,128)(2,1)S(1)}, u32[]{:S(2)}, u32[]{:S(2)}) collective-permute-start(bf16[64,64,128]{2,1,0:T(8,128)(2,1)S(1)} %collective-permute-done.33.refs_2_), channel_id=1, source_target_pairs={{0,1},{1,0},{2,3},{3,2},{4,5},{5,4},{6,7},{7,6},{8,9},{9,8},{10,11... | collective-permute-start | bytes 3145736 | tf_op jit(solution)/shard_map/ppermute | solution.py:350
  215.7 11.2 %copy-start.20 = (bf16[64,64,128]{2,1,0:T(8,128)(2,1)}, bf16[64,64,128]{2,1,0:T(8,128)(2,1)S(1)}, u32[]{:S(2)}) copy-start(bf16[64,64,128]{2,1,0:T(8,128)(2,1)S(1)} %collective-permute-done.28.refs_4_) | copy-start | bytes 3145732
  215.7 23.9 %collective-permute-start.37 = (bf16[64,64,128]{2,1,0:T(8,128)(2,1)S(1)}, bf16[64,64,128]{2,1,0:T(8,128)(2,1)S(1)}, u32[]{:S(2)}, u32[]{:S(2)}) collective-permute-start(bf16[64,64,128]{2,1,0:T(8,128)(2,1)S(1)} %collective-permute-done.34.refs_1_), channel_id=1, source_target_pairs={{0,1},{1,0},{2,3},{3,2},{4,5},{5,4},{6,7},{7,6},{8,9},{9,8},{10,11... | collective-permute-start | bytes 3145736 | tf_op jit(solution)/shard_map/ppermute | solution.py:350
  216.2 23.4 %collective-permute-start.38 = (bf16[64,64,128]{2,1,0:T(8,128)(2,1)S(1)}, bf16[64,64,128]{2,1,0:T(8,128)(2,1)S(1)}, u32[]{:S(2)}, u32[]{:S(2)}) collective-permute-start(bf16[64,64,128]{2,1,0:T(8,128)(2,1)S(1)} %collective-permute-done.35.refs_0_), channel_id=1, source_target_pairs={{0,1},{1,0},{2,3},{3,2},{4,5},{5,4},{6,7},{7,6},{8,9},{9,8},{10,11... | collective-permute-start | bytes 3145736 | tf_op jit(solution)/shard_map/ppermute | solution.py:350
  226.9 1.0 copy-start.23
  227.8 1.0 copy-start.24
  238.0 14.9 %copy-start.16 = (f32[64,64,128]{2,1,0:T(8,128)S(1)}, f32[64,64,128]{2,1,0:T(8,128)}, u32[]{:S(2)}) copy-start(f32[64,64,128]{2,1,0:T(8,128)} %get-tuple-element.46) | copy-start | bytes 6291460
  238.0 14.9 %collective-permute-start.31 = (bf16[64,64,128]{2,1,0:T(8,128)(2,1)S(1)}, bf16[64,64,128]{2,1,0:T(8,128)(2,1)S(1)}, u32[]{:S(2)}, u32[]{:S(2)}) collective-permute-start(bf16[64,64,128]{2,1,0:T(8,128)(2,1)S(1)} %get-tuple-element.47), channel_id=1, source_target_pairs={{0,8},{1,17},{2,10},{3,19},{4,12},{5,21},{6,14},{7,23},{8,0},{9,25... | collective-permute-start | bytes 3145736 | tf_op jit(solution)/shard_map/ppermute | solution.py:347
  239.5 1.0 copy-start.19
  239.5 1.3 copy-start.21
  240.8 1.1 copy-start.22
  251.1 20.6 %collective-permute-start.39 = (bf16[64,64,128]{2,1,0:T(8,128)(2,1)S(1)}, bf16[64,64,128]{2,1,0:T(8,128)(2,1)S(1)}, u32[]{:S(2)}, u32[]{:S(2)}) collective-permute-start(bf16[64,64,128]{2,1,0:T(8,128)(2,1)S(1)} %get-tuple-element.49), channel_id=1, source_target_pairs={{0,8},{1,17},{2,10},{3,19},{4,12},{5,21},{6,14},{7,23},{8,0},{9,25... | collective-permute-start | bytes 3145736 | tf_op jit(solution)/shard_map/ppermute | solution.py:347
  252.9 18.8 %copy-start.18 = (f32[64,64,128]{2,1,0:T(8,128)S(1)}, f32[64,64,128]{2,1,0:T(8,128)}, u32[]{:S(2)}) copy-start(f32[64,64,128]{2,1,0:T(8,128)} %get-tuple-element.48) | copy-start | bytes 6291460
  254.1 27.8 %collective-permute-start.32 = (bf16[32,64,128]{2,1,0:T(8,128)(2,1)}, bf16[32,64,128]{2,1,0:T(8,128)(2,1)S(1)}, u32[]{:S(2)}, u32[]{:S(2)}) collective-permute-start(bf16[32,64,128]{2,1,0:T(8,128)(2,1)} %slice.25), channel_id=1, source_target_pairs={{0,16},{1,9},{2,18},{3,11},{4,20},{5,13},{6,22},{7,15},{8,24},{9,1... | collective-permute-start | bytes 1572872 | tf_op jit(solution)/shard_map/ppermute | solution.py:347
  272.0 1.3 copy-start.6
  274.2 9.4 %collective-permute-start.40 = (bf16[32,64,128]{2,1,0:T(8,128)(2,1)}, bf16[32,64,128]{2,1,0:T(8,128)(2,1)S(1)}, u32[]{:S(2)}, u32[]{:S(2)}) collective-permute-start(bf16[32,64,128]{2,1,0:T(8,128)(2,1)} %slice.24), channel_id=1, source_target_pairs={{0,16},{1,9},{2,18},{3,11},{4,20},{5,13},{6,22},{7,15},{8,24},{9,1... | collective-permute-start | bytes 1572872 | tf_op jit(solution)/shard_map/ppermute | solution.py:347
  276.1 1.9 copy-start.8
  280.3 1.6 copy-start.7
  (2 other events, 1.4 us)

commit v2 on v0

v2 whole, which is shorter than its diff:
```python
import functools
import math

import jax
import jax.numpy as jnp
from jax import lax
from jax.experimental import pallas as pl
from jax.experimental.pallas import tpu as pltpu
from jax.sharding import PartitionSpec as P

NEG_SAMPLES = 15
GROUPS = 2
PARTS = 2
F32 = jnp.float32
BF16 = jnp.bfloat16

ANY = pl.BlockSpec(memory_space=pl.ANY)
HBM = pl.BlockSpec(memory_space=pltpu.HBM)
IN_VMEM = pl.BlockSpec(memory_space=pltpu.VMEM)
IN_SMEM = pl.BlockSpec(memory_space=pltpu.SMEM)


def params(mib):
    return pltpu.CompilerParams(vmem_limit_bytes=mib * 2**20)


def cost(microseconds):
    return pl.CostEstimate(flops=0, bytes_accessed=int(microseconds * 3.69e6), transcendentals=0)


def in_hbm(x):
    return pltpu.with_memory_space_constraint(x, pltpu.HBM)


def over_tiles(slots, unroll, first, second):
    unroll = math.gcd(slots, unroll)

    def body(at, carry):
        found = [first(at * unroll + n) for n in range(unroll)]
        for n, one in enumerate(found):
            second(at * unroll + n, one)
        return carry

    lax.fori_loop(0, slots // unroll, body, 0)


def count_sums(counts, rows, cols, band_rows, band_cols, deps):
    slots, tile, _ = counts.shape
    pieces = math.gcd(slots, 10)
    piece = slots // pieces

    def kernel(counts_ref, rows_hbm, cols_hbm, *refs):
        word_ref, context_ref, held, rows_ref, cols_ref, sems = refs[len(deps) :]
        lists = [
            pltpu.make_async_copy(rows_hbm, rows_ref, sems.at[pieces]),
            pltpu.make_async_copy(cols_hbm, cols_ref, sems.at[pieces + 1]),
        ]

        def arriving(n):
            part = pl.ds(n * piece, piece)
            return pltpu.make_async_copy(counts_ref.at[part], held.at[part], sems.at[n])

        for copy in lists + [arriving(n) for n in range(pieces)]:
            copy.start()
        word_ref[...] = jnp.zeros_like(word_ref)
        context_ref[...] = jnp.zeros_like(context_ref)
        for copy in lists:
            copy.wait()

        def sums(n):
            values = held[n].astype(F32)
            return (
                jnp.sum(jnp.sum(values.T.reshape(tile // 8, 8, tile), axis=0), axis=0, keepdims=True),
                jnp.sum(jnp.sum(values.reshape(tile // 8, 8, tile), axis=0), axis=0, keepdims=True),
            )

        def add(n, found):
            word_ref[pl.ds(rows_ref[n], 1), :] += found[0]
            context_ref[pl.ds(cols_ref[n], 1), :] += found[1]

        def one_piece(at, carry):
            arriving(at).wait()
            over_tiles(
                piece, 16, lambda n: sums(at * piece + n), lambda n, found: add(at * piece + n, found)
            )
            return carry

        lax.fori_loop(0, pieces, one_piece, 0)

    return pl.pallas_call(
        kernel,
        in_specs=[HBM, ANY, ANY] + [ANY] * len(deps),
        out_specs=[IN_VMEM] * 2,
        out_shape=[
            jax.ShapeDtypeStruct((band_rows, tile), F32),
            jax.ShapeDtypeStruct((band_cols, tile), F32),
        ],
        scratch_shapes=[
            pltpu.VMEM(counts.shape, counts.dtype),
            pltpu.SMEM((slots,), jnp.int32),
            pltpu.SMEM((slots,), jnp.int32),
            pltpu.SemaphoreType.DMA((pieces + 2,)),
        ],
        compiler_params=params(48),
        cost_estimate=cost(0.01),
        name="count_sums",
    )(counts, rows, cols, *deps)


def smoothed(contexts):
    band_cols, tile = contexts[0].shape

    def kernel(*refs):
        power_ref, log_ref = refs[len(contexts) :]
        total = refs[0][...]
        for ref in refs[1 : len(contexts)]:
            total = total + ref[...]
        root = jnp.sqrt(total)
        powers = root * jnp.sqrt(root)
        power_ref[...] = jnp.sum(powers.reshape(band_cols // 8, 8, tile), axis=0)
        log_ref[...] = jnp.maximum(0.75 * jnp.log(total), 0.0)

    return pl.pallas_call(
        kernel,
        out_shape=[
            jax.ShapeDtypeStruct((8, tile), F32),
            jax.ShapeDtypeStruct((band_cols, tile), F32),
        ],
        compiler_params=params(16),
        name="smoothed",
    )(*contexts)


def turn_panel(panel, tile, group, deps):
    blocks, width = panel.shape[0] // tile, panel.shape[1]
    part = width // GROUPS

    def kernel(in_ref, *refs):
        out_ref = refs[-1]
        for n in range(blocks):
            turned = in_ref[n * tile : (n + 1) * tile, :].astype(F32).T.astype(BF16)
            out_ref[n] = turned[group * part : (group + 1) * part]

    return pl.pallas_call(
        kernel,
        in_specs=[IN_VMEM] + [ANY] * len(deps),
        out_specs=IN_VMEM,
        out_shape=jax.ShapeDtypeStruct((blocks, part, tile), BF16),
        compiler_params=params(16),
        name="turn_panel",
    )(panel, *deps)


def add_up(terms, count, width, dtypes, deps=(), other=None):
    tile = terms[0][0].shape[-1]
    n_terms = len(terms)

    def kernel(place_ref, *refs):
        outs = refs[n_terms + (other is not None) + len(deps) :]

        def write():
            total = refs[0][...].astype(F32)
            for ref in refs[1:n_terms]:
                total = total + ref[...].astype(F32)
            for out in outs:
                out[...] = total.astype(out.dtype)

        if other is None:
            write()
        else:
            pl.when(place_ref[0] < other[2])(write)

            @pl.when(place_ref[0] >= other[2])
            def _():
                outs[0][...] = refs[n_terms][...]

    shape = (count, width, tile)
    blocks = [pl.BlockSpec(shape, lambda n, _, at=at: (*at, 0)) for _, at in terms]
    arrays = [array for array, _ in terms]
    if other is None:
        place = jnp.zeros((1,), jnp.int32)
    else:
        place = other[1]
        blocks.append(pl.BlockSpec(shape, lambda n, _: (0, 0, 0)))
        arrays.append(other[0])
    return pl.pallas_call(
        kernel,
        grid_spec=pltpu.PrefetchScalarGridSpec(
            num_scalar_prefetch=1,
            grid=(1,),
            in_specs=blocks + [ANY] * len(deps),
            out_specs=[pl.BlockSpec(shape, lambda n, _: (0, 0, 0))] * len(dtypes),
        ),
        out_shape=[jax.ShapeDtypeStruct(shape, dtype) for dtype in dtypes],
        compiler_params=params(24),
        cost_estimate=cost(0.01),
        name="add_up",
    )(place, *arrays, *deps)


def word_products(index, blocks, chips, block_rows, tiles=None, source=None, deps=()):
    shape = (tiles if source is None else source[0]).shape
    slots, tile, _ = shape
    share, width, _ = blocks[0].shape
    slot_count = 2 * chips - 1
    n_in = len(blocks)
    chip_list = 3 * slots
    pieces = math.gcd(slots, 10)
    piece = slots // pieces
    n_powers = 0 if source is None else len(source[2])

    def kernel(index_ref, *refs):
        if source is None:
            tiles_ref, *refs = refs
        else:
            counts_hbm, first_ref, second_ref, *refs = refs
            power_refs, (log_ref, *refs) = refs[:n_powers], refs[n_powers:]
        block_refs, refs = refs[:n_in], refs[n_in + len(deps) :]
        if source is not None:
            tiles_ref, *refs = refs
        outs, refs = refs[:slot_count], refs[slot_count:]
        acc, band, sems, *refs = refs
        copies = [
            pltpu.make_async_copy(ref, band.at[pl.ds(n * share, share)], sems.at[n])
            for n, ref in enumerate(block_refs)
        ]
        for copy in copies:
            copy.start()
        acc[...] = jnp.zeros_like(acc)
        if source is not None:
            word_log, shift, counts_ref, count_sems = refs

            def arriving(n):
                part = pl.ds(n * piece, piece)
                return pltpu.make_async_copy(
                    counts_hbm.at[part], counts_ref.at[part], count_sems.at[n]
                )

            for n in range(pieces):
                arriving(n).start()
            rows = first_ref.shape[0]
            word_log[:rows] = jnp.log(jnp.maximum(first_ref[...], 1.0))
            word_log[rows:] = jnp.log(jnp.maximum(second_ref[...], 1.0))
            power = power_refs[0][...]
            for ref in power_refs[1:]:
                power = power + ref[...]
            power = jnp.sum(jnp.sum(power, axis=0, keepdims=True), axis=1, keepdims=True)
            shift[...] = (jnp.log(power) - math.log(NEG_SAMPLES)) - log_ref[...]
        for copy in copies:
            copy.wait()

        def product(n):
            if source is None:
                made = tiles_ref[n]
            else:
                word = word_log[pl.ds(index_ref[n], 1), :]
                word = jnp.broadcast_to(word, (tile, tile)).T
                context = shift[pl.ds(index_ref[slots + n], 1), :]
                pointwise = jnp.log(counts_ref[n].astype(F32)) + (context - word)
                made = jnp.maximum(pointwise, 0.0).astype(BF16)
                tiles_ref[n] = made
            return lax.dot_general(
                band[index_ref[2 * slots + n]],
                made,
                (((1,), (1,)), ((), ())),
                preferred_element_type=F32,
            )

        def add(n, found):
            acc[index_ref[n]] += found

        def one_piece(at, carry):
            if source is not None:
                arriving(at).wait()
            over_tiles(
                piece,
                16,
                lambda n: product(at * piece + n),
                lambda n, found: add(at * piece + n, found),
            )
            return carry

        lax.fori_loop(0, pieces, one_piece, 0)
        for slot, out in enumerate(outs):

            at = index_ref[chip_list + slot]

            @pl.when((at >= 0) & (at < chips))
            def _():
                out[...] = acc[pl.ds(at * block_rows, block_rows)].astype(out.dtype)

    out_shape = [
        pltpu.VMEM((block_rows, width, tile), F32 if slot == chips - 1 else BF16)
        for slot in range(slot_count)
    ]
    out_specs = [IN_VMEM] * slot_count
    scratch = [
        pltpu.VMEM((chips * block_rows, width, tile), F32),
        pltpu.VMEM((n_in * share, width, tile), BF16),
        pltpu.SemaphoreType.DMA((n_in,)),
    ]
    if source is None:
        operands, operand_specs = [tiles], [IN_VMEM]
    else:
        operands = [in_hbm(source[0]), *source[1], *source[2], source[3]]
        operand_specs = [HBM] + [IN_VMEM] * (len(operands) - 1)
    if source is not None:
        out_shape = [pltpu.VMEM(shape, BF16)] + out_shape
        out_specs = [IN_VMEM] + out_specs
        scratch += [
            pltpu.VMEM((2 * source[1][0].shape[0], tile), F32),
            pltpu.VMEM(source[3].shape, F32),
            pltpu.VMEM(shape, jnp.int32),
            pltpu.SemaphoreType.DMA((pieces,)),
        ]
    outs = pl.pallas_call(
        kernel,
        in_specs=[IN_SMEM] + operand_specs + [ANY] * (n_in + len(deps)),
        out_specs=out_specs,
        out_shape=out_shape,
        scratch_shapes=scratch,
        compiler_params=params(40 if source is not None else 32),
        cost_estimate=cost(0.01),
        name="word_products" if source is None else "ppmi_word_products",
    )(index, *operands, *blocks, *deps)
    if source is not None:
        tiles, *outs = outs
    given = {distance: outs[chips - 1 - distance] for distance in range(1, chips)}
    kept = {distance: outs[chips - 1 + distance] for distance in range(1, chips)}
    return tiles, given, outs[chips - 1], kept


def context_products(index, tiles, blocks, band_cols, deps):
    slots, tile, _ = tiles.shape
    block_rows, part, _ = blocks[0].shape
    slot_count = len(blocks)
    chips = (slot_count + 1) // 2
    half = band_cols // 2
    chip_list = 3 * slots

    def kernel(index_ref, tiles_ref, *refs):
        block_refs, refs = refs[:slot_count], refs[slot_count + len(deps) :]
        send, keep, acc, band, sems = refs

        def each_copy(act):
            for slot in range(slot_count):
                at = index_ref[chip_list + slot]

                @pl.when((at >= 0) & (at < chips))
                def _():
                    rows = pl.ds(at * block_rows, block_rows)
                    act(pltpu.make_async_copy(block_refs[slot], band.at[rows], sems.at[slot]))

        each_copy(lambda copy: copy.start())
        acc[...] = jnp.zeros_like(acc)
        each_copy(lambda copy: copy.wait())

        def product(n):
            return jnp.dot(band[index_ref[n]], tiles_ref[n], preferred_element_type=F32)

        def add(n, found):
            acc[index_ref[2 * slots + n]] += found

        over_tiles(slots, 16, product, add)
        send[...] = acc[half:].astype(BF16)
        keep[...] = acc[:half]

    shape = (half, part, tile)
    return pl.pallas_call(
        kernel,
        in_specs=[IN_SMEM, IN_VMEM] + [ANY] * (slot_count + len(deps)),
        out_specs=[IN_VMEM] * 2,
        out_shape=[jax.ShapeDtypeStruct(shape, BF16), jax.ShapeDtypeStruct(shape, F32)],
        scratch_shapes=[
            pltpu.VMEM((band_cols, part, tile), F32),
            pltpu.VMEM((chips * block_rows, part, tile), BF16),
            pltpu.SemaphoreType.DMA((slot_count,)),
        ],
        compiler_params=params(20),
        cost_estimate=cost(0.01),
        name="context_products",
    )(index, tiles, *blocks, *deps)


def turn_back(pieces, start, blocks, scale, pinned=False, deps=()):
    _, _, tile = pieces[0][0].shape
    terms = [term for piece in pieces for term in piece]
    width = sum(piece[0].shape[1] for piece in pieces)
    step = math.gcd(blocks, 8)

    def kernel(start_ref, *refs):
        out_ref, reads = refs[-1], list(refs[: len(terms)])
        for n in range(step):
            columns, at = [], 0
            for piece in pieces:
                columns.append(sum(ref[n].astype(F32) for ref in reads[at : at + len(piece)]))
                at += len(piece)
            out_ref[n * tile : (n + 1) * tile, :] = jnp.concatenate(columns, axis=0).T * scale

    return pl.pallas_call(
        kernel,
        grid_spec=pltpu.PrefetchScalarGridSpec(
            num_scalar_prefetch=1,
            grid=(blocks // step,),
            in_specs=[
                pl.BlockSpec((step, term.shape[1], tile), lambda n, at: (at[0] + n, 0, 0))
                for term in terms
            ]
            + [ANY] * len(deps),
            out_specs=pl.BlockSpec((step * tile, width), lambda n, at: (n, 0)),
        ),
        out_shape=jax.ShapeDtypeStruct((blocks * tile, width), F32),
        compiler_params=params(32),
        cost_estimate=cost(0.01),
        name="turn_back",
    )(start // step, *[in_hbm(term) if pinned else term for term in terms], *deps)


def shards(n_row, n_col, tile_counts, tile_rows, tile_cols, panel):
    counts, rows, cols = tile_counts[0, 0], tile_rows[0, 0], tile_cols[0, 0]
    tile = counts.shape[-1]
    share = panel.shape[0] // tile
    band_rows, band_cols = share * n_col, share * n_row
    chips, bits = n_col // 2, n_row.bit_length() - 1
    block_rows = 2 * share
    my_row, my_col = lax.axis_index("row"), lax.axis_index("col")
    chip, core = my_col // 2, my_col % 2

    def row_swap(x, step):
        pairs = []
        for r in range(n_row):
            for c in range(n_col):
                bit = step if c % 2 == 0 else bits - 1 - step
                pairs.append((r * n_col + c, (r ^ (1 << bit)) * n_col + c))
        return lax.ppermute(x, ("row", "col"), pairs)

    def core_swap(x, keep=lambda c, z: True):
        return lax.ppermute(
            x, "col", [(i, i ^ 1) for i in range(n_col) if keep(i % 2, i // 2)]
        )

    def along(x):
        pairs = []
        for z in range(chips - 1):
            pairs.append((2 * z, 2 * z + 2))
            pairs.append((2 * (chips - 1 - z) + 1, 2 * (chips - 2 - z) + 1))
        return lax.ppermute(x, "col", pairs)

    def row_xor(x, mask):
        return lax.ppermute(x, "row", [(r, r ^ mask) for r in range(n_row)])

    def chip_xor(x, mask):
        return lax.ppermute(x, "col", [(c, c ^ (2 * mask)) for c in range(n_col)])

    sign = jnp.where(core == 0, 1, -1)
    slot_chip = (jnp.arange(2 * chips - 1, dtype=jnp.int32) - (chips - 1)) * sign + chip
    differ = (cols // share) ^ my_row
    turned = sum(((differ >> b) & 1) << (bits - 1 - b) for b in range(bits))
    col_place = jnp.where(core == 0, turned, differ) * share + cols % share
    index = jnp.concatenate([rows, cols, col_place, slot_chip])
    behind = jnp.where(core == 0, chip, chips - 1 - chip).reshape(1)

    def spread(block):
        return {0: block} | {1 << (bits - 1 - step): row_swap(block, step) for step in range(bits)}

    def spread_on(blocks, deps=None):
        blocks = dict(blocks)
        for step in range(1, bits):
            bit = 1 << (bits - 1 - step)
            for at in sorted(blocks):
                if at & -at > bit:
                    block = blocks[at]
                    if deps is not None:
                        shape = block.shape
                        (block,) = add_up([(block, (0, 0))], *shape[:2], [BF16], deps)
                    blocks[at | bit] = row_swap(block, step)
        return [blocks[at] for at in range(n_row)]

    turned_panel = turn_panel(panel, tile, 0, ())
    panel_blocks = spread_on(spread(turned_panel))

    word_part, context = count_sums(counts, rows, cols, band_rows, band_cols, (turned_panel,))
    contexts = [context] + [row_xor(context, mask) for mask in range(1, n_row)]
    power, context_log = smoothed(contexts)
    next_blocks = spread(turn_panel(panel, tile, 1, (power,)))
    half = band_rows // 2
    first, second = word_part[:half], word_part[half:]
    totals = jnp.where(core == 0, first, second) + core_swap(jnp.where(core == 0, second, first))
    for step in range(chips.bit_length() - 1):
        totals = totals + chip_xor(totals, 1 << step)
    other_half = core_swap(totals)
    halves = [jnp.where(core == 0, totals, other_half), jnp.where(core == 0, other_half, totals)]
    power = power + core_swap(power)
    powers = [power] + [chip_xor(power, mask) for mask in range(1, chips)]

    part = panel.shape[1] // (GROUPS * PARTS)
    groups = [None] * GROUPS
    near = [[{} for _ in range(PARTS)] for _ in range(GROUPS)]
    swapped = [[{} for _ in range(PARTS)] for _ in range(GROUPS)]
    own = [[None] * PARTS for _ in range(GROUPS)]
    word_pieces, context_pieces = [], []
    stages = [[[] for _ in range(PARTS)] for _ in range(GROUPS)]
    source = (counts, halves, powers, context_log)
    tiles, *groups[0] = word_products(index, panel_blocks, chips, block_rows, source=source)
    got, passed = [None] * PARTS, {}
    last = ()

    def contexts_of(group, deps):
        for n in range(PARTS):
            blocks = [near[group][n][d] for d in range(chips - 1, 0, -1)] + [own[group][n]]
            blocks += [swapped[group][n][d] for d in range(1, chips)]
            send, keep = context_products(index, tiles, blocks, band_cols, deps)
            deps = (send,)
            stages[group][n].append(send)
            terms, count = [(keep, 0)], band_cols // 2
            for step in range(bits):
                terms.append((row_swap(send, step), 0))
                stages[group][n].append(terms[-1][0])
                if step < bits - 1:
                    count //= 2
                    (send,) = add_up([(x, (2 * y + 1, 0)) for x, y in terms], count, part, [BF16])
                    terms = [(x, 2 * y) for x, y in terms]
            context_pieces.append([x for x, _ in terms])

    for slot in range(chips * GROUPS + chips - 2):
        group, step = slot // chips, slot % chips + 1
        before, hop = group - 1, step + 1
        if group < GROUPS and step < chips:
            given, mine, kept = groups[group]
            if step == 1:
                both = [(mine, (0, 0)), (core_swap(mine), (0, 0))]
            if step == 2:
                (mine_sum,) = add_up(both, block_rows, part * PARTS, [F32], last)
            far = chips - step
            passed[far] = core_swap(
                given[far], lambda c, z, far=far: z >= far if c == 0 else z < chips - far
            )
        for n in range(PARTS):
            if group < GROUPS and step == chips:
                if group:
                    last = (*last, stages[before][n][0])
                terms = [(got[n], (0, 0)), (core_swap(got[n]), (0, 0)), (mine_sum, (0, n))]
                payload, whole = add_up(terms, block_rows, part, [BF16, F32], last)
                own[group][n] = payload
                word_pieces.append([whole])
            elif group < GROUPS:
                terms = [(kept[far], (0, n)), (passed[far], (0, n))]
                if step > 1:
                    terms.append((got[n], (0, 0)))
                other = None
                if group > 0 and hop < chips:
                    other = (near[before][n][hop - 1], behind, step)
                (payload,) = add_up(terms, block_rows, part, [BF16], last, other)
            else:
                payload = near[before][n][hop - 1]
                if GROUPS > 1:
                    last = (*last, stages[before - 1][n][min(step, bits)])
                (payload,) = add_up([(payload, (0, 0))], block_rows, part, [BF16], last)
            got[n] = along(payload)
            last = (payload,)
            if group < GROUPS and step == chips:
                arrived = (group, 1)
            elif group > 0 and hop < chips:
                arrived = (before, hop)
            else:
                continue
            near[arrived[0]][n][arrived[1]] = got[n]
            swapped[arrived[0]][n][arrived[1]] = core_swap(got[n])
        if step == 1 and group < GROUPS - 1:
            panel_blocks = spread_on(next_blocks, last)
        if step == 2 and group < GROUPS - 1:
            _, *groups[group + 1] = word_products(
                index, panel_blocks, chips, block_rows, tiles=tiles, deps=last
            )
            last = (*last, groups[group + 1][0][1])
            if group + 2 < GROUPS:
                next_blocks = spread(turn_panel(panel, tile, group + 2, last))
        if group > 0 and step == chips - 1 and group < GROUPS:
            contexts_of(before, last)
        if group == GROUPS and hop == chips - 1:
            contexts_of(before, ())
    deps = (stages[-1][-1][0],)
    word_out = turn_back(word_pieces, (core * share).reshape(1), share, 1.0, True, deps)
    zero = jnp.zeros((1,), jnp.int32)
    return word_out, turn_back(context_pieces, zero, share, 1.0 / tile)


def solution(mesh):
    in_specs = (
        P("row", "col", None, None, None),
        P("row", "col", None),
        P("row", "col", None),
        P(("col", "row"), None),
    )
    out_specs = (P(("row", "col"), None), P(("col", "row"), None))
    body = functools.partial(shards, mesh.shape["row"], mesh.shape["col"])
    return jax.shard_map(body, mesh=mesh, in_specs=in_specs, out_specs=out_specs, check_vma=False)
```

time: 646 us -> 261 us (0.40)
  waiting for transfers between devices: 466 us -> 66.2 us
  starting transfers between devices: 0.42 us -> 119 us
  other arithmetic: 84 us -> 0.16 us
  Pallas kernels: 0 us -> 63 us
  matrix products: 27.9 us -> 0 us
  local copies, waits for them, and re-layouts: 35.5 us -> 9.72 us
  blocking collectives: 16.6 us -> 0 us
  between operations: 14.9 us -> 1.54 us
    reduce_scatter x2 -> x0, waiting for transfers between devices: 253 us -> none  [the longest x1 168 us: shards(): lax.psum_scatter(word_partial, 'col', scatter_dimension=0, tiled=True)]
    all_gather x2 -> x0, waiting for transfers between devices: 132 us -> none  [the longest x1 80.3 us: shards(): lax.all_gather(word_share.astype(jnp.bfloat16), 'col', axis=0, tiled=True)]
    ppermute x0 -> x69, starting transfers between devices: none -> 119 us  [the longest x20 71.5 us: along(): return lax.ppermute(x, 'col', pairs)]
    psum x2 -> x0, waiting for transfers between devices: 79.4 us -> none  [the longest x1 41.7 us: shards(): context_totals = lax.psum(context_part, 'row')]
    scatter-add x4 -> x0, other arithmetic: 70 us -> none  [the longest x1 33.3 us: shards(): jax.ops.segment_sum(context_product, context_cols, num_segments=band_cols)]
    ppermute x0 -> x69, waiting for transfers between devices: none -> 66.2 us  [the longest x20 38.9 us: along(): return lax.ppermute(x, 'col', pairs)]
    pallas_call x0 -> x39, Pallas kernels: none -> 63 us  [the longest x2 19.2 us: word_products(): pl.pallas_call(kernel, in_specs=[IN_SMEM] + operand_specs + [ANY] * (n_in...]
    dot_general x2 -> x0, matrix products: 27.9 us -> none  [the longest x1 15.1 us: shards(): jnp.einsum('nji,njk->nik', tiles, word_picked, preferred_element_type=jnp...]
  transfers between devices with their start and end apart: 6 -> 69, of which waited for: 6 -> 27; matrix products, arithmetic and copies ran while one was open for 1% -> 0% of each run, Pallas kernels for 0% -> 17%
where the time goes in v2:
time: 261 us; the launch traced here: 260 us
  starting transfers between devices  119 us (46%)
  waiting for transfers between devices  66.2 us (25%)
  Pallas kernels  63 us (24%)
  local copies, waits for them, and re-layouts  9.72 us (4%)
    ppermute x20, starting transfers between devices, along(): return lax.ppermute(x, 'col', pairs)  71.5 us
    ppermute x20, waiting for transfers between devices, along(): return lax.ppermute(x, 'col', pairs)  38.9 us
    pallas_call x2, Pallas kernels, word_products(): pl.pallas_call(kernel, in_specs=[IN_SMEM] + operand_specs + [ANY] * (n_in...  19.2 us
    ppermute x14, waiting for transfers between devices, row_swap(): return lax.ppermute(x, ('row', 'col'), pairs)  19.1 us
    ppermute x14, starting transfers between devices, row_swap(): return lax.ppermute(x, ('row', 'col'), pairs)  17.8 us
    ppermute x27, starting transfers between devices, core_swap(): lax.ppermute(x, 'col', [(i, i ^ 1) for i in range(n_col) if keep(i % 2, i...  16.7 us
    pallas_call x4, Pallas kernels, context_products(): pl.pallas_call(kernel, in_specs=[IN_SMEM, IN_VMEM] + [ANY] * (slot_count...  16.3 us
    pallas_call x27, Pallas kernels, add_up(): pl.pallas_call(kernel, grid_spec=pltpu.PrefetchScalarGridSpec(num_scalar_...  13.8 us
  transfers between devices with their start and end apart: 69, of which 27 were waited for; matrix products, arithmetic and copies ran while one was open for 0% of the time, Pallas kernels for 17%

profile of v2, /device:TPU:0, one launch (start us, length us, event | category | flops | bytes accessed | tf_op | source)
XLA Modules:
  0.0 259.5 jit_solution(2411578127896299954)
XLA Ops:
  2.2 3.0 %collective-permute-start.12 = (bf16[32,64,128]{2,1,0:T(8,128)(2,1)S(1)}, bf16[32,64,128]{2,1,0:T(8,128)(2,1)S(1)}, u32[]{:S(2)}, u32[]{:S(2)}) collective-permute-start(bf16[32,64,128]{2,1,0:T(8,128)(2,1)S(1)} %turn_panel.2.refs_0_.refs_8_), channel_id=1, source_target_pairs={{0,8},{1,17},{2,10},{3,19},{4,12},{5,21},{6,14},{7,23},{8,0},{9,25... | collective-permute-start | bytes 1572872 | tf_op jit(solution)/shard_map/ppermute | solution.py:435
  6.6 4.9 %count_sums.1 = (f32[256,128]{1,0:T(8,128)S(1)}, f32[128,128]{1,0:T(8,128)S(1)}) custom-call(s32[160,128,128]{2,1,0:T(8,128)} %bitcast.12, s32[160]{0:T(256)S(1)} %bitcast.10, s32[160]{0:T(256)S(1)} %bitcast.7, bf16[32,64,128]{2,1,0:T(8,128)(2,1)S(1)} %turn_panel.2.refs_0_.refs_8_), custom_call_target="tpu_custom_call" | custom-call | bytes 36900 | tf_op jit(solution)/shard_map/count_sums/pallas_call | solution.py:90
  14.6 1.7 collective-permute-start.1
  17.4 1.6 collective-permute-done.1
  19.0 2.0 collective-permute-start.6
  21.0 2.6 %collective-permute-start.2 = (f32[128,128]{1,0:T(8,128)S(1)}, f32[128,128]{1,0:T(8,128)S(1)}, u32[]{:S(2)}, u32[]{:S(2)}) collective-permute-start(f32[128,128]{1,0:T(8,128)S(1)} %add.46), channel_id=1, source_target_pairs={{0,4},{1,5},{2,6},{3,7},{4,0},{5,1},{6,2},{7,3},{8,12},{9,13},{10,... | collective-permute-start | bytes 196616 | tf_op jit(solution)/shard_map/ppermute | solution.py:453
  25.0 4.7 %collective-permute-start.7 = (f32[8,128]{1,0:T(8,128)S(1)}, f32[8,128]{1,0:T(8,128)S(1)}, u32[]{:S(2)}, u32[]{:S(2)}) collective-permute-start(f32[8,128]{1,0:T(8,128)S(1)} %get-tuple-element.39.refs_0_), channel_id=1, source_target_pairs={{0,1},{1,0},{2,3},{3,2},{4,5},{5,4},{6,7},{7,6},{8,9},{9,8},{10,11... | collective-permute-start | bytes 12296 | tf_op jit(solution)/shard_map/ppermute | solution.py:438
  30.5 3.6 %collective-permute-start.10 = (f32[8,128]{1,0:T(8,128)S(1)}, f32[8,128]{1,0:T(8,128)S(1)}, u32[]{:S(2)}, u32[]{:S(2)}) collective-permute-start(f32[8,128]{1,0:T(8,128)S(1)} %add.48.refs_3_), channel_id=1, source_target_pairs={{0,6},{1,7},{2,4},{3,5},{4,2},{5,3},{6,0},{7,1},{8,14},{9,15},{10,... | collective-permute-start | bytes 12296 | tf_op jit(solution)/shard_map/ppermute | solution.py:453
  35.9 1.8 collective-permute-done.8.refs_4_
  39.6 10.8 %ppmi_word_products.1 = (bf16[160,128,128]{2,1,0:T(8,128)(2,1)S(1)}, bf16[64,64,128]{2,1,0:T(8,128)(2,1)S(1)}, bf16[64,64,128]{2,1,0:T(8,128)(2,1)S(1)}, bf16[64...) custom-call(s32[487]{0:T(512)S(1)} %pad_add_fusion.index_ref, ...), custom_call_target="tpu_custom_call" | custom-call | bytes 36900 | tf_op jit(solution)/shard_map/ppmi_word_products/pallas_call | solution.py:316
  50.5 1.3 collective-permute-start.16
  51.8 1.3 collective-permute-start.15
  55.4 2.4 collective-permute-start.17
  58.1 1.9 collective-permute-start.19
  60.1 1.3 collective-permute-start.14
  61.4 1.3 collective-permute-done.21.refs_0_.refs_3_
  62.8 1.4 collective-permute-start.20
  64.4 1.5 collective-permute-start.22
  66.4 3.6 %collective-permute-done.19.refs_2_ = bf16[64,32,128]{2,1,0:T(8,128)(2,1)S(1)} collective-permute-done((bf16[64,32,128]{2,1,0:T(8,128)(2,1)S(1)}, bf16[64,32,128]{2,1,0:T(8,128)(2,1)S(1)}, u32[]{:S(2)}, u32[]{:S(2)}) %collective-permute-start.19) | collective-permute-done | bytes 524320 | tf_op jit(solution)/shard_map/ppermute | solution.py:447
  70.1 4.4 %collective-permute-start.18 = (bf16[64,32,128]{2,1,0:T(8,128)(2,1)S(1)}, bf16[64,32,128]{2,1,0:T(8,128)(2,1)S(1)}, u32[]{:S(2)}, u32[]{:S(2)}) collective-permute-start(bf16[64,32,128]{2,1,0:T(8,128)(2,1)S(1)} %add_up.29.refs_3_), channel_id=1, source_target_pairs={{0,2},{7,5},{2,4},{5,3},{4,6},{3,1},{8,10},{15,13},{10,12},{13,11}... | collective-permute-start | bytes 1572872 | tf_op jit(solution)/shard_map/ppermute | solution.py:447
  74.9 1.9 collective-permute-start.26
  77.6 8.4 %word_products.1 = (bf16[64,64,128]{2,1,0:T(8,128)(2,1)}, bf16[64,64,128]{2,1,0:T(8,128)(2,1)}, bf16[64,64,128]{2,1,0:T(8,128)(2,1)S(1)}, f32[64,64,128]{2,1,0:T...) custom-call(s32[487]{0:T(512)S(1)} %pad_add_fusion.index_ref, ...), custom_call_target="tpu_custom_call" | custom-call | bytes 36900 | tf_op jit(solution)/shard_map/word_products/pallas_call | solution.py:316
  87.4 3.6 %collective-permute-start.23 = (bf16[64,32,128]{2,1,0:T(8,128)(2,1)S(1)}, bf16[64,32,128]{2,1,0:T(8,128)(2,1)S(1)}, u32[]{:S(2)}, u32[]{:S(2)}) collective-permute-start(bf16[64,32,128]{2,1,0:T(8,128)(2,1)S(1)} %add_up.32.refs_3_), channel_id=1, source_target_pairs={{0,2},{7,5},{2,4},{5,3},{4,6},{3,1},{8,10},{15,13},{10,12},{13,11}... | collective-permute-start | bytes 1572872 | tf_op jit(solution)/shard_map/ppermute | solution.py:447
  91.5 2.7 %collective-permute-start.27 = (bf16[64,32,128]{2,1,0:T(8,128)(2,1)S(1)}, bf16[64,32,128]{2,1,0:T(8,128)(2,1)S(1)}, u32[]{:S(2)}, u32[]{:S(2)}) collective-permute-start(bf16[64,32,128]{2,1,0:T(8,128)(2,1)S(1)} %add_up.34.refs_3_), channel_id=1, source_target_pairs={{0,2},{7,5},{2,4},{5,3},{4,6},{3,1},{8,10},{15,13},{10,12},{13,11}... | collective-permute-start | bytes 1572872 | tf_op jit(solution)/shard_map/ppermute | solution.py:447
  94.1 3.5 %collective-permute-done.23.refs_0_ = bf16[64,32,128]{2,1,0:T(8,128)(2,1)S(1)} collective-permute-done((bf16[64,32,128]{2,1,0:T(8,128)(2,1)S(1)}, bf16[64,32,128]{2,1,0:T(8,128)(2,1)S(1)}, u32[]{:S(2)}, u32[]{:S(2)}) %collective-permute-start.23) | collective-permute-done | bytes 524320 | tf_op jit(solution)/shard_map/ppermute | solution.py:447
  98.9 4.3 %collective-permute-done.27.refs_0_ = bf16[64,32,128]{2,1,0:T(8,128)(2,1)S(1)} collective-permute-done((bf16[64,32,128]{2,1,0:T(8,128)(2,1)S(1)}, bf16[64,32,128]{2,1,0:T(8,128)(2,1)S(1)}, u32[]{:S(2)}, u32[]{:S(2)}) %collective-permute-start.27) | collective-permute-done | bytes 524320 | tf_op jit(solution)/shard_map/ppermute | solution.py:447
  105.9 5.2 %collective-permute-start.32 = (bf16[64,32,128]{2,1,0:T(8,128)(2,1)}, bf16[64,32,128]{2,1,0:T(8,128)(2,1)}, u32[]{:S(2)}, u32[]{:S(2)}) collective-permute-start(bf16[64,32,128]{2,1,0:T(8,128)(2,1)} %get-tuple-element.51.refs_3_), channel_id=1, source_target_pairs={{0,2},{7,5},{2,4},{5,3},{4,6},{3,1},{8,10},{15,13},{10,12},{13,11}... | collective-permute-start | bytes 1572872 | tf_op jit(solution)/shard_map/ppermute | solution.py:447
  114.4 2.7 %collective-permute-start.34 = (bf16[64,32,128]{2,1,0:T(8,128)(2,1)}, bf16[64,32,128]{2,1,0:T(8,128)(2,1)}, u32[]{:S(2)}, u32[]{:S(2)}) collective-permute-start(bf16[64,32,128]{2,1,0:T(8,128)(2,1)} %get-tuple-element.58.refs_3_), channel_id=1, source_target_pairs={{0,2},{7,5},{2,4},{5,3},{4,6},{3,1},{8,10},{15,13},{10,12},{13,11}... | collective-permute-start | bytes 1572872 | tf_op jit(solution)/shard_map/ppermute | solution.py:447
  118.6 1.4 add_up.37.refs_3_
  120.0 4.3 %collective-permute-start.33 = (bf16[64,32,128]{2,1,0:T(8,128)(2,1)S(1)}, bf16[64,32,128]{2,1,0:T(8,128)(2,1)S(1)}, u32[]{:S(2)}, u32[]{:S(2)}) collective-permute-start(bf16[64,32,128]{2,1,0:T(8,128)(2,1)S(1)} %add_up.37.refs_3_), channel_id=1, source_target_pairs={{0,2},{7,5},{2,4},{5,3},{4,6},{3,1},{8,10},{15,13},{10,12},{13,11}... | collective-permute-start | bytes 1572872 | tf_op jit(solution)/shard_map/ppermute | solution.py:447
  124.3 1.3 collective-permute-start.29
  125.7 1.4 add_up.38.refs_4_.refs_2_
  127.0 3.2 %collective-permute-start.36 = (bf16[64,32,128]{2,1,0:T(8,128)(2,1)S(1)}, bf16[64,32,128]{2,1,0:T(8,128)(2,1)S(1)}, u32[]{:S(2)}, u32[]{:S(2)}) collective-permute-start(bf16[64,32,128]{2,1,0:T(8,128)(2,1)S(1)} %add_up.38.refs_4_.refs_2_), channel_id=1, source_target_pairs={{0,2},{7,5},{2,4},{5,3},{4,6},{3,1},{8,10},{15,13},{10,12},{13,11}... | collective-permute-start | bytes 1572872 | tf_op jit(solution)/shard_map/ppermute | solution.py:447
  131.3 4.4 %collective-permute-start.35 = (bf16[64,32,128]{2,1,0:T(8,128)(2,1)S(1)}, bf16[64,32,128]{2,1,0:T(8,128)(2,1)S(1)}, u32[]{:S(2)}, u32[]{:S(2)}) collective-permute-start(bf16[64,32,128]{2,1,0:T(8,128)(2,1)S(1)} %add_up.39.refs_4_), channel_id=1, source_target_pairs={{0,2},{7,5},{2,4},{5,3},{4,6},{3,1},{8,10},{15,13},{10,12},{13,11}... | collective-permute-start | bytes 1572872 | tf_op jit(solution)/shard_map/ppermute | solution.py:447
  137.2 4.4 %collective-permute-start.40 = (bf16[64,32,128]{2,1,0:T(8,128)(2,1)S(1)}, bf16[64,32,128]{2,1,0:T(8,128)(2,1)S(1)}, u32[]{:S(2)}, u32[]{:S(2)}) collective-permute-start(bf16[64,32,128]{2,1,0:T(8,128)(2,1)S(1)} %add_up.40.refs_3_), channel_id=1, source_target_pairs={{0,2},{7,5},{2,4},{5,3},{4,6},{3,1},{8,10},{15,13},{10,12},{13,11}... | collective-permute-start | bytes 1572872 | tf_op jit(solution)/shard_map/ppermute | solution.py:447
  144.1 4.1 %collective-permute-done.40.refs_2_.refs_0_ = bf16[64,32,128]{2,1,0:T(8,128)(2,1)S(1)} collective-permute-done((bf16[64,32,128]{2,1,0:T(8,128)(2,1)S(1)}, bf16[64,32,128]{2,1,0:T(8,128)(2,1)S(1)}, u32[]{:S(2)}, u32[]{:S(2)}) %collective-permute-start.40) | collective-permute-done | bytes 524320 | tf_op jit(solution)/shard_map/ppermute | solution.py:447
  148.3 4.4 %collective-permute-start.37 = (bf16[64,32,128]{2,1,0:T(8,128)(2,1)S(1)}, bf16[64,32,128]{2,1,0:T(8,128)(2,1)S(1)}, u32[]{:S(2)}, u32[]{:S(2)}) collective-permute-start(bf16[64,32,128]{2,1,0:T(8,128)(2,1)S(1)} %add_up.41.refs_3_), channel_id=1, source_target_pairs={{0,2},{7,5},{2,4},{5,3},{4,6},{3,1},{8,10},{15,13},{10,12},{13,11}... | collective-permute-start | bytes 1572872 | tf_op jit(solution)/shard_map/ppermute | solution.py:447
  153.1 3.2 %collective-permute-start.44 = (bf16[64,32,128]{2,1,0:T(8,128)(2,1)S(1)}, bf16[64,32,128]{2,1,0:T(8,128)(2,1)S(1)}, u32[]{:S(2)}, u32[]{:S(2)}) collective-permute-start(bf16[64,32,128]{2,1,0:T(8,128)(2,1)S(1)} %add_up.43.refs_7_.refs_3_), channel_id=1, source_target_pairs={{0,2},{7,5},{2,4},{5,3},{4,6},{3,1},{8,10},{15,13},{10,12},{13,11}... | collective-permute-start | bytes 1572872 | tf_op jit(solution)/shard_map/ppermute | solution.py:447
  157.0 2.3 collective-permute-done.37.refs_0_
  159.3 5.6 %collective-permute-done.44.refs_0_ = bf16[64,32,128]{2,1,0:T(8,128)(2,1)S(1)} collective-permute-done((bf16[64,32,128]{2,1,0:T(8,128)(2,1)S(1)}, bf16[64,32,128]{2,1,0:T(8,128)(2,1)S(1)}, u32[]{:S(2)}, u32[]{:S(2)}) %collective-permute-start.44) | collective-permute-done | bytes 524320 | tf_op jit(solution)/shard_map/ppermute | solution.py:447
  164.9 2.4 add_up.42.refs_2_
  167.4 4.4 %context_products.4 = (bf16[64,32,128]{2,1,0:T(8,128)(2,1)S(1)}, f32[64,32,128]{2,1,0:T(8,128)S(1)}) custom-call(s32[487]{0:T(512)S(1)} %pad_add_fusion.index_ref, bf16[160,128,128]{2,1,0:T(8,128)(2,1)S(1)} %bitcast.6, bf16[64,32,128]{2,1,0:T(8,128)(2,1)S(1)} %collective-permute-done.35.refs_2_.refs_0_, ...), custom_call_target="tpu_custom_call" | custom-call | bytes 36900 | tf_op jit(solution)/shard_map/context_products/pallas_call | solution.py:369
  171.9 1.5 collective-permute-start.51
  173.3 4.4 %context_products.5 = (bf16[64,32,128]{2,1,0:T(8,128)(2,1)S(1)}, f32[64,32,128]{2,1,0:T(8,128)S(1)}) custom-call(s32[487]{0:T(512)S(1)} %pad_add_fusion.index_ref, bf16[160,128,128]{2,1,0:T(8,128)(2,1)S(1)} %bitcast.6, bf16[64,32,128]{2,1,0:T(8,128)(2,1)S(1)} %collective-permute-done.40.refs_2_.refs_0_, ...), custom_call_target="tpu_custom_call" | custom-call | bytes 36900 | tf_op jit(solution)/shard_map/context_products/pallas_call | solution.py:369
  179.6 4.7 %collective-permute-start.50 = (bf16[64,32,128]{2,1,0:T(8,128)(2,1)S(1)}, bf16[64,32,128]{2,1,0:T(8,128)(2,1)S(1)}, u32[]{:S(2)}, u32[]{:S(2)}) collective-permute-start(bf16[64,32,128]{2,1,0:T(8,128)(2,1)S(1)} %get-tuple-element.62.refs_3_), channel_id=1, source_target_pairs={{0,2},{7,5},{2,4},{5,3},{4,6},{3,1},{8,10},{15,13},{10,12},{13,11}... | collective-permute-start | bytes 1572872 | tf_op jit(solution)/shard_map/ppermute | solution.py:447
  184.5 3.3 %collective-permute-start.49 = (bf16[64,32,128]{2,1,0:T(8,128)(2,1)S(1)}, bf16[64,32,128]{2,1,0:T(8,128)(2,1)S(1)}, u32[]{:S(2)}, u32[]{:S(2)}) collective-permute-start(bf16[64,32,128]{2,1,0:T(8,128)(2,1)S(1)} %get-tuple-element.65.refs_1_.refs_3_), channel_id=1, source_target_pairs={{0,2},{7,5},{2,4},{5,3},{4,6},{3,1},{8,10},{15,13},{10,12},{13,11}... | collective-permute-start | bytes 1572872 | tf_op jit(solution)/shard_map/ppermute | solution.py:447
  187.8 3.2 %collective-permute-done.50.refs_0_.refs_2_ = bf16[64,32,128]{2,1,0:T(8,128)(2,1)S(1)} collective-permute-done((bf16[64,32,128]{2,1,0:T(8,128)(2,1)S(1)}, bf16[64,32,128]{2,1,0:T(8,128)(2,1)S(1)}, u32[]{:S(2)}, u32[]{:S(2)}) %collective-permute-start.50) | collective-permute-done | bytes 524320 | tf_op jit(solution)/shard_map/ppermute | solution.py:447
  191.0 4.4 %collective-permute-start.54 = (bf16[64,32,128]{2,1,0:T(8,128)(2,1)S(1)}, bf16[64,32,128]{2,1,0:T(8,128)(2,1)S(1)}, u32[]{:S(2)}, u32[]{:S(2)}) collective-permute-start(bf16[64,32,128]{2,1,0:T(8,128)(2,1)S(1)} %add_up.46.refs_1_), channel_id=1, source_target_pairs={{0,2},{7,5},{2,4},{5,3},{4,6},{3,1},{8,10},{15,13},{10,12},{13,11}... | collective-permute-start | bytes 1572872 | tf_op jit(solution)/shard_map/ppermute | solution.py:447
  196.7 4.4 %collective-permute-start.53 = (bf16[64,32,128]{2,1,0:T(8,128)(2,1)S(1)}, bf16[64,32,128]{2,1,0:T(8,128)(2,1)S(1)}, u32[]{:S(2)}, u32[]{:S(2)}) collective-permute-start(bf16[64,32,128]{2,1,0:T(8,128)(2,1)S(1)} %add_up.47.refs_1_), channel_id=1, source_target_pairs={{0,2},{7,5},{2,4},{5,3},{4,6},{3,1},{8,10},{15,13},{10,12},{13,11}... | collective-permute-start | bytes 1572872 | tf_op jit(solution)/shard_map/ppermute | solution.py:447
  201.2 1.4 collective-permute-start.55
  203.4 4.2 %collective-permute-done.55.refs_2_ = bf16[32,32,128]{2,1,0:T(8,128)(2,1)S(1)} collective-permute-done((bf16[32,32,128]{2,1,0:T(8,128)(2,1)S(1)}, bf16[32,32,128]{2,1,0:T(8,128)(2,1)S(1)}, u32[]{:S(2)}, u32[]{:S(2)}) %collective-permute-start.55) | collective-permute-done | bytes 262176 | tf_op jit(solution)/shard_map/ppermute | solution.py:435
  207.7 3.3 %collective-permute-start.61 = (bf16[64,32,128]{2,1,0:T(8,128)(2,1)S(1)}, bf16[64,32,128]{2,1,0:T(8,128)(2,1)S(1)}, u32[]{:S(2)}, u32[]{:S(2)}) collective-permute-start(bf16[64,32,128]{2,1,0:T(8,128)(2,1)S(1)} %add_up.49.refs_1_), channel_id=1, source_target_pairs={{0,2},{7,5},{2,4},{5,3},{4,6},{3,1},{8,10},{15,13},{10,12},{13,11}... | collective-permute-start | bytes 1572872 | tf_op jit(solution)/shard_map/ppermute | solution.py:447
  211.1 2.7 %collective-permute-start.57 = (bf16[64,32,128]{2,1,0:T(8,128)(2,1)S(1)}, bf16[64,32,128]{2,1,0:T(8,128)(2,1)S(1)}, u32[]{:S(2)}, u32[]{:S(2)}) collective-permute-start(bf16[64,32,128]{2,1,0:T(8,128)(2,1)S(1)} %add_up.51), channel_id=1, source_target_pairs={{0,2},{7,5},{2,4},{5,3},{4,6},{3,1},{8,10},{15,13},{10,12},{13,11}... | collective-permute-start | bytes 1572872 | tf_op jit(solution)/shard_map/ppermute | solution.py:447
  214.3 3.3 %collective-permute-done.61.refs_0_ = bf16[64,32,128]{2,1,0:T(8,128)(2,1)S(1)} collective-permute-done((bf16[64,32,128]{2,1,0:T(8,128)(2,1)S(1)}, bf16[64,32,128]{2,1,0:T(8,128)(2,1)S(1)}, u32[]{:S(2)}, u32[]{:S(2)}) %collective-permute-start.61) | collective-permute-done | bytes 524320 | tf_op jit(solution)/shard_map/ppermute | solution.py:447
  218.1 5.1 %collective-permute-done.57.refs_0_ = bf16[64,32,128]{2,1,0:T(8,128)(2,1)S(1)} collective-permute-done((bf16[64,32,128]{2,1,0:T(8,128)(2,1)S(1)}, bf16[64,32,128]{2,1,0:T(8,128)(2,1)S(1)}, u32[]{:S(2)}, u32[]{:S(2)}) %collective-permute-start.57) | collective-permute-done | bytes 524320 | tf_op jit(solution)/shard_map/ppermute | solution.py:447
  223.2 3.7 %context_products.6 = (bf16[64,32,128]{2,1,0:T(8,128)(2,1)S(1)}, f32[64,32,128]{2,1,0:T(8,128)S(1)}) custom-call(s32[487]{0:T(512)S(1)} %pad_add_fusion.index_ref, bf16[160,128,128]{2,1,0:T(8,128)(2,1)S(1)} %bitcast.6, bf16[64,32,128]{2,1,0:T(8,128)(2,1)S(1)} %collective-permute-done.61.refs_0_, ...), custom_call_target="tpu_custom_call" | custom-call | bytes 36900 | tf_op jit(solution)/shard_map/context_products/pallas_call | solution.py:369
  227.0 3.7 %context_products.7 = (bf16[64,32,128]{2,1,0:T(8,128)(2,1)S(1)}, f32[64,32,128]{2,1,0:T(8,128)S(1)}) custom-call(s32[487]{0:T(512)S(1)} %pad_add_fusion.index_ref, bf16[160,128,128]{2,1,0:T(8,128)(2,1)S(1)} %bitcast.6, bf16[64,32,128]{2,1,0:T(8,128)(2,1)S(1)} %collective-permute-done.57.refs_0_, ...), custom_call_target="tpu_custom_call" | custom-call | bytes 36900 | tf_op jit(solution)/shard_map/context_products/pallas_call | solution.py:369
  230.7 1.5 collective-permute-start.67
  232.8 7.2 %collective-permute-done.67.refs_1_.refs_10_ = bf16[64,32,128]{2,1,0:T(8,128)(2,1)S(1)} collective-permute-done((bf16[64,32,128]{2,1,0:T(8,128)(2,1)S(1)}, bf16[64,32,128]{2,1,0:T(8,128)(2,1)S(1)}, u32[]{:S(2)}, u32[]{:S(2)}) %collective-permute-start.67) | collective-permute-done | bytes 524320 | tf_op jit(solution)/shard_map/ppermute | solution.py:435
  240.8 1.4 collective-permute-start.68
  242.2 5.6 %collective-permute-done.65.refs_1_.refs_7_ = bf16[64,32,128]{2,1,0:T(8,128)(2,1)S(1)} collective-permute-done((bf16[64,32,128]{2,1,0:T(8,128)(2,1)S(1)}, bf16[64,32,128]{2,1,0:T(8,128)(2,1)S(1)}, u32[]{:S(2)}, u32[]{:S(2)}) %collective-permute-start.65) | collective-permute-done | bytes 524320 | tf_op jit(solution)/shard_map/ppermute | solution.py:435
  248.8 1.4 collective-permute-start.66
  251.3 4.3 %turn_back.2 = f32[4096,128]{1,0:T(8,128)} custom-call(s32[1]{0:T(128)S(6)} %select_n.64.start_ref, f32[64,32,128]{2,1,0:T(8,128)} %copy-done.17, f32[64,32,128]{2,1,0:T(8,128)} %copy-done.18, f32[64,32,128]{2,1,0:T(8,128)} %copy-done.19, f32[64,32,128]{2,1,0:T(8,128)} %copy-done.20, bf16[64,32,128]{2,1,0:T(8,128)(2,1)S(1)} %copy-done.22), custom_call_target="tpu_custom_call" | custom-call | bytes 36900 | tf_op jit(solution)/shard_map/turn_back/pallas_call | solution.py:400
  255.7 3.8 %turn_back.3 = f32[4096,128]{1,0:T(8,128)} custom-call(s32[1]{0:T(128)} %constant.92.clone.1.place_ref.start_ref, f32[64,32,128]{2,1,0:T(8,128)S(1)} %get-tuple-element.66.refs_0_, bf16[64,32,128]{2,1,0:T(8,128)(2,1)S(1)} %collective-permute-done.51.refs_2_.refs_1_, bf16[32,32,128]{2,1,0:T(8,128)(2,1)S(1)} %collective-permute-done.55.refs_2_, ...), custom_call_target="tpu_custom_call" | custom-call | bytes 36900 | tf_op jit(solution)/shard_map/turn_back/pallas_call | solution.py:400
  (187 shorter events, 42.9 us)
Async XLA Ops:
  2.2 14.1 %collective-permute-start.12 = (bf16[32,64,128]{2,1,0:T(8,128)(2,1)S(1)}, bf16[32,64,128]{2,1,0:T(8,128)(2,1)S(1)}, u32[]{:S(2)}, u32[]{:S(2)}) collective-permute-start(bf16[32,64,128]{2,1,0:T(8,128)(2,1)S(1)} %turn_panel.2.refs_0_.refs_8_), channel_id=1, source_target_pairs={{0,8},{1,17},{2,10},{3,19},{4,12},{5,21},{6,14},{7,23},{8,0},{9,25... | collective-permute-start | bytes 1572872 | tf_op jit(solution)/shard_map/ppermute | solution.py:435
  11.5 9.4 %collective-permute-start.4 = (f32[128,128]{1,0:T(8,128)S(1)}, f32[128,128]{1,0:T(8,128)S(1)}, u32[]{:S(2)}, u32[]{:S(2)}) collective-permute-start(f32[128,128]{1,0:T(8,128)S(1)} %get-tuple-element.38.refs_0_), channel_id=1, source_target_pairs={{0,8},{8,0},{16,24},{24,16},{1,9},{9,1},{17,25},{25,17},{2,10},{10... | collective-permute-start | bytes 196616 | tf_op jit(solution)/shard_map/ppermute | solution.py:450
  12.6 11.0 %collective-permute-start.5 = (f32[128,128]{1,0:T(8,128)S(1)}, f32[128,128]{1,0:T(8,128)S(1)}, u32[]{:S(2)}, u32[]{:S(2)}) collective-permute-start(f32[128,128]{1,0:T(8,128)S(1)} %get-tuple-element.38.refs_0_), channel_id=1, source_target_pairs={{0,16},{8,24},{16,0},{24,8},{1,17},{9,25},{17,1},{25,9},{2,18},{10... | collective-permute-start | bytes 196616 | tf_op jit(solution)/shard_map/ppermute | solution.py:450
  13.6 25.0 %collective-permute-start.11 = (bf16[32,64,128]{2,1,0:T(8,128)(2,1)S(1)}, bf16[32,64,128]{2,1,0:T(8,128)(2,1)S(1)}, u32[]{:S(2)}, u32[]{:S(2)}) collective-permute-start(bf16[32,64,128]{2,1,0:T(8,128)(2,1)S(1)} %turn_panel.2.refs_0_.refs_8_), channel_id=1, source_target_pairs={{0,16},{1,9},{2,18},{3,11},{4,20},{5,13},{6,22},{7,15},{8,24},{9,1... | collective-permute-start | bytes 1572872 | tf_op jit(solution)/shard_map/ppermute | solution.py:435
  16.3 22.4 %collective-permute-start.13 = (bf16[32,64,128]{2,1,0:T(8,128)(2,1)S(1)}, bf16[32,64,128]{2,1,0:T(8,128)(2,1)S(1)}, u32[]{:S(2)}, u32[]{:S(2)}) collective-permute-start(bf16[32,64,128]{2,1,0:T(8,128)(2,1)S(1)} %collective-permute-done.12.refs_10_), channel_id=1, source_target_pairs={{0,16},{1,9},{2,18},{3,11},{4,20},{5,13},{6,22},{7,15},{8,24},{9,1... | collective-permute-start | bytes 1572872 | tf_op jit(solution)/shard_map/ppermute | solution.py:435
  19.0 5.9 %collective-permute-start.6 = (f32[128,128]{1,0:T(8,128)S(1)}, f32[128,128]{1,0:T(8,128)S(1)}, u32[]{:S(2)}, u32[]{:S(2)}) collective-permute-start(f32[128,128]{1,0:T(8,128)S(1)} %get-tuple-element.38.refs_0_), channel_id=1, source_target_pairs={{0,24},{8,16},{16,8},{24,0},{1,25},{9,17},{17,9},{25,1},{2,26},{10... | collective-permute-start | bytes 196616 | tf_op jit(solution)/shard_map/ppermute | solution.py:450
  21.0 8.7 %collective-permute-start.2 = (f32[128,128]{1,0:T(8,128)S(1)}, f32[128,128]{1,0:T(8,128)S(1)}, u32[]{:S(2)}, u32[]{:S(2)}) collective-permute-start(f32[128,128]{1,0:T(8,128)S(1)} %add.46), channel_id=1, source_target_pairs={{0,4},{1,5},{2,6},{3,7},{4,0},{5,1},{6,2},{7,3},{8,12},{9,13},{10,... | collective-permute-start | bytes 196616 | tf_op jit(solution)/shard_map/ppermute | solution.py:453
  25.0 5.6 %collective-permute-start.7 = (f32[8,128]{1,0:T(8,128)S(1)}, f32[8,128]{1,0:T(8,128)S(1)}, u32[]{:S(2)}, u32[]{:S(2)}) collective-permute-start(f32[8,128]{1,0:T(8,128)S(1)} %get-tuple-element.39.refs_0_), channel_id=1, source_target_pairs={{0,1},{1,0},{2,3},{3,2},{4,5},{5,4},{6,7},{7,6},{8,9},{9,8},{10,11... | collective-permute-start | bytes 12296 | tf_op jit(solution)/shard_map/ppermute | solution.py:438
  30.5 5.4 %collective-permute-start.10 = (f32[8,128]{1,0:T(8,128)S(1)}, f32[8,128]{1,0:T(8,128)S(1)}, u32[]{:S(2)}, u32[]{:S(2)}) collective-permute-start(f32[8,128]{1,0:T(8,128)S(1)} %add.48.refs_3_), channel_id=1, source_target_pairs={{0,6},{1,7},{2,4},{3,5},{4,2},{5,3},{6,0},{7,1},{8,14},{9,15},{10,... | collective-permute-start | bytes 12296 | tf_op jit(solution)/shard_map/ppermute | solution.py:453
  34.1 4.5 %collective-permute-start.9 = (f32[8,128]{1,0:T(8,128)S(1)}, f32[8,128]{1,0:T(8,128)S(1)}, u32[]{:S(2)}, u32[]{:S(2)}) collective-permute-start(f32[8,128]{1,0:T(8,128)S(1)} %add.48.refs_3_), channel_id=1, source_target_pairs={{0,4},{1,5},{2,6},{3,7},{4,0},{5,1},{6,2},{7,3},{8,12},{9,13},{10,... | collective-permute-start | bytes 12296 | tf_op jit(solution)/shard_map/ppermute | solution.py:453
  50.5 4.6 %collective-permute-start.16 = (bf16[64,64,128]{2,1,0:T(8,128)(2,1)S(1)}, bf16[64,64,128]{2,1,0:T(8,128)(2,1)S(1)}, u32[]{:S(2)}, u32[]{:S(2)}) collective-permute-start(bf16[64,64,128]{2,1,0:T(8,128)(2,1)S(1)} %get-tuple-element.46), channel_id=1, source_target_pairs={{1,0},{6,7},{9,8},{14,15},{17,16},{22,23},{25,24},{30,31}} | collective-permute-start | bytes 3145736 | tf_op jit(solution)/shard_map/ppermute | solution.py:438
  51.8 11.0 %collective-permute-start.15 = (bf16[64,64,128]{2,1,0:T(8,128)(2,1)S(1)}, bf16[64,64,128]{2,1,0:T(8,128)(2,1)S(1)}, u32[]{:S(2)}, u32[]{:S(2)}) collective-permute-start(bf16[64,64,128]{2,1,0:T(8,128)(2,1)S(1)} %get-tuple-element.44), channel_id=1, source_target_pairs={{1,0},{3,2},{4,5},{6,7},{9,8},{11,10},{12,13},{14,15},{17,16},{19,... | collective-permute-start | bytes 3145736 | tf_op jit(solution)/shard_map/ppermute | solution.py:438
  53.4 9.2 %collective-permute-start.21 = (bf16[32,64,128]{2,1,0:T(8,128)(2,1)S(1)}, bf16[32,64,128]{2,1,0:T(8,128)(2,1)S(1)}, u32[]{:S(2)}, u32[]{:S(2)}) collective-permute-start(bf16[32,64,128]{2,1,0:T(8,128)(2,1)S(1)} %turn_panel.3.refs_1_), channel_id=1, source_target_pairs={{0,8},{1,17},{2,10},{3,19},{4,12},{5,21},{6,14},{7,23},{8,0},{9,25... | collective-permute-start | bytes 1572872 | tf_op jit(solution)/shard_map/ppermute | solution.py:435
  55.4 9.1 %collective-permute-start.17 = (bf16[64,32,128]{2,1,0:T(8,128)(2,1)S(1)}, bf16[64,32,128]{2,1,0:T(8,128)(2,1)S(1)}, u32[]{:S(2)}, u32[]{:S(2)}) collective-permute-start(bf16[64,32,128]{2,1,0:T(8,128)(2,1)S(1)} %add_up.27.refs_2_), channel_id=1, source_target_pairs={{0,2},{7,5},{2,4},{5,3},{4,6},{3,1},{8,10},{15,13},{10,12},{13,11}... | collective-permute-start | bytes 1572872 | tf_op jit(solution)/shard_map/ppermute | solution.py:447
  58.1 11.9 %collective-permute-start.19 = (bf16[64,32,128]{2,1,0:T(8,128)(2,1)S(1)}, bf16[64,32,128]{2,1,0:T(8,128)(2,1)S(1)}, u32[]{:S(2)}, u32[]{:S(2)}) collective-permute-start(bf16[64,32,128]{2,1,0:T(8,128)(2,1)S(1)} %add_up.28.refs_3_.refs_1_.refs_2_), channel_id=1, source_target_pairs={{0,2},{7,5},{2,4},{5,3},{4,6},{3,1},{8,10},{15,13},{10,12},{13,11}... | collective-permute-start | bytes 1572872 | tf_op jit(solution)/shard_map/ppermute | solution.py:447
  60.1 26.0 %collective-permute-start.14 = (bf16[64,64,128]{2,1,0:T(8,128)(2,1)S(1)}, bf16[64,64,128]{2,1,0:T(8,128)(2,1)S(1)}, u32[]{:S(2)}, u32[]{:S(2)}) collective-permute-start(bf16[64,64,128]{2,1,0:T(8,128)(2,1)S(1)} %get-tuple-element.42), channel_id=1, source_target_pairs={{1,0},{2,3},{3,2},{4,5},{5,4},{6,7},{9,8},{10,11},{11,10},{12,13},... | collective-permute-start | bytes 3145736 | tf_op jit(solution)/shard_map/ppermute | solution.py:438
  62.7 41.1 %collective-permute-start.25 = (f32[64,64,128]{2,1,0:T(8,128)S(1)}, f32[64,64,128]{2,1,0:T(8,128)S(1)}, u32[]{:S(2)}, u32[]{:S(2)}) collective-permute-start(f32[64,64,128]{2,1,0:T(8,128)S(1)} %get-tuple-element.49.refs_0_), channel_id=1, source_target_pairs={{0,1},{1,0},{2,3},{3,2},{4,5},{5,4},{6,7},{7,6},{8,9},{9,8},{10,11... | collective-permute-start | bytes 6291464 | tf_op jit(solution)/shard_map/ppermute | solution.py:438
  62.8 12.2 %collective-permute-start.20 = (bf16[32,64,128]{2,1,0:T(8,128)(2,1)S(1)}, bf16[32,64,128]{2,1,0:T(8,128)(2,1)S(1)}, u32[]{:S(2)}, u32[]{:S(2)}) collective-permute-start(bf16[32,64,128]{2,1,0:T(8,128)(2,1)S(1)} %turn_panel.3.refs_1_), channel_id=1, source_target_pairs={{0,16},{1,9},{2,18},{3,11},{4,20},{5,13},{6,22},{7,15},{8,24},{9,1... | collective-permute-start | bytes 1572872 | tf_op jit(solution)/shard_map/ppermute | solution.py:435
  64.4 13.1 %collective-permute-start.22 = (bf16[32,64,128]{2,1,0:T(8,128)(2,1)S(1)}, bf16[32,64,128]{2,1,0:T(8,128)(2,1)S(1)}, u32[]{:S(2)}, u32[]{:S(2)}) collective-permute-start(bf16[32,64,128]{2,1,0:T(8,128)(2,1)S(1)} %add_up.31), channel_id=1, source_target_pairs={{0,16},{1,9},{2,18},{3,11},{4,20},{5,13},{6,22},{7,15},{8,24},{9,1... | collective-permute-start | bytes 1572872 | tf_op jit(solution)/shard_map/ppermute | solution.py:435
  70.1 16.0 %collective-permute-start.18 = (bf16[64,32,128]{2,1,0:T(8,128)(2,1)S(1)}, bf16[64,32,128]{2,1,0:T(8,128)(2,1)S(1)}, u32[]{:S(2)}, u32[]{:S(2)}) collective-permute-start(bf16[64,32,128]{2,1,0:T(8,128)(2,1)S(1)} %add_up.29.refs_3_), channel_id=1, source_target_pairs={{0,2},{7,5},{2,4},{5,3},{4,6},{3,1},{8,10},{15,13},{10,12},{13,11}... | collective-permute-start | bytes 1572872 | tf_op jit(solution)/shard_map/ppermute | solution.py:447
  74.9 16.1 %collective-permute-start.26 = (bf16[64,32,128]{2,1,0:T(8,128)(2,1)S(1)}, bf16[64,32,128]{2,1,0:T(8,128)(2,1)S(1)}, u32[]{:S(2)}, u32[]{:S(2)}) collective-permute-start(bf16[64,32,128]{2,1,0:T(8,128)(2,1)S(1)} %add_up.30.refs_5_.refs_3_), channel_id=1, source_target_pairs={{0,2},{7,5},{2,4},{5,3},{4,6},{3,1},{8,10},{15,13},{10,12},{13,11}... | collective-permute-start | bytes 1572872 | tf_op jit(solution)/shard_map/ppermute | solution.py:447
  87.4 10.3 %collective-permute-start.23 = (bf16[64,32,128]{2,1,0:T(8,128)(2,1)S(1)}, bf16[64,32,128]{2,1,0:T(8,128)(2,1)S(1)}, u32[]{:S(2)}, u32[]{:S(2)}) collective-permute-start(bf16[64,32,128]{2,1,0:T(8,128)(2,1)S(1)} %add_up.32.refs_3_), channel_id=1, source_target_pairs={{0,2},{7,5},{2,4},{5,3},{4,6},{3,1},{8,10},{15,13},{10,12},{13,11}... | collective-permute-start | bytes 1572872 | tf_op jit(solution)/shard_map/ppermute | solution.py:447
  91.5 11.8 %collective-permute-start.27 = (bf16[64,32,128]{2,1,0:T(8,128)(2,1)S(1)}, bf16[64,32,128]{2,1,0:T(8,128)(2,1)S(1)}, u32[]{:S(2)}, u32[]{:S(2)}) collective-permute-start(bf16[64,32,128]{2,1,0:T(8,128)(2,1)S(1)} %add_up.34.refs_3_), channel_id=1, source_target_pairs={{0,2},{7,5},{2,4},{5,3},{4,6},{3,1},{8,10},{15,13},{10,12},{13,11}... | collective-permute-start | bytes 1572872 | tf_op jit(solution)/shard_map/ppermute | solution.py:447
  97.7 6.4 %collective-permute-start.24 = (bf16[64,32,128]{2,1,0:T(8,128)(2,1)S(1)}, bf16[64,32,128]{2,1,0:T(8,128)(2,1)S(1)}, u32[]{:S(2)}, u32[]{:S(2)}) collective-permute-start(bf16[64,32,128]{2,1,0:T(8,128)(2,1)S(1)} %collective-permute-done.23.refs_0_), channel_id=1, source_target_pairs={{0,1},{1,0},{2,3},{3,2},{4,5},{5,4},{6,7},{7,6},{8,9},{9,8},{10,11... | collective-permute-start | bytes 1572872 | tf_op jit(solution)/shard_map/ppermute | solution.py:438
  97.7 19.4 %collective-permute-start.31 = (bf16[64,64,128]{2,1,0:T(8,128)(2,1)}, bf16[64,64,128]{2,1,0:T(8,128)(2,1)}, u32[]{:S(2)}, u32[]{:S(2)}) collective-permute-start(bf16[64,64,128]{2,1,0:T(8,128)(2,1)} %get-tuple-element.57), channel_id=1, source_target_pairs={{1,0},{6,7},{9,8},{14,15},{17,16},{22,23},{25,24},{30,31}} | collective-permute-start | bytes 3145736 | tf_op jit(solution)/shard_map/ppermute | solution.py:438
  103.3 9.2 %collective-permute-start.28 = (bf16[64,32,128]{2,1,0:T(8,128)(2,1)S(1)}, bf16[64,32,128]{2,1,0:T(8,128)(2,1)S(1)}, u32[]{:S(2)}, u32[]{:S(2)}) collective-permute-start(bf16[64,32,128]{2,1,0:T(8,128)(2,1)S(1)} %collective-permute-done.27.refs_0_), channel_id=1, source_target_pairs={{0,1},{1,0},{2,3},{3,2},{4,5},{5,4},{6,7},{7,6},{8,9},{9,8},{10,11... | collective-permute-start | bytes 1572872 | tf_op jit(solution)/shard_map/ppermute | solution.py:438
  103.3 49.9 %collective-permute-start.39 = (f32[64,64,128]{2,1,0:T(8,128)}, f32[64,64,128]{2,1,0:T(8,128)}, u32[]{:S(2)}, u32[]{:S(2)}) collective-permute-start(f32[64,64,128]{2,1,0:T(8,128)} %get-tuple-element.59.refs_0_), channel_id=1, source_target_pairs={{0,1},{1,0},{2,3},{3,2},{4,5},{5,4},{6,7},{7,6},{8,9},{9,8},{10,11... | collective-permute-start | bytes 6291464 | tf_op jit(solution)/shard_map/ppermute | solution.py:438
  105.9 11.4 %collective-permute-start.32 = (bf16[64,32,128]{2,1,0:T(8,128)(2,1)}, bf16[64,32,128]{2,1,0:T(8,128)(2,1)}, u32[]{:S(2)}, u32[]{:S(2)}) collective-permute-start(bf16[64,32,128]{2,1,0:T(8,128)(2,1)} %get-tuple-element.51.refs_3_), channel_id=1, source_target_pairs={{0,2},{7,5},{2,4},{5,3},{4,6},{3,1},{8,10},{15,13},{10,12},{13,11}... | collective-permute-start | bytes 1572872 | tf_op jit(solution)/shard_map/ppermute | solution.py:447
  111.1 19.1 %collective-permute-start.30 = (bf16[64,64,128]{2,1,0:T(8,128)(2,1)}, bf16[64,64,128]{2,1,0:T(8,128)(2,1)S(1)}, u32[]{:S(2)}, u32[]{:S(2)}) collective-permute-start(bf16[64,64,128]{2,1,0:T(8,128)(2,1)} %get-tuple-element.55), channel_id=1, source_target_pairs={{1,0},{3,2},{4,5},{6,7},{9,8},{11,10},{12,13},{14,15},{17,16},{19,... | collective-permute-start | bytes 3145736 | tf_op jit(solution)/shard_map/ppermute | solution.py:438
  114.4 11.3 %collective-permute-start.34 = (bf16[64,32,128]{2,1,0:T(8,128)(2,1)}, bf16[64,32,128]{2,1,0:T(8,128)(2,1)}, u32[]{:S(2)}, u32[]{:S(2)}) collective-permute-start(bf16[64,32,128]{2,1,0:T(8,128)(2,1)} %get-tuple-element.58.refs_3_), channel_id=1, source_target_pairs={{0,2},{7,5},{2,4},{5,3},{4,6},{3,1},{8,10},{15,13},{10,12},{13,11}... | collective-permute-start | bytes 1572872 | tf_op jit(solution)/shard_map/ppermute | solution.py:447
  120.0 11.0 %collective-permute-start.33 = (bf16[64,32,128]{2,1,0:T(8,128)(2,1)S(1)}, bf16[64,32,128]{2,1,0:T(8,128)(2,1)S(1)}, u32[]{:S(2)}, u32[]{:S(2)}) collective-permute-start(bf16[64,32,128]{2,1,0:T(8,128)(2,1)S(1)} %add_up.37.refs_3_), channel_id=1, source_target_pairs={{0,2},{7,5},{2,4},{5,3},{4,6},{3,1},{8,10},{15,13},{10,12},{13,11}... | collective-permute-start | bytes 1572872 | tf_op jit(solution)/shard_map/ppermute | solution.py:447
  124.3 17.3 %collective-permute-start.29 = (bf16[64,64,128]{2,1,0:T(8,128)(2,1)S(1)}, bf16[64,64,128]{2,1,0:T(8,128)(2,1)S(1)}, u32[]{:S(2)}, u32[]{:S(2)}) collective-permute-start(bf16[64,64,128]{2,1,0:T(8,128)(2,1)S(1)} %copy-done.14), channel_id=1, source_target_pairs={{1,0},{2,3},{3,2},{4,5},{5,4},{6,7},{9,8},{10,11},{11,10},{12,13},... | collective-permute-start | bytes 3145736 | tf_op jit(solution)/shard_map/ppermute | solution.py:438
  127.0 9.9 %collective-permute-start.36 = (bf16[64,32,128]{2,1,0:T(8,128)(2,1)S(1)}, bf16[64,32,128]{2,1,0:T(8,128)(2,1)S(1)}, u32[]{:S(2)}, u32[]{:S(2)}) collective-permute-start(bf16[64,32,128]{2,1,0:T(8,128)(2,1)S(1)} %add_up.38.refs_4_.refs_2_), channel_id=1, source_target_pairs={{0,2},{7,5},{2,4},{5,3},{4,6},{3,1},{8,10},{15,13},{10,12},{13,11}... | collective-permute-start | bytes 1572872 | tf_op jit(solution)/shard_map/ppermute | solution.py:447
  131.3 11.2 %collective-permute-start.35 = (bf16[64,32,128]{2,1,0:T(8,128)(2,1)S(1)}, bf16[64,32,128]{2,1,0:T(8,128)(2,1)S(1)}, u32[]{:S(2)}, u32[]{:S(2)}) collective-permute-start(bf16[64,32,128]{2,1,0:T(8,128)(2,1)S(1)} %add_up.39.refs_4_), channel_id=1, source_target_pairs={{0,2},{7,5},{2,4},{5,3},{4,6},{3,1},{8,10},{15,13},{10,12},{13,11}... | collective-permute-start | bytes 1572872 | tf_op jit(solution)/shard_map/ppermute | solution.py:447
  137.2 11.1 %collective-permute-start.40 = (bf16[64,32,128]{2,1,0:T(8,128)(2,1)S(1)}, bf16[64,32,128]{2,1,0:T(8,128)(2,1)S(1)}, u32[]{:S(2)}, u32[]{:S(2)}) collective-permute-start(bf16[64,32,128]{2,1,0:T(8,128)(2,1)S(1)} %add_up.40.refs_3_), channel_id=1, source_target_pairs={{0,2},{7,5},{2,4},{5,3},{4,6},{3,1},{8,10},{15,13},{10,12},{13,11}... | collective-permute-start | bytes 1572872 | tf_op jit(solution)/shard_map/ppermute | solution.py:447
  141.6 14.7 %collective-permute-start.41 = (bf16[64,32,128]{2,1,0:T(8,128)(2,1)}, bf16[64,32,128]{2,1,0:T(8,128)(2,1)S(1)}, u32[]{:S(2)}, u32[]{:S(2)}) collective-permute-start(bf16[64,32,128]{2,1,0:T(8,128)(2,1)} %collective-permute-done.32.refs_2_), channel_id=1, source_target_pairs={{0,1},{1,0},{2,3},{3,2},{4,5},{5,4},{6,7},{7,6},{8,9},{9,8},{10,11... | collective-permute-start | bytes 1572872 | tf_op jit(solution)/shard_map/ppermute | solution.py:438
  141.7 14.7 %collective-permute-start.42 = (bf16[64,32,128]{2,1,0:T(8,128)(2,1)S(1)}, bf16[64,32,128]{2,1,0:T(8,128)(2,1)S(1)}, u32[]{:S(2)}, u32[]{:S(2)}) collective-permute-start(bf16[64,32,128]{2,1,0:T(8,128)(2,1)S(1)} %collective-permute-done.33.refs_2_.refs_3_.refs_1_), channel_id=1, source_target_pairs={{0,1},{1,0},{2,3},{3,2},{4,5},{5,4},{6,7},{7,6},{8,9},{9,8},{10,11... | collective-permute-start | bytes 1572872 | tf_op jit(solution)/shard_map/ppermute | solution.py:438
  142.5 14.4 %collective-permute-start.43 = (bf16[64,32,128]{2,1,0:T(8,128)(2,1)S(1)}, bf16[64,32,128]{2,1,0:T(8,128)(2,1)S(1)}, u32[]{:S(2)}, u32[]{:S(2)}) collective-permute-start(bf16[64,32,128]{2,1,0:T(8,128)(2,1)S(1)} %collective-permute-done.35.refs_2_.refs_0_), channel_id=1, source_target_pairs={{0,1},{1,0},{2,3},{3,2},{4,5},{5,4},{6,7},{7,6},{8,9},{9,8},{10,11... | collective-permute-start | bytes 1572872 | tf_op jit(solution)/shard_map/ppermute | solution.py:438
  148.3 11.1 %collective-permute-start.37 = (bf16[64,32,128]{2,1,0:T(8,128)(2,1)S(1)}, bf16[64,32,128]{2,1,0:T(8,128)(2,1)S(1)}, u32[]{:S(2)}, u32[]{:S(2)}) collective-permute-start(bf16[64,32,128]{2,1,0:T(8,128)(2,1)S(1)} %add_up.41.refs_3_), channel_id=1, source_target_pairs={{0,2},{7,5},{2,4},{5,3},{4,6},{3,1},{8,10},{15,13},{10,12},{13,11}... | collective-permute-start | bytes 1572872 | tf_op jit(solution)/shard_map/ppermute | solution.py:447
  153.1 11.8 %collective-permute-start.44 = (bf16[64,32,128]{2,1,0:T(8,128)(2,1)S(1)}, bf16[64,32,128]{2,1,0:T(8,128)(2,1)S(1)}, u32[]{:S(2)}, u32[]{:S(2)}) collective-permute-start(bf16[64,32,128]{2,1,0:T(8,128)(2,1)S(1)} %add_up.43.refs_7_.refs_3_), channel_id=1, source_target_pairs={{0,2},{7,5},{2,4},{5,3},{4,6},{3,1},{8,10},{15,13},{10,12},{13,11}... | collective-permute-start | bytes 1572872 | tf_op jit(solution)/shard_map/ppermute | solution.py:447
  156.3 15.5 %collective-permute-start.46 = (bf16[64,32,128]{2,1,0:T(8,128)(2,1)}, bf16[64,32,128]{2,1,0:T(8,128)(2,1)S(1)}, u32[]{:S(2)}, u32[]{:S(2)}) collective-permute-start(bf16[64,32,128]{2,1,0:T(8,128)(2,1)} %collective-permute-done.34.refs_2_), channel_id=1, source_target_pairs={{0,1},{1,0},{2,3},{3,2},{4,5},{5,4},{6,7},{7,6},{8,9},{9,8},{10,11... | collective-permute-start | bytes 1572872 | tf_op jit(solution)/shard_map/ppermute | solution.py:438
  156.4 16.9 %collective-permute-start.47 = (bf16[64,32,128]{2,1,0:T(8,128)(2,1)S(1)}, bf16[64,32,128]{2,1,0:T(8,128)(2,1)S(1)}, u32[]{:S(2)}, u32[]{:S(2)}) collective-permute-start(bf16[64,32,128]{2,1,0:T(8,128)(2,1)S(1)} %collective-permute-done.36.refs_2_.refs_3_.refs_1_), channel_id=1, source_target_pairs={{0,1},{1,0},{2,3},{3,2},{4,5},{5,4},{6,7},{7,6},{8,9},{9,8},{10,11... | collective-permute-start | bytes 1572872 | tf_op jit(solution)/shard_map/ppermute | solution.py:438
  156.9 16.4 %collective-permute-start.48 = (bf16[64,32,128]{2,1,0:T(8,128)(2,1)S(1)}, bf16[64,32,128]{2,1,0:T(8,128)(2,1)S(1)}, u32[]{:S(2)}, u32[]{:S(2)}) collective-permute-start(bf16[64,32,128]{2,1,0:T(8,128)(2,1)S(1)} %collective-permute-done.40.refs_2_.refs_0_), channel_id=1, source_target_pairs={{0,1},{1,0},{2,3},{3,2},{4,5},{5,4},{6,7},{7,6},{8,9},{9,8},{10,11... | collective-permute-start | bytes 1572872 | tf_op jit(solution)/shard_map/ppermute | solution.py:438
  159.3 19.1 %collective-permute-start.38 = (bf16[64,32,128]{2,1,0:T(8,128)(2,1)S(1)}, bf16[64,32,128]{2,1,0:T(8,128)(2,1)S(1)}, u32[]{:S(2)}, u32[]{:S(2)}) collective-permute-start(bf16[64,32,128]{2,1,0:T(8,128)(2,1)S(1)} %collective-permute-done.37.refs_0_), channel_id=1, source_target_pairs={{0,1},{1,0},{2,3},{3,2},{4,5},{5,4},{6,7},{7,6},{8,9},{9,8},{10,11... | collective-permute-start | bytes 1572872 | tf_op jit(solution)/shard_map/ppermute | solution.py:438
  164.9 19.4 %collective-permute-start.45 = (bf16[64,32,128]{2,1,0:T(8,128)(2,1)S(1)}, bf16[64,32,128]{2,1,0:T(8,128)(2,1)S(1)}, u32[]{:S(2)}, u32[]{:S(2)}) collective-permute-start(bf16[64,32,128]{2,1,0:T(8,128)(2,1)S(1)} %collective-permute-done.44.refs_0_), channel_id=1, source_target_pairs={{0,1},{1,0},{2,3},{3,2},{4,5},{5,4},{6,7},{7,6},{8,9},{9,8},{10,11... | collective-permute-start | bytes 1572872 | tf_op jit(solution)/shard_map/ppermute | solution.py:438
  171.9 15.9 %collective-permute-start.51 = (bf16[64,32,128]{2,1,0:T(8,128)(2,1)S(1)}, bf16[64,32,128]{2,1,0:T(8,128)(2,1)S(1)}, u32[]{:S(2)}, u32[]{:S(2)}) collective-permute-start(bf16[64,32,128]{2,1,0:T(8,128)(2,1)S(1)} %get-tuple-element.60.refs_4_.refs_7_), channel_id=1, source_target_pairs={{0,8},{1,17},{2,10},{3,19},{4,12},{5,21},{6,14},{7,23},{8,0},{9,25... | collective-permute-start | bytes 1572872 | tf_op jit(solution)/shard_map/ppermute | solution.py:435
  177.7 17.7 %collective-permute-start.52 = (bf16[64,32,128]{2,1,0:T(8,128)(2,1)S(1)}, bf16[64,32,128]{2,1,0:T(8,128)(2,1)S(1)}, u32[]{:S(2)}, u32[]{:S(2)}) collective-permute-start(bf16[64,32,128]{2,1,0:T(8,128)(2,1)S(1)} %get-tuple-element.63.refs_4_), channel_id=1, source_target_pairs={{0,8},{1,17},{2,10},{3,19},{4,12},{5,21},{6,14},{7,23},{8,0},{9,25... | collective-permute-start | bytes 1572872 | tf_op jit(solution)/shard_map/ppermute | solution.py:435
  179.6 11.4 %collective-permute-start.50 = (bf16[64,32,128]{2,1,0:T(8,128)(2,1)S(1)}, bf16[64,32,128]{2,1,0:T(8,128)(2,1)S(1)}, u32[]{:S(2)}, u32[]{:S(2)}) collective-permute-start(bf16[64,32,128]{2,1,0:T(8,128)(2,1)S(1)} %get-tuple-element.62.refs_3_), channel_id=1, source_target_pairs={{0,2},{7,5},{2,4},{5,3},{4,6},{3,1},{8,10},{15,13},{10,12},{13,11}... | collective-permute-start | bytes 1572872 | tf_op jit(solution)/shard_map/ppermute | solution.py:447
  184.5 12.1 %collective-permute-start.49 = (bf16[64,32,128]{2,1,0:T(8,128)(2,1)S(1)}, bf16[64,32,128]{2,1,0:T(8,128)(2,1)S(1)}, u32[]{:S(2)}, u32[]{:S(2)}) collective-permute-start(bf16[64,32,128]{2,1,0:T(8,128)(2,1)S(1)} %get-tuple-element.65.refs_1_.refs_3_), channel_id=1, source_target_pairs={{0,2},{7,5},{2,4},{5,3},{4,6},{3,1},{8,10},{15,13},{10,12},{13,11}... | collective-permute-start | bytes 1572872 | tf_op jit(solution)/shard_map/ppermute | solution.py:447
  191.0 16.6 %collective-permute-start.54 = (bf16[64,32,128]{2,1,0:T(8,128)(2,1)S(1)}, bf16[64,32,128]{2,1,0:T(8,128)(2,1)S(1)}, u32[]{:S(2)}, u32[]{:S(2)}) collective-permute-start(bf16[64,32,128]{2,1,0:T(8,128)(2,1)S(1)} %add_up.46.refs_1_), channel_id=1, source_target_pairs={{0,2},{7,5},{2,4},{5,3},{4,6},{3,1},{8,10},{15,13},{10,12},{13,11}... | collective-permute-start | bytes 1572872 | tf_op jit(solution)/shard_map/ppermute | solution.py:447
  196.7 14.3 %collective-permute-start.53 = (bf16[64,32,128]{2,1,0:T(8,128)(2,1)S(1)}, bf16[64,32,128]{2,1,0:T(8,128)(2,1)S(1)}, u32[]{:S(2)}, u32[]{:S(2)}) collective-permute-start(bf16[64,32,128]{2,1,0:T(8,128)(2,1)S(1)} %add_up.47.refs_1_), channel_id=1, source_target_pairs={{0,2},{7,5},{2,4},{5,3},{4,6},{3,1},{8,10},{15,13},{10,12},{13,11}... | collective-permute-start | bytes 1572872 | tf_op jit(solution)/shard_map/ppermute | solution.py:447
  201.2 6.4 %collective-permute-start.55 = (bf16[32,32,128]{2,1,0:T(8,128)(2,1)S(1)}, bf16[32,32,128]{2,1,0:T(8,128)(2,1)S(1)}, u32[]{:S(2)}, u32[]{:S(2)}) collective-permute-start(bf16[32,32,128]{2,1,0:T(8,128)(2,1)S(1)} %add_up.48), channel_id=1, source_target_pairs={{0,16},{1,9},{2,18},{3,11},{4,20},{5,13},{6,22},{7,15},{8,24},{9,1... | collective-permute-start | bytes 786440 | tf_op jit(solution)/shard_map/ppermute | solution.py:435
  202.6 8.3 %collective-permute-start.56 = (bf16[32,32,128]{2,1,0:T(8,128)(2,1)S(1)}, bf16[32,32,128]{2,1,0:T(8,128)(2,1)S(1)}, u32[]{:S(2)}, u32[]{:S(2)}) collective-permute-start(bf16[32,32,128]{2,1,0:T(8,128)(2,1)S(1)} %add_up.50), channel_id=1, source_target_pairs={{0,16},{1,9},{2,18},{3,11},{4,20},{5,13},{6,22},{7,15},{8,24},{9,1... | collective-permute-start | bytes 786440 | tf_op jit(solution)/shard_map/ppermute | solution.py:435
  203.4 14.2 %collective-permute-start.62 = (bf16[64,32,128]{2,1,0:T(8,128)(2,1)S(1)}, bf16[64,32,128]{2,1,0:T(8,128)(2,1)S(1)}, u32[]{:S(2)}, u32[]{:S(2)}) collective-permute-start(bf16[64,32,128]{2,1,0:T(8,128)(2,1)S(1)} %collective-permute-done.50.refs_0_.refs_2_), channel_id=1, source_target_pairs={{0,1},{1,0},{2,3},{3,2},{4,5},{5,4},{6,7},{7,6},{8,9},{9,8},{10,11... | collective-permute-start | bytes 1572872 | tf_op jit(solution)/shard_map/ppermute | solution.py:438
  207.7 9.9 %collective-permute-start.61 = (bf16[64,32,128]{2,1,0:T(8,128)(2,1)S(1)}, bf16[64,32,128]{2,1,0:T(8,128)(2,1)S(1)}, u32[]{:S(2)}, u32[]{:S(2)}) collective-permute-start(bf16[64,32,128]{2,1,0:T(8,128)(2,1)S(1)} %add_up.49.refs_1_), channel_id=1, source_target_pairs={{0,2},{7,5},{2,4},{5,3},{4,6},{3,1},{8,10},{15,13},{10,12},{13,11}... | collective-permute-start | bytes 1572872 | tf_op jit(solution)/shard_map/ppermute | solution.py:447
  211.1 12.1 %collective-permute-start.57 = (bf16[64,32,128]{2,1,0:T(8,128)(2,1)S(1)}, bf16[64,32,128]{2,1,0:T(8,128)(2,1)S(1)}, u32[]{:S(2)}, u32[]{:S(2)}) collective-permute-start(bf16[64,32,128]{2,1,0:T(8,128)(2,1)S(1)} %add_up.51), channel_id=1, source_target_pairs={{0,2},{7,5},{2,4},{5,3},{4,6},{3,1},{8,10},{15,13},{10,12},{13,11}... | collective-permute-start | bytes 1572872 | tf_op jit(solution)/shard_map/ppermute | solution.py:447
  213.8 13.2 %collective-permute-start.58 = (bf16[64,32,128]{2,1,0:T(8,128)(2,1)S(1)}, bf16[64,32,128]{2,1,0:T(8,128)(2,1)S(1)}, u32[]{:S(2)}, u32[]{:S(2)}) collective-permute-start(bf16[64,32,128]{2,1,0:T(8,128)(2,1)S(1)} %collective-permute-done.49.refs_0_.refs_2_), channel_id=1, source_target_pairs={{0,1},{1,0},{2,3},{3,2},{4,5},{5,4},{6,7},{7,6},{8,9},{9,8},{10,11... | collective-permute-start | bytes 1572872 | tf_op jit(solution)/shard_map/ppermute | solution.py:438
  213.8 9.4 %collective-permute-start.63 = (bf16[64,32,128]{2,1,0:T(8,128)(2,1)S(1)}, bf16[64,32,128]{2,1,0:T(8,128)(2,1)S(1)}, u32[]{:S(2)}, u32[]{:S(2)}) collective-permute-start(bf16[64,32,128]{2,1,0:T(8,128)(2,1)S(1)} %collective-permute-done.54.refs_0_.refs_1_), channel_id=1, source_target_pairs={{0,1},{1,0},{2,3},{3,2},{4,5},{5,4},{6,7},{7,6},{8,9},{9,8},{10,11... | collective-permute-start | bytes 1572872 | tf_op jit(solution)/shard_map/ppermute | solution.py:438
  217.6 5.6 %collective-permute-start.64 = (bf16[64,32,128]{2,1,0:T(8,128)(2,1)S(1)}, bf16[64,32,128]{2,1,0:T(8,128)(2,1)S(1)}, u32[]{:S(2)}, u32[]{:S(2)}) collective-permute-start(bf16[64,32,128]{2,1,0:T(8,128)(2,1)S(1)} %collective-permute-done.61.refs_0_), channel_id=1, source_target_pairs={{0,1},{1,0},{2,3},{3,2},{4,5},{5,4},{6,7},{7,6},{8,9},{9,8},{10,11... | collective-permute-start | bytes 1572872 | tf_op jit(solution)/shard_map/ppermute | solution.py:438
  217.6 9.4 %collective-permute-start.59 = (bf16[64,32,128]{2,1,0:T(8,128)(2,1)S(1)}, bf16[64,32,128]{2,1,0:T(8,128)(2,1)S(1)}, u32[]{:S(2)}, u32[]{:S(2)}) collective-permute-start(bf16[64,32,128]{2,1,0:T(8,128)(2,1)S(1)} %collective-permute-done.53.refs_0_.refs_1_), channel_id=1, source_target_pairs={{0,1},{1,0},{2,3},{3,2},{4,5},{5,4},{6,7},{7,6},{8,9},{9,8},{10,11... | collective-permute-start | bytes 1572872 | tf_op jit(solution)/shard_map/ppermute | solution.py:438
  230.7 9.2 %collective-permute-start.67 = (bf16[64,32,128]{2,1,0:T(8,128)(2,1)S(1)}, bf16[64,32,128]{2,1,0:T(8,128)(2,1)S(1)}, u32[]{:S(2)}, u32[]{:S(2)}) collective-permute-start(bf16[64,32,128]{2,1,0:T(8,128)(2,1)S(1)} %get-tuple-element.69.refs_4_), channel_id=1, source_target_pairs={{0,8},{1,17},{2,10},{3,19},{4,12},{5,21},{6,14},{7,23},{8,0},{9,25... | collective-permute-start | bytes 1572872 | tf_op jit(solution)/shard_map/ppermute | solution.py:435
  232.3 15.6 %collective-permute-start.65 = (bf16[64,32,128]{2,1,0:T(8,128)(2,1)S(1)}, bf16[64,32,128]{2,1,0:T(8,128)(2,1)S(1)}, u32[]{:S(2)}, u32[]{:S(2)}) collective-permute-start(bf16[64,32,128]{2,1,0:T(8,128)(2,1)S(1)} %get-tuple-element.68.refs_7_), channel_id=1, source_target_pairs={{0,8},{1,17},{2,10},{3,19},{4,12},{5,21},{6,14},{7,23},{8,0},{9,25... | collective-permute-start | bytes 1572872 | tf_op jit(solution)/shard_map/ppermute | solution.py:435
  240.8 14.8 %collective-permute-start.68 = (bf16[32,32,128]{2,1,0:T(8,128)(2,1)}, bf16[32,32,128]{2,1,0:T(8,128)(2,1)}, u32[]{:S(2)}, u32[]{:S(2)}) collective-permute-start(bf16[32,32,128]{2,1,0:T(8,128)(2,1)} %add_up.53), channel_id=1, source_target_pairs={{0,16},{1,9},{2,18},{3,11},{4,20},{5,13},{6,22},{7,15},{8,24},{9,1... | collective-permute-start | bytes 786440 | tf_op jit(solution)/shard_map/ppermute | solution.py:435
  248.8 6.9 %collective-permute-start.66 = (bf16[32,32,128]{2,1,0:T(8,128)(2,1)}, bf16[32,32,128]{2,1,0:T(8,128)(2,1)}, u32[]{:S(2)}, u32[]{:S(2)}) collective-permute-start(bf16[32,32,128]{2,1,0:T(8,128)(2,1)} %add_up.52), channel_id=1, source_target_pairs={{0,16},{1,9},{2,18},{3,11},{4,20},{5,13},{6,22},{7,15},{8,24},{9,1... | collective-permute-start | bytes 786440 | tf_op jit(solution)/shard_map/ppermute | solution.py:435
  (37 other events, 298.7 us)

commit v3 on v2

--- a/solution.py
+++ b/solution.py
@@ -89,7 +89,7 @@
 
     return pl.pallas_call(
         kernel,
-        in_specs=[HBM, ANY, ANY] + [ANY] * len(deps),
+        in_specs=[HBM] * 3 + [ANY] * len(deps),
         out_specs=[IN_VMEM] * 2,
         out_shape=[
             jax.ShapeDtypeStruct((band_rows, tile), F32),
@@ -104,31 +104,53 @@
         compiler_params=params(48),
         cost_estimate=cost(0.01),
         name="count_sums",
-    )(counts, rows, cols, *deps)
-
-
-def smoothed(contexts):
-    band_cols, tile = contexts[0].shape
-
-    def kernel(*refs):
-        power_ref, log_ref = refs[len(contexts) :]
+    )(in_hbm(counts), in_hbm(rows), in_hbm(cols), *deps)
+
+
+def bundles(core, word_part, contexts):
+    band_rows, tile = word_part.shape
+    band_cols = contexts[0].shape[0]
+    half = band_rows // 2
+
+    def kernel(core_ref, word_ref, *refs):
+        keep_ref, give_ref, log_ref = refs[len(contexts) :]
         total = refs[0][...]
         for ref in refs[1 : len(contexts)]:
             total = total + ref[...]
         root = jnp.sqrt(total)
         powers = root * jnp.sqrt(root)
-        power_ref[...] = jnp.sum(powers.reshape(band_cols // 8, 8, tile), axis=0)
+        power = jnp.sum(powers.reshape(band_cols // 8, 8, tile), axis=0)
+        for ref, at in ((keep_ref, core_ref[0]), (give_ref, 1 - core_ref[0])):
+            ref[:half] = word_ref[pl.ds(pl.multiple_of(at * half, half), half), :]
+            ref[half:] = power
         log_ref[...] = jnp.maximum(0.75 * jnp.log(total), 0.0)
 
     return pl.pallas_call(
         kernel,
+        in_specs=[IN_SMEM] + [IN_VMEM] * (1 + len(contexts)),
+        out_specs=[IN_VMEM] * 3,
         out_shape=[
-            jax.ShapeDtypeStruct((8, tile), F32),
+            jax.ShapeDtypeStruct((half + 8, tile), F32),
+            jax.ShapeDtypeStruct((half + 8, tile), F32),
             jax.ShapeDtypeStruct((band_cols, tile), F32),
         ],
         compiler_params=params(16),
-        name="smoothed",
-    )(*contexts)
+        name="bundles",
+    )(core, word_part, *contexts)
+
+
+def plus(a, b):
+    def kernel(a_ref, b_ref, out_ref):
+        out_ref[...] = a_ref[...] + b_ref[...]
+
+    return pl.pallas_call(
+        kernel,
+        in_specs=[IN_VMEM] * 2,
+        out_specs=IN_VMEM,
+        out_shape=jax.ShapeDtypeStruct(a.shape, a.dtype),
+        compiler_params=params(16),
+        name="plus",
+    )(a, b)
 
 
 def turn_panel(panel, tile, group, deps):
@@ -148,7 +170,7 @@
         out_shape=jax.ShapeDtypeStruct((blocks, part, tile), BF16),
         compiler_params=params(16),
         name="turn_panel",
-    )(panel, *deps)
+    )(in_hbm(panel), *deps)
 
 
 def add_up(terms, count, width, dtypes, deps=(), other=None):
@@ -191,7 +213,10 @@
             in_specs=blocks + [ANY] * len(deps),
             out_specs=[pl.BlockSpec(shape, lambda n, _: (0, 0, 0))] * len(dtypes),
         ),
-        out_shape=[jax.ShapeDtypeStruct(shape, dtype) for dtype in dtypes],
+        out_shape=[
+            (pltpu.HBM if len(dtypes) > 1 and dtype == F32 else jax.ShapeDtypeStruct)(shape, dtype)
+            for dtype in dtypes
+        ],
         compiler_params=params(24),
         cost_estimate=cost(0.01),
         name="add_up",
@@ -207,14 +232,12 @@
     chip_list = 3 * slots
     pieces = math.gcd(slots, 10)
     piece = slots // pieces
-    n_powers = 0 if source is None else len(source[2])
 
     def kernel(index_ref, *refs):
         if source is None:
             tiles_ref, *refs = refs
         else:
-            counts_hbm, first_ref, second_ref, *refs = refs
-            power_refs, (log_ref, *refs) = refs[:n_powers], refs[n_powers:]
+            counts_hbm, core_ref, own_ref, other_ref, log_ref, *refs = refs
         block_refs, refs = refs[:n_in], refs[n_in + len(deps) :]
         if source is not None:
             tiles_ref, *refs = refs
@@ -238,12 +261,11 @@
 
             for n in range(pieces):
                 arriving(n).start()
-            rows = first_ref.shape[0]
-            word_log[:rows] = jnp.log(jnp.maximum(first_ref[...], 1.0))
-            word_log[rows:] = jnp.log(jnp.maximum(second_ref[...], 1.0))
-            power = power_refs[0][...]
-            for ref in power_refs[1:]:
-                power = power + ref[...]
+            half = own_ref.shape[0] - 8
+            for ref, at in ((own_ref, core_ref[0]), (other_ref, 1 - core_ref[0])):
+                rows = pl.ds(pl.multiple_of(at * half, half), half)
+                word_log[rows, :] = jnp.log(jnp.maximum(ref[:half], 1.0))
+            power = own_ref[half:]
             power = jnp.sum(jnp.sum(power, axis=0, keepdims=True), axis=1, keepdims=True)
             shift[...] = (jnp.log(power) - math.log(NEG_SAMPLES)) - log_ref[...]
         for copy in copies:
@@ -290,7 +312,7 @@
                 out[...] = acc[pl.ds(at * block_rows, block_rows)].astype(out.dtype)
 
     out_shape = [
-        pltpu.VMEM((block_rows, width, tile), F32 if slot == chips - 1 else BF16)
+        pltpu.VMEM((block_rows, width, tile), BF16)
         for slot in range(slot_count)
     ]
     out_specs = [IN_VMEM] * slot_count
@@ -302,14 +324,14 @@
     if source is None:
         operands, operand_specs = [tiles], [IN_VMEM]
     else:
-        operands = [in_hbm(source[0]), *source[1], *source[2], source[3]]
-        operand_specs = [HBM] + [IN_VMEM] * (len(operands) - 1)
+        operands = [in_hbm(source[0]), *source[1:]]
+        operand_specs = [HBM, IN_SMEM] + [IN_VMEM] * 3
     if source is not None:
         out_shape = [pltpu.VMEM(shape, BF16)] + out_shape
         out_specs = [IN_VMEM] + out_specs
         scratch += [
-            pltpu.VMEM((2 * source[1][0].shape[0], tile), F32),
-            pltpu.VMEM(source[3].shape, F32),
+            pltpu.VMEM((chips * block_rows, tile), F32),
+            pltpu.VMEM(source[-1].shape, F32),
             pltpu.VMEM(shape, jnp.int32),
             pltpu.SemaphoreType.DMA((pieces,)),
         ]
@@ -481,17 +503,12 @@
 
     word_part, context = count_sums(counts, rows, cols, band_rows, band_cols, (turned_panel,))
     contexts = [context] + [row_xor(context, mask) for mask in range(1, n_row)]
-    power, context_log = smoothed(contexts)
-    next_blocks = spread(turn_panel(panel, tile, 1, (power,)))
-    half = band_rows // 2
-    first, second = word_part[:half], word_part[half:]
-    totals = jnp.where(core == 0, first, second) + core_swap(jnp.where(core == 0, second, first))
+    this_core = core.reshape(1)
+    bundle, given, context_log = bundles(this_core, word_part, contexts)
+    next_blocks = spread(turn_panel(panel, tile, 1, (bundle,)))
+    bundle = plus(bundle, core_swap(given))
     for step in range(chips.bit_length() - 1):
-        totals = totals + chip_xor(totals, 1 << step)
-    other_half = core_swap(totals)
-    halves = [jnp.where(core == 0, totals, other_half), jnp.where(core == 0, other_half, totals)]
-    power = power + core_swap(power)
-    powers = [power] + [chip_xor(power, mask) for mask in range(1, chips)]
+        bundle = plus(bundle, chip_xor(bundle, 1 << step))
 
     part = panel.shape[1] // (GROUPS * PARTS)
     groups = [None] * GROUPS
@@ -500,27 +517,25 @@
     own = [[None] * PARTS for _ in range(GROUPS)]
     word_pieces, context_pieces = [], []
     stages = [[[] for _ in range(PARTS)] for _ in range(GROUPS)]
-    source = (counts, halves, powers, context_log)
+    source = (counts, this_core, bundle, core_swap(bundle), context_log)
     tiles, *groups[0] = word_products(index, panel_blocks, chips, block_rows, source=source)
     got, passed = [None] * PARTS, {}
     last = ()
 
-    def contexts_of(group, deps):
-        for n in range(PARTS):
-            blocks = [near[group][n][d] for d in range(chips - 1, 0, -1)] + [own[group][n]]
-            blocks += [swapped[group][n][d] for d in range(1, chips)]
-            send, keep = context_products(index, tiles, blocks, band_cols, deps)
-            deps = (send,)
-            stages[group][n].append(send)
-            terms, count = [(keep, 0)], band_cols // 2
-            for step in range(bits):
-                terms.append((row_swap(send, step), 0))
-                stages[group][n].append(terms[-1][0])
-                if step < bits - 1:
-                    count //= 2
-                    (send,) = add_up([(x, (2 * y + 1, 0)) for x, y in terms], count, part, [BF16])
-                    terms = [(x, 2 * y) for x, y in terms]
-            context_pieces.append([x for x, _ in terms])
+    def contexts_of(group, n, deps):
+        blocks = [near[group][n][d] for d in range(chips - 1, 0, -1)] + [own[group][n]]
+        blocks += [swapped[group][n][d] for d in range(1, chips)]
+        send, keep = context_products(index, tiles, blocks, band_cols, deps)
+        stages[group][n].append(send)
+        terms, count = [(keep, 0)], band_cols // 2
+        for step in range(bits):
+            terms.append((row_swap(send, step), 0))
+            stages[group][n].append(terms[-1][0])
+            if step < bits - 1:
+                count //= 2
+                (send,) = add_up([(x, (2 * y + 1, 0)) for x, y in terms], count, part, [BF16])
+                terms = [(x, 2 * y) for x, y in terms]
+        context_pieces.append([x for x, _ in terms])
 
     for slot in range(chips * GROUPS + chips - 2):
         group, step = slot // chips, slot % chips + 1
@@ -539,9 +554,13 @@
             if group < GROUPS and step == chips:
                 if group:
                     last = (*last, stages[before][n][0])
+                    if n:
+                        (got[n],) = add_up([(got[n], (0, 0))], block_rows, part, [BF16], first_sent)
                 terms = [(got[n], (0, 0)), (core_swap(got[n]), (0, 0)), (mine_sum, (0, n))]
                 payload, whole = add_up(terms, block_rows, part, [BF16, F32], last)
                 own[group][n] = payload
+                if group and n + 1 < PARTS:
+                    contexts_of(before, n + 1, (payload,))
                 word_pieces.append([whole])
             elif group < GROUPS:
                 terms = [(kept[far], (0, n)), (passed[far], (0, n))]
@@ -564,8 +583,13 @@
                 arrived = (before, hop)
             else:
                 continue
+            if group == GROUPS and hop == chips - 1 and n > 0:
+                gate = stages[before][n - 1][:1]
+                (got[n],) = add_up([(got[n], (0, 0))], block_rows, part, [BF16], gate)
             near[arrived[0]][n][arrived[1]] = got[n]
             swapped[arrived[0]][n][arrived[1]] = core_swap(got[n])
+            if group == GROUPS and hop == chips - 1:
+                contexts_of(before, n, ())
         if step == 1 and group < GROUPS - 1:
             panel_blocks = spread_on(next_blocks, last)
         if step == 2 and group < GROUPS - 1:
@@ -576,9 +600,8 @@
             if group + 2 < GROUPS:
                 next_blocks = spread(turn_panel(panel, tile, group + 2, last))
         if group > 0 and step == chips - 1 and group < GROUPS:
-            contexts_of(before, last)
-        if group == GROUPS and hop == chips - 1:
-            contexts_of(before, ())
+            contexts_of(before, 0, last)
+            first_sent = stages[before][0][:1]
     deps = (stages[-1][-1][0],)
     word_out = turn_back(word_pieces, (core * share).reshape(1), share, 1.0, True, deps)
     zero = jnp.zeros((1,), jnp.int32)

time: 261 us -> 243 us (0.931)
  waiting for transfers between devices: 66.2 us -> 54.9 us
  local copies, waits for them, and re-layouts: 9.72 us -> 3.42 us
  starting transfers between devices: 119 us -> 114 us
  Pallas kernels: 63 us -> 67.5 us
    ppermute x20, waiting for transfers between devices: 38.9 us -> 25.3 us  [along(): return lax.ppermute(x, 'col', pairs)]
    ppermute x20, starting transfers between devices: 71.5 us -> 79.4 us  [along(): return lax.ppermute(x, 'col', pairs)]
    unnamed x64 -> x52, local copies, waits for them, and re-layouts: 9.72 us -> 3.42 us
    ppermute x5 -> x2, starting transfers between devices: 8.69 us -> 4.29 us  [chip_xor(): return lax.ppermute(x, 'col', [(c, c ^ 2 * mask) for c in range(n_col)])]
    ppermute x27 -> x26, starting transfers between devices: 16.7 us -> 12.6 us  [core_swap(): lax.ppermute(x, 'col', [(i, i ^ 1) for i in range(n_col) if keep(i % 2, i...]
    ppermute x14, starting transfers between devices: 17.8 us -> 14.1 us  [row_swap(): return lax.ppermute(x, ('row', 'col'), pairs)]
    pallas_call x27 -> x29, Pallas kernels: 13.8 us -> 17.5 us  [add_up(): pl.pallas_call(kernel, grid_spec=pltpu.PrefetchScalarGridSpec(num_scalar_...]
    ppermute x5 -> x2, waiting for transfers between devices: 5.3 us -> 5.4 us  [chip_xor(): return lax.ppermute(x, 'col', [(c, c ^ 2 * mask) for c in range(n_col)])]
  transfers between devices with their start and end apart: 69 -> 65, of which waited for: 27 -> 26; matrix products, arithmetic and copies ran while one was open for 0% -> 0% of each run, Pallas kernels for 17% -> 21%
where the time goes in v3:
time: 243 us; the launch traced here: 241 us
  starting transfers between devices  114 us (47%)
  Pallas kernels  67.5 us (28%)
  waiting for transfers between devices  54.9 us (23%)
  local copies, waits for them, and re-layouts  3.42 us (1%)
    ppermute x20, starting transfers between devices, along(): return lax.ppermute(x, 'col', pairs)  79.4 us
    ppermute x20, waiting for transfers between devices, along(): return lax.ppermute(x, 'col', pairs)  25.3 us
    pallas_call x2, Pallas kernels, word_products(): pl.pallas_call(kernel, in_specs=[IN_SMEM] + operand_specs + [ANY] * (n_in...  18.2 us
    ppermute x14, waiting for transfers between devices, row_swap(): return lax.ppermute(x, ('row', 'col'), pairs)  18 us
    pallas_call x29, Pallas kernels, add_up(): pl.pallas_call(kernel, grid_spec=pltpu.PrefetchScalarGridSpec(num_scalar_...  17.5 us
    pallas_call x4, Pallas kernels, context_products(): pl.pallas_call(kernel, in_specs=[IN_SMEM, IN_VMEM] + [ANY] * (slot_count...  15.6 us
    ppermute x14, starting transfers between devices, row_swap(): return lax.ppermute(x, ('row', 'col'), pairs)  14.1 us
    ppermute x26, starting transfers between devices, core_swap(): lax.ppermute(x, 'col', [(i, i ^ 1) for i in range(n_col) if keep(i % 2, i...  12.6 us
  transfers between devices with their start and end apart: 65, of which 26 were waited for; matrix products, arithmetic and copies ran while one was open for 0% of the time, Pallas kernels for 21%

profile of v3, /device:TPU:0, one launch (start us, length us, event | category | flops | bytes accessed | tf_op | source)
XLA Modules:
  0.0 241.3 jit_solution(16516785168118578821)
XLA Ops:
  0.6 1.5 turn_panel.2.refs_0_.refs_5_
  2.2 3.0 %collective-permute-start.8 = (bf16[32,64,128]{2,1,0:T(8,128)(2,1)S(1)}, bf16[32,64,128]{2,1,0:T(8,128)(2,1)S(1)}, u32[]{:S(2)}, u32[]{:S(2)}) collective-permute-start(bf16[32,64,128]{2,1,0:T(8,128)(2,1)S(1)} %turn_panel.2.refs_0_.refs_5_), channel_id=1, source_target_pairs={{0,8},{1,17},{2,10},{3,19},{4,12},{5,21},{6,14},{7,23},{8,0},{9,25... | collective-permute-start | bytes 1572872 | tf_op jit(solution)/shard_map/ppermute | solution.py:457
  5.2 4.9 %count_sums.1 = (f32[256,128]{1,0:T(8,128)S(1)}, f32[128,128]{1,0:T(8,128)S(1)}) custom-call(s32[160,128,128]{2,1,0:T(8,128)} %bitcast.8, s32[160]{0:T(256)} %bitcast.13, s32[160]{0:T(256)} %bitcast.10, bf16[32,64,128]{2,1,0:T(8,128)(2,1)S(1)} %turn_panel.2.refs_0_.refs_5_), custom_call_target="tpu_custom_call" | custom-call | bytes 36900 | tf_op jit(solution)/shard_map/count_sums/pallas_call | solution.py:90
  10.2 2.0 collective-permute-start.1
  12.2 1.4 collective-permute-start.2
  13.6 1.5 collective-permute-start.7
  15.7 2.5 %collective-permute-done.2.refs_3_ = f32[128,128]{1,0:T(8,128)S(1)} collective-permute-done((f32[128,128]{1,0:T(8,128)S(1)}, f32[128,128]{1,0:T(8,128)S(1)}, u32[]{:S(2)}, u32[]{:S(2)}) %collective-permute-start.2) | collective-permute-done | bytes 65568 | tf_op jit(solution)/shard_map/ppermute | solution.py:472
  19.5 1.6 collective-permute-start.4
  21.2 2.7 %collective-permute-done.4.b_ref = f32[136,128]{1,0:T(8,128)S(1)} collective-permute-done((f32[136,128]{1,0:T(8,128)S(1)}, f32[136,128]{1,0:T(8,128)S(1)}, u32[]{:S(2)}, u32[]{:S(2)}) %collective-permute-start.4) | collective-permute-done | bytes 69664 | tf_op jit(solution)/shard_map/ppermute | solution.py:475
  23.9 2.6 %collective-permute-start.5 = (f32[136,128]{1,0:T(8,128)S(1)}, f32[136,128]{1,0:T(8,128)S(1)}, u32[]{:S(2)}, u32[]{:S(2)}) collective-permute-start(f32[136,128]{1,0:T(8,128)S(1)} %plus.4.a_ref), channel_id=1, source_target_pairs={{0,4},{1,5},{2,6},{3,7},{4,0},{5,1},{6,2},{7,3},{8,12},{9,13},{10,... | collective-permute-start | bytes 208904 | tf_op jit(solution)/shard_map/ppermute | solution.py:475
  26.6 2.7 %collective-permute-done.5.b_ref = f32[136,128]{1,0:T(8,128)S(1)} collective-permute-done((f32[136,128]{1,0:T(8,128)S(1)}, f32[136,128]{1,0:T(8,128)S(1)}, u32[]{:S(2)}, u32[]{:S(2)}) %collective-permute-start.5) | collective-permute-done | bytes 69664 | tf_op jit(solution)/shard_map/ppermute | solution.py:475
  31.4 10.5 %ppmi_word_products.1 = (bf16[160,128,128]{2,1,0:T(8,128)(2,1)S(1)}, bf16[64,64,128]{2,1,0:T(8,128)(2,1)S(1)}, bf16[64,64,128]{2,1,0:T(8,128)(2,1)S(1)}, bf16[64...) custom-call(s32[487]{0:T(512)S(1)} %pad_add_fusion.index_ref, ...), custom_call_target="tpu_custom_call" | custom-call | bytes 36900 | tf_op jit(solution)/shard_map/ppmi_word_products/pallas_call | solution.py:338
  42.0 1.3 collective-permute-start.12
  43.3 1.3 collective-permute-start.11
  44.6 1.6 turn_panel.3.refs_1_
  46.2 1.6 collective-permute-start.17
  48.1 2.9 %collective-permute-start.13 = (bf16[64,32,128]{2,1,0:T(8,128)(2,1)S(1)}, bf16[64,32,128]{2,1,0:T(8,128)(2,1)S(1)}, u32[]{:S(2)}, u32[]{:S(2)}) collective-permute-start(bf16[64,32,128]{2,1,0:T(8,128)(2,1)S(1)} %add_up.29.refs_2_), channel_id=1, source_target_pairs={{0,2},{7,5},{2,4},{5,3},{4,6},{3,1},{8,10},{15,13},{10,12},{13,11}... | collective-permute-start | bytes 1572872 | tf_op jit(solution)/shard_map/ppermute | solution.py:469
  50.9 1.3 collective-permute-start.10
  52.6 5.0 %collective-permute-start.15 = (bf16[64,32,128]{2,1,0:T(8,128)(2,1)S(1)}, bf16[64,32,128]{2,1,0:T(8,128)(2,1)S(1)}, u32[]{:S(2)}, u32[]{:S(2)}) collective-permute-start(bf16[64,32,128]{2,1,0:T(8,128)(2,1)S(1)} %add_up.30.refs_3_.refs_1_.refs_2_), channel_id=1, source_target_pairs={{0,2},{7,5},{2,4},{5,3},{4,6},{3,1},{8,10},{15,13},{10,12},{13,11}... | collective-permute-start | bytes 1572872 | tf_op jit(solution)/shard_map/ppermute | solution.py:469
  58.3 1.6 collective-permute-start.18
  60.3 4.7 %collective-permute-start.14 = (bf16[64,32,128]{2,1,0:T(8,128)(2,1)S(1)}, bf16[64,32,128]{2,1,0:T(8,128)(2,1)S(1)}, u32[]{:S(2)}, u32[]{:S(2)}) collective-permute-start(bf16[64,32,128]{2,1,0:T(8,128)(2,1)S(1)} %add_up.31.refs_3_), channel_id=1, source_target_pairs={{0,2},{7,5},{2,4},{5,3},{4,6},{3,1},{8,10},{15,13},{10,12},{13,11}... | collective-permute-start | bytes 1572872 | tf_op jit(solution)/shard_map/ppermute | solution.py:469
  65.6 1.3 collective-permute-done.16.refs_2_
  66.8 4.7 %collective-permute-start.22 = (bf16[64,32,128]{2,1,0:T(8,128)(2,1)S(1)}, bf16[64,32,128]{2,1,0:T(8,128)(2,1)S(1)}, u32[]{:S(2)}, u32[]{:S(2)}) collective-permute-start(bf16[64,32,128]{2,1,0:T(8,128)(2,1)S(1)} %add_up.32.refs_5_.refs_3_), channel_id=1, source_target_pairs={{0,2},{7,5},{2,4},{5,3},{4,6},{3,1},{8,10},{15,13},{10,12},{13,11}... | collective-permute-start | bytes 1572872 | tf_op jit(solution)/shard_map/ppermute | solution.py:469
  72.5 7.7 %word_products.1 = (bf16[64,64,128]{2,1,0:T(8,128)(2,1)}, bf16[64,64,128]{2,1,0:T(8,128)(2,1)}, bf16[64,64,128]{2,1,0:T(8,128)(2,1)S(1)}, bf16[64,64,128]{2,1,0:...) custom-call(s32[487]{0:T(512)S(1)} %pad_add_fusion.index_ref, ...), custom_call_target="tpu_custom_call" | custom-call | bytes 36900 | tf_op jit(solution)/shard_map/word_products/pallas_call | solution.py:338
  82.1 4.7 %collective-permute-start.19 = (bf16[64,32,128]{2,1,0:T(8,128)(2,1)S(1)}, bf16[64,32,128]{2,1,0:T(8,128)(2,1)S(1)}, u32[]{:S(2)}, u32[]{:S(2)}) collective-permute-start(bf16[64,32,128]{2,1,0:T(8,128)(2,1)S(1)} %add_up.34.refs_3_), channel_id=1, source_target_pairs={{0,2},{7,5},{2,4},{5,3},{4,6},{3,1},{8,10},{15,13},{10,12},{13,11}... | collective-permute-start | bytes 1572872 | tf_op jit(solution)/shard_map/ppermute | solution.py:469
  87.3 2.7 %collective-permute-start.23 = (bf16[64,32,128]{2,1,0:T(8,128)(2,1)S(1)}, bf16[64,32,128]{2,1,0:T(8,128)(2,1)}, u32[]{:S(2)}, u32[]{:S(2)}) collective-permute-start(bf16[64,32,128]{2,1,0:T(8,128)(2,1)S(1)} %add_up.36.refs_3_), channel_id=1, source_target_pairs={{0,2},{7,5},{2,4},{5,3},{4,6},{3,1},{8,10},{15,13},{10,12},{13,11}... | collective-permute-start | bytes 1572872 | tf_op jit(solution)/shard_map/ppermute | solution.py:469
  90.0 3.5 %collective-permute-done.19.refs_0_ = bf16[64,32,128]{2,1,0:T(8,128)(2,1)S(1)} collective-permute-done((bf16[64,32,128]{2,1,0:T(8,128)(2,1)S(1)}, bf16[64,32,128]{2,1,0:T(8,128)(2,1)S(1)}, u32[]{:S(2)}, u32[]{:S(2)}) %collective-permute-start.19) | collective-permute-done | bytes 524320 | tf_op jit(solution)/shard_map/ppermute | solution.py:469
  94.8 4.3 %collective-permute-done.23.refs_0_ = bf16[64,32,128]{2,1,0:T(8,128)(2,1)} collective-permute-done((bf16[64,32,128]{2,1,0:T(8,128)(2,1)S(1)}, bf16[64,32,128]{2,1,0:T(8,128)(2,1)}, u32[]{:S(2)}, u32[]{:S(2)}) %collective-permute-start.23) | collective-permute-done | bytes 524320 | tf_op jit(solution)/shard_map/ppermute | solution.py:469
  100.6 5.3 %collective-permute-start.28 = (bf16[64,32,128]{2,1,0:T(8,128)(2,1)}, bf16[64,32,128]{2,1,0:T(8,128)(2,1)}, u32[]{:S(2)}, u32[]{:S(2)}) collective-permute-start(bf16[64,32,128]{2,1,0:T(8,128)(2,1)} %get-tuple-element.53.refs_3_), channel_id=1, source_target_pairs={{0,2},{7,5},{2,4},{5,3},{4,6},{3,1},{8,10},{15,13},{10,12},{13,11}... | collective-permute-start | bytes 1572872 | tf_op jit(solution)/shard_map/ppermute | solution.py:469
  107.2 2.5 %add_up.38 = (bf16[64,32,128]{2,1,0:T(8,128)(2,1)S(1)}, f32[64,32,128]{2,1,0:T(8,128)}) custom-call(s32[1]{0:T(128)} %constant.92.clone.1.place_ref.start_ref, bf16[64,32,128]{2,1,0:T(8,128)(2,1)} %collective-permute-done.23.refs_0_, bf16[64,32,128]{2,1,0:T(8,128)(2,1)} %collective-permute-done.24.refs_1_, f32[64,64,128]{2,1,0:T(8,128)S(1)} %add_up.35.refs_2_, ...), custom_call_target="tpu_custom_call" | custom-call | bytes 36900 | tf_op jit(solution)/shard_map/add_up/pallas_call | solution.py:208
  109.7 1.4 collective-permute-start.30
  112.1 1.4 add_up.39.refs_3_
  113.5 4.7 %collective-permute-start.29 = (bf16[64,32,128]{2,1,0:T(8,128)(2,1)S(1)}, bf16[64,32,128]{2,1,0:T(8,128)(2,1)S(1)}, u32[]{:S(2)}, u32[]{:S(2)}) collective-permute-start(bf16[64,32,128]{2,1,0:T(8,128)(2,1)S(1)} %add_up.39.refs_3_), channel_id=1, source_target_pairs={{0,2},{7,5},{2,4},{5,3},{4,6},{3,1},{8,10},{15,13},{10,12},{13,11}... | collective-permute-start | bytes 1572872 | tf_op jit(solution)/shard_map/ppermute | solution.py:469
  118.2 1.3 collective-permute-start.25
  120.8 3.8 %collective-permute-start.32 = (bf16[64,32,128]{2,1,0:T(8,128)(2,1)S(1)}, bf16[64,32,128]{2,1,0:T(8,128)(2,1)S(1)}, u32[]{:S(2)}, u32[]{:S(2)}) collective-permute-start(bf16[64,32,128]{2,1,0:T(8,128)(2,1)S(1)} %add_up.40.refs_4_.refs_2_), channel_id=1, source_target_pairs={{0,2},{7,5},{2,4},{5,3},{4,6},{3,1},{8,10},{15,13},{10,12},{13,11}... | collective-permute-start | bytes 1572872 | tf_op jit(solution)/shard_map/ppermute | solution.py:469
  124.9 1.3 add_up.41.refs_4_
  126.2 4.5 %collective-permute-start.31 = (bf16[64,32,128]{2,1,0:T(8,128)(2,1)S(1)}, bf16[64,32,128]{2,1,0:T(8,128)(2,1)S(1)}, u32[]{:S(2)}, u32[]{:S(2)}) collective-permute-start(bf16[64,32,128]{2,1,0:T(8,128)(2,1)S(1)} %add_up.41.refs_4_), channel_id=1, source_target_pairs={{0,2},{7,5},{2,4},{5,3},{4,6},{3,1},{8,10},{15,13},{10,12},{13,11}... | collective-permute-start | bytes 1572872 | tf_op jit(solution)/shard_map/ppermute | solution.py:469
  131.2 1.3 add_up.42.refs_3_
  132.5 4.4 %collective-permute-start.36 = (bf16[64,32,128]{2,1,0:T(8,128)(2,1)S(1)}, bf16[64,32,128]{2,1,0:T(8,128)(2,1)S(1)}, u32[]{:S(2)}, u32[]{:S(2)}) collective-permute-start(bf16[64,32,128]{2,1,0:T(8,128)(2,1)S(1)} %add_up.42.refs_3_), channel_id=1, source_target_pairs={{0,2},{7,5},{2,4},{5,3},{4,6},{3,1},{8,10},{15,13},{10,12},{13,11}... | collective-permute-start | bytes 1572872 | tf_op jit(solution)/shard_map/ppermute | solution.py:469
  137.9 4.7 %collective-permute-start.33 = (bf16[64,32,128]{2,1,0:T(8,128)(2,1)S(1)}, bf16[64,32,128]{2,1,0:T(8,128)(2,1)S(1)}, u32[]{:S(2)}, u32[]{:S(2)}) collective-permute-start(bf16[64,32,128]{2,1,0:T(8,128)(2,1)S(1)} %add_up.43.refs_3_), channel_id=1, source_target_pairs={{0,2},{7,5},{2,4},{5,3},{4,6},{3,1},{8,10},{15,13},{10,12},{13,11}... | collective-permute-start | bytes 1572872 | tf_op jit(solution)/shard_map/ppermute | solution.py:469
  144.8 3.7 %collective-permute-start.40 = (bf16[64,32,128]{2,1,0:T(8,128)(2,1)S(1)}, bf16[64,32,128]{2,1,0:T(8,128)(2,1)S(1)}, u32[]{:S(2)}, u32[]{:S(2)}) collective-permute-start(bf16[64,32,128]{2,1,0:T(8,128)(2,1)S(1)} %add_up.45.refs_7_.refs_3_), channel_id=1, source_target_pairs={{0,2},{7,5},{2,4},{5,3},{4,6},{3,1},{8,10},{15,13},{10,12},{13,11}... | collective-permute-start | bytes 1572872 | tf_op jit(solution)/shard_map/ppermute | solution.py:469
  150.9 4.4 %context_products.4 = (bf16[64,32,128]{2,1,0:T(8,128)(2,1)S(1)}, f32[64,32,128]{2,1,0:T(8,128)S(1)}) custom-call(s32[487]{0:T(512)S(1)} %pad_add_fusion.index_ref, bf16[160,128,128]{2,1,0:T(8,128)(2,1)S(1)} %bitcast.7, bf16[64,32,128]{2,1,0:T(8,128)(2,1)S(1)} %collective-permute-done.31.refs_2_.refs_0_, ...), custom_call_target="tpu_custom_call" | custom-call | bytes 36900 | tf_op jit(solution)/shard_map/context_products/pallas_call | solution.py:391
  157.8 3.7 %collective-permute-start.46 = (bf16[64,32,128]{2,1,0:T(8,128)(2,1)S(1)}, bf16[64,32,128]{2,1,0:T(8,128)(2,1)S(1)}, u32[]{:S(2)}, u32[]{:S(2)}) collective-permute-start(bf16[64,32,128]{2,1,0:T(8,128)(2,1)S(1)} %get-tuple-element.64.refs_7_.refs_3_), channel_id=1, source_target_pairs={{0,2},{7,5},{2,4},{5,3},{4,6},{3,1},{8,10},{15,13},{10,12},{13,11}... | collective-permute-start | bytes 1572872 | tf_op jit(solution)/shard_map/ppermute | solution.py:469
  161.5 3.7 %context_products.5 = (bf16[64,32,128]{2,1,0:T(8,128)(2,1)S(1)}, f32[64,32,128]{2,1,0:T(8,128)S(1)}) custom-call(s32[487]{0:T(512)S(1)} %pad_add_fusion.index_ref, bf16[160,128,128]{2,1,0:T(8,128)(2,1)S(1)} %bitcast.7, bf16[64,32,128]{2,1,0:T(8,128)(2,1)S(1)} %collective-permute-done.36.refs_2_.refs_0_, ...), custom_call_target="tpu_custom_call" | custom-call | bytes 36900 | tf_op jit(solution)/shard_map/context_products/pallas_call | solution.py:391
  165.3 1.6 collective-permute-start.48
  168.0 4.2 %collective-permute-start.45 = (bf16[64,32,128]{2,1,0:T(8,128)(2,1)S(1)}, bf16[64,32,128]{2,1,0:T(8,128)(2,1)S(1)}, u32[]{:S(2)}, u32[]{:S(2)}) collective-permute-start(bf16[64,32,128]{2,1,0:T(8,128)(2,1)S(1)} %get-tuple-element.67.refs_1_.refs_3_), channel_id=1, source_target_pairs={{0,2},{7,5},{2,4},{5,3},{4,6},{3,1},{8,10},{15,13},{10,12},{13,11}... | collective-permute-start | bytes 1572872 | tf_op jit(solution)/shard_map/ppermute | solution.py:469
  172.3 2.7 %collective-permute-start.50 = (bf16[64,32,128]{2,1,0:T(8,128)(2,1)S(1)}, bf16[64,32,128]{2,1,0:T(8,128)(2,1)S(1)}, u32[]{:S(2)}, u32[]{:S(2)}) collective-permute-start(bf16[64,32,128]{2,1,0:T(8,128)(2,1)S(1)} %add_up.49.refs_1_), channel_id=1, source_target_pairs={{0,2},{7,5},{2,4},{5,3},{4,6},{3,1},{8,10},{15,13},{10,12},{13,11}... | collective-permute-start | bytes 1572872 | tf_op jit(solution)/shard_map/ppermute | solution.py:469
  175.7 3.2 %collective-permute-done.45.refs_0_.refs_2_ = bf16[64,32,128]{2,1,0:T(8,128)(2,1)S(1)} collective-permute-done((bf16[64,32,128]{2,1,0:T(8,128)(2,1)S(1)}, bf16[64,32,128]{2,1,0:T(8,128)(2,1)S(1)}, u32[]{:S(2)}, u32[]{:S(2)}) %collective-permute-start.45) | collective-permute-done | bytes 524320 | tf_op jit(solution)/shard_map/ppermute | solution.py:469
  178.9 2.6 %collective-permute-done.51.refs_2_ = bf16[32,32,128]{2,1,0:T(8,128)(2,1)S(1)} collective-permute-done((bf16[32,32,128]{2,1,0:T(8,128)(2,1)S(1)}, bf16[32,32,128]{2,1,0:T(8,128)(2,1)S(1)}, u32[]{:S(2)}, u32[]{:S(2)}) %collective-permute-start.51) | collective-permute-done | bytes 262176 | tf_op jit(solution)/shard_map/ppermute | solution.py:457
  181.6 2.9 %collective-permute-done.50.refs_0_.refs_1_ = bf16[64,32,128]{2,1,0:T(8,128)(2,1)S(1)} collective-permute-done((bf16[64,32,128]{2,1,0:T(8,128)(2,1)S(1)}, bf16[64,32,128]{2,1,0:T(8,128)(2,1)S(1)}, u32[]{:S(2)}, u32[]{:S(2)}) %collective-permute-start.50) | collective-permute-done | bytes 524320 | tf_op jit(solution)/shard_map/ppermute | solution.py:469
  184.6 4.4 %collective-permute-start.54 = (bf16[64,32,128]{2,1,0:T(8,128)(2,1)S(1)}, bf16[64,32,128]{2,1,0:T(8,128)(2,1)S(1)}, u32[]{:S(2)}, u32[]{:S(2)}) collective-permute-start(bf16[64,32,128]{2,1,0:T(8,128)(2,1)S(1)} %add_up.52.refs_1_), channel_id=1, source_target_pairs={{0,2},{7,5},{2,4},{5,3},{4,6},{3,1},{8,10},{15,13},{10,12},{13,11}... | collective-permute-start | bytes 1572872 | tf_op jit(solution)/shard_map/ppermute | solution.py:469
  189.0 2.7 %collective-permute-start.49 = (bf16[64,32,128]{2,1,0:T(8,128)(2,1)S(1)}, bf16[64,32,128]{2,1,0:T(8,128)(2,1)S(1)}, u32[]{:S(2)}, u32[]{:S(2)}) collective-permute-start(bf16[64,32,128]{2,1,0:T(8,128)(2,1)S(1)} %add_up.50.refs_1_), channel_id=1, source_target_pairs={{0,2},{7,5},{2,4},{5,3},{4,6},{3,1},{8,10},{15,13},{10,12},{13,11}... | collective-permute-start | bytes 1572872 | tf_op jit(solution)/shard_map/ppermute | solution.py:469
  192.8 2.8 %collective-permute-done.54.refs_0_ = bf16[64,32,128]{2,1,0:T(8,128)(2,1)S(1)} collective-permute-done((bf16[64,32,128]{2,1,0:T(8,128)(2,1)S(1)}, bf16[64,32,128]{2,1,0:T(8,128)(2,1)S(1)}, u32[]{:S(2)}, u32[]{:S(2)}) %collective-permute-start.54) | collective-permute-done | bytes 524320 | tf_op jit(solution)/shard_map/ppermute | solution.py:469
  195.6 2.6 %collective-permute-done.52.refs_2_.refs_5_ = bf16[32,32,128]{2,1,0:T(8,128)(2,1)S(1)} collective-permute-done((bf16[32,32,128]{2,1,0:T(8,128)(2,1)S(1)}, bf16[32,32,128]{2,1,0:T(8,128)(2,1)S(1)}, u32[]{:S(2)}, u32[]{:S(2)}) %collective-permute-start.52) | collective-permute-done | bytes 262176 | tf_op jit(solution)/shard_map/ppermute | solution.py:457
  198.2 3.0 %collective-permute-done.49.refs_0_.refs_1_ = bf16[64,32,128]{2,1,0:T(8,128)(2,1)S(1)} collective-permute-done((bf16[64,32,128]{2,1,0:T(8,128)(2,1)S(1)}, bf16[64,32,128]{2,1,0:T(8,128)(2,1)S(1)}, u32[]{:S(2)}, u32[]{:S(2)}) %collective-permute-start.49) | collective-permute-done | bytes 524320 | tf_op jit(solution)/shard_map/ppermute | solution.py:469
  201.3 4.4 %collective-permute-start.53 = (bf16[64,32,128]{2,1,0:T(8,128)(2,1)S(1)}, bf16[64,32,128]{2,1,0:T(8,128)(2,1)S(1)}, u32[]{:S(2)}, u32[]{:S(2)}) collective-permute-start(bf16[64,32,128]{2,1,0:T(8,128)(2,1)S(1)} %add_up.54), channel_id=1, source_target_pairs={{0,2},{7,5},{2,4},{5,3},{4,6},{3,1},{8,10},{15,13},{10,12},{13,11}... | collective-permute-start | bytes 1572872 | tf_op jit(solution)/shard_map/ppermute | solution.py:469
  206.4 3.7 %context_products.6 = (bf16[64,32,128]{2,1,0:T(8,128)(2,1)S(1)}, f32[64,32,128]{2,1,0:T(8,128)S(1)}) custom-call(s32[487]{0:T(512)S(1)} %pad_add_fusion.index_ref, bf16[160,128,128]{2,1,0:T(8,128)(2,1)S(1)} %bitcast.7, bf16[64,32,128]{2,1,0:T(8,128)(2,1)S(1)} %collective-permute-done.54.refs_0_, ...), custom_call_target="tpu_custom_call" | custom-call | bytes 36900 | tf_op jit(solution)/shard_map/context_products/pallas_call | solution.py:391
  210.1 2.3 collective-permute-done.53.refs_0_
  213.2 1.3 collective-permute-done.60.refs_6_
  214.5 3.7 %context_products.7 = (bf16[64,32,128]{2,1,0:T(8,128)(2,1)S(1)}, f32[64,32,128]{2,1,0:T(8,128)S(1)}) custom-call(s32[487]{0:T(512)S(1)} %pad_add_fusion.index_ref, bf16[160,128,128]{2,1,0:T(8,128)(2,1)S(1)} %bitcast.7, bf16[64,32,128]{2,1,0:T(8,128)(2,1)S(1)} %add_up.55.refs_0_, bf16[64,32,128]{2,1,0:T(8,128)(2,1)S(1)} %collective-permute-done.49.refs_0_.refs_1_, ...), custom_call_target="tpu_custom_call" | custom-call | bytes 36900 | tf_op jit(solution)/shard_map/context_products/pallas_call | solution.py:391
  218.8 3.0 %collective-permute-done.61.refs_1_.refs_7_ = bf16[64,32,128]{2,1,0:T(8,128)(2,1)S(1)} collective-permute-done((bf16[64,32,128]{2,1,0:T(8,128)(2,1)S(1)}, bf16[64,32,128]{2,1,0:T(8,128)(2,1)S(1)}, u32[]{:S(2)}, u32[]{:S(2)}) %collective-permute-start.61) | collective-permute-done | bytes 524320 | tf_op jit(solution)/shard_map/ppermute | solution.py:457
  223.2 6.7 %collective-permute-done.63.refs_1_.refs_10_ = bf16[64,32,128]{2,1,0:T(8,128)(2,1)S(1)} collective-permute-done((bf16[64,32,128]{2,1,0:T(8,128)(2,1)S(1)}, bf16[64,32,128]{2,1,0:T(8,128)(2,1)S(1)}, u32[]{:S(2)}, u32[]{:S(2)}) %collective-permute-start.63) | collective-permute-done | bytes 524320 | tf_op jit(solution)/shard_map/ppermute | solution.py:457
  232.3 4.3 %turn_back.2 = f32[4096,128]{1,0:T(8,128)} custom-call(s32[1]{0:T(128)S(6)} %select_n.44.start_ref, f32[64,32,128]{2,1,0:T(8,128)} %get-tuple-element.52.refs_0_, f32[64,32,128]{2,1,0:T(8,128)} %get-tuple-element.54.refs_1_, f32[64,32,128]{2,1,0:T(8,128)} %get-tuple-element.63.refs_2_, f32[64,32,128]{2,1,0:T(8,128)} %get-tuple-element.66.refs_3_, ...), custom_call_target="tpu_custom_call" | custom-call | bytes 36900 | tf_op jit(solution)/shard_map/turn_back/pallas_call | solution.py:422
  237.5 3.8 %turn_back.3 = f32[4096,128]{1,0:T(8,128)} custom-call(s32[1]{0:T(128)} %constant.92.clone.1.place_ref.start_ref, f32[64,32,128]{2,1,0:T(8,128)S(1)} %get-tuple-element.68.refs_0_, bf16[64,32,128]{2,1,0:T(8,128)(2,1)S(1)} %collective-permute-done.47.refs_2_.refs_1_, bf16[32,32,128]{2,1,0:T(8,128)(2,1)S(1)} %collective-permute-done.51.refs_2_, ...), custom_call_target="tpu_custom_call" | custom-call | bytes 36900 | tf_op jit(solution)/shard_map/turn_back/pallas_call | solution.py:422
  (166 shorter events, 34.4 us)
Async XLA Ops:
  2.2 13.0 %collective-permute-start.8 = (bf16[32,64,128]{2,1,0:T(8,128)(2,1)S(1)}, bf16[32,64,128]{2,1,0:T(8,128)(2,1)S(1)}, u32[]{:S(2)}, u32[]{:S(2)}) collective-permute-start(bf16[32,64,128]{2,1,0:T(8,128)(2,1)S(1)} %turn_panel.2.refs_0_.refs_5_), channel_id=1, source_target_pairs={{0,8},{1,17},{2,10},{3,19},{4,12},{5,21},{6,14},{7,23},{8,0},{9,25... | collective-permute-start | bytes 1572872 | tf_op jit(solution)/shard_map/ppermute | solution.py:457
  10.1 5.6 %collective-permute-start = (f32[128,128]{1,0:T(8,128)S(1)}, f32[128,128]{1,0:T(8,128)S(1)}, u32[]{:S(2)}, u32[]{:S(2)}) collective-permute-start(f32[128,128]{1,0:T(8,128)S(1)} %get-tuple-element.39.refs_0_), channel_id=1, source_target_pairs={{0,8},{8,0},{16,24},{24,16},{1,9},{9,1},{17,25},{25,17},{2,10},{10... | collective-permute-start | bytes 196616 | tf_op jit(solution)/shard_map/ppermute | solution.py:472
  10.2 5.5 %collective-permute-start.1 = (f32[128,128]{1,0:T(8,128)S(1)}, f32[128,128]{1,0:T(8,128)S(1)}, u32[]{:S(2)}, u32[]{:S(2)}) collective-permute-start(f32[128,128]{1,0:T(8,128)S(1)} %get-tuple-element.39.refs_0_), channel_id=1, source_target_pairs={{0,16},{8,24},{16,0},{24,8},{1,17},{9,25},{17,1},{25,9},{2,18},{10... | collective-permute-start | bytes 196616 | tf_op jit(solution)/shard_map/ppermute | solution.py:472
  12.2 5.9 %collective-permute-start.2 = (f32[128,128]{1,0:T(8,128)S(1)}, f32[128,128]{1,0:T(8,128)S(1)}, u32[]{:S(2)}, u32[]{:S(2)}) collective-permute-start(f32[128,128]{1,0:T(8,128)S(1)} %get-tuple-element.39.refs_0_), channel_id=1, source_target_pairs={{0,24},{8,16},{16,8},{24,0},{1,25},{9,17},{17,9},{25,1},{2,26},{10... | collective-permute-start | bytes 196616 | tf_op jit(solution)/shard_map/ppermute | solution.py:472
  13.6 17.0 %collective-permute-start.7 = (bf16[32,64,128]{2,1,0:T(8,128)(2,1)S(1)}, bf16[32,64,128]{2,1,0:T(8,128)(2,1)S(1)}, u32[]{:S(2)}, u32[]{:S(2)}) collective-permute-start(bf16[32,64,128]{2,1,0:T(8,128)(2,1)S(1)} %turn_panel.2.refs_0_.refs_5_), channel_id=1, source_target_pairs={{0,16},{1,9},{2,18},{3,11},{4,20},{5,13},{6,22},{7,15},{8,24},{9,1... | collective-permute-start | bytes 1572872 | tf_op jit(solution)/shard_map/ppermute | solution.py:457
  15.1 15.5 %collective-permute-start.9 = (bf16[32,64,128]{2,1,0:T(8,128)(2,1)S(1)}, bf16[32,64,128]{2,1,0:T(8,128)(2,1)S(1)}, u32[]{:S(2)}, u32[]{:S(2)}) collective-permute-start(bf16[32,64,128]{2,1,0:T(8,128)(2,1)S(1)} %collective-permute-done.8.refs_7_), channel_id=1, source_target_pairs={{0,16},{1,9},{2,18},{3,11},{4,20},{5,13},{6,22},{7,15},{8,24},{9,1... | collective-permute-start | bytes 1572872 | tf_op jit(solution)/shard_map/ppermute | solution.py:457
  19.5 4.4 %collective-permute-start.4 = (f32[136,128]{1,0:T(8,128)S(1)}, f32[136,128]{1,0:T(8,128)S(1)}, u32[]{:S(2)}, u32[]{:S(2)}) collective-permute-start(f32[136,128]{1,0:T(8,128)S(1)} %plus.3.a_ref), channel_id=1, source_target_pairs={{0,2},{1,3},{2,0},{3,1},{4,6},{5,7},{6,4},{7,5},{8,10},{9,11},{10,... | collective-permute-start | bytes 208904 | tf_op jit(solution)/shard_map/ppermute | solution.py:475
  23.9 5.4 %collective-permute-start.5 = (f32[136,128]{1,0:T(8,128)S(1)}, f32[136,128]{1,0:T(8,128)S(1)}, u32[]{:S(2)}, u32[]{:S(2)}) collective-permute-start(f32[136,128]{1,0:T(8,128)S(1)} %plus.4.a_ref), channel_id=1, source_target_pairs={{0,4},{1,5},{2,6},{3,7},{4,0},{5,1},{6,2},{7,3},{8,12},{9,13},{10,... | collective-permute-start | bytes 208904 | tf_op jit(solution)/shard_map/ppermute | solution.py:475
  29.3 1.3 collective-permute-start.6
  42.0 5.8 %collective-permute-start.12 = (bf16[64,64,128]{2,1,0:T(8,128)(2,1)S(1)}, bf16[64,64,128]{2,1,0:T(8,128)(2,1)S(1)}, u32[]{:S(2)}, u32[]{:S(2)}) collective-permute-start(bf16[64,64,128]{2,1,0:T(8,128)(2,1)S(1)} %get-tuple-element.48), channel_id=1, source_target_pairs={{1,0},{6,7},{9,8},{14,15},{17,16},{22,23},{25,24},{30,31}} | collective-permute-start | bytes 3145736 | tf_op jit(solution)/shard_map/ppermute | solution.py:460
  43.3 15.0 %collective-permute-start.11 = (bf16[64,64,128]{2,1,0:T(8,128)(2,1)S(1)}, bf16[64,64,128]{2,1,0:T(8,128)(2,1)S(1)}, u32[]{:S(2)}, u32[]{:S(2)}) collective-permute-start(bf16[64,64,128]{2,1,0:T(8,128)(2,1)S(1)} %get-tuple-element.46), channel_id=1, source_target_pairs={{1,0},{3,2},{4,5},{6,7},{9,8},{11,10},{12,13},{14,15},{17,16},{19,... | collective-permute-start | bytes 3145736 | tf_op jit(solution)/shard_map/ppermute | solution.py:460
  46.2 11.4 %collective-permute-start.17 = (bf16[32,64,128]{2,1,0:T(8,128)(2,1)S(1)}, bf16[32,64,128]{2,1,0:T(8,128)(2,1)S(1)}, u32[]{:S(2)}, u32[]{:S(2)}) collective-permute-start(bf16[32,64,128]{2,1,0:T(8,128)(2,1)S(1)} %turn_panel.3.refs_1_), channel_id=1, source_target_pairs={{0,8},{1,17},{2,10},{3,19},{4,12},{5,21},{6,14},{7,23},{8,0},{9,25... | collective-permute-start | bytes 1572872 | tf_op jit(solution)/shard_map/ppermute | solution.py:457
  48.1 11.8 %collective-permute-start.13 = (bf16[64,32,128]{2,1,0:T(8,128)(2,1)S(1)}, bf16[64,32,128]{2,1,0:T(8,128)(2,1)S(1)}, u32[]{:S(2)}, u32[]{:S(2)}) collective-permute-start(bf16[64,32,128]{2,1,0:T(8,128)(2,1)S(1)} %add_up.29.refs_2_), channel_id=1, source_target_pairs={{0,2},{7,5},{2,4},{5,3},{4,6},{3,1},{8,10},{15,13},{10,12},{13,11}... | collective-permute-start | bytes 1572872 | tf_op jit(solution)/shard_map/ppermute | solution.py:469
  50.9 29.3 %collective-permute-start.10 = (bf16[64,64,128]{2,1,0:T(8,128)(2,1)S(1)}, bf16[64,64,128]{2,1,0:T(8,128)(2,1)S(1)}, u32[]{:S(2)}, u32[]{:S(2)}) collective-permute-start(bf16[64,64,128]{2,1,0:T(8,128)(2,1)S(1)} %get-tuple-element.44), channel_id=1, source_target_pairs={{1,0},{2,3},{3,2},{4,5},{5,4},{6,7},{9,8},{10,11},{11,10},{12,13},... | collective-permute-start | bytes 3145736 | tf_op jit(solution)/shard_map/ppermute | solution.py:460
  52.6 12.4 %collective-permute-start.15 = (bf16[64,32,128]{2,1,0:T(8,128)(2,1)S(1)}, bf16[64,32,128]{2,1,0:T(8,128)(2,1)S(1)}, u32[]{:S(2)}, u32[]{:S(2)}) collective-permute-start(bf16[64,32,128]{2,1,0:T(8,128)(2,1)S(1)} %add_up.30.refs_3_.refs_1_.refs_2_), channel_id=1, source_target_pairs={{0,2},{7,5},{2,4},{5,3},{4,6},{3,1},{8,10},{15,13},{10,12},{13,11}... | collective-permute-start | bytes 1572872 | tf_op jit(solution)/shard_map/ppermute | solution.py:469
  57.6 9.2 %collective-permute-start.16 = (bf16[32,64,128]{2,1,0:T(8,128)(2,1)S(1)}, bf16[32,64,128]{2,1,0:T(8,128)(2,1)S(1)}, u32[]{:S(2)}, u32[]{:S(2)}) collective-permute-start(bf16[32,64,128]{2,1,0:T(8,128)(2,1)S(1)} %turn_panel.3.refs_1_), channel_id=1, source_target_pairs={{0,16},{1,9},{2,18},{3,11},{4,20},{5,13},{6,22},{7,15},{8,24},{9,1... | collective-permute-start | bytes 1572872 | tf_op jit(solution)/shard_map/ppermute | solution.py:457
  58.3 14.2 %collective-permute-start.18 = (bf16[32,64,128]{2,1,0:T(8,128)(2,1)S(1)}, bf16[32,64,128]{2,1,0:T(8,128)(2,1)S(1)}, u32[]{:S(2)}, u32[]{:S(2)}) collective-permute-start(bf16[32,64,128]{2,1,0:T(8,128)(2,1)S(1)} %add_up.33), channel_id=1, source_target_pairs={{0,16},{1,9},{2,18},{3,11},{4,20},{5,13},{6,22},{7,15},{8,24},{9,1... | collective-permute-start | bytes 1572872 | tf_op jit(solution)/shard_map/ppermute | solution.py:457
  60.3 19.9 %collective-permute-start.14 = (bf16[64,32,128]{2,1,0:T(8,128)(2,1)S(1)}, bf16[64,32,128]{2,1,0:T(8,128)(2,1)S(1)}, u32[]{:S(2)}, u32[]{:S(2)}) collective-permute-start(bf16[64,32,128]{2,1,0:T(8,128)(2,1)S(1)} %add_up.31.refs_3_), channel_id=1, source_target_pairs={{0,2},{7,5},{2,4},{5,3},{4,6},{3,1},{8,10},{15,13},{10,12},{13,11}... | collective-permute-start | bytes 1572872 | tf_op jit(solution)/shard_map/ppermute | solution.py:469
  65.0 34.1 %collective-permute-start.21 = (bf16[64,64,128]{2,1,0:T(8,128)(2,1)S(1)}, bf16[64,64,128]{2,1,0:T(8,128)(2,1)S(1)}, u32[]{:S(2)}, u32[]{:S(2)}) collective-permute-start(bf16[64,64,128]{2,1,0:T(8,128)(2,1)S(1)} %get-tuple-element.51.refs_0_), channel_id=1, source_target_pairs={{0,1},{1,0},{2,3},{3,2},{4,5},{5,4},{6,7},{7,6},{8,9},{9,8},{10,11... | collective-permute-start | bytes 3145736 | tf_op jit(solution)/shard_map/ppermute | solution.py:460
  66.8 20.0 %collective-permute-start.22 = (bf16[64,32,128]{2,1,0:T(8,128)(2,1)S(1)}, bf16[64,32,128]{2,1,0:T(8,128)(2,1)S(1)}, u32[]{:S(2)}, u32[]{:S(2)}) collective-permute-start(bf16[64,32,128]{2,1,0:T(8,128)(2,1)S(1)} %add_up.32.refs_5_.refs_3_), channel_id=1, source_target_pairs={{0,2},{7,5},{2,4},{5,3},{4,6},{3,1},{8,10},{15,13},{10,12},{13,11}... | collective-permute-start | bytes 1572872 | tf_op jit(solution)/shard_map/ppermute | solution.py:469
  82.1 11.3 %collective-permute-start.19 = (bf16[64,32,128]{2,1,0:T(8,128)(2,1)S(1)}, bf16[64,32,128]{2,1,0:T(8,128)(2,1)S(1)}, u32[]{:S(2)}, u32[]{:S(2)}) collective-permute-start(bf16[64,32,128]{2,1,0:T(8,128)(2,1)S(1)} %add_up.34.refs_3_), channel_id=1, source_target_pairs={{0,2},{7,5},{2,4},{5,3},{4,6},{3,1},{8,10},{15,13},{10,12},{13,11}... | collective-permute-start | bytes 1572872 | tf_op jit(solution)/shard_map/ppermute | solution.py:469
  87.3 11.8 %collective-permute-start.23 = (bf16[64,32,128]{2,1,0:T(8,128)(2,1)S(1)}, bf16[64,32,128]{2,1,0:T(8,128)(2,1)}, u32[]{:S(2)}, u32[]{:S(2)}) collective-permute-start(bf16[64,32,128]{2,1,0:T(8,128)(2,1)S(1)} %add_up.36.refs_3_), channel_id=1, source_target_pairs={{0,2},{7,5},{2,4},{5,3},{4,6},{3,1},{8,10},{15,13},{10,12},{13,11}... | collective-permute-start | bytes 1572872 | tf_op jit(solution)/shard_map/ppermute | solution.py:469
  93.5 5.8 %collective-permute-start.20 = (bf16[64,32,128]{2,1,0:T(8,128)(2,1)S(1)}, bf16[64,32,128]{2,1,0:T(8,128)(2,1)S(1)}, u32[]{:S(2)}, u32[]{:S(2)}) collective-permute-start(bf16[64,32,128]{2,1,0:T(8,128)(2,1)S(1)} %collective-permute-done.19.refs_0_), channel_id=1, source_target_pairs={{0,1},{1,0},{2,3},{3,2},{4,5},{5,4},{6,7},{7,6},{8,9},{9,8},{10,11... | collective-permute-start | bytes 1572872 | tf_op jit(solution)/shard_map/ppermute | solution.py:460
  93.5 17.7 %collective-permute-start.27 = (bf16[64,64,128]{2,1,0:T(8,128)(2,1)}, bf16[64,64,128]{2,1,0:T(8,128)(2,1)}, u32[]{:S(2)}, u32[]{:S(2)}) collective-permute-start(bf16[64,64,128]{2,1,0:T(8,128)(2,1)} %get-tuple-element.59), channel_id=1, source_target_pairs={{1,0},{6,7},{9,8},{14,15},{17,16},{22,23},{25,24},{30,31}} | collective-permute-start | bytes 3145736 | tf_op jit(solution)/shard_map/ppermute | solution.py:460
  99.1 8.1 %collective-permute-start.24 = (bf16[64,32,128]{2,1,0:T(8,128)(2,1)}, bf16[64,32,128]{2,1,0:T(8,128)(2,1)}, u32[]{:S(2)}, u32[]{:S(2)}) collective-permute-start(bf16[64,32,128]{2,1,0:T(8,128)(2,1)} %collective-permute-done.23.refs_0_), channel_id=1, source_target_pairs={{0,1},{1,0},{2,3},{3,2},{4,5},{5,4},{6,7},{7,6},{8,9},{9,8},{10,11... | collective-permute-start | bytes 1572872 | tf_op jit(solution)/shard_map/ppermute | solution.py:460
  100.6 11.5 %collective-permute-start.28 = (bf16[64,32,128]{2,1,0:T(8,128)(2,1)}, bf16[64,32,128]{2,1,0:T(8,128)(2,1)}, u32[]{:S(2)}, u32[]{:S(2)}) collective-permute-start(bf16[64,32,128]{2,1,0:T(8,128)(2,1)} %get-tuple-element.53.refs_3_), channel_id=1, source_target_pairs={{0,2},{7,5},{2,4},{5,3},{4,6},{3,1},{8,10},{15,13},{10,12},{13,11}... | collective-permute-start | bytes 1572872 | tf_op jit(solution)/shard_map/ppermute | solution.py:469
  105.9 18.8 %collective-permute-start.26 = (bf16[64,64,128]{2,1,0:T(8,128)(2,1)}, bf16[64,64,128]{2,1,0:T(8,128)(2,1)}, u32[]{:S(2)}, u32[]{:S(2)}) collective-permute-start(bf16[64,64,128]{2,1,0:T(8,128)(2,1)} %get-tuple-element.57), channel_id=1, source_target_pairs={{1,0},{3,2},{4,5},{6,7},{9,8},{11,10},{12,13},{14,15},{17,16},{19,... | collective-permute-start | bytes 3145736 | tf_op jit(solution)/shard_map/ppermute | solution.py:460
  109.7 9.8 %collective-permute-start.30 = (bf16[64,32,128]{2,1,0:T(8,128)(2,1)S(1)}, bf16[64,32,128]{2,1,0:T(8,128)(2,1)S(1)}, u32[]{:S(2)}, u32[]{:S(2)}) collective-permute-start(bf16[64,32,128]{2,1,0:T(8,128)(2,1)S(1)} %get-tuple-element.60.refs_3_), channel_id=1, source_target_pairs={{0,2},{7,5},{2,4},{5,3},{4,6},{3,1},{8,10},{15,13},{10,12},{13,11}... | collective-permute-start | bytes 1572872 | tf_op jit(solution)/shard_map/ppermute | solution.py:469
  113.5 11.4 %collective-permute-start.29 = (bf16[64,32,128]{2,1,0:T(8,128)(2,1)S(1)}, bf16[64,32,128]{2,1,0:T(8,128)(2,1)S(1)}, u32[]{:S(2)}, u32[]{:S(2)}) collective-permute-start(bf16[64,32,128]{2,1,0:T(8,128)(2,1)S(1)} %add_up.39.refs_3_), channel_id=1, source_target_pairs={{0,2},{7,5},{2,4},{5,3},{4,6},{3,1},{8,10},{15,13},{10,12},{13,11}... | collective-permute-start | bytes 1572872 | tf_op jit(solution)/shard_map/ppermute | solution.py:469
  118.2 18.7 %collective-permute-start.25 = (bf16[64,64,128]{2,1,0:T(8,128)(2,1)S(1)}, bf16[64,64,128]{2,1,0:T(8,128)(2,1)S(1)}, u32[]{:S(2)}, u32[]{:S(2)}) collective-permute-start(bf16[64,64,128]{2,1,0:T(8,128)(2,1)S(1)} %copy-done.16), channel_id=1, source_target_pairs={{1,0},{2,3},{3,2},{4,5},{5,4},{6,7},{9,8},{10,11},{11,10},{12,13},... | collective-permute-start | bytes 3145736 | tf_op jit(solution)/shard_map/ppermute | solution.py:460
  120.8 10.4 %collective-permute-start.32 = (bf16[64,32,128]{2,1,0:T(8,128)(2,1)S(1)}, bf16[64,32,128]{2,1,0:T(8,128)(2,1)S(1)}, u32[]{:S(2)}, u32[]{:S(2)}) collective-permute-start(bf16[64,32,128]{2,1,0:T(8,128)(2,1)S(1)} %add_up.40.refs_4_.refs_2_), channel_id=1, source_target_pairs={{0,2},{7,5},{2,4},{5,3},{4,6},{3,1},{8,10},{15,13},{10,12},{13,11}... | collective-permute-start | bytes 1572872 | tf_op jit(solution)/shard_map/ppermute | solution.py:469
  124.6 20.2 %collective-permute-start.35 = (bf16[64,64,128]{2,1,0:T(8,128)(2,1)S(1)}, bf16[64,64,128]{2,1,0:T(8,128)(2,1)S(1)}, u32[]{:S(2)}, u32[]{:S(2)}) collective-permute-start(bf16[64,64,128]{2,1,0:T(8,128)(2,1)S(1)} %copy-done.14), channel_id=1, source_target_pairs={{0,1},{1,0},{2,3},{3,2},{4,5},{5,4},{6,7},{7,6},{8,9},{9,8},{10,11... | collective-permute-start | bytes 3145736 | tf_op jit(solution)/shard_map/ppermute | solution.py:460
  126.2 11.2 %collective-permute-start.31 = (bf16[64,32,128]{2,1,0:T(8,128)(2,1)S(1)}, bf16[64,32,128]{2,1,0:T(8,128)(2,1)S(1)}, u32[]{:S(2)}, u32[]{:S(2)}) collective-permute-start(bf16[64,32,128]{2,1,0:T(8,128)(2,1)S(1)} %add_up.41.refs_4_), channel_id=1, source_target_pairs={{0,2},{7,5},{2,4},{5,3},{4,6},{3,1},{8,10},{15,13},{10,12},{13,11}... | collective-permute-start | bytes 1572872 | tf_op jit(solution)/shard_map/ppermute | solution.py:469
  132.5 11.1 %collective-permute-start.36 = (bf16[64,32,128]{2,1,0:T(8,128)(2,1)S(1)}, bf16[64,32,128]{2,1,0:T(8,128)(2,1)S(1)}, u32[]{:S(2)}, u32[]{:S(2)}) collective-permute-start(bf16[64,32,128]{2,1,0:T(8,128)(2,1)S(1)} %add_up.42.refs_3_), channel_id=1, source_target_pairs={{0,2},{7,5},{2,4},{5,3},{4,6},{3,1},{8,10},{15,13},{10,12},{13,11}... | collective-permute-start | bytes 1572872 | tf_op jit(solution)/shard_map/ppermute | solution.py:469
  137.9 11.3 %collective-permute-start.33 = (bf16[64,32,128]{2,1,0:T(8,128)(2,1)S(1)}, bf16[64,32,128]{2,1,0:T(8,128)(2,1)S(1)}, u32[]{:S(2)}, u32[]{:S(2)}) collective-permute-start(bf16[64,32,128]{2,1,0:T(8,128)(2,1)S(1)} %add_up.43.refs_3_), channel_id=1, source_target_pairs={{0,2},{7,5},{2,4},{5,3},{4,6},{3,1},{8,10},{15,13},{10,12},{13,11}... | collective-permute-start | bytes 1572872 | tf_op jit(solution)/shard_map/ppermute | solution.py:469
  142.5 7.4 %collective-permute-start.37 = (bf16[64,32,128]{2,1,0:T(8,128)(2,1)}, bf16[64,32,128]{2,1,0:T(8,128)(2,1)S(1)}, u32[]{:S(2)}, u32[]{:S(2)}) collective-permute-start(bf16[64,32,128]{2,1,0:T(8,128)(2,1)} %collective-permute-done.28.refs_2_), channel_id=1, source_target_pairs={{0,1},{1,0},{2,3},{3,2},{4,5},{5,4},{6,7},{7,6},{8,9},{9,8},{10,11... | collective-permute-start | bytes 1572872 | tf_op jit(solution)/shard_map/ppermute | solution.py:460
  142.6 7.6 %collective-permute-start.38 = (bf16[64,32,128]{2,1,0:T(8,128)(2,1)S(1)}, bf16[64,32,128]{2,1,0:T(8,128)(2,1)S(1)}, u32[]{:S(2)}, u32[]{:S(2)}) collective-permute-start(bf16[64,32,128]{2,1,0:T(8,128)(2,1)S(1)} %collective-permute-done.29.refs_2_.refs_3_.refs_1_), channel_id=1, source_target_pairs={{0,1},{1,0},{2,3},{3,2},{4,5},{5,4},{6,7},{7,6},{8,9},{9,8},{10,11... | collective-permute-start | bytes 1572872 | tf_op jit(solution)/shard_map/ppermute | solution.py:460
  143.6 7.2 %collective-permute-start.39 = (bf16[64,32,128]{2,1,0:T(8,128)(2,1)S(1)}, bf16[64,32,128]{2,1,0:T(8,128)(2,1)S(1)}, u32[]{:S(2)}, u32[]{:S(2)}) collective-permute-start(bf16[64,32,128]{2,1,0:T(8,128)(2,1)S(1)} %collective-permute-done.31.refs_2_.refs_0_), channel_id=1, source_target_pairs={{0,1},{1,0},{2,3},{3,2},{4,5},{5,4},{6,7},{7,6},{8,9},{9,8},{10,11... | collective-permute-start | bytes 1572872 | tf_op jit(solution)/shard_map/ppermute | solution.py:460
  144.8 10.5 %collective-permute-start.40 = (bf16[64,32,128]{2,1,0:T(8,128)(2,1)S(1)}, bf16[64,32,128]{2,1,0:T(8,128)(2,1)S(1)}, u32[]{:S(2)}, u32[]{:S(2)}) collective-permute-start(bf16[64,32,128]{2,1,0:T(8,128)(2,1)S(1)} %add_up.45.refs_7_.refs_3_), channel_id=1, source_target_pairs={{0,2},{7,5},{2,4},{5,3},{4,6},{3,1},{8,10},{15,13},{10,12},{13,11}... | collective-permute-start | bytes 1572872 | tf_op jit(solution)/shard_map/ppermute | solution.py:469
  149.2 6.9 %collective-permute-start.34 = (bf16[64,32,128]{2,1,0:T(8,128)(2,1)S(1)}, bf16[64,32,128]{2,1,0:T(8,128)(2,1)S(1)}, u32[]{:S(2)}, u32[]{:S(2)}) collective-permute-start(bf16[64,32,128]{2,1,0:T(8,128)(2,1)S(1)} %collective-permute-done.33.refs_0_), channel_id=1, source_target_pairs={{0,1},{1,0},{2,3},{3,2},{4,5},{5,4},{6,7},{7,6},{8,9},{9,8},{10,11... | collective-permute-start | bytes 1572872 | tf_op jit(solution)/shard_map/ppermute | solution.py:460
  149.9 7.8 %collective-permute-start.42 = (bf16[64,32,128]{2,1,0:T(8,128)(2,1)S(1)}, bf16[64,32,128]{2,1,0:T(8,128)(2,1)S(1)}, u32[]{:S(2)}, u32[]{:S(2)}) collective-permute-start(bf16[64,32,128]{2,1,0:T(8,128)(2,1)S(1)} %collective-permute-done.30.refs_2_), channel_id=1, source_target_pairs={{0,1},{1,0},{2,3},{3,2},{4,5},{5,4},{6,7},{7,6},{8,9},{9,8},{10,11... | collective-permute-start | bytes 1572872 | tf_op jit(solution)/shard_map/ppermute | solution.py:460
  150.2 11.3 %collective-permute-start.43 = (bf16[64,32,128]{2,1,0:T(8,128)(2,1)S(1)}, bf16[64,32,128]{2,1,0:T(8,128)(2,1)S(1)}, u32[]{:S(2)}, u32[]{:S(2)}) collective-permute-start(bf16[64,32,128]{2,1,0:T(8,128)(2,1)S(1)} %collective-permute-done.32.refs_2_.refs_3_.refs_1_), channel_id=1, source_target_pairs={{0,1},{1,0},{2,3},{3,2},{4,5},{5,4},{6,7},{7,6},{8,9},{9,8},{10,11... | collective-permute-start | bytes 1572872 | tf_op jit(solution)/shard_map/ppermute | solution.py:460
  150.8 10.7 %collective-permute-start.44 = (bf16[64,32,128]{2,1,0:T(8,128)(2,1)S(1)}, bf16[64,32,128]{2,1,0:T(8,128)(2,1)S(1)}, u32[]{:S(2)}, u32[]{:S(2)}) collective-permute-start(bf16[64,32,128]{2,1,0:T(8,128)(2,1)S(1)} %collective-permute-done.36.refs_2_.refs_0_), channel_id=1, source_target_pairs={{0,1},{1,0},{2,3},{3,2},{4,5},{5,4},{6,7},{7,6},{8,9},{9,8},{10,11... | collective-permute-start | bytes 1572872 | tf_op jit(solution)/shard_map/ppermute | solution.py:460
  155.4 11.4 %collective-permute-start.41 = (bf16[64,32,128]{2,1,0:T(8,128)(2,1)S(1)}, bf16[64,32,128]{2,1,0:T(8,128)(2,1)S(1)}, u32[]{:S(2)}, u32[]{:S(2)}) collective-permute-start(bf16[64,32,128]{2,1,0:T(8,128)(2,1)S(1)} %add_up.47.refs_0_), channel_id=1, source_target_pairs={{0,1},{1,0},{2,3},{3,2},{4,5},{5,4},{6,7},{7,6},{8,9},{9,8},{10,11... | collective-permute-start | bytes 1572872 | tf_op jit(solution)/shard_map/ppermute | solution.py:460
  156.2 16.1 %collective-permute-start.47 = (bf16[64,32,128]{2,1,0:T(8,128)(2,1)S(1)}, bf16[64,32,128]{2,1,0:T(8,128)(2,1)S(1)}, u32[]{:S(2)}, u32[]{:S(2)}) collective-permute-start(bf16[64,32,128]{2,1,0:T(8,128)(2,1)S(1)} %get-tuple-element.62.refs_4_.refs_1_), channel_id=1, source_target_pairs={{0,8},{1,17},{2,10},{3,19},{4,12},{5,21},{6,14},{7,23},{8,0},{9,25... | collective-permute-start | bytes 1572872 | tf_op jit(solution)/shard_map/ppermute | solution.py:457
  157.8 14.4 %collective-permute-start.46 = (bf16[64,32,128]{2,1,0:T(8,128)(2,1)S(1)}, bf16[64,32,128]{2,1,0:T(8,128)(2,1)S(1)}, u32[]{:S(2)}, u32[]{:S(2)}) collective-permute-start(bf16[64,32,128]{2,1,0:T(8,128)(2,1)S(1)} %get-tuple-element.64.refs_7_.refs_3_), channel_id=1, source_target_pairs={{0,2},{7,5},{2,4},{5,3},{4,6},{3,1},{8,10},{15,13},{10,12},{13,11}... | collective-permute-start | bytes 1572872 | tf_op jit(solution)/shard_map/ppermute | solution.py:469
  165.3 13.6 %collective-permute-start.48 = (bf16[64,32,128]{2,1,0:T(8,128)(2,1)S(1)}, bf16[64,32,128]{2,1,0:T(8,128)(2,1)S(1)}, u32[]{:S(2)}, u32[]{:S(2)}) collective-permute-start(bf16[64,32,128]{2,1,0:T(8,128)(2,1)S(1)} %get-tuple-element.65.refs_4_), channel_id=1, source_target_pairs={{0,8},{1,17},{2,10},{3,19},{4,12},{5,21},{6,14},{7,23},{8,0},{9,25... | collective-permute-start | bytes 1572872 | tf_op jit(solution)/shard_map/ppermute | solution.py:457
  168.0 10.9 %collective-permute-start.45 = (bf16[64,32,128]{2,1,0:T(8,128)(2,1)S(1)}, bf16[64,32,128]{2,1,0:T(8,128)(2,1)S(1)}, u32[]{:S(2)}, u32[]{:S(2)}) collective-permute-start(bf16[64,32,128]{2,1,0:T(8,128)(2,1)S(1)} %get-tuple-element.67.refs_1_.refs_3_), channel_id=1, source_target_pairs={{0,2},{7,5},{2,4},{5,3},{4,6},{3,1},{8,10},{15,13},{10,12},{13,11}... | collective-permute-start | bytes 1572872 | tf_op jit(solution)/shard_map/ppermute | solution.py:469
  172.3 12.1 %collective-permute-start.50 = (bf16[64,32,128]{2,1,0:T(8,128)(2,1)S(1)}, bf16[64,32,128]{2,1,0:T(8,128)(2,1)S(1)}, u32[]{:S(2)}, u32[]{:S(2)}) collective-permute-start(bf16[64,32,128]{2,1,0:T(8,128)(2,1)S(1)} %add_up.49.refs_1_), channel_id=1, source_target_pairs={{0,2},{7,5},{2,4},{5,3},{4,6},{3,1},{8,10},{15,13},{10,12},{13,11}... | collective-permute-start | bytes 1572872 | tf_op jit(solution)/shard_map/ppermute | solution.py:469
  175.1 6.4 %collective-permute-start.51 = (bf16[32,32,128]{2,1,0:T(8,128)(2,1)S(1)}, bf16[32,32,128]{2,1,0:T(8,128)(2,1)S(1)}, u32[]{:S(2)}, u32[]{:S(2)}) collective-permute-start(bf16[32,32,128]{2,1,0:T(8,128)(2,1)S(1)} %add_up.51), channel_id=1, source_target_pairs={{0,16},{1,9},{2,18},{3,11},{4,20},{5,13},{6,22},{7,15},{8,24},{9,1... | collective-permute-start | bytes 786440 | tf_op jit(solution)/shard_map/ppermute | solution.py:457
  184.6 11.1 %collective-permute-start.54 = (bf16[64,32,128]{2,1,0:T(8,128)(2,1)S(1)}, bf16[64,32,128]{2,1,0:T(8,128)(2,1)S(1)}, u32[]{:S(2)}, u32[]{:S(2)}) collective-permute-start(bf16[64,32,128]{2,1,0:T(8,128)(2,1)S(1)} %add_up.52.refs_1_), channel_id=1, source_target_pairs={{0,2},{7,5},{2,4},{5,3},{4,6},{3,1},{8,10},{15,13},{10,12},{13,11}... | collective-permute-start | bytes 1572872 | tf_op jit(solution)/shard_map/ppermute | solution.py:469
  189.0 12.3 %collective-permute-start.49 = (bf16[64,32,128]{2,1,0:T(8,128)(2,1)S(1)}, bf16[64,32,128]{2,1,0:T(8,128)(2,1)S(1)}, u32[]{:S(2)}, u32[]{:S(2)}) collective-permute-start(bf16[64,32,128]{2,1,0:T(8,128)(2,1)S(1)} %add_up.50.refs_1_), channel_id=1, source_target_pairs={{0,2},{7,5},{2,4},{5,3},{4,6},{3,1},{8,10},{15,13},{10,12},{13,11}... | collective-permute-start | bytes 1572872 | tf_op jit(solution)/shard_map/ppermute | solution.py:469
  191.8 6.4 %collective-permute-start.52 = (bf16[32,32,128]{2,1,0:T(8,128)(2,1)S(1)}, bf16[32,32,128]{2,1,0:T(8,128)(2,1)S(1)}, u32[]{:S(2)}, u32[]{:S(2)}) collective-permute-start(bf16[32,32,128]{2,1,0:T(8,128)(2,1)S(1)} %add_up.53), channel_id=1, source_target_pairs={{0,16},{1,9},{2,18},{3,11},{4,20},{5,13},{6,22},{7,15},{8,24},{9,1... | collective-permute-start | bytes 786440 | tf_op jit(solution)/shard_map/ppermute | solution.py:457
  192.3 13.5 %collective-permute-start.55 = (bf16[64,32,128]{2,1,0:T(8,128)(2,1)S(1)}, bf16[64,32,128]{2,1,0:T(8,128)(2,1)S(1)}, u32[]{:S(2)}, u32[]{:S(2)}) collective-permute-start(bf16[64,32,128]{2,1,0:T(8,128)(2,1)S(1)} %collective-permute-done.46.refs_0_.refs_2_), channel_id=1, source_target_pairs={{0,1},{1,0},{2,3},{3,2},{4,5},{5,4},{6,7},{7,6},{8,9},{9,8},{10,11... | collective-permute-start | bytes 1572872 | tf_op jit(solution)/shard_map/ppermute | solution.py:460
  192.3 14.0 %collective-permute-start.56 = (bf16[64,32,128]{2,1,0:T(8,128)(2,1)S(1)}, bf16[64,32,128]{2,1,0:T(8,128)(2,1)S(1)}, u32[]{:S(2)}, u32[]{:S(2)}) collective-permute-start(bf16[64,32,128]{2,1,0:T(8,128)(2,1)S(1)} %collective-permute-done.50.refs_0_.refs_1_), channel_id=1, source_target_pairs={{0,1},{1,0},{2,3},{3,2},{4,5},{5,4},{6,7},{7,6},{8,9},{9,8},{10,11... | collective-permute-start | bytes 1572872 | tf_op jit(solution)/shard_map/ppermute | solution.py:460
  195.6 10.7 %collective-permute-start.57 = (bf16[64,32,128]{2,1,0:T(8,128)(2,1)S(1)}, bf16[64,32,128]{2,1,0:T(8,128)(2,1)S(1)}, u32[]{:S(2)}, u32[]{:S(2)}) collective-permute-start(bf16[64,32,128]{2,1,0:T(8,128)(2,1)S(1)} %collective-permute-done.54.refs_0_), channel_id=1, source_target_pairs={{0,1},{1,0},{2,3},{3,2},{4,5},{5,4},{6,7},{7,6},{8,9},{9,8},{10,11... | collective-permute-start | bytes 1572872 | tf_op jit(solution)/shard_map/ppermute | solution.py:460
  201.3 11.1 %collective-permute-start.53 = (bf16[64,32,128]{2,1,0:T(8,128)(2,1)S(1)}, bf16[64,32,128]{2,1,0:T(8,128)(2,1)S(1)}, u32[]{:S(2)}, u32[]{:S(2)}) collective-permute-start(bf16[64,32,128]{2,1,0:T(8,128)(2,1)S(1)} %add_up.54), channel_id=1, source_target_pairs={{0,2},{7,5},{2,4},{5,3},{4,6},{3,1},{8,10},{15,13},{10,12},{13,11}... | collective-permute-start | bytes 1572872 | tf_op jit(solution)/shard_map/ppermute | solution.py:469
  205.8 7.4 %collective-permute-start.58 = (bf16[64,32,128]{2,1,0:T(8,128)(2,1)S(1)}, bf16[64,32,128]{2,1,0:T(8,128)(2,1)S(1)}, u32[]{:S(2)}, u32[]{:S(2)}) collective-permute-start(bf16[64,32,128]{2,1,0:T(8,128)(2,1)S(1)} %collective-permute-done.45.refs_0_.refs_2_), channel_id=1, source_target_pairs={{0,1},{1,0},{2,3},{3,2},{4,5},{5,4},{6,7},{7,6},{8,9},{9,8},{10,11... | collective-permute-start | bytes 1572872 | tf_op jit(solution)/shard_map/ppermute | solution.py:460
  205.9 7.3 %collective-permute-start.59 = (bf16[64,32,128]{2,1,0:T(8,128)(2,1)S(1)}, bf16[64,32,128]{2,1,0:T(8,128)(2,1)S(1)}, u32[]{:S(2)}, u32[]{:S(2)}) collective-permute-start(bf16[64,32,128]{2,1,0:T(8,128)(2,1)S(1)} %collective-permute-done.49.refs_0_.refs_1_), channel_id=1, source_target_pairs={{0,1},{1,0},{2,3},{3,2},{4,5},{5,4},{6,7},{7,6},{8,9},{9,8},{10,11... | collective-permute-start | bytes 1572872 | tf_op jit(solution)/shard_map/ppermute | solution.py:460
  212.5 2.0 collective-permute-start.60
  212.6 9.2 %collective-permute-start.61 = (bf16[64,32,128]{2,1,0:T(8,128)(2,1)S(1)}, bf16[64,32,128]{2,1,0:T(8,128)(2,1)S(1)}, u32[]{:S(2)}, u32[]{:S(2)}) collective-permute-start(bf16[64,32,128]{2,1,0:T(8,128)(2,1)S(1)} %get-tuple-element.70.refs_1_), channel_id=1, source_target_pairs={{0,8},{1,17},{2,10},{3,19},{4,12},{5,21},{6,14},{7,23},{8,0},{9,25... | collective-permute-start | bytes 1572872 | tf_op jit(solution)/shard_map/ppermute | solution.py:457
  218.2 11.6 %collective-permute-start.63 = (bf16[64,32,128]{2,1,0:T(8,128)(2,1)S(1)}, bf16[64,32,128]{2,1,0:T(8,128)(2,1)S(1)}, u32[]{:S(2)}, u32[]{:S(2)}) collective-permute-start(bf16[64,32,128]{2,1,0:T(8,128)(2,1)S(1)} %get-tuple-element.71.refs_4_), channel_id=1, source_target_pairs={{0,8},{1,17},{2,10},{3,19},{4,12},{5,21},{6,14},{7,23},{8,0},{9,25... | collective-permute-start | bytes 1572872 | tf_op jit(solution)/shard_map/ppermute | solution.py:457
  222.7 14.0 %collective-permute-start.62 = (bf16[32,32,128]{2,1,0:T(8,128)(2,1)}, bf16[32,32,128]{2,1,0:T(8,128)(2,1)}, u32[]{:S(2)}, u32[]{:S(2)}) collective-permute-start(bf16[32,32,128]{2,1,0:T(8,128)(2,1)} %add_up.56), channel_id=1, source_target_pairs={{0,16},{1,9},{2,18},{3,11},{4,20},{5,13},{6,22},{7,15},{8,24},{9,1... | collective-permute-start | bytes 786440 | tf_op jit(solution)/shard_map/ppermute | solution.py:457
  230.8 6.7 %collective-permute-start.64 = (bf16[32,32,128]{2,1,0:T(8,128)(2,1)}, bf16[32,32,128]{2,1,0:T(8,128)(2,1)}, u32[]{:S(2)}, u32[]{:S(2)}) collective-permute-start(bf16[32,32,128]{2,1,0:T(8,128)(2,1)} %add_up.57), channel_id=1, source_target_pairs={{0,16},{1,9},{2,18},{3,11},{4,20},{5,13},{6,22},{7,15},{8,24},{9,1... | collective-permute-start | bytes 786440 | tf_op jit(solution)/shard_map/ppermute | solution.py:457
  (27 other events, 225.5 us)

commit v4 on v3

--- a/solution.py
+++ b/solution.py
@@ -354,14 +354,15 @@
 
 def context_products(index, tiles, blocks, band_cols, deps):
     slots, tile, _ = tiles.shape
-    block_rows, part, _ = blocks[0].shape
-    slot_count = len(blocks)
+    block_rows, part, _ = blocks[0][0].shape
+    slot_count, parts = len(blocks), len(blocks[0])
+    width = part * parts
     chips = (slot_count + 1) // 2
     half = band_cols // 2
     chip_list = 3 * slots
 
     def kernel(index_ref, tiles_ref, *refs):
-        block_refs, refs = refs[:slot_count], refs[slot_count + len(deps) :]
+        block_refs, refs = refs[: slot_count * parts], refs[slot_count * parts + len(deps) :]
         send, keep, acc, band, sems = refs
 
         def each_copy(act):
@@ -370,8 +371,13 @@
 
                 @pl.when((at >= 0) & (at < chips))
                 def _():
-                    rows = pl.ds(at * block_rows, block_rows)
-                    act(pltpu.make_async_copy(block_refs[slot], band.at[rows], sems.at[slot]))
+                    for n in range(parts):
+                        rows, columns = pl.ds(at * block_rows, block_rows), pl.ds(n * part, part)
+                        act(
+                            pltpu.make_async_copy(
+                                block_refs[slot * parts + n], band.at[rows, columns], sems.at[slot, n]
+                            )
+                        )
 
         each_copy(lambda copy: copy.start())
         acc[...] = jnp.zeros_like(acc)
@@ -387,21 +393,21 @@
         send[...] = acc[half:].astype(BF16)
         keep[...] = acc[:half]
 
-    shape = (half, part, tile)
+    shape = (half, width, tile)
     return pl.pallas_call(
         kernel,
-        in_specs=[IN_SMEM, IN_VMEM] + [ANY] * (slot_count + len(deps)),
+        in_specs=[IN_SMEM, IN_VMEM] + [ANY] * (slot_count * parts + len(deps)),
         out_specs=[IN_VMEM] * 2,
         out_shape=[jax.ShapeDtypeStruct(shape, BF16), jax.ShapeDtypeStruct(shape, F32)],
         scratch_shapes=[
-            pltpu.VMEM((band_cols, part, tile), F32),
-            pltpu.VMEM((chips * block_rows, part, tile), BF16),
-            pltpu.SemaphoreType.DMA((slot_count,)),
+            pltpu.VMEM((band_cols, width, tile), F32),
+            pltpu.VMEM((chips * block_rows, width, tile), BF16),
+            pltpu.SemaphoreType.DMA((slot_count, parts)),
         ],
-        compiler_params=params(20),
+        compiler_params=params(32),
         cost_estimate=cost(0.01),
         name="context_products",
-    )(index, tiles, *blocks, *deps)
+    )(index, tiles, *[ref for block in blocks for ref in block], *deps)
 
 
 def turn_back(pieces, start, blocks, scale, pinned=False, deps=()):
@@ -505,7 +511,6 @@
     contexts = [context] + [row_xor(context, mask) for mask in range(1, n_row)]
     this_core = core.reshape(1)
     bundle, given, context_log = bundles(this_core, word_part, contexts)
-    next_blocks = spread(turn_panel(panel, tile, 1, (bundle,)))
     bundle = plus(bundle, core_swap(given))
     for step in range(chips.bit_length() - 1):
         bundle = plus(bundle, chip_xor(bundle, 1 << step))
@@ -516,26 +521,30 @@
     swapped = [[{} for _ in range(PARTS)] for _ in range(GROUPS)]
     own = [[None] * PARTS for _ in range(GROUPS)]
     word_pieces, context_pieces = [], []
-    stages = [[[] for _ in range(PARTS)] for _ in range(GROUPS)]
+    stages, through = [], []
     source = (counts, this_core, bundle, core_swap(bundle), context_log)
     tiles, *groups[0] = word_products(index, panel_blocks, chips, block_rows, source=source)
     got, passed = [None] * PARTS, {}
     last = ()
 
-    def contexts_of(group, n, deps):
-        blocks = [near[group][n][d] for d in range(chips - 1, 0, -1)] + [own[group][n]]
-        blocks += [swapped[group][n][d] for d in range(1, chips)]
+    def contexts_of(group, parts, deps):
+        blocks = [[near[group][n][d] for n in parts] for d in range(chips - 1, 0, -1)]
+        blocks.append([own[group][n] for n in parts])
+        blocks += [[swapped[group][n][d] for n in parts] for d in range(1, chips)]
         send, keep = context_products(index, tiles, blocks, band_cols, deps)
-        stages[group][n].append(send)
+        sent = [send]
         terms, count = [(keep, 0)], band_cols // 2
         for step in range(bits):
             terms.append((row_swap(send, step), 0))
-            stages[group][n].append(terms[-1][0])
+            sent.append(terms[-1][0])
             if step < bits - 1:
                 count //= 2
-                (send,) = add_up([(x, (2 * y + 1, 0)) for x, y in terms], count, part, [BF16])
+                (send,) = add_up(
+                    [(x, (2 * y + 1, 0)) for x, y in terms], count, part * len(parts), [BF16]
+                )
                 terms = [(x, 2 * y) for x, y in terms]
         context_pieces.append([x for x, _ in terms])
+        return sent
 
     for slot in range(chips * GROUPS + chips - 2):
         group, step = slot // chips, slot % chips + 1
@@ -552,15 +561,11 @@
             )
         for n in range(PARTS):
             if group < GROUPS and step == chips:
-                if group:
-                    last = (*last, stages[before][n][0])
-                    if n:
-                        (got[n],) = add_up([(got[n], (0, 0))], block_rows, part, [BF16], first_sent)
                 terms = [(got[n], (0, 0)), (core_swap(got[n]), (0, 0)), (mine_sum, (0, n))]
                 payload, whole = add_up(terms, block_rows, part, [BF16, F32], last)
                 own[group][n] = payload
-                if group and n + 1 < PARTS:
-                    contexts_of(before, n + 1, (payload,))
+                if group and n == PARTS - 1:
+                    through = contexts_of(before, range(PARTS), (payload,))
                 word_pieces.append([whole])
             elif group < GROUPS:
                 terms = [(kept[far], (0, n)), (passed[far], (0, n))]
@@ -572,11 +577,13 @@
                 (payload,) = add_up(terms, block_rows, part, [BF16], last, other)
             else:
                 payload = near[before][n][hop - 1]
-                if GROUPS > 1:
-                    last = (*last, stages[before - 1][n][min(step, bits)])
+                if through and n == (0 if step == 1 else PARTS - 1):
+                    last = (*last, through[min(step - 1, bits)])
                 (payload,) = add_up([(payload, (0, 0))], block_rows, part, [BF16], last)
             got[n] = along(payload)
             last = (payload,)
+            if n == 0 and step == 1 and group < GROUPS - 1:
+                next_blocks = spread(turn_panel(panel, tile, group + 1, last))
             if group < GROUPS and step == chips:
                 arrived = (group, 1)
             elif group > 0 and hop < chips:
@@ -584,25 +591,20 @@
             else:
                 continue
             if group == GROUPS and hop == chips - 1 and n > 0:
-                gate = stages[before][n - 1][:1]
-                (got[n],) = add_up([(got[n], (0, 0))], block_rows, part, [BF16], gate)
+                (got[n],) = add_up([(got[n], (0, 0))], block_rows, part, [BF16], stages[:1])
             near[arrived[0]][n][arrived[1]] = got[n]
             swapped[arrived[0]][n][arrived[1]] = core_swap(got[n])
             if group == GROUPS and hop == chips - 1:
-                contexts_of(before, n, ())
-        if step == 1 and group < GROUPS - 1:
+                stages = contexts_of(before, (n,), through[-1:])
+        if step == 2 and group < GROUPS - 1:
             panel_blocks = spread_on(next_blocks, last)
-        if step == 2 and group < GROUPS - 1:
+        if step == chips - 1 and group < GROUPS - 1:
             _, *groups[group + 1] = word_products(
                 index, panel_blocks, chips, block_rows, tiles=tiles, deps=last
             )
-            last = (*last, groups[group + 1][0][1])
-            if group + 2 < GROUPS:
-                next_blocks = spread(turn_panel(panel, tile, group + 2, last))
-        if group > 0 and step == chips - 1 and group < GROUPS:
-            contexts_of(before, 0, last)
-            first_sent = stages[before][0][:1]
-    deps = (stages[-1][-1][0],)
+            made = (groups[group + 1][0][1],)
+
+    deps = (stages[0],)
     word_out = turn_back(word_pieces, (core * share).reshape(1), share, 1.0, True, deps)
     zero = jnp.zeros((1,), jnp.int32)
     return word_out, turn_back(context_pieces, zero, share, 1.0 / tile)

time: 243 us -> 234 us (0.963)
  Pallas kernels: 67.5 us -> 61.5 us
    ppermute x14 -> x12, waiting for transfers between devices: 18 us -> 11.9 us  [row_swap(): return lax.ppermute(x, ('row', 'col'), pairs)]
    ppermute x20, waiting for transfers between devices: 25.3 us -> 29.2 us  [along(): return lax.ppermute(x, 'col', pairs)]
    pallas_call x4 -> x3, Pallas kernels: 15.6 us -> 12.4 us  [context_products(): pl.pallas_call(kernel, in_specs=[IN_SMEM, IN_VMEM] + [ANY] * (slot_count...]
    pallas_call x29 -> x27, Pallas kernels: 17.5 us -> 14.6 us  [add_up(): pl.pallas_call(kernel, grid_spec=pltpu.PrefetchScalarGridSpec(num_scalar_...]
    ppermute x14 -> x12, starting transfers between devices: 14.1 us -> 13 us  [row_swap(): return lax.ppermute(x, ('row', 'col'), pairs)]
  transfers between devices with their start and end apart: 65 -> 63, of which waited for: 26 -> 23; matrix products, arithmetic and copies ran while one was open for 0% -> 0% of each run, Pallas kernels for 21% -> 20%
where the time goes in v4:
time: 234 us; the launch traced here: 233 us
  starting transfers between devices  112 us (48%)
  Pallas kernels  61.5 us (26%)
  waiting for transfers between devices  54.7 us (23%)
  local copies, waits for them, and re-layouts  3.22 us (1%)
    ppermute x20, starting transfers between devices, along(): return lax.ppermute(x, 'col', pairs)  77.8 us
    ppermute x20, waiting for transfers between devices, along(): return lax.ppermute(x, 'col', pairs)  29.2 us
    pallas_call x2, Pallas kernels, word_products(): pl.pallas_call(kernel, in_specs=[IN_SMEM] + operand_specs + [ANY] * (n_in...  18.3 us
    pallas_call x27, Pallas kernels, add_up(): pl.pallas_call(kernel, grid_spec=pltpu.PrefetchScalarGridSpec(num_scalar_...  14.6 us
    ppermute x26, starting transfers between devices, core_swap(): lax.ppermute(x, 'col', [(i, i ^ 1) for i in range(n_col) if keep(i % 2, i...  13 us
    ppermute x12, starting transfers between devices, row_swap(): return lax.ppermute(x, ('row', 'col'), pairs)  13 us
    pallas_call x3, Pallas kernels, context_products(): pl.pallas_call(kernel, in_specs=[IN_SMEM, IN_VMEM] + [ANY] * (slot_count...  12.4 us
    ppermute x12, waiting for transfers between devices, row_swap(): return lax.ppermute(x, ('row', 'col'), pairs)  11.9 us
  transfers between devices with their start and end apart: 63, of which 23 were waited for; matrix products, arithmetic and copies ran while one was open for 0% of the time, Pallas kernels for 20%

profile of v4, /device:TPU:0, one launch (start us, length us, event | category | flops | bytes accessed | tf_op | source)
XLA Modules:
  0.0 232.7 jit_solution(12926326191148104811)
XLA Ops:
  0.6 1.5 turn_panel.2.refs_0_.refs_5_
  2.2 3.0 %collective-permute-start.8 = (bf16[32,64,128]{2,1,0:T(8,128)(2,1)S(1)}, bf16[32,64,128]{2,1,0:T(8,128)(2,1)S(1)}, u32[]{:S(2)}, u32[]{:S(2)}) collective-permute-start(bf16[32,64,128]{2,1,0:T(8,128)(2,1)S(1)} %turn_panel.2.refs_0_.refs_5_), channel_id=1, source_target_pairs={{0,8},{1,17},{2,10},{3,19},{4,12},{5,21},{6,14},{7,23},{8,0},{9,25... | collective-permute-start | bytes 1572872 | tf_op jit(solution)/shard_map/ppermute | solution.py:463
  5.2 4.9 %count_sums.1 = (f32[256,128]{1,0:T(8,128)S(1)}, f32[128,128]{1,0:T(8,128)S(1)}) custom-call(s32[160,128,128]{2,1,0:T(8,128)} %bitcast.8, s32[160]{0:T(256)} %bitcast.13, s32[160]{0:T(256)} %bitcast.10, bf16[32,64,128]{2,1,0:T(8,128)(2,1)S(1)} %turn_panel.2.refs_0_.refs_5_), custom_call_target="tpu_custom_call" | custom-call | bytes 36900 | tf_op jit(solution)/shard_map/count_sums/pallas_call | solution.py:90
  10.1 2.0 collective-permute-start.1
  12.2 1.4 collective-permute-start.2
  13.6 1.5 collective-permute-start.7
  15.7 2.5 %collective-permute-done.2.refs_3_ = f32[128,128]{1,0:T(8,128)S(1)} collective-permute-done((f32[128,128]{1,0:T(8,128)S(1)}, f32[128,128]{1,0:T(8,128)S(1)}, u32[]{:S(2)}, u32[]{:S(2)}) %collective-permute-start.2) | collective-permute-done | bytes 65568 | tf_op jit(solution)/shard_map/ppermute | solution.py:478
  19.5 1.6 collective-permute-start.4
  21.2 2.7 %collective-permute-done.4.b_ref = f32[136,128]{1,0:T(8,128)S(1)} collective-permute-done((f32[136,128]{1,0:T(8,128)S(1)}, f32[136,128]{1,0:T(8,128)S(1)}, u32[]{:S(2)}, u32[]{:S(2)}) %collective-permute-start.4) | collective-permute-done | bytes 69664 | tf_op jit(solution)/shard_map/ppermute | solution.py:481
  23.9 2.7 %collective-permute-start.5 = (f32[136,128]{1,0:T(8,128)S(1)}, f32[136,128]{1,0:T(8,128)S(1)}, u32[]{:S(2)}, u32[]{:S(2)}) collective-permute-start(f32[136,128]{1,0:T(8,128)S(1)} %plus.4.a_ref), channel_id=1, source_target_pairs={{0,4},{1,5},{2,6},{3,7},{4,0},{5,1},{6,2},{7,3},{8,12},{9,13},{10,... | collective-permute-start | bytes 208904 | tf_op jit(solution)/shard_map/ppermute | solution.py:481
  26.6 2.7 %collective-permute-done.5.b_ref = f32[136,128]{1,0:T(8,128)S(1)} collective-permute-done((f32[136,128]{1,0:T(8,128)S(1)}, f32[136,128]{1,0:T(8,128)S(1)}, u32[]{:S(2)}, u32[]{:S(2)}) %collective-permute-start.5) | collective-permute-done | bytes 69664 | tf_op jit(solution)/shard_map/ppermute | solution.py:481
  31.4 10.5 %ppmi_word_products.1 = (bf16[160,128,128]{2,1,0:T(8,128)(2,1)S(1)}, bf16[64,64,128]{2,1,0:T(8,128)(2,1)S(1)}, bf16[64,64,128]{2,1,0:T(8,128)(2,1)S(1)}, bf16[64...) custom-call(s32[487]{0:T(512)S(1)} %pad_add_fusion.index_ref, ...), custom_call_target="tpu_custom_call" | custom-call | bytes 36900 | tf_op jit(solution)/shard_map/ppmi_word_products/pallas_call | solution.py:338
  42.0 1.3 collective-permute-start.12
  43.3 1.3 collective-permute-start.11
  44.6 2.0 collective-permute-done.12.refs_1_
  46.9 1.3 collective-permute-start.13
  48.2 1.3 collective-permute-start.10
  49.8 5.0 %collective-permute-start.15 = (bf16[64,32,128]{2,1,0:T(8,128)(2,1)S(1)}, bf16[64,32,128]{2,1,0:T(8,128)(2,1)S(1)}, u32[]{:S(2)}, u32[]{:S(2)}) collective-permute-start(bf16[64,32,128]{2,1,0:T(8,128)(2,1)S(1)} %add_up.28.refs_3_.refs_2_), channel_id=1, source_target_pairs={{0,2},{7,5},{2,4},{5,3},{4,6},{3,1},{8,10},{15,13},{10,12},{13,11}... | collective-permute-start | bytes 1572872 | tf_op jit(solution)/shard_map/ppermute | solution.py:475
  54.9 1.6 turn_panel.3.refs_1_
  56.4 1.6 collective-permute-start.23
  58.5 5.1 %collective-permute-start.14 = (bf16[64,32,128]{2,1,0:T(8,128)(2,1)S(1)}, bf16[64,32,128]{2,1,0:T(8,128)(2,1)S(1)}, u32[]{:S(2)}, u32[]{:S(2)}) collective-permute-start(bf16[64,32,128]{2,1,0:T(8,128)(2,1)S(1)} %add_up.29.refs_3_), channel_id=1, source_target_pairs={{0,2},{7,5},{2,4},{5,3},{4,6},{3,1},{8,10},{15,13},{10,12},{13,11}... | collective-permute-start | bytes 1572872 | tf_op jit(solution)/shard_map/ppermute | solution.py:475
  64.0 3.0 %collective-permute-start.19 = (bf16[64,32,128]{2,1,0:T(8,128)(2,1)S(1)}, bf16[64,32,128]{2,1,0:T(8,128)(2,1)S(1)}, u32[]{:S(2)}, u32[]{:S(2)}) collective-permute-start(bf16[64,32,128]{2,1,0:T(8,128)(2,1)S(1)} %add_up.30.refs_3_.refs_1_), channel_id=1, source_target_pairs={{0,2},{7,5},{2,4},{5,3},{4,6},{3,1},{8,10},{15,13},{10,12},{13,11}... | collective-permute-start | bytes 1572872 | tf_op jit(solution)/shard_map/ppermute | solution.py:475
  67.8 1.7 collective-permute-start.24
  70.7 4.4 %collective-permute-start.16 = (bf16[64,32,128]{2,1,0:T(8,128)(2,1)S(1)}, bf16[64,32,128]{2,1,0:T(8,128)(2,1)S(1)}, u32[]{:S(2)}, u32[]{:S(2)}) collective-permute-start(bf16[64,32,128]{2,1,0:T(8,128)(2,1)S(1)} %add_up.31.refs_3_), channel_id=1, source_target_pairs={{0,2},{7,5},{2,4},{5,3},{4,6},{3,1},{8,10},{15,13},{10,12},{13,11}... | collective-permute-start | bytes 1572872 | tf_op jit(solution)/shard_map/ppermute | solution.py:475
  76.3 4.4 %collective-permute-start.20 = (bf16[64,32,128]{2,1,0:T(8,128)(2,1)S(1)}, bf16[64,32,128]{2,1,0:T(8,128)(2,1)S(1)}, u32[]{:S(2)}, u32[]{:S(2)}) collective-permute-start(bf16[64,32,128]{2,1,0:T(8,128)(2,1)S(1)} %add_up.33.refs_3_.refs_5_), channel_id=1, source_target_pairs={{0,2},{7,5},{2,4},{5,3},{4,6},{3,1},{8,10},{15,13},{10,12},{13,11}... | collective-permute-start | bytes 1572872 | tf_op jit(solution)/shard_map/ppermute | solution.py:475
  80.7 1.3 collective-permute-done.24.refs_4_
  82.1 7.8 %word_products.1 = (bf16[64,64,128]{2,1,0:T(8,128)(2,1)}, bf16[64,64,128]{2,1,0:T(8,128)(2,1)}, bf16[64,64,128]{2,1,0:T(8,128)(2,1)S(1)}, bf16[64,64,128]{2,1,0:...) custom-call(s32[487]{0:T(512)S(1)} %pad_add_fusion.index_ref, ...), custom_call_target="tpu_custom_call" | custom-call | bytes 36900 | tf_op jit(solution)/shard_map/word_products/pallas_call | solution.py:338
  90.0 1.3 collective-permute-start.27
  91.3 2.1 collective-permute-start.21
  93.7 1.3 add_up.34
  95.0 3.9 %collective-permute-start.28 = (bf16[64,32,128]{2,1,0:T(8,128)(2,1)}, bf16[64,32,128]{2,1,0:T(8,128)(2,1)}, u32[]{:S(2)}, u32[]{:S(2)}) collective-permute-start(bf16[64,32,128]{2,1,0:T(8,128)(2,1)} %get-tuple-element.49.refs_3_.refs_6_), channel_id=1, source_target_pairs={{0,2},{7,5},{2,4},{5,3},{4,6},{3,1},{8,10},{15,13},{10,12},{13,11}... | collective-permute-start | bytes 1572872 | tf_op jit(solution)/shard_map/ppermute | solution.py:475
  98.9 1.3 collective-permute-start.26
  100.2 1.3 add_up.35
  101.5 3.4 %collective-permute-start.30 = (bf16[64,32,128]{2,1,0:T(8,128)(2,1)}, bf16[64,32,128]{2,1,0:T(8,128)(2,1)}, u32[]{:S(2)}, u32[]{:S(2)}) collective-permute-start(bf16[64,32,128]{2,1,0:T(8,128)(2,1)} %get-tuple-element.58.refs_3_.refs_7_), channel_id=1, source_target_pairs={{0,2},{7,5},{2,4},{5,3},{4,6},{3,1},{8,10},{15,13},{10,12},{13,11}... | collective-permute-start | bytes 1572872 | tf_op jit(solution)/shard_map/ppermute | solution.py:475
  106.4 1.5 add_up.37.refs_3_
  107.9 4.3 %collective-permute-start.29 = (bf16[64,32,128]{2,1,0:T(8,128)(2,1)S(1)}, bf16[64,32,128]{2,1,0:T(8,128)(2,1)S(1)}, u32[]{:S(2)}, u32[]{:S(2)}) collective-permute-start(bf16[64,32,128]{2,1,0:T(8,128)(2,1)S(1)} %add_up.37.refs_3_), channel_id=1, source_target_pairs={{0,2},{7,5},{2,4},{5,3},{4,6},{3,1},{8,10},{15,13},{10,12},{13,11}... | collective-permute-start | bytes 1572872 | tf_op jit(solution)/shard_map/ppermute | solution.py:475
  112.2 1.3 collective-permute-start.25
  113.5 1.4 add_up.38.refs_4_.refs_2_
  114.9 3.9 %collective-permute-start.32 = (bf16[64,32,128]{2,1,0:T(8,128)(2,1)S(1)}, bf16[64,32,128]{2,1,0:T(8,128)(2,1)S(1)}, u32[]{:S(2)}, u32[]{:S(2)}) collective-permute-start(bf16[64,32,128]{2,1,0:T(8,128)(2,1)S(1)} %add_up.38.refs_4_.refs_2_), channel_id=1, source_target_pairs={{0,2},{7,5},{2,4},{5,3},{4,6},{3,1},{8,10},{15,13},{10,12},{13,11}... | collective-permute-start | bytes 1572872 | tf_op jit(solution)/shard_map/ppermute | solution.py:475
  119.1 4.6 %collective-permute-start.31 = (bf16[64,32,128]{2,1,0:T(8,128)(2,1)S(1)}, bf16[64,32,128]{2,1,0:T(8,128)(2,1)S(1)}, u32[]{:S(2)}, u32[]{:S(2)}) collective-permute-start(bf16[64,32,128]{2,1,0:T(8,128)(2,1)S(1)} %add_up.39.refs_4_), channel_id=1, source_target_pairs={{0,2},{7,5},{2,4},{5,3},{4,6},{3,1},{8,10},{15,13},{10,12},{13,11}... | collective-permute-start | bytes 1572872 | tf_op jit(solution)/shard_map/ppermute | solution.py:475
  123.7 1.7 collective-permute-done.32.refs_2_.refs_3_
  125.7 4.4 %collective-permute-start.36 = (bf16[64,32,128]{2,1,0:T(8,128)(2,1)S(1)}, bf16[64,32,128]{2,1,0:T(8,128)(2,1)S(1)}, u32[]{:S(2)}, u32[]{:S(2)}) collective-permute-start(bf16[64,32,128]{2,1,0:T(8,128)(2,1)S(1)} %add_up.40.refs_3_), channel_id=1, source_target_pairs={{0,2},{7,5},{2,4},{5,3},{4,6},{3,1},{8,10},{15,13},{10,12},{13,11}... | collective-permute-start | bytes 1572872 | tf_op jit(solution)/shard_map/ppermute | solution.py:475
  131.5 4.4 %collective-permute-start.33 = (bf16[64,32,128]{2,1,0:T(8,128)(2,1)S(1)}, bf16[64,32,128]{2,1,0:T(8,128)(2,1)S(1)}, u32[]{:S(2)}, u32[]{:S(2)}) collective-permute-start(bf16[64,32,128]{2,1,0:T(8,128)(2,1)S(1)} %add_up.41.refs_3_), channel_id=1, source_target_pairs={{0,2},{7,5},{2,4},{5,3},{4,6},{3,1},{8,10},{15,13},{10,12},{13,11}... | collective-permute-start | bytes 1572872 | tf_op jit(solution)/shard_map/ppermute | solution.py:475
  137.3 4.7 %collective-permute-start.37 = (bf16[64,32,128]{2,1,0:T(8,128)(2,1)S(1)}, bf16[64,32,128]{2,1,0:T(8,128)(2,1)S(1)}, u32[]{:S(2)}, u32[]{:S(2)}) collective-permute-start(bf16[64,32,128]{2,1,0:T(8,128)(2,1)S(1)} %add_up.43.refs_3_), channel_id=1, source_target_pairs={{0,2},{7,5},{2,4},{5,3},{4,6},{3,1},{8,10},{15,13},{10,12},{13,11}... | collective-permute-start | bytes 1572872 | tf_op jit(solution)/shard_map/ppermute | solution.py:475
  142.8 5.8 %collective-permute-done.37.refs_0_ = bf16[64,32,128]{2,1,0:T(8,128)(2,1)S(1)} collective-permute-done((bf16[64,32,128]{2,1,0:T(8,128)(2,1)S(1)}, bf16[64,32,128]{2,1,0:T(8,128)(2,1)S(1)}, u32[]{:S(2)}, u32[]{:S(2)}) %collective-permute-start.37) | collective-permute-done | bytes 524320 | tf_op jit(solution)/shard_map/ppermute | solution.py:475
  151.3 4.4 %collective-permute-start.40 = (bf16[64,32,128]{2,1,0:T(8,128)(2,1)S(1)}, bf16[64,32,128]{2,1,0:T(8,128)(2,1)S(1)}, u32[]{:S(2)}, u32[]{:S(2)}) collective-permute-start(bf16[64,32,128]{2,1,0:T(8,128)(2,1)S(1)} %get-tuple-element.61.refs_3_), channel_id=1, source_target_pairs={{0,2},{7,5},{2,4},{5,3},{4,6},{3,1},{8,10},{15,13},{10,12},{13,11}... | collective-permute-start | bytes 1572872 | tf_op jit(solution)/shard_map/ppermute | solution.py:475
  156.8 2.9 %collective-permute-start.39 = (bf16[64,32,128]{2,1,0:T(8,128)(2,1)S(1)}, bf16[64,32,128]{2,1,0:T(8,128)(2,1)S(1)}, u32[]{:S(2)}, u32[]{:S(2)}) collective-permute-start(bf16[64,32,128]{2,1,0:T(8,128)(2,1)S(1)} %get-tuple-element.63.refs_14_.refs_1_.refs_3_), channel_id=1, source_target_pairs={{0,2},{7,5},{2,4},{5,3},{4,6},{3,1},{8,10},{15,13},{10,12},{13,11}... | collective-permute-start | bytes 1572872 | tf_op jit(solution)/shard_map/ppermute | solution.py:475
  159.8 5.0 %context_products.3 = (bf16[64,64,128]{2,1,0:T(8,128)(2,1)S(1)}, f32[64,64,128]{2,1,0:T(8,128)S(1)}) custom-call(s32[487]{0:T(512)S(1)} %pad_add_fusion.index_ref, bf16[160,128,128]{2,1,0:T(8,128)(2,1)S(1)} %bitcast.7, bf16[64,32,128]{2,1,0:T(8,128)(2,1)S(1)} %collective-permute-done.31.refs_2_.refs_0_, ...), custom_call_target="tpu_custom_call" | custom-call | bytes 36900 | tf_op jit(solution)/shard_map/context_products/pallas_call | solution.py:397
  164.8 1.6 collective-permute-start.49
  166.5 2.8 %collective-permute-start.48 = (bf16[64,32,128]{2,1,0:T(8,128)(2,1)S(1)}, bf16[64,32,128]{2,1,0:T(8,128)(2,1)S(1)}, u32[]{:S(2)}, u32[]{:S(2)}) collective-permute-start(bf16[64,32,128]{2,1,0:T(8,128)(2,1)S(1)} %add_up.46.refs_1_), channel_id=1, source_target_pairs={{0,2},{7,5},{2,4},{5,3},{4,6},{3,1},{8,10},{15,13},{10,12},{13,11}... | collective-permute-start | bytes 1572872 | tf_op jit(solution)/shard_map/ppermute | solution.py:475
  169.4 6.5 %collective-permute-done.48.refs_0_.refs_1_ = bf16[64,32,128]{2,1,0:T(8,128)(2,1)S(1)} collective-permute-done((bf16[64,32,128]{2,1,0:T(8,128)(2,1)S(1)}, bf16[64,32,128]{2,1,0:T(8,128)(2,1)S(1)}, u32[]{:S(2)}, u32[]{:S(2)}) %collective-permute-start.48) | collective-permute-done | bytes 524320 | tf_op jit(solution)/shard_map/ppermute | solution.py:475
  176.0 4.4 %collective-permute-start.51 = (bf16[64,32,128]{2,1,0:T(8,128)(2,1)S(1)}, bf16[64,32,128]{2,1,0:T(8,128)(2,1)S(1)}, u32[]{:S(2)}, u32[]{:S(2)}) collective-permute-start(bf16[64,32,128]{2,1,0:T(8,128)(2,1)S(1)} %add_up.48.refs_1_), channel_id=1, source_target_pairs={{0,2},{7,5},{2,4},{5,3},{4,6},{3,1},{8,10},{15,13},{10,12},{13,11}... | collective-permute-start | bytes 1572872 | tf_op jit(solution)/shard_map/ppermute | solution.py:475
  180.4 2.0 collective-permute-start.47
  183.5 3.6 %collective-permute-done.51.refs_0_ = bf16[64,32,128]{2,1,0:T(8,128)(2,1)S(1)} collective-permute-done((bf16[64,32,128]{2,1,0:T(8,128)(2,1)S(1)}, bf16[64,32,128]{2,1,0:T(8,128)(2,1)S(1)}, u32[]{:S(2)}, u32[]{:S(2)}) %collective-permute-start.51) | collective-permute-done | bytes 524320 | tf_op jit(solution)/shard_map/ppermute | solution.py:475
  187.1 5.6 %collective-permute-done.47.refs_0_.refs_1_ = bf16[64,32,128]{2,1,0:T(8,128)(2,1)S(1)} collective-permute-done((bf16[64,32,128]{2,1,0:T(8,128)(2,1)S(1)}, bf16[64,32,128]{2,1,0:T(8,128)(2,1)S(1)}, u32[]{:S(2)}, u32[]{:S(2)}) %collective-permute-start.47) | collective-permute-done | bytes 524320 | tf_op jit(solution)/shard_map/ppermute | solution.py:475
  192.8 4.4 %collective-permute-start.50 = (bf16[64,32,128]{2,1,0:T(8,128)(2,1)S(1)}, bf16[64,32,128]{2,1,0:T(8,128)(2,1)S(1)}, u32[]{:S(2)}, u32[]{:S(2)}) collective-permute-start(bf16[64,32,128]{2,1,0:T(8,128)(2,1)S(1)} %add_up.49), channel_id=1, source_target_pairs={{0,2},{7,5},{2,4},{5,3},{4,6},{3,1},{8,10},{15,13},{10,12},{13,11}... | collective-permute-start | bytes 1572872 | tf_op jit(solution)/shard_map/ppermute | solution.py:475
  197.8 3.7 %context_products.4 = (bf16[64,32,128]{2,1,0:T(8,128)(2,1)S(1)}, f32[64,32,128]{2,1,0:T(8,128)S(1)}) custom-call(s32[487]{0:T(512)S(1)} %pad_add_fusion.index_ref, bf16[160,128,128]{2,1,0:T(8,128)(2,1)S(1)} %bitcast.7, bf16[64,32,128]{2,1,0:T(8,128)(2,1)S(1)} %collective-permute-done.51.refs_0_, ...), custom_call_target="tpu_custom_call" | custom-call | bytes 36900 | tf_op jit(solution)/shard_map/context_products/pallas_call | solution.py:397
  201.6 2.3 collective-permute-done.50.refs_0_
  204.6 1.3 collective-permute-done.58.refs_6_
  205.9 3.7 %context_products.5 = (bf16[64,32,128]{2,1,0:T(8,128)(2,1)S(1)}, f32[64,32,128]{2,1,0:T(8,128)S(1)}) custom-call(s32[487]{0:T(512)S(1)} %pad_add_fusion.index_ref, bf16[160,128,128]{2,1,0:T(8,128)(2,1)S(1)} %bitcast.7, bf16[64,32,128]{2,1,0:T(8,128)(2,1)S(1)} %add_up.51.refs_0_, bf16[64,32,128]{2,1,0:T(8,128)(2,1)S(1)} %collective-permute-done.47.refs_0_.refs_1_, ...), custom_call_target="tpu_custom_call" | custom-call | bytes 36900 | tf_op jit(solution)/shard_map/context_products/pallas_call | solution.py:397
  210.3 3.0 %collective-permute-done.59.refs_1_.refs_4_ = bf16[64,32,128]{2,1,0:T(8,128)(2,1)S(1)} collective-permute-done((bf16[64,32,128]{2,1,0:T(8,128)(2,1)S(1)}, bf16[64,32,128]{2,1,0:T(8,128)(2,1)S(1)}, u32[]{:S(2)}, u32[]{:S(2)}) %collective-permute-start.59) | collective-permute-done | bytes 524320 | tf_op jit(solution)/shard_map/ppermute | solution.py:463
  214.6 6.7 %collective-permute-done.61.refs_1_.refs_7_ = bf16[64,32,128]{2,1,0:T(8,128)(2,1)S(1)} collective-permute-done((bf16[64,32,128]{2,1,0:T(8,128)(2,1)S(1)}, bf16[64,32,128]{2,1,0:T(8,128)(2,1)S(1)}, u32[]{:S(2)}, u32[]{:S(2)}) %collective-permute-start.61) | collective-permute-done | bytes 524320 | tf_op jit(solution)/shard_map/ppermute | solution.py:463
  223.8 4.3 %turn_back.2 = f32[4096,128]{1,0:T(8,128)} custom-call(s32[1]{0:T(128)S(6)} %select_n.44.start_ref, f32[64,32,128]{2,1,0:T(8,128)} %get-tuple-element.48.refs_0_, f32[64,32,128]{2,1,0:T(8,128)} %get-tuple-element.50.refs_1_, f32[64,32,128]{2,1,0:T(8,128)} %get-tuple-element.60.refs_2_, f32[64,32,128]{2,1,0:T(8,128)} %get-tuple-element.62.refs_3_, ...), custom_call_target="tpu_custom_call" | custom-call | bytes 36900 | tf_op jit(solution)/shard_map/turn_back/pallas_call | solution.py:428
  228.9 3.7 %turn_back.3 = f32[4096,128]{1,0:T(8,128)} custom-call(s32[1]{0:T(128)} %constant.92.clone.1.place_ref.start_ref, f32[64,64,128]{2,1,0:T(8,128)S(1)} %get-tuple-element.65.refs_0_, bf16[64,64,128]{2,1,0:T(8,128)(2,1)S(1)} %collective-permute-done.49.refs_2_.refs_1_, bf16[32,64,128]{2,1,0:T(8,128)(2,1)S(1)} %copy-done.2, f32[64,32,128]{2,1,0:T(8,128)S(1)} %copy-done.4, ...), custom_call_target="tpu_custom_call" | custom-call | bytes 36900 | tf_op jit(solution)/shard_map/turn_back/pallas_call | solution.py:428
  (157 shorter events, 26.2 us)
Async XLA Ops:
  2.2 13.0 %collective-permute-start.8 = (bf16[32,64,128]{2,1,0:T(8,128)(2,1)S(1)}, bf16[32,64,128]{2,1,0:T(8,128)(2,1)S(1)}, u32[]{:S(2)}, u32[]{:S(2)}) collective-permute-start(bf16[32,64,128]{2,1,0:T(8,128)(2,1)S(1)} %turn_panel.2.refs_0_.refs_5_), channel_id=1, source_target_pairs={{0,8},{1,17},{2,10},{3,19},{4,12},{5,21},{6,14},{7,23},{8,0},{9,25... | collective-permute-start | bytes 1572872 | tf_op jit(solution)/shard_map/ppermute | solution.py:463
  10.1 5.6 %collective-permute-start = (f32[128,128]{1,0:T(8,128)S(1)}, f32[128,128]{1,0:T(8,128)S(1)}, u32[]{:S(2)}, u32[]{:S(2)}) collective-permute-start(f32[128,128]{1,0:T(8,128)S(1)} %get-tuple-element.37.refs_0_), channel_id=1, source_target_pairs={{0,8},{8,0},{16,24},{24,16},{1,9},{9,1},{17,25},{25,17},{2,10},{10... | collective-permute-start | bytes 196616 | tf_op jit(solution)/shard_map/ppermute | solution.py:478
  10.1 5.5 %collective-permute-start.1 = (f32[128,128]{1,0:T(8,128)S(1)}, f32[128,128]{1,0:T(8,128)S(1)}, u32[]{:S(2)}, u32[]{:S(2)}) collective-permute-start(f32[128,128]{1,0:T(8,128)S(1)} %get-tuple-element.37.refs_0_), channel_id=1, source_target_pairs={{0,16},{8,24},{16,0},{24,8},{1,17},{9,25},{17,1},{25,9},{2,18},{10... | collective-permute-start | bytes 196616 | tf_op jit(solution)/shard_map/ppermute | solution.py:478
  12.2 5.9 %collective-permute-start.2 = (f32[128,128]{1,0:T(8,128)S(1)}, f32[128,128]{1,0:T(8,128)S(1)}, u32[]{:S(2)}, u32[]{:S(2)}) collective-permute-start(f32[128,128]{1,0:T(8,128)S(1)} %get-tuple-element.37.refs_0_), channel_id=1, source_target_pairs={{0,24},{8,16},{16,8},{24,0},{1,25},{9,17},{17,9},{25,1},{2,26},{10... | collective-permute-start | bytes 196616 | tf_op jit(solution)/shard_map/ppermute | solution.py:478
  13.6 17.0 %collective-permute-start.7 = (bf16[32,64,128]{2,1,0:T(8,128)(2,1)S(1)}, bf16[32,64,128]{2,1,0:T(8,128)(2,1)S(1)}, u32[]{:S(2)}, u32[]{:S(2)}) collective-permute-start(bf16[32,64,128]{2,1,0:T(8,128)(2,1)S(1)} %turn_panel.2.refs_0_.refs_5_), channel_id=1, source_target_pairs={{0,16},{1,9},{2,18},{3,11},{4,20},{5,13},{6,22},{7,15},{8,24},{9,1... | collective-permute-start | bytes 1572872 | tf_op jit(solution)/shard_map/ppermute | solution.py:463
  15.1 15.5 %collective-permute-start.9 = (bf16[32,64,128]{2,1,0:T(8,128)(2,1)S(1)}, bf16[32,64,128]{2,1,0:T(8,128)(2,1)S(1)}, u32[]{:S(2)}, u32[]{:S(2)}) collective-permute-start(bf16[32,64,128]{2,1,0:T(8,128)(2,1)S(1)} %collective-permute-done.8.refs_7_), channel_id=1, source_target_pairs={{0,16},{1,9},{2,18},{3,11},{4,20},{5,13},{6,22},{7,15},{8,24},{9,1... | collective-permute-start | bytes 1572872 | tf_op jit(solution)/shard_map/ppermute | solution.py:463
  18.2 1.3 collective-permute-start.3
  19.5 4.4 %collective-permute-start.4 = (f32[136,128]{1,0:T(8,128)S(1)}, f32[136,128]{1,0:T(8,128)S(1)}, u32[]{:S(2)}, u32[]{:S(2)}) collective-permute-start(f32[136,128]{1,0:T(8,128)S(1)} %plus.3.a_ref), channel_id=1, source_target_pairs={{0,2},{1,3},{2,0},{3,1},{4,6},{5,7},{6,4},{7,5},{8,10},{9,11},{10,... | collective-permute-start | bytes 208904 | tf_op jit(solution)/shard_map/ppermute | solution.py:481
  23.9 5.4 %collective-permute-start.5 = (f32[136,128]{1,0:T(8,128)S(1)}, f32[136,128]{1,0:T(8,128)S(1)}, u32[]{:S(2)}, u32[]{:S(2)}) collective-permute-start(f32[136,128]{1,0:T(8,128)S(1)} %plus.4.a_ref), channel_id=1, source_target_pairs={{0,4},{1,5},{2,6},{3,7},{4,0},{5,1},{6,2},{7,3},{8,12},{9,13},{10,... | collective-permute-start | bytes 208904 | tf_op jit(solution)/shard_map/ppermute | solution.py:481
  29.3 1.3 collective-permute-start.6
  42.0 40.1 %copy-start = (bf16[160,128,128]{2,1,0:T(8,128)(2,1)}, bf16[160,128,128]{2,1,0:T(8,128)(2,1)S(1)}, u32[]{:S(2)}) copy-start(bf16[160,128,128]{2,1,0:T(8,128)(2,1)S(1)} %get-tuple-element.51.refs_0_.tiles_ref) | copy-start | bytes 15728644
  42.0 4.6 %collective-permute-start.12 = (bf16[64,64,128]{2,1,0:T(8,128)(2,1)S(1)}, bf16[64,64,128]{2,1,0:T(8,128)(2,1)S(1)}, u32[]{:S(2)}, u32[]{:S(2)}) collective-permute-start(bf16[64,64,128]{2,1,0:T(8,128)(2,1)S(1)} %get-tuple-element.46), channel_id=1, source_target_pairs={{1,0},{6,7},{9,8},{14,15},{17,16},{22,23},{25,24},{30,31}} | collective-permute-start | bytes 3145736 | tf_op jit(solution)/shard_map/ppermute | solution.py:466
  43.3 14.7 %collective-permute-start.11 = (bf16[64,64,128]{2,1,0:T(8,128)(2,1)S(1)}, bf16[64,64,128]{2,1,0:T(8,128)(2,1)S(1)}, u32[]{:S(2)}, u32[]{:S(2)}) collective-permute-start(bf16[64,64,128]{2,1,0:T(8,128)(2,1)S(1)} %get-tuple-element.44), channel_id=1, source_target_pairs={{1,0},{3,2},{4,5},{6,7},{9,8},{11,10},{12,13},{14,15},{17,16},{19,... | collective-permute-start | bytes 3145736 | tf_op jit(solution)/shard_map/ppermute | solution.py:466
  46.9 11.2 %collective-permute-start.13 = (bf16[64,32,128]{2,1,0:T(8,128)(2,1)S(1)}, bf16[64,32,128]{2,1,0:T(8,128)(2,1)S(1)}, u32[]{:S(2)}, u32[]{:S(2)}) collective-permute-start(bf16[64,32,128]{2,1,0:T(8,128)(2,1)S(1)} %add_up.27.refs_2_.refs_0_), channel_id=1, source_target_pairs={{0,2},{7,5},{2,4},{5,3},{4,6},{3,1},{8,10},{15,13},{10,12},{13,11}... | collective-permute-start | bytes 1572872 | tf_op jit(solution)/shard_map/ppermute | solution.py:475
  48.2 19.6 %collective-permute-start.10 = (bf16[64,64,128]{2,1,0:T(8,128)(2,1)S(1)}, bf16[64,64,128]{2,1,0:T(8,128)(2,1)S(1)}, u32[]{:S(2)}, u32[]{:S(2)}) collective-permute-start(bf16[64,64,128]{2,1,0:T(8,128)(2,1)S(1)} %get-tuple-element.42), channel_id=1, source_target_pairs={{1,0},{2,3},{3,2},{4,5},{5,4},{6,7},{9,8},{10,11},{11,10},{12,13},... | collective-permute-start | bytes 3145736 | tf_op jit(solution)/shard_map/ppermute | solution.py:466
  49.8 13.7 %collective-permute-start.15 = (bf16[64,32,128]{2,1,0:T(8,128)(2,1)S(1)}, bf16[64,32,128]{2,1,0:T(8,128)(2,1)S(1)}, u32[]{:S(2)}, u32[]{:S(2)}) collective-permute-start(bf16[64,32,128]{2,1,0:T(8,128)(2,1)S(1)} %add_up.28.refs_3_.refs_2_), channel_id=1, source_target_pairs={{0,2},{7,5},{2,4},{5,3},{4,6},{3,1},{8,10},{15,13},{10,12},{13,11}... | collective-permute-start | bytes 1572872 | tf_op jit(solution)/shard_map/ppermute | solution.py:475
  56.4 10.7 %collective-permute-start.23 = (bf16[32,64,128]{2,1,0:T(8,128)(2,1)S(1)}, bf16[32,64,128]{2,1,0:T(8,128)(2,1)S(1)}, u32[]{:S(2)}, u32[]{:S(2)}) collective-permute-start(bf16[32,64,128]{2,1,0:T(8,128)(2,1)S(1)} %turn_panel.3.refs_1_), channel_id=1, source_target_pairs={{0,8},{1,17},{2,10},{3,19},{4,12},{5,21},{6,14},{7,23},{8,0},{9,25... | collective-permute-start | bytes 1572872 | tf_op jit(solution)/shard_map/ppermute | solution.py:463
  58.5 11.8 %collective-permute-start.14 = (bf16[64,32,128]{2,1,0:T(8,128)(2,1)S(1)}, bf16[64,32,128]{2,1,0:T(8,128)(2,1)S(1)}, u32[]{:S(2)}, u32[]{:S(2)}) collective-permute-start(bf16[64,32,128]{2,1,0:T(8,128)(2,1)S(1)} %add_up.29.refs_3_), channel_id=1, source_target_pairs={{0,2},{7,5},{2,4},{5,3},{4,6},{3,1},{8,10},{15,13},{10,12},{13,11}... | collective-permute-start | bytes 1572872 | tf_op jit(solution)/shard_map/ppermute | solution.py:475
  64.0 11.8 %collective-permute-start.19 = (bf16[64,32,128]{2,1,0:T(8,128)(2,1)S(1)}, bf16[64,32,128]{2,1,0:T(8,128)(2,1)S(1)}, u32[]{:S(2)}, u32[]{:S(2)}) collective-permute-start(bf16[64,32,128]{2,1,0:T(8,128)(2,1)S(1)} %add_up.30.refs_3_.refs_1_), channel_id=1, source_target_pairs={{0,2},{7,5},{2,4},{5,3},{4,6},{3,1},{8,10},{15,13},{10,12},{13,11}... | collective-permute-start | bytes 1572872 | tf_op jit(solution)/shard_map/ppermute | solution.py:475
  67.1 26.3 %collective-permute-start.18 = (bf16[64,64,128]{2,1,0:T(8,128)(2,1)S(1)}, bf16[64,64,128]{2,1,0:T(8,128)(2,1)S(1)}, u32[]{:S(2)}, u32[]{:S(2)}) collective-permute-start(bf16[64,64,128]{2,1,0:T(8,128)(2,1)S(1)} %get-tuple-element.47.refs_0_), channel_id=1, source_target_pairs={{0,1},{1,0},{2,3},{3,2},{4,5},{5,4},{6,7},{7,6},{8,9},{9,8},{10,11... | collective-permute-start | bytes 3145736 | tf_op jit(solution)/shard_map/ppermute | solution.py:466
  67.2 13.5 %collective-permute-start.22 = (bf16[32,64,128]{2,1,0:T(8,128)(2,1)S(1)}, bf16[32,64,128]{2,1,0:T(8,128)(2,1)S(1)}, u32[]{:S(2)}, u32[]{:S(2)}) collective-permute-start(bf16[32,64,128]{2,1,0:T(8,128)(2,1)S(1)} %turn_panel.3.refs_1_), channel_id=1, source_target_pairs={{0,16},{1,9},{2,18},{3,11},{4,20},{5,13},{6,22},{7,15},{8,24},{9,1... | collective-permute-start | bytes 1572872 | tf_op jit(solution)/shard_map/ppermute | solution.py:463
  67.8 14.3 %collective-permute-start.24 = (bf16[32,64,128]{2,1,0:T(8,128)(2,1)S(1)}, bf16[32,64,128]{2,1,0:T(8,128)(2,1)S(1)}, u32[]{:S(2)}, u32[]{:S(2)}) collective-permute-start(bf16[32,64,128]{2,1,0:T(8,128)(2,1)S(1)} %add_up.36), channel_id=1, source_target_pairs={{0,16},{1,9},{2,18},{3,11},{4,20},{5,13},{6,22},{7,15},{8,24},{9,1... | collective-permute-start | bytes 1572872 | tf_op jit(solution)/shard_map/ppermute | solution.py:463
  70.7 19.2 %collective-permute-start.16 = (bf16[64,32,128]{2,1,0:T(8,128)(2,1)S(1)}, bf16[64,32,128]{2,1,0:T(8,128)(2,1)S(1)}, u32[]{:S(2)}, u32[]{:S(2)}) collective-permute-start(bf16[64,32,128]{2,1,0:T(8,128)(2,1)S(1)} %add_up.31.refs_3_), channel_id=1, source_target_pairs={{0,2},{7,5},{2,4},{5,3},{4,6},{3,1},{8,10},{15,13},{10,12},{13,11}... | collective-permute-start | bytes 1572872 | tf_op jit(solution)/shard_map/ppermute | solution.py:475
  76.3 15.0 %collective-permute-start.20 = (bf16[64,32,128]{2,1,0:T(8,128)(2,1)S(1)}, bf16[64,32,128]{2,1,0:T(8,128)(2,1)S(1)}, u32[]{:S(2)}, u32[]{:S(2)}) collective-permute-start(bf16[64,32,128]{2,1,0:T(8,128)(2,1)S(1)} %add_up.33.refs_3_.refs_5_), channel_id=1, source_target_pairs={{0,2},{7,5},{2,4},{5,3},{4,6},{3,1},{8,10},{15,13},{10,12},{13,11}... | collective-permute-start | bytes 1572872 | tf_op jit(solution)/shard_map/ppermute | solution.py:475
  89.9 3.8 %collective-permute-start.17 = (bf16[64,32,128]{2,1,0:T(8,128)(2,1)S(1)}, bf16[64,32,128]{2,1,0:T(8,128)(2,1)S(1)}, u32[]{:S(2)}, u32[]{:S(2)}) collective-permute-start(bf16[64,32,128]{2,1,0:T(8,128)(2,1)S(1)} %collective-permute-done.16.refs_0_), channel_id=1, source_target_pairs={{0,1},{1,0},{2,3},{3,2},{4,5},{5,4},{6,7},{7,6},{8,9},{9,8},{10,11... | collective-permute-start | bytes 1572872 | tf_op jit(solution)/shard_map/ppermute | solution.py:466
  90.0 14.9 %collective-permute-start.27 = (bf16[64,64,128]{2,1,0:T(8,128)(2,1)}, bf16[64,64,128]{2,1,0:T(8,128)(2,1)}, u32[]{:S(2)}, u32[]{:S(2)}) collective-permute-start(bf16[64,64,128]{2,1,0:T(8,128)(2,1)} %get-tuple-element.57), channel_id=1, source_target_pairs={{1,0},{6,7},{9,8},{14,15},{17,16},{22,23},{25,24},{30,31}} | collective-permute-start | bytes 3145736 | tf_op jit(solution)/shard_map/ppermute | solution.py:466
  91.3 8.9 %collective-permute-start.21 = (bf16[64,32,128]{2,1,0:T(8,128)(2,1)S(1)}, bf16[64,32,128]{2,1,0:T(8,128)(2,1)S(1)}, u32[]{:S(2)}, u32[]{:S(2)}) collective-permute-start(bf16[64,32,128]{2,1,0:T(8,128)(2,1)S(1)} %collective-permute-done.20.refs_0_), channel_id=1, source_target_pairs={{0,1},{1,0},{2,3},{3,2},{4,5},{5,4},{6,7},{7,6},{8,9},{9,8},{10,11... | collective-permute-start | bytes 1572872 | tf_op jit(solution)/shard_map/ppermute | solution.py:466
  95.0 10.1 %collective-permute-start.28 = (bf16[64,32,128]{2,1,0:T(8,128)(2,1)}, bf16[64,32,128]{2,1,0:T(8,128)(2,1)}, u32[]{:S(2)}, u32[]{:S(2)}) collective-permute-start(bf16[64,32,128]{2,1,0:T(8,128)(2,1)} %get-tuple-element.49.refs_3_.refs_6_), channel_id=1, source_target_pairs={{0,2},{7,5},{2,4},{5,3},{4,6},{3,1},{8,10},{15,13},{10,12},{13,11}... | collective-permute-start | bytes 1572872 | tf_op jit(solution)/shard_map/ppermute | solution.py:475
  98.9 19.9 %collective-permute-start.26 = (bf16[64,64,128]{2,1,0:T(8,128)(2,1)}, bf16[64,64,128]{2,1,0:T(8,128)(2,1)S(1)}, u32[]{:S(2)}, u32[]{:S(2)}) collective-permute-start(bf16[64,64,128]{2,1,0:T(8,128)(2,1)} %get-tuple-element.55), channel_id=1, source_target_pairs={{1,0},{3,2},{4,5},{6,7},{9,8},{11,10},{12,13},{14,15},{17,16},{19,... | collective-permute-start | bytes 3145736 | tf_op jit(solution)/shard_map/ppermute | solution.py:466
  101.5 12.0 %collective-permute-start.30 = (bf16[64,32,128]{2,1,0:T(8,128)(2,1)}, bf16[64,32,128]{2,1,0:T(8,128)(2,1)}, u32[]{:S(2)}, u32[]{:S(2)}) collective-permute-start(bf16[64,32,128]{2,1,0:T(8,128)(2,1)} %get-tuple-element.58.refs_3_.refs_7_), channel_id=1, source_target_pairs={{0,2},{7,5},{2,4},{5,3},{4,6},{3,1},{8,10},{15,13},{10,12},{13,11}... | collective-permute-start | bytes 1572872 | tf_op jit(solution)/shard_map/ppermute | solution.py:475
  107.9 11.0 %collective-permute-start.29 = (bf16[64,32,128]{2,1,0:T(8,128)(2,1)S(1)}, bf16[64,32,128]{2,1,0:T(8,128)(2,1)S(1)}, u32[]{:S(2)}, u32[]{:S(2)}) collective-permute-start(bf16[64,32,128]{2,1,0:T(8,128)(2,1)S(1)} %add_up.37.refs_3_), channel_id=1, source_target_pairs={{0,2},{7,5},{2,4},{5,3},{4,6},{3,1},{8,10},{15,13},{10,12},{13,11}... | collective-permute-start | bytes 1572872 | tf_op jit(solution)/shard_map/ppermute | solution.py:475
  112.2 18.0 %collective-permute-start.25 = (bf16[64,64,128]{2,1,0:T(8,128)(2,1)S(1)}, bf16[64,64,128]{2,1,0:T(8,128)(2,1)S(1)}, u32[]{:S(2)}, u32[]{:S(2)}) collective-permute-start(bf16[64,64,128]{2,1,0:T(8,128)(2,1)S(1)} %copy-done.19), channel_id=1, source_target_pairs={{1,0},{2,3},{3,2},{4,5},{5,4},{6,7},{9,8},{10,11},{11,10},{12,13},... | collective-permute-start | bytes 3145736 | tf_op jit(solution)/shard_map/ppermute | solution.py:466
  114.9 10.5 %collective-permute-start.32 = (bf16[64,32,128]{2,1,0:T(8,128)(2,1)S(1)}, bf16[64,32,128]{2,1,0:T(8,128)(2,1)S(1)}, u32[]{:S(2)}, u32[]{:S(2)}) collective-permute-start(bf16[64,32,128]{2,1,0:T(8,128)(2,1)S(1)} %add_up.38.refs_4_.refs_2_), channel_id=1, source_target_pairs={{0,2},{7,5},{2,4},{5,3},{4,6},{3,1},{8,10},{15,13},{10,12},{13,11}... | collective-permute-start | bytes 1572872 | tf_op jit(solution)/shard_map/ppermute | solution.py:475
  119.1 11.9 %collective-permute-start.31 = (bf16[64,32,128]{2,1,0:T(8,128)(2,1)S(1)}, bf16[64,32,128]{2,1,0:T(8,128)(2,1)S(1)}, u32[]{:S(2)}, u32[]{:S(2)}) collective-permute-start(bf16[64,32,128]{2,1,0:T(8,128)(2,1)S(1)} %add_up.39.refs_4_), channel_id=1, source_target_pairs={{0,2},{7,5},{2,4},{5,3},{4,6},{3,1},{8,10},{15,13},{10,12},{13,11}... | collective-permute-start | bytes 1572872 | tf_op jit(solution)/shard_map/ppermute | solution.py:475
  125.7 11.1 %collective-permute-start.36 = (bf16[64,32,128]{2,1,0:T(8,128)(2,1)S(1)}, bf16[64,32,128]{2,1,0:T(8,128)(2,1)S(1)}, u32[]{:S(2)}, u32[]{:S(2)}) collective-permute-start(bf16[64,32,128]{2,1,0:T(8,128)(2,1)S(1)} %add_up.40.refs_3_), channel_id=1, source_target_pairs={{0,2},{7,5},{2,4},{5,3},{4,6},{3,1},{8,10},{15,13},{10,12},{13,11}... | collective-permute-start | bytes 1572872 | tf_op jit(solution)/shard_map/ppermute | solution.py:475
  130.2 18.5 %collective-permute-start.35 = (bf16[64,64,128]{2,1,0:T(8,128)(2,1)S(1)}, bf16[64,64,128]{2,1,0:T(8,128)(2,1)S(1)}, u32[]{:S(2)}, u32[]{:S(2)}) collective-permute-start(bf16[64,64,128]{2,1,0:T(8,128)(2,1)S(1)} %copy-done.15), channel_id=1, source_target_pairs={{0,1},{1,0},{2,3},{3,2},{4,5},{5,4},{6,7},{7,6},{8,9},{9,8},{10,11... | collective-permute-start | bytes 3145736 | tf_op jit(solution)/shard_map/ppermute | solution.py:466
  131.5 11.1 %collective-permute-start.33 = (bf16[64,32,128]{2,1,0:T(8,128)(2,1)S(1)}, bf16[64,32,128]{2,1,0:T(8,128)(2,1)S(1)}, u32[]{:S(2)}, u32[]{:S(2)}) collective-permute-start(bf16[64,32,128]{2,1,0:T(8,128)(2,1)S(1)} %add_up.41.refs_3_), channel_id=1, source_target_pairs={{0,2},{7,5},{2,4},{5,3},{4,6},{3,1},{8,10},{15,13},{10,12},{13,11}... | collective-permute-start | bytes 1572872 | tf_op jit(solution)/shard_map/ppermute | solution.py:475
  137.3 11.3 %collective-permute-start.37 = (bf16[64,32,128]{2,1,0:T(8,128)(2,1)S(1)}, bf16[64,32,128]{2,1,0:T(8,128)(2,1)S(1)}, u32[]{:S(2)}, u32[]{:S(2)}) collective-permute-start(bf16[64,32,128]{2,1,0:T(8,128)(2,1)S(1)} %add_up.43.refs_3_), channel_id=1, source_target_pairs={{0,2},{7,5},{2,4},{5,3},{4,6},{3,1},{8,10},{15,13},{10,12},{13,11}... | collective-permute-start | bytes 1572872 | tf_op jit(solution)/shard_map/ppermute | solution.py:475
  142.0 7.4 %collective-permute-start.42 = (bf16[64,32,128]{2,1,0:T(8,128)(2,1)}, bf16[64,32,128]{2,1,0:T(8,128)(2,1)S(1)}, u32[]{:S(2)}, u32[]{:S(2)}) collective-permute-start(bf16[64,32,128]{2,1,0:T(8,128)(2,1)} %collective-permute-done.30.refs_2_.refs_5_), channel_id=1, source_target_pairs={{0,1},{1,0},{2,3},{3,2},{4,5},{5,4},{6,7},{7,6},{8,9},{9,8},{10,11... | collective-permute-start | bytes 1572872 | tf_op jit(solution)/shard_map/ppermute | solution.py:466
  142.0 7.5 %collective-permute-start.41 = (bf16[64,32,128]{2,1,0:T(8,128)(2,1)}, bf16[64,32,128]{2,1,0:T(8,128)(2,1)S(1)}, u32[]{:S(2)}, u32[]{:S(2)}) collective-permute-start(bf16[64,32,128]{2,1,0:T(8,128)(2,1)} %collective-permute-done.28.refs_2_.refs_4_), channel_id=1, source_target_pairs={{0,1},{1,0},{2,3},{3,2},{4,5},{5,4},{6,7},{7,6},{8,9},{9,8},{10,11... | collective-permute-start | bytes 1572872 | tf_op jit(solution)/shard_map/ppermute | solution.py:466
  142.6 7.3 %collective-permute-start.34 = (bf16[64,32,128]{2,1,0:T(8,128)(2,1)S(1)}, bf16[64,32,128]{2,1,0:T(8,128)(2,1)S(1)}, u32[]{:S(2)}, u32[]{:S(2)}) collective-permute-start(bf16[64,32,128]{2,1,0:T(8,128)(2,1)S(1)} %collective-permute-done.33.refs_0_), channel_id=1, source_target_pairs={{0,1},{1,0},{2,3},{3,2},{4,5},{5,4},{6,7},{7,6},{8,9},{9,8},{10,11... | collective-permute-start | bytes 1572872 | tf_op jit(solution)/shard_map/ppermute | solution.py:466
  148.6 2.6 %collective-permute-start.38 = (bf16[64,32,128]{2,1,0:T(8,128)(2,1)S(1)}, bf16[64,32,128]{2,1,0:T(8,128)(2,1)S(1)}, u32[]{:S(2)}, u32[]{:S(2)}) collective-permute-start(bf16[64,32,128]{2,1,0:T(8,128)(2,1)S(1)} %collective-permute-done.37.refs_0_), channel_id=1, source_target_pairs={{0,1},{1,0},{2,3},{3,2},{4,5},{5,4},{6,7},{7,6},{8,9},{9,8},{10,11... | collective-permute-start | bytes 1572872 | tf_op jit(solution)/shard_map/ppermute | solution.py:466
  148.8 8.0 %collective-permute-start.44 = (bf16[64,32,128]{2,1,0:T(8,128)(2,1)S(1)}, bf16[64,32,128]{2,1,0:T(8,128)(2,1)S(1)}, u32[]{:S(2)}, u32[]{:S(2)}) collective-permute-start(bf16[64,32,128]{2,1,0:T(8,128)(2,1)S(1)} %collective-permute-done.32.refs_2_.refs_3_), channel_id=1, source_target_pairs={{0,1},{1,0},{2,3},{3,2},{4,5},{5,4},{6,7},{7,6},{8,9},{9,8},{10,11... | collective-permute-start | bytes 1572872 | tf_op jit(solution)/shard_map/ppermute | solution.py:466
  149.4 10.3 %collective-permute-start.43 = (bf16[64,32,128]{2,1,0:T(8,128)(2,1)S(1)}, bf16[64,32,128]{2,1,0:T(8,128)(2,1)S(1)}, u32[]{:S(2)}, u32[]{:S(2)}) collective-permute-start(bf16[64,32,128]{2,1,0:T(8,128)(2,1)S(1)} %collective-permute-done.29.refs_2_.refs_3_), channel_id=1, source_target_pairs={{0,1},{1,0},{2,3},{3,2},{4,5},{5,4},{6,7},{7,6},{8,9},{9,8},{10,11... | collective-permute-start | bytes 1572872 | tf_op jit(solution)/shard_map/ppermute | solution.py:466
  149.5 10.3 %collective-permute-start.46 = (bf16[64,32,128]{2,1,0:T(8,128)(2,1)S(1)}, bf16[64,32,128]{2,1,0:T(8,128)(2,1)S(1)}, u32[]{:S(2)}, u32[]{:S(2)}) collective-permute-start(bf16[64,32,128]{2,1,0:T(8,128)(2,1)S(1)} %collective-permute-done.36.refs_2_.refs_1_), channel_id=1, source_target_pairs={{0,1},{1,0},{2,3},{3,2},{4,5},{5,4},{6,7},{7,6},{8,9},{9,8},{10,11... | collective-permute-start | bytes 1572872 | tf_op jit(solution)/shard_map/ppermute | solution.py:466
  149.9 9.8 %collective-permute-start.45 = (bf16[64,32,128]{2,1,0:T(8,128)(2,1)S(1)}, bf16[64,32,128]{2,1,0:T(8,128)(2,1)S(1)}, u32[]{:S(2)}, u32[]{:S(2)}) collective-permute-start(bf16[64,32,128]{2,1,0:T(8,128)(2,1)S(1)} %collective-permute-done.31.refs_2_.refs_0_), channel_id=1, source_target_pairs={{0,1},{1,0},{2,3},{3,2},{4,5},{5,4},{6,7},{7,6},{8,9},{9,8},{10,11... | collective-permute-start | bytes 1572872 | tf_op jit(solution)/shard_map/ppermute | solution.py:466
  151.3 15.1 %collective-permute-start.40 = (bf16[64,32,128]{2,1,0:T(8,128)(2,1)S(1)}, bf16[64,32,128]{2,1,0:T(8,128)(2,1)S(1)}, u32[]{:S(2)}, u32[]{:S(2)}) collective-permute-start(bf16[64,32,128]{2,1,0:T(8,128)(2,1)S(1)} %get-tuple-element.61.refs_3_), channel_id=1, source_target_pairs={{0,2},{7,5},{2,4},{5,3},{4,6},{3,1},{8,10},{15,13},{10,12},{13,11}... | collective-permute-start | bytes 1572872 | tf_op jit(solution)/shard_map/ppermute | solution.py:475
  156.8 12.4 %collective-permute-start.39 = (bf16[64,32,128]{2,1,0:T(8,128)(2,1)S(1)}, bf16[64,32,128]{2,1,0:T(8,128)(2,1)S(1)}, u32[]{:S(2)}, u32[]{:S(2)}) collective-permute-start(bf16[64,32,128]{2,1,0:T(8,128)(2,1)S(1)} %get-tuple-element.63.refs_14_.refs_1_.refs_3_), channel_id=1, source_target_pairs={{0,2},{7,5},{2,4},{5,3},{4,6},{3,1},{8,10},{15,13},{10,12},{13,11}... | collective-permute-start | bytes 1572872 | tf_op jit(solution)/shard_map/ppermute | solution.py:475
  164.8 17.8 %collective-permute-start.49 = (bf16[64,64,128]{2,1,0:T(8,128)(2,1)S(1)}, bf16[64,64,128]{2,1,0:T(8,128)(2,1)S(1)}, u32[]{:S(2)}, u32[]{:S(2)}) collective-permute-start(bf16[64,64,128]{2,1,0:T(8,128)(2,1)S(1)} %get-tuple-element.64.refs_2_), channel_id=1, source_target_pairs={{0,8},{1,17},{2,10},{3,19},{4,12},{5,21},{6,14},{7,23},{8,0},{9,25... | collective-permute-start | bytes 3145736 | tf_op jit(solution)/shard_map/ppermute | solution.py:463
  166.5 9.4 %collective-permute-start.48 = (bf16[64,32,128]{2,1,0:T(8,128)(2,1)S(1)}, bf16[64,32,128]{2,1,0:T(8,128)(2,1)S(1)}, u32[]{:S(2)}, u32[]{:S(2)}) collective-permute-start(bf16[64,32,128]{2,1,0:T(8,128)(2,1)S(1)} %add_up.46.refs_1_), channel_id=1, source_target_pairs={{0,2},{7,5},{2,4},{5,3},{4,6},{3,1},{8,10},{15,13},{10,12},{13,11}... | collective-permute-start | bytes 1572872 | tf_op jit(solution)/shard_map/ppermute | solution.py:475
  176.0 11.1 %collective-permute-start.51 = (bf16[64,32,128]{2,1,0:T(8,128)(2,1)S(1)}, bf16[64,32,128]{2,1,0:T(8,128)(2,1)S(1)}, u32[]{:S(2)}, u32[]{:S(2)}) collective-permute-start(bf16[64,32,128]{2,1,0:T(8,128)(2,1)S(1)} %add_up.48.refs_1_), channel_id=1, source_target_pairs={{0,2},{7,5},{2,4},{5,3},{4,6},{3,1},{8,10},{15,13},{10,12},{13,11}... | collective-permute-start | bytes 1572872 | tf_op jit(solution)/shard_map/ppermute | solution.py:475
  180.4 12.3 %collective-permute-start.47 = (bf16[64,32,128]{2,1,0:T(8,128)(2,1)S(1)}, bf16[64,32,128]{2,1,0:T(8,128)(2,1)S(1)}, u32[]{:S(2)}, u32[]{:S(2)}) collective-permute-start(bf16[64,32,128]{2,1,0:T(8,128)(2,1)S(1)} %add_up.47.refs_1_), channel_id=1, source_target_pairs={{0,2},{7,5},{2,4},{5,3},{4,6},{3,1},{8,10},{15,13},{10,12},{13,11}... | collective-permute-start | bytes 1572872 | tf_op jit(solution)/shard_map/ppermute | solution.py:475
  182.5 14.7 %collective-permute-start.52 = (bf16[64,32,128]{2,1,0:T(8,128)(2,1)S(1)}, bf16[64,32,128]{2,1,0:T(8,128)(2,1)S(1)}, u32[]{:S(2)}, u32[]{:S(2)}) collective-permute-start(bf16[64,32,128]{2,1,0:T(8,128)(2,1)S(1)} %collective-permute-done.40.refs_0_.refs_2_), channel_id=1, source_target_pairs={{0,1},{1,0},{2,3},{3,2},{4,5},{5,4},{6,7},{7,6},{8,9},{9,8},{10,11... | collective-permute-start | bytes 1572872 | tf_op jit(solution)/shard_map/ppermute | solution.py:466
  182.7 14.6 %collective-permute-start.55 = (bf16[32,64,128]{2,1,0:T(8,128)(2,1)S(1)}, bf16[32,64,128]{2,1,0:T(8,128)(2,1)S(1)}, u32[]{:S(2)}, u32[]{:S(2)}) collective-permute-start(bf16[32,64,128]{2,1,0:T(8,128)(2,1)S(1)} %add_up.50), channel_id=1, source_target_pairs={{0,16},{1,9},{2,18},{3,11},{4,20},{5,13},{6,22},{7,15},{8,24},{9,1... | collective-permute-start | bytes 1572872 | tf_op jit(solution)/shard_map/ppermute | solution.py:463
  183.2 14.6 %collective-permute-start.53 = (bf16[64,32,128]{2,1,0:T(8,128)(2,1)S(1)}, bf16[64,32,128]{2,1,0:T(8,128)(2,1)S(1)}, u32[]{:S(2)}, u32[]{:S(2)}) collective-permute-start(bf16[64,32,128]{2,1,0:T(8,128)(2,1)S(1)} %collective-permute-done.48.refs_0_.refs_1_), channel_id=1, source_target_pairs={{0,1},{1,0},{2,3},{3,2},{4,5},{5,4},{6,7},{7,6},{8,9},{9,8},{10,11... | collective-permute-start | bytes 1572872 | tf_op jit(solution)/shard_map/ppermute | solution.py:466
  187.1 10.7 %collective-permute-start.54 = (bf16[64,32,128]{2,1,0:T(8,128)(2,1)S(1)}, bf16[64,32,128]{2,1,0:T(8,128)(2,1)S(1)}, u32[]{:S(2)}, u32[]{:S(2)}) collective-permute-start(bf16[64,32,128]{2,1,0:T(8,128)(2,1)S(1)} %collective-permute-done.51.refs_0_), channel_id=1, source_target_pairs={{0,1},{1,0},{2,3},{3,2},{4,5},{5,4},{6,7},{7,6},{8,9},{9,8},{10,11... | collective-permute-start | bytes 1572872 | tf_op jit(solution)/shard_map/ppermute | solution.py:466
  192.8 11.1 %collective-permute-start.50 = (bf16[64,32,128]{2,1,0:T(8,128)(2,1)S(1)}, bf16[64,32,128]{2,1,0:T(8,128)(2,1)S(1)}, u32[]{:S(2)}, u32[]{:S(2)}) collective-permute-start(bf16[64,32,128]{2,1,0:T(8,128)(2,1)S(1)} %add_up.49), channel_id=1, source_target_pairs={{0,2},{7,5},{2,4},{5,3},{4,6},{3,1},{8,10},{15,13},{10,12},{13,11}... | collective-permute-start | bytes 1572872 | tf_op jit(solution)/shard_map/ppermute | solution.py:475
  197.2 7.4 %collective-permute-start.56 = (bf16[64,32,128]{2,1,0:T(8,128)(2,1)S(1)}, bf16[64,32,128]{2,1,0:T(8,128)(2,1)S(1)}, u32[]{:S(2)}, u32[]{:S(2)}) collective-permute-start(bf16[64,32,128]{2,1,0:T(8,128)(2,1)S(1)} %collective-permute-done.39.refs_0_.refs_2_), channel_id=1, source_target_pairs={{0,1},{1,0},{2,3},{3,2},{4,5},{5,4},{6,7},{7,6},{8,9},{9,8},{10,11... | collective-permute-start | bytes 1572872 | tf_op jit(solution)/shard_map/ppermute | solution.py:466
  197.3 7.3 %collective-permute-start.57 = (bf16[64,32,128]{2,1,0:T(8,128)(2,1)S(1)}, bf16[64,32,128]{2,1,0:T(8,128)(2,1)S(1)}, u32[]{:S(2)}, u32[]{:S(2)}) collective-permute-start(bf16[64,32,128]{2,1,0:T(8,128)(2,1)S(1)} %collective-permute-done.47.refs_0_.refs_1_), channel_id=1, source_target_pairs={{0,1},{1,0},{2,3},{3,2},{4,5},{5,4},{6,7},{7,6},{8,9},{9,8},{10,11... | collective-permute-start | bytes 1572872 | tf_op jit(solution)/shard_map/ppermute | solution.py:466
  204.0 2.0 collective-permute-start.58
  204.0 9.2 %collective-permute-start.59 = (bf16[64,32,128]{2,1,0:T(8,128)(2,1)S(1)}, bf16[64,32,128]{2,1,0:T(8,128)(2,1)S(1)}, u32[]{:S(2)}, u32[]{:S(2)}) collective-permute-start(bf16[64,32,128]{2,1,0:T(8,128)(2,1)S(1)} %get-tuple-element.66.refs_1_), channel_id=1, source_target_pairs={{0,8},{1,17},{2,10},{3,19},{4,12},{5,21},{6,14},{7,23},{8,0},{9,25... | collective-permute-start | bytes 1572872 | tf_op jit(solution)/shard_map/ppermute | solution.py:463
  209.7 11.6 %collective-permute-start.61 = (bf16[64,32,128]{2,1,0:T(8,128)(2,1)S(1)}, bf16[64,32,128]{2,1,0:T(8,128)(2,1)S(1)}, u32[]{:S(2)}, u32[]{:S(2)}) collective-permute-start(bf16[64,32,128]{2,1,0:T(8,128)(2,1)S(1)} %get-tuple-element.67.refs_4_), channel_id=1, source_target_pairs={{0,8},{1,17},{2,10},{3,19},{4,12},{5,21},{6,14},{7,23},{8,0},{9,25... | collective-permute-start | bytes 1572872 | tf_op jit(solution)/shard_map/ppermute | solution.py:463
  214.1 14.0 %collective-permute-start.60 = (bf16[32,32,128]{2,1,0:T(8,128)(2,1)}, bf16[32,32,128]{2,1,0:T(8,128)(2,1)S(1)}, u32[]{:S(2)}, u32[]{:S(2)}) collective-permute-start(bf16[32,32,128]{2,1,0:T(8,128)(2,1)} %add_up.52), channel_id=1, source_target_pairs={{0,16},{1,9},{2,18},{3,11},{4,20},{5,13},{6,22},{7,15},{8,24},{9,1... | collective-permute-start | bytes 786440 | tf_op jit(solution)/shard_map/ppermute | solution.py:463
  222.2 6.7 %collective-permute-start.62 = (bf16[32,32,128]{2,1,0:T(8,128)(2,1)}, bf16[32,32,128]{2,1,0:T(8,128)(2,1)}, u32[]{:S(2)}, u32[]{:S(2)}) collective-permute-start(bf16[32,32,128]{2,1,0:T(8,128)(2,1)} %add_up.53), channel_id=1, source_target_pairs={{0,16},{1,9},{2,18},{3,11},{4,20},{5,13},{6,22},{7,15},{8,24},{9,1... | collective-permute-start | bytes 786440 | tf_op jit(solution)/shard_map/ppermute | solution.py:463
  (24 other events, 204.3 us)

commit v5 on v4

--- a/solution.py
+++ b/solution.py
@@ -46,7 +46,7 @@
 
 def count_sums(counts, rows, cols, band_rows, band_cols, deps):
     slots, tile, _ = counts.shape
-    pieces = math.gcd(slots, 10)
+    pieces = math.gcd(slots, 5)
     piece = slots // pieces
 
     def kernel(counts_ref, rows_hbm, cols_hbm, *refs):
@@ -81,7 +81,7 @@
         def one_piece(at, carry):
             arriving(at).wait()
             over_tiles(
-                piece, 16, lambda n: sums(at * piece + n), lambda n, found: add(at * piece + n, found)
+                piece, 32, lambda n: sums(at * piece + n), lambda n, found: add(at * piece + n, found)
             )
             return carry
 
@@ -230,7 +230,7 @@
     slot_count = 2 * chips - 1
     n_in = len(blocks)
     chip_list = 3 * slots
-    pieces = math.gcd(slots, 10)
+    pieces = math.gcd(slots, 5)
     piece = slots // pieces
 
     def kernel(index_ref, *refs):
@@ -296,7 +296,7 @@
                 arriving(at).wait()
             over_tiles(
                 piece,
-                16,
+                32,
                 lambda n: product(at * piece + n),
                 lambda n, found: add(at * piece + n, found),
             )
@@ -389,7 +389,7 @@
         def add(n, found):
             acc[index_ref[2 * slots + n]] += found
 
-        over_tiles(slots, 16, product, add)
+        over_tiles(slots, 80, product, add)
         send[...] = acc[half:].astype(BF16)
         keep[...] = acc[:half]
 
@@ -414,7 +414,7 @@
     _, _, tile = pieces[0][0].shape
     terms = [term for piece in pieces for term in piece]
     width = sum(piece[0].shape[1] for piece in pieces)
-    step = math.gcd(blocks, 8)
+    step = math.gcd(blocks, 16)
 
     def kernel(start_ref, *refs):
         out_ref, reads = refs[-1], list(refs[: len(terms)])

time: 234 us -> 230 us (0.983)
  Pallas kernels: 61.5 us -> 54.3 us
  waiting for transfers between devices: 54.7 us -> 57.5 us
    pallas_call x3, Pallas kernels: 12.4 us -> 9.52 us  [context_products(): pl.pallas_call(kernel, in_specs=[IN_SMEM, IN_VMEM] + [ANY] * (slot_count...]
    ppermute x12, waiting for transfers between devices: 11.9 us -> 14.3 us  [row_swap(): return lax.ppermute(x, ('row', 'col'), pairs)]
    pallas_call x2, Pallas kernels: 8.07 us -> 5.7 us  [turn_back(): pl.pallas_call(kernel, grid_spec=pltpu.PrefetchScalarGridSpec(num_scalar_...]
  transfers between devices with their start and end apart: 63 -> 63, of which waited for: 23 -> 21; matrix products, arithmetic and copies ran while one was open for 0% -> 0% of each run, Pallas kernels for 20% -> 18%
where the time goes in v5:
time: 230 us; the launch traced here: 229 us
  starting transfers between devices  112 us (49%)
  waiting for transfers between devices  57.5 us (25%)
  Pallas kernels  54.3 us (24%)
  local copies, waits for them, and re-layouts  3.22 us (1%)
    ppermute x20, starting transfers between devices, along(): return lax.ppermute(x, 'col', pairs)  77.9 us
    ppermute x20, waiting for transfers between devices, along(): return lax.ppermute(x, 'col', pairs)  29.5 us
    pallas_call x2, Pallas kernels, word_products(): pl.pallas_call(kernel, in_specs=[IN_SMEM] + operand_specs + [ANY] * (n_in...  16.5 us
    pallas_call x27, Pallas kernels, add_up(): pl.pallas_call(kernel, grid_spec=pltpu.PrefetchScalarGridSpec(num_scalar_...  14.6 us
    ppermute x12, waiting for transfers between devices, row_swap(): return lax.ppermute(x, ('row', 'col'), pairs)  14.3 us
    ppermute x26, starting transfers between devices, core_swap(): lax.ppermute(x, 'col', [(i, i ^ 1) for i in range(n_col) if keep(i % 2, i...  13.7 us
    ppermute x12, starting transfers between devices, row_swap(): return lax.ppermute(x, ('row', 'col'), pairs)  12.6 us
    pallas_call x3, Pallas kernels, context_products(): pl.pallas_call(kernel, in_specs=[IN_SMEM, IN_VMEM] + [ANY] * (slot_count...  9.52 us
  transfers between devices with their start and end apart: 63, of which 21 were waited for; matrix products, arithmetic and copies ran while one was open for 0% of the time, Pallas kernels for 18%

profile of v5, /device:TPU:0, one launch (start us, length us, event | category | flops | bytes accessed | tf_op | source)
XLA Modules:
  0.0 228.7 jit_solution(704649914528548809)
XLA Ops:
  0.6 1.5 turn_panel.2.refs_0_.refs_5_
  2.2 3.0 %collective-permute-start.8 = (bf16[32,64,128]{2,1,0:T(8,128)(2,1)S(1)}, bf16[32,64,128]{2,1,0:T(8,128)(2,1)S(1)}, u32[]{:S(2)}, u32[]{:S(2)}) collective-permute-start(bf16[32,64,128]{2,1,0:T(8,128)(2,1)S(1)} %turn_panel.2.refs_0_.refs_5_), channel_id=1, source_target_pairs={{0,8},{1,17},{2,10},{3,19},{4,12},{5,21},{6,14},{7,23},{8,0},{9,25... | collective-permute-start | bytes 1572872 | tf_op jit(solution)/shard_map/ppermute | solution.py:463
  5.2 4.8 %count_sums.1 = (f32[256,128]{1,0:T(8,128)S(1)}, f32[128,128]{1,0:T(8,128)S(1)}) custom-call(s32[160,128,128]{2,1,0:T(8,128)} %bitcast.8, s32[160]{0:T(256)} %bitcast.13, s32[160]{0:T(256)} %bitcast.10, bf16[32,64,128]{2,1,0:T(8,128)(2,1)S(1)} %turn_panel.2.refs_0_.refs_5_), custom_call_target="tpu_custom_call" | custom-call | bytes 36900 | tf_op jit(solution)/shard_map/count_sums/pallas_call | solution.py:90
  10.1 2.0 collective-permute-start.1
  12.1 1.4 collective-permute-start.2
  13.6 1.5 collective-permute-start.7
  15.6 2.5 %collective-permute-done.2.refs_3_ = f32[128,128]{1,0:T(8,128)S(1)} collective-permute-done((f32[128,128]{1,0:T(8,128)S(1)}, f32[128,128]{1,0:T(8,128)S(1)}, u32[]{:S(2)}, u32[]{:S(2)}) %collective-permute-start.2) | collective-permute-done | bytes 65568 | tf_op jit(solution)/shard_map/ppermute | solution.py:478
  19.5 1.6 collective-permute-start.4
  21.1 2.7 %collective-permute-done.4.b_ref = f32[136,128]{1,0:T(8,128)S(1)} collective-permute-done((f32[136,128]{1,0:T(8,128)S(1)}, f32[136,128]{1,0:T(8,128)S(1)}, u32[]{:S(2)}, u32[]{:S(2)}) %collective-permute-start.4) | collective-permute-done | bytes 69664 | tf_op jit(solution)/shard_map/ppermute | solution.py:481
  23.9 2.7 %collective-permute-start.5 = (f32[136,128]{1,0:T(8,128)S(1)}, f32[136,128]{1,0:T(8,128)S(1)}, u32[]{:S(2)}, u32[]{:S(2)}) collective-permute-start(f32[136,128]{1,0:T(8,128)S(1)} %plus.4.a_ref), channel_id=1, source_target_pairs={{0,4},{1,5},{2,6},{3,7},{4,0},{5,1},{6,2},{7,3},{8,12},{9,13},{10,... | collective-permute-start | bytes 208904 | tf_op jit(solution)/shard_map/ppermute | solution.py:481
  26.5 2.7 %collective-permute-done.5.b_ref = f32[136,128]{1,0:T(8,128)S(1)} collective-permute-done((f32[136,128]{1,0:T(8,128)S(1)}, f32[136,128]{1,0:T(8,128)S(1)}, u32[]{:S(2)}, u32[]{:S(2)}) %collective-permute-start.5) | collective-permute-done | bytes 69664 | tf_op jit(solution)/shard_map/ppermute | solution.py:481
  31.4 9.2 %ppmi_word_products.1 = (bf16[160,128,128]{2,1,0:T(8,128)(2,1)S(1)}, bf16[64,64,128]{2,1,0:T(8,128)(2,1)S(1)}, bf16[64,64,128]{2,1,0:T(8,128)(2,1)S(1)}, bf16[64...) custom-call(s32[487]{0:T(512)S(1)} %pad_add_fusion.index_ref, ...), custom_call_target="tpu_custom_call" | custom-call | bytes 36900 | tf_op jit(solution)/shard_map/ppmi_word_products/pallas_call | solution.py:338
  40.6 1.3 collective-permute-start.12
  41.9 1.3 collective-permute-start.11
  43.2 2.0 collective-permute-done.12.refs_1_
  45.5 1.3 collective-permute-start.13
  46.8 1.3 collective-permute-start.10
  48.4 5.0 %collective-permute-start.15 = (bf16[64,32,128]{2,1,0:T(8,128)(2,1)S(1)}, bf16[64,32,128]{2,1,0:T(8,128)(2,1)S(1)}, u32[]{:S(2)}, u32[]{:S(2)}) collective-permute-start(bf16[64,32,128]{2,1,0:T(8,128)(2,1)S(1)} %add_up.28.refs_3_.refs_2_), channel_id=1, source_target_pairs={{0,2},{7,5},{2,4},{5,3},{4,6},{3,1},{8,10},{15,13},{10,12},{13,11}... | collective-permute-start | bytes 1572872 | tf_op jit(solution)/shard_map/ppermute | solution.py:475
  53.5 1.6 turn_panel.3.refs_1_
  55.0 1.7 collective-permute-start.23
  57.2 5.1 %collective-permute-start.14 = (bf16[64,32,128]{2,1,0:T(8,128)(2,1)S(1)}, bf16[64,32,128]{2,1,0:T(8,128)(2,1)S(1)}, u32[]{:S(2)}, u32[]{:S(2)}) collective-permute-start(bf16[64,32,128]{2,1,0:T(8,128)(2,1)S(1)} %add_up.29.refs_3_), channel_id=1, source_target_pairs={{0,2},{7,5},{2,4},{5,3},{4,6},{3,1},{8,10},{15,13},{10,12},{13,11}... | collective-permute-start | bytes 1572872 | tf_op jit(solution)/shard_map/ppermute | solution.py:475
  62.8 2.9 %collective-permute-start.19 = (bf16[64,32,128]{2,1,0:T(8,128)(2,1)S(1)}, bf16[64,32,128]{2,1,0:T(8,128)(2,1)S(1)}, u32[]{:S(2)}, u32[]{:S(2)}) collective-permute-start(bf16[64,32,128]{2,1,0:T(8,128)(2,1)S(1)} %add_up.30.refs_3_.refs_1_), channel_id=1, source_target_pairs={{0,2},{7,5},{2,4},{5,3},{4,6},{3,1},{8,10},{15,13},{10,12},{13,11}... | collective-permute-start | bytes 1572872 | tf_op jit(solution)/shard_map/ppermute | solution.py:475
  66.4 1.7 collective-permute-start.24
  69.4 4.4 %collective-permute-start.16 = (bf16[64,32,128]{2,1,0:T(8,128)(2,1)S(1)}, bf16[64,32,128]{2,1,0:T(8,128)(2,1)S(1)}, u32[]{:S(2)}, u32[]{:S(2)}) collective-permute-start(bf16[64,32,128]{2,1,0:T(8,128)(2,1)S(1)} %add_up.31.refs_3_), channel_id=1, source_target_pairs={{0,2},{7,5},{2,4},{5,3},{4,6},{3,1},{8,10},{15,13},{10,12},{13,11}... | collective-permute-start | bytes 1572872 | tf_op jit(solution)/shard_map/ppermute | solution.py:475
  75.1 4.4 %collective-permute-start.20 = (bf16[64,32,128]{2,1,0:T(8,128)(2,1)S(1)}, bf16[64,32,128]{2,1,0:T(8,128)(2,1)S(1)}, u32[]{:S(2)}, u32[]{:S(2)}) collective-permute-start(bf16[64,32,128]{2,1,0:T(8,128)(2,1)S(1)} %add_up.33.refs_3_.refs_5_), channel_id=1, source_target_pairs={{0,2},{7,5},{2,4},{5,3},{4,6},{3,1},{8,10},{15,13},{10,12},{13,11}... | collective-permute-start | bytes 1572872 | tf_op jit(solution)/shard_map/ppermute | solution.py:475
  80.7 7.3 %word_products.1 = (bf16[64,64,128]{2,1,0:T(8,128)(2,1)}, bf16[64,64,128]{2,1,0:T(8,128)(2,1)}, bf16[64,64,128]{2,1,0:T(8,128)(2,1)S(1)}, bf16[64,64,128]{2,1,0:...) custom-call(s32[487]{0:T(512)S(1)} %pad_add_fusion.index_ref, ...), custom_call_target="tpu_custom_call" | custom-call | bytes 36900 | tf_op jit(solution)/shard_map/word_products/pallas_call | solution.py:338
  88.1 1.3 collective-permute-start.27
  89.4 2.1 collective-permute-start.21
  91.8 1.3 add_up.34
  93.1 3.9 %collective-permute-start.28 = (bf16[64,32,128]{2,1,0:T(8,128)(2,1)}, bf16[64,32,128]{2,1,0:T(8,128)(2,1)}, u32[]{:S(2)}, u32[]{:S(2)}) collective-permute-start(bf16[64,32,128]{2,1,0:T(8,128)(2,1)} %get-tuple-element.49.refs_3_.refs_6_), channel_id=1, source_target_pairs={{0,2},{7,5},{2,4},{5,3},{4,6},{3,1},{8,10},{15,13},{10,12},{13,11}... | collective-permute-start | bytes 1572872 | tf_op jit(solution)/shard_map/ppermute | solution.py:475
  97.0 1.3 collective-permute-start.26
  98.3 1.3 add_up.35
  99.6 3.6 %collective-permute-start.30 = (bf16[64,32,128]{2,1,0:T(8,128)(2,1)}, bf16[64,32,128]{2,1,0:T(8,128)(2,1)}, u32[]{:S(2)}, u32[]{:S(2)}) collective-permute-start(bf16[64,32,128]{2,1,0:T(8,128)(2,1)} %get-tuple-element.58.refs_3_.refs_7_), channel_id=1, source_target_pairs={{0,2},{7,5},{2,4},{5,3},{4,6},{3,1},{8,10},{15,13},{10,12},{13,11}... | collective-permute-start | bytes 1572872 | tf_op jit(solution)/shard_map/ppermute | solution.py:475
  104.4 1.5 add_up.37.refs_3_
  106.0 4.3 %collective-permute-start.29 = (bf16[64,32,128]{2,1,0:T(8,128)(2,1)S(1)}, bf16[64,32,128]{2,1,0:T(8,128)(2,1)S(1)}, u32[]{:S(2)}, u32[]{:S(2)}) collective-permute-start(bf16[64,32,128]{2,1,0:T(8,128)(2,1)S(1)} %add_up.37.refs_3_), channel_id=1, source_target_pairs={{0,2},{7,5},{2,4},{5,3},{4,6},{3,1},{8,10},{15,13},{10,12},{13,11}... | collective-permute-start | bytes 1572872 | tf_op jit(solution)/shard_map/ppermute | solution.py:475
  110.3 1.3 collective-permute-start.25
  111.6 1.4 add_up.38.refs_4_.refs_2_
  113.0 3.9 %collective-permute-start.32 = (bf16[64,32,128]{2,1,0:T(8,128)(2,1)S(1)}, bf16[64,32,128]{2,1,0:T(8,128)(2,1)S(1)}, u32[]{:S(2)}, u32[]{:S(2)}) collective-permute-start(bf16[64,32,128]{2,1,0:T(8,128)(2,1)S(1)} %add_up.38.refs_4_.refs_2_), channel_id=1, source_target_pairs={{0,2},{7,5},{2,4},{5,3},{4,6},{3,1},{8,10},{15,13},{10,12},{13,11}... | collective-permute-start | bytes 1572872 | tf_op jit(solution)/shard_map/ppermute | solution.py:475
  117.2 4.6 %collective-permute-start.31 = (bf16[64,32,128]{2,1,0:T(8,128)(2,1)S(1)}, bf16[64,32,128]{2,1,0:T(8,128)(2,1)S(1)}, u32[]{:S(2)}, u32[]{:S(2)}) collective-permute-start(bf16[64,32,128]{2,1,0:T(8,128)(2,1)S(1)} %add_up.39.refs_4_), channel_id=1, source_target_pairs={{0,2},{7,5},{2,4},{5,3},{4,6},{3,1},{8,10},{15,13},{10,12},{13,11}... | collective-permute-start | bytes 1572872 | tf_op jit(solution)/shard_map/ppermute | solution.py:475
  121.8 1.7 collective-permute-done.32.refs_2_.refs_3_
  123.8 4.4 %collective-permute-start.36 = (bf16[64,32,128]{2,1,0:T(8,128)(2,1)S(1)}, bf16[64,32,128]{2,1,0:T(8,128)(2,1)S(1)}, u32[]{:S(2)}, u32[]{:S(2)}) collective-permute-start(bf16[64,32,128]{2,1,0:T(8,128)(2,1)S(1)} %add_up.40.refs_3_), channel_id=1, source_target_pairs={{0,2},{7,5},{2,4},{5,3},{4,6},{3,1},{8,10},{15,13},{10,12},{13,11}... | collective-permute-start | bytes 1572872 | tf_op jit(solution)/shard_map/ppermute | solution.py:475
  129.6 4.4 %collective-permute-start.33 = (bf16[64,32,128]{2,1,0:T(8,128)(2,1)S(1)}, bf16[64,32,128]{2,1,0:T(8,128)(2,1)S(1)}, u32[]{:S(2)}, u32[]{:S(2)}) collective-permute-start(bf16[64,32,128]{2,1,0:T(8,128)(2,1)S(1)} %add_up.41.refs_3_), channel_id=1, source_target_pairs={{0,2},{7,5},{2,4},{5,3},{4,6},{3,1},{8,10},{15,13},{10,12},{13,11}... | collective-permute-start | bytes 1572872 | tf_op jit(solution)/shard_map/ppermute | solution.py:475
  135.4 4.7 %collective-permute-start.37 = (bf16[64,32,128]{2,1,0:T(8,128)(2,1)S(1)}, bf16[64,32,128]{2,1,0:T(8,128)(2,1)S(1)}, u32[]{:S(2)}, u32[]{:S(2)}) collective-permute-start(bf16[64,32,128]{2,1,0:T(8,128)(2,1)S(1)} %add_up.43.refs_3_), channel_id=1, source_target_pairs={{0,2},{7,5},{2,4},{5,3},{4,6},{3,1},{8,10},{15,13},{10,12},{13,11}... | collective-permute-start | bytes 1572872 | tf_op jit(solution)/shard_map/ppermute | solution.py:475
  140.9 5.8 %collective-permute-done.37.refs_0_ = bf16[64,32,128]{2,1,0:T(8,128)(2,1)S(1)} collective-permute-done((bf16[64,32,128]{2,1,0:T(8,128)(2,1)S(1)}, bf16[64,32,128]{2,1,0:T(8,128)(2,1)S(1)}, u32[]{:S(2)}, u32[]{:S(2)}) %collective-permute-start.37) | collective-permute-done | bytes 524320 | tf_op jit(solution)/shard_map/ppermute | solution.py:475
  149.3 4.4 %collective-permute-start.40 = (bf16[64,32,128]{2,1,0:T(8,128)(2,1)S(1)}, bf16[64,32,128]{2,1,0:T(8,128)(2,1)S(1)}, u32[]{:S(2)}, u32[]{:S(2)}) collective-permute-start(bf16[64,32,128]{2,1,0:T(8,128)(2,1)S(1)} %get-tuple-element.61.refs_3_), channel_id=1, source_target_pairs={{0,2},{7,5},{2,4},{5,3},{4,6},{3,1},{8,10},{15,13},{10,12},{13,11}... | collective-permute-start | bytes 1572872 | tf_op jit(solution)/shard_map/ppermute | solution.py:475
  154.9 2.9 %collective-permute-start.39 = (bf16[64,32,128]{2,1,0:T(8,128)(2,1)S(1)}, bf16[64,32,128]{2,1,0:T(8,128)(2,1)S(1)}, u32[]{:S(2)}, u32[]{:S(2)}) collective-permute-start(bf16[64,32,128]{2,1,0:T(8,128)(2,1)S(1)} %get-tuple-element.63.refs_14_.refs_1_.refs_3_), channel_id=1, source_target_pairs={{0,2},{7,5},{2,4},{5,3},{4,6},{3,1},{8,10},{15,13},{10,12},{13,11}... | collective-permute-start | bytes 1572872 | tf_op jit(solution)/shard_map/ppermute | solution.py:475
  157.9 3.9 %context_products.3 = (bf16[64,64,128]{2,1,0:T(8,128)(2,1)S(1)}, f32[64,64,128]{2,1,0:T(8,128)S(1)}) custom-call(s32[487]{0:T(512)S(1)} %pad_add_fusion.index_ref, bf16[160,128,128]{2,1,0:T(8,128)(2,1)S(1)} %bitcast.7, bf16[64,32,128]{2,1,0:T(8,128)(2,1)S(1)} %collective-permute-done.31.refs_2_.refs_0_, ...), custom_call_target="tpu_custom_call" | custom-call | bytes 36900 | tf_op jit(solution)/shard_map/context_products/pallas_call | solution.py:397
  161.9 1.7 collective-permute-start.49
  163.7 2.8 %collective-permute-start.48 = (bf16[64,32,128]{2,1,0:T(8,128)(2,1)S(1)}, bf16[64,32,128]{2,1,0:T(8,128)(2,1)S(1)}, u32[]{:S(2)}, u32[]{:S(2)}) collective-permute-start(bf16[64,32,128]{2,1,0:T(8,128)(2,1)S(1)} %add_up.46.refs_1_), channel_id=1, source_target_pairs={{0,2},{7,5},{2,4},{5,3},{4,6},{3,1},{8,10},{15,13},{10,12},{13,11}... | collective-permute-start | bytes 1572872 | tf_op jit(solution)/shard_map/ppermute | solution.py:475
  166.6 6.5 %collective-permute-done.48.refs_0_.refs_1_ = bf16[64,32,128]{2,1,0:T(8,128)(2,1)S(1)} collective-permute-done((bf16[64,32,128]{2,1,0:T(8,128)(2,1)S(1)}, bf16[64,32,128]{2,1,0:T(8,128)(2,1)S(1)}, u32[]{:S(2)}, u32[]{:S(2)}) %collective-permute-start.48) | collective-permute-done | bytes 524320 | tf_op jit(solution)/shard_map/ppermute | solution.py:475
  173.2 4.4 %collective-permute-start.51 = (bf16[64,32,128]{2,1,0:T(8,128)(2,1)S(1)}, bf16[64,32,128]{2,1,0:T(8,128)(2,1)S(1)}, u32[]{:S(2)}, u32[]{:S(2)}) collective-permute-start(bf16[64,32,128]{2,1,0:T(8,128)(2,1)S(1)} %add_up.48.refs_1_), channel_id=1, source_target_pairs={{0,2},{7,5},{2,4},{5,3},{4,6},{3,1},{8,10},{15,13},{10,12},{13,11}... | collective-permute-start | bytes 1572872 | tf_op jit(solution)/shard_map/ppermute | solution.py:475
  177.6 2.0 collective-permute-start.47
  181.2 3.1 %collective-permute-done.51.refs_0_ = bf16[64,32,128]{2,1,0:T(8,128)(2,1)S(1)} collective-permute-done((bf16[64,32,128]{2,1,0:T(8,128)(2,1)S(1)}, bf16[64,32,128]{2,1,0:T(8,128)(2,1)S(1)}, u32[]{:S(2)}, u32[]{:S(2)}) %collective-permute-start.51) | collective-permute-done | bytes 524320 | tf_op jit(solution)/shard_map/ppermute | solution.py:475
  184.3 5.6 %collective-permute-done.47.refs_0_.refs_1_ = bf16[64,32,128]{2,1,0:T(8,128)(2,1)S(1)} collective-permute-done((bf16[64,32,128]{2,1,0:T(8,128)(2,1)S(1)}, bf16[64,32,128]{2,1,0:T(8,128)(2,1)S(1)}, u32[]{:S(2)}, u32[]{:S(2)}) %collective-permute-start.47) | collective-permute-done | bytes 524320 | tf_op jit(solution)/shard_map/ppermute | solution.py:475
  190.0 4.4 %collective-permute-start.50 = (bf16[64,32,128]{2,1,0:T(8,128)(2,1)S(1)}, bf16[64,32,128]{2,1,0:T(8,128)(2,1)S(1)}, u32[]{:S(2)}, u32[]{:S(2)}) collective-permute-start(bf16[64,32,128]{2,1,0:T(8,128)(2,1)S(1)} %add_up.49), channel_id=1, source_target_pairs={{0,2},{7,5},{2,4},{5,3},{4,6},{3,1},{8,10},{15,13},{10,12},{13,11}... | collective-permute-start | bytes 1572872 | tf_op jit(solution)/shard_map/ppermute | solution.py:475
  195.0 2.8 %context_products.4 = (bf16[64,32,128]{2,1,0:T(8,128)(2,1)S(1)}, f32[64,32,128]{2,1,0:T(8,128)S(1)}) custom-call(s32[487]{0:T(512)S(1)} %pad_add_fusion.index_ref, bf16[160,128,128]{2,1,0:T(8,128)(2,1)S(1)} %bitcast.7, bf16[64,32,128]{2,1,0:T(8,128)(2,1)S(1)} %collective-permute-done.51.refs_0_, ...), custom_call_target="tpu_custom_call" | custom-call | bytes 36900 | tf_op jit(solution)/shard_map/context_products/pallas_call | solution.py:397
  197.8 3.2 %collective-permute-done.50.refs_0_ = bf16[64,32,128]{2,1,0:T(8,128)(2,1)S(1)} collective-permute-done((bf16[64,32,128]{2,1,0:T(8,128)(2,1)S(1)}, bf16[64,32,128]{2,1,0:T(8,128)(2,1)S(1)}, u32[]{:S(2)}, u32[]{:S(2)}) %collective-permute-start.50) | collective-permute-done | bytes 524320 | tf_op jit(solution)/shard_map/ppermute | solution.py:475
  201.7 1.4 collective-permute-done.58.refs_6_
  203.1 2.8 %context_products.5 = (bf16[64,32,128]{2,1,0:T(8,128)(2,1)S(1)}, f32[64,32,128]{2,1,0:T(8,128)S(1)}) custom-call(s32[487]{0:T(512)S(1)} %pad_add_fusion.index_ref, bf16[160,128,128]{2,1,0:T(8,128)(2,1)S(1)} %bitcast.7, bf16[64,32,128]{2,1,0:T(8,128)(2,1)S(1)} %add_up.51.refs_0_, bf16[64,32,128]{2,1,0:T(8,128)(2,1)S(1)} %collective-permute-done.47.refs_0_.refs_1_, ...), custom_call_target="tpu_custom_call" | custom-call | bytes 36900 | tf_op jit(solution)/shard_map/context_products/pallas_call | solution.py:397
  206.4 4.1 %collective-permute-done.59.refs_1_.refs_4_ = bf16[64,32,128]{2,1,0:T(8,128)(2,1)S(1)} collective-permute-done((bf16[64,32,128]{2,1,0:T(8,128)(2,1)S(1)}, bf16[64,32,128]{2,1,0:T(8,128)(2,1)S(1)}, u32[]{:S(2)}, u32[]{:S(2)}) %collective-permute-start.59) | collective-permute-done | bytes 524320 | tf_op jit(solution)/shard_map/ppermute | solution.py:463
  211.6 6.8 %collective-permute-done.61.refs_1_.refs_7_ = bf16[64,32,128]{2,1,0:T(8,128)(2,1)S(1)} collective-permute-done((bf16[64,32,128]{2,1,0:T(8,128)(2,1)S(1)}, bf16[64,32,128]{2,1,0:T(8,128)(2,1)S(1)}, u32[]{:S(2)}, u32[]{:S(2)}) %collective-permute-start.61) | collective-permute-done | bytes 524320 | tf_op jit(solution)/shard_map/ppermute | solution.py:463
  220.8 3.1 %turn_back.2 = f32[4096,128]{1,0:T(8,128)} custom-call(s32[1]{0:T(128)S(6)} %select_n.44.start_ref, f32[64,32,128]{2,1,0:T(8,128)} %get-tuple-element.48.refs_0_, f32[64,32,128]{2,1,0:T(8,128)} %get-tuple-element.50.refs_1_, f32[64,32,128]{2,1,0:T(8,128)} %get-tuple-element.60.refs_2_, f32[64,32,128]{2,1,0:T(8,128)} %get-tuple-element.62.refs_3_, ...), custom_call_target="tpu_custom_call" | custom-call | bytes 36900 | tf_op jit(solution)/shard_map/turn_back/pallas_call | solution.py:428
  223.8 2.2 collective-permute-done.62.refs_8_
  226.1 2.6 %turn_back.3 = f32[4096,128]{1,0:T(8,128)} custom-call(s32[1]{0:T(128)} %constant.92.clone.1.place_ref.start_ref, f32[64,64,128]{2,1,0:T(8,128)S(1)} %get-tuple-element.65.refs_0_, bf16[64,64,128]{2,1,0:T(8,128)(2,1)S(1)} %collective-permute-done.49.refs_2_.refs_1_, bf16[32,64,128]{2,1,0:T(8,128)(2,1)S(1)} %copy-done.2, f32[64,32,128]{2,1,0:T(8,128)S(1)} %copy-done.4, ...), custom_call_target="tpu_custom_call" | custom-call | bytes 36900 | tf_op jit(solution)/shard_map/turn_back/pallas_call | solution.py:428
  (157 shorter events, 26.6 us)
Async XLA Ops:
  2.2 12.9 %collective-permute-start.8 = (bf16[32,64,128]{2,1,0:T(8,128)(2,1)S(1)}, bf16[32,64,128]{2,1,0:T(8,128)(2,1)S(1)}, u32[]{:S(2)}, u32[]{:S(2)}) collective-permute-start(bf16[32,64,128]{2,1,0:T(8,128)(2,1)S(1)} %turn_panel.2.refs_0_.refs_5_), channel_id=1, source_target_pairs={{0,8},{1,17},{2,10},{3,19},{4,12},{5,21},{6,14},{7,23},{8,0},{9,25... | collective-permute-start | bytes 1572872 | tf_op jit(solution)/shard_map/ppermute | solution.py:463
  10.0 5.6 %collective-permute-start = (f32[128,128]{1,0:T(8,128)S(1)}, f32[128,128]{1,0:T(8,128)S(1)}, u32[]{:S(2)}, u32[]{:S(2)}) collective-permute-start(f32[128,128]{1,0:T(8,128)S(1)} %get-tuple-element.37.refs_0_), channel_id=1, source_target_pairs={{0,8},{8,0},{16,24},{24,16},{1,9},{9,1},{17,25},{25,17},{2,10},{10... | collective-permute-start | bytes 196616 | tf_op jit(solution)/shard_map/ppermute | solution.py:478
  10.1 5.5 %collective-permute-start.1 = (f32[128,128]{1,0:T(8,128)S(1)}, f32[128,128]{1,0:T(8,128)S(1)}, u32[]{:S(2)}, u32[]{:S(2)}) collective-permute-start(f32[128,128]{1,0:T(8,128)S(1)} %get-tuple-element.37.refs_0_), channel_id=1, source_target_pairs={{0,16},{8,24},{16,0},{24,8},{1,17},{9,25},{17,1},{25,9},{2,18},{10... | collective-permute-start | bytes 196616 | tf_op jit(solution)/shard_map/ppermute | solution.py:478
  12.1 5.9 %collective-permute-start.2 = (f32[128,128]{1,0:T(8,128)S(1)}, f32[128,128]{1,0:T(8,128)S(1)}, u32[]{:S(2)}, u32[]{:S(2)}) collective-permute-start(f32[128,128]{1,0:T(8,128)S(1)} %get-tuple-element.37.refs_0_), channel_id=1, source_target_pairs={{0,24},{8,16},{16,8},{24,0},{1,25},{9,17},{17,9},{25,1},{2,26},{10... | collective-permute-start | bytes 196616 | tf_op jit(solution)/shard_map/ppermute | solution.py:478
  13.6 17.0 %collective-permute-start.7 = (bf16[32,64,128]{2,1,0:T(8,128)(2,1)S(1)}, bf16[32,64,128]{2,1,0:T(8,128)(2,1)S(1)}, u32[]{:S(2)}, u32[]{:S(2)}) collective-permute-start(bf16[32,64,128]{2,1,0:T(8,128)(2,1)S(1)} %turn_panel.2.refs_0_.refs_5_), channel_id=1, source_target_pairs={{0,16},{1,9},{2,18},{3,11},{4,20},{5,13},{6,22},{7,15},{8,24},{9,1... | collective-permute-start | bytes 1572872 | tf_op jit(solution)/shard_map/ppermute | solution.py:463
  15.1 15.5 %collective-permute-start.9 = (bf16[32,64,128]{2,1,0:T(8,128)(2,1)S(1)}, bf16[32,64,128]{2,1,0:T(8,128)(2,1)S(1)}, u32[]{:S(2)}, u32[]{:S(2)}) collective-permute-start(bf16[32,64,128]{2,1,0:T(8,128)(2,1)S(1)} %collective-permute-done.8.refs_7_), channel_id=1, source_target_pairs={{0,16},{1,9},{2,18},{3,11},{4,20},{5,13},{6,22},{7,15},{8,24},{9,1... | collective-permute-start | bytes 1572872 | tf_op jit(solution)/shard_map/ppermute | solution.py:463
  18.1 1.3 collective-permute-start.3
  19.5 4.4 %collective-permute-start.4 = (f32[136,128]{1,0:T(8,128)S(1)}, f32[136,128]{1,0:T(8,128)S(1)}, u32[]{:S(2)}, u32[]{:S(2)}) collective-permute-start(f32[136,128]{1,0:T(8,128)S(1)} %plus.3.a_ref), channel_id=1, source_target_pairs={{0,2},{1,3},{2,0},{3,1},{4,6},{5,7},{6,4},{7,5},{8,10},{9,11},{10,... | collective-permute-start | bytes 208904 | tf_op jit(solution)/shard_map/ppermute | solution.py:481
  23.9 5.4 %collective-permute-start.5 = (f32[136,128]{1,0:T(8,128)S(1)}, f32[136,128]{1,0:T(8,128)S(1)}, u32[]{:S(2)}, u32[]{:S(2)}) collective-permute-start(f32[136,128]{1,0:T(8,128)S(1)} %plus.4.a_ref), channel_id=1, source_target_pairs={{0,4},{1,5},{2,6},{3,7},{4,0},{5,1},{6,2},{7,3},{8,12},{9,13},{10,... | collective-permute-start | bytes 208904 | tf_op jit(solution)/shard_map/ppermute | solution.py:481
  29.2 1.3 collective-permute-start.6
  40.6 40.1 %copy-start = (bf16[160,128,128]{2,1,0:T(8,128)(2,1)}, bf16[160,128,128]{2,1,0:T(8,128)(2,1)S(1)}, u32[]{:S(2)}) copy-start(bf16[160,128,128]{2,1,0:T(8,128)(2,1)S(1)} %get-tuple-element.51.refs_0_.tiles_ref) | copy-start | bytes 15728644
  40.6 4.6 %collective-permute-start.12 = (bf16[64,64,128]{2,1,0:T(8,128)(2,1)S(1)}, bf16[64,64,128]{2,1,0:T(8,128)(2,1)S(1)}, u32[]{:S(2)}, u32[]{:S(2)}) collective-permute-start(bf16[64,64,128]{2,1,0:T(8,128)(2,1)S(1)} %get-tuple-element.46), channel_id=1, source_target_pairs={{1,0},{6,7},{9,8},{14,15},{17,16},{22,23},{25,24},{30,31}} | collective-permute-start | bytes 3145736 | tf_op jit(solution)/shard_map/ppermute | solution.py:466
  41.9 14.9 %collective-permute-start.11 = (bf16[64,64,128]{2,1,0:T(8,128)(2,1)S(1)}, bf16[64,64,128]{2,1,0:T(8,128)(2,1)S(1)}, u32[]{:S(2)}, u32[]{:S(2)}) collective-permute-start(bf16[64,64,128]{2,1,0:T(8,128)(2,1)S(1)} %get-tuple-element.44), channel_id=1, source_target_pairs={{1,0},{3,2},{4,5},{6,7},{9,8},{11,10},{12,13},{14,15},{17,16},{19,... | collective-permute-start | bytes 3145736 | tf_op jit(solution)/shard_map/ppermute | solution.py:466
  45.5 11.3 %collective-permute-start.13 = (bf16[64,32,128]{2,1,0:T(8,128)(2,1)S(1)}, bf16[64,32,128]{2,1,0:T(8,128)(2,1)S(1)}, u32[]{:S(2)}, u32[]{:S(2)}) collective-permute-start(bf16[64,32,128]{2,1,0:T(8,128)(2,1)S(1)} %add_up.27.refs_2_.refs_0_), channel_id=1, source_target_pairs={{0,2},{7,5},{2,4},{5,3},{4,6},{3,1},{8,10},{15,13},{10,12},{13,11}... | collective-permute-start | bytes 1572872 | tf_op jit(solution)/shard_map/ppermute | solution.py:475
  46.8 19.6 %collective-permute-start.10 = (bf16[64,64,128]{2,1,0:T(8,128)(2,1)S(1)}, bf16[64,64,128]{2,1,0:T(8,128)(2,1)S(1)}, u32[]{:S(2)}, u32[]{:S(2)}) collective-permute-start(bf16[64,64,128]{2,1,0:T(8,128)(2,1)S(1)} %get-tuple-element.42), channel_id=1, source_target_pairs={{1,0},{2,3},{3,2},{4,5},{5,4},{6,7},{9,8},{10,11},{11,10},{12,13},... | collective-permute-start | bytes 3145736 | tf_op jit(solution)/shard_map/ppermute | solution.py:466
  48.4 13.9 %collective-permute-start.15 = (bf16[64,32,128]{2,1,0:T(8,128)(2,1)S(1)}, bf16[64,32,128]{2,1,0:T(8,128)(2,1)S(1)}, u32[]{:S(2)}, u32[]{:S(2)}) collective-permute-start(bf16[64,32,128]{2,1,0:T(8,128)(2,1)S(1)} %add_up.28.refs_3_.refs_2_), channel_id=1, source_target_pairs={{0,2},{7,5},{2,4},{5,3},{4,6},{3,1},{8,10},{15,13},{10,12},{13,11}... | collective-permute-start | bytes 1572872 | tf_op jit(solution)/shard_map/ppermute | solution.py:475
  55.0 10.8 %collective-permute-start.23 = (bf16[32,64,128]{2,1,0:T(8,128)(2,1)S(1)}, bf16[32,64,128]{2,1,0:T(8,128)(2,1)S(1)}, u32[]{:S(2)}, u32[]{:S(2)}) collective-permute-start(bf16[32,64,128]{2,1,0:T(8,128)(2,1)S(1)} %turn_panel.3.refs_1_), channel_id=1, source_target_pairs={{0,8},{1,17},{2,10},{3,19},{4,12},{5,21},{6,14},{7,23},{8,0},{9,25... | collective-permute-start | bytes 1572872 | tf_op jit(solution)/shard_map/ppermute | solution.py:463
  57.2 11.8 %collective-permute-start.14 = (bf16[64,32,128]{2,1,0:T(8,128)(2,1)S(1)}, bf16[64,32,128]{2,1,0:T(8,128)(2,1)S(1)}, u32[]{:S(2)}, u32[]{:S(2)}) collective-permute-start(bf16[64,32,128]{2,1,0:T(8,128)(2,1)S(1)} %add_up.29.refs_3_), channel_id=1, source_target_pairs={{0,2},{7,5},{2,4},{5,3},{4,6},{3,1},{8,10},{15,13},{10,12},{13,11}... | collective-permute-start | bytes 1572872 | tf_op jit(solution)/shard_map/ppermute | solution.py:475
  62.8 11.8 %collective-permute-start.19 = (bf16[64,32,128]{2,1,0:T(8,128)(2,1)S(1)}, bf16[64,32,128]{2,1,0:T(8,128)(2,1)S(1)}, u32[]{:S(2)}, u32[]{:S(2)}) collective-permute-start(bf16[64,32,128]{2,1,0:T(8,128)(2,1)S(1)} %add_up.30.refs_3_.refs_1_), channel_id=1, source_target_pairs={{0,2},{7,5},{2,4},{5,3},{4,6},{3,1},{8,10},{15,13},{10,12},{13,11}... | collective-permute-start | bytes 1572872 | tf_op jit(solution)/shard_map/ppermute | solution.py:475
  65.7 25.8 %collective-permute-start.18 = (bf16[64,64,128]{2,1,0:T(8,128)(2,1)S(1)}, bf16[64,64,128]{2,1,0:T(8,128)(2,1)S(1)}, u32[]{:S(2)}, u32[]{:S(2)}) collective-permute-start(bf16[64,64,128]{2,1,0:T(8,128)(2,1)S(1)} %get-tuple-element.47.refs_0_), channel_id=1, source_target_pairs={{0,1},{1,0},{2,3},{3,2},{4,5},{5,4},{6,7},{7,6},{8,9},{9,8},{10,11... | collective-permute-start | bytes 3145736 | tf_op jit(solution)/shard_map/ppermute | solution.py:466
  65.8 13.7 %collective-permute-start.22 = (bf16[32,64,128]{2,1,0:T(8,128)(2,1)S(1)}, bf16[32,64,128]{2,1,0:T(8,128)(2,1)S(1)}, u32[]{:S(2)}, u32[]{:S(2)}) collective-permute-start(bf16[32,64,128]{2,1,0:T(8,128)(2,1)S(1)} %turn_panel.3.refs_1_), channel_id=1, source_target_pairs={{0,16},{1,9},{2,18},{3,11},{4,20},{5,13},{6,22},{7,15},{8,24},{9,1... | collective-permute-start | bytes 1572872 | tf_op jit(solution)/shard_map/ppermute | solution.py:463
  66.4 14.3 %collective-permute-start.24 = (bf16[32,64,128]{2,1,0:T(8,128)(2,1)S(1)}, bf16[32,64,128]{2,1,0:T(8,128)(2,1)S(1)}, u32[]{:S(2)}, u32[]{:S(2)}) collective-permute-start(bf16[32,64,128]{2,1,0:T(8,128)(2,1)S(1)} %add_up.36), channel_id=1, source_target_pairs={{0,16},{1,9},{2,18},{3,11},{4,20},{5,13},{6,22},{7,15},{8,24},{9,1... | collective-permute-start | bytes 1572872 | tf_op jit(solution)/shard_map/ppermute | solution.py:463
  69.4 18.5 %collective-permute-start.16 = (bf16[64,32,128]{2,1,0:T(8,128)(2,1)S(1)}, bf16[64,32,128]{2,1,0:T(8,128)(2,1)S(1)}, u32[]{:S(2)}, u32[]{:S(2)}) collective-permute-start(bf16[64,32,128]{2,1,0:T(8,128)(2,1)S(1)} %add_up.31.refs_3_), channel_id=1, source_target_pairs={{0,2},{7,5},{2,4},{5,3},{4,6},{3,1},{8,10},{15,13},{10,12},{13,11}... | collective-permute-start | bytes 1572872 | tf_op jit(solution)/shard_map/ppermute | solution.py:475
  75.1 14.3 %collective-permute-start.20 = (bf16[64,32,128]{2,1,0:T(8,128)(2,1)S(1)}, bf16[64,32,128]{2,1,0:T(8,128)(2,1)S(1)}, u32[]{:S(2)}, u32[]{:S(2)}) collective-permute-start(bf16[64,32,128]{2,1,0:T(8,128)(2,1)S(1)} %add_up.33.refs_3_.refs_5_), channel_id=1, source_target_pairs={{0,2},{7,5},{2,4},{5,3},{4,6},{3,1},{8,10},{15,13},{10,12},{13,11}... | collective-permute-start | bytes 1572872 | tf_op jit(solution)/shard_map/ppermute | solution.py:475
  88.0 3.8 %collective-permute-start.17 = (bf16[64,32,128]{2,1,0:T(8,128)(2,1)S(1)}, bf16[64,32,128]{2,1,0:T(8,128)(2,1)S(1)}, u32[]{:S(2)}, u32[]{:S(2)}) collective-permute-start(bf16[64,32,128]{2,1,0:T(8,128)(2,1)S(1)} %collective-permute-done.16.refs_0_), channel_id=1, source_target_pairs={{0,1},{1,0},{2,3},{3,2},{4,5},{5,4},{6,7},{7,6},{8,9},{9,8},{10,11... | collective-permute-start | bytes 1572872 | tf_op jit(solution)/shard_map/ppermute | solution.py:466
  88.1 15.1 %collective-permute-start.27 = (bf16[64,64,128]{2,1,0:T(8,128)(2,1)}, bf16[64,64,128]{2,1,0:T(8,128)(2,1)}, u32[]{:S(2)}, u32[]{:S(2)}) collective-permute-start(bf16[64,64,128]{2,1,0:T(8,128)(2,1)} %get-tuple-element.57), channel_id=1, source_target_pairs={{1,0},{6,7},{9,8},{14,15},{17,16},{22,23},{25,24},{30,31}} | collective-permute-start | bytes 3145736 | tf_op jit(solution)/shard_map/ppermute | solution.py:466
  89.4 8.9 %collective-permute-start.21 = (bf16[64,32,128]{2,1,0:T(8,128)(2,1)S(1)}, bf16[64,32,128]{2,1,0:T(8,128)(2,1)S(1)}, u32[]{:S(2)}, u32[]{:S(2)}) collective-permute-start(bf16[64,32,128]{2,1,0:T(8,128)(2,1)S(1)} %collective-permute-done.20.refs_0_), channel_id=1, source_target_pairs={{0,1},{1,0},{2,3},{3,2},{4,5},{5,4},{6,7},{7,6},{8,9},{9,8},{10,11... | collective-permute-start | bytes 1572872 | tf_op jit(solution)/shard_map/ppermute | solution.py:466
  93.1 10.1 %collective-permute-start.28 = (bf16[64,32,128]{2,1,0:T(8,128)(2,1)}, bf16[64,32,128]{2,1,0:T(8,128)(2,1)}, u32[]{:S(2)}, u32[]{:S(2)}) collective-permute-start(bf16[64,32,128]{2,1,0:T(8,128)(2,1)} %get-tuple-element.49.refs_3_.refs_6_), channel_id=1, source_target_pairs={{0,2},{7,5},{2,4},{5,3},{4,6},{3,1},{8,10},{15,13},{10,12},{13,11}... | collective-permute-start | bytes 1572872 | tf_op jit(solution)/shard_map/ppermute | solution.py:475
  97.0 19.9 %collective-permute-start.26 = (bf16[64,64,128]{2,1,0:T(8,128)(2,1)}, bf16[64,64,128]{2,1,0:T(8,128)(2,1)S(1)}, u32[]{:S(2)}, u32[]{:S(2)}) collective-permute-start(bf16[64,64,128]{2,1,0:T(8,128)(2,1)} %get-tuple-element.55), channel_id=1, source_target_pairs={{1,0},{3,2},{4,5},{6,7},{9,8},{11,10},{12,13},{14,15},{17,16},{19,... | collective-permute-start | bytes 3145736 | tf_op jit(solution)/shard_map/ppermute | solution.py:466
  99.6 12.0 %collective-permute-start.30 = (bf16[64,32,128]{2,1,0:T(8,128)(2,1)}, bf16[64,32,128]{2,1,0:T(8,128)(2,1)}, u32[]{:S(2)}, u32[]{:S(2)}) collective-permute-start(bf16[64,32,128]{2,1,0:T(8,128)(2,1)} %get-tuple-element.58.refs_3_.refs_7_), channel_id=1, source_target_pairs={{0,2},{7,5},{2,4},{5,3},{4,6},{3,1},{8,10},{15,13},{10,12},{13,11}... | collective-permute-start | bytes 1572872 | tf_op jit(solution)/shard_map/ppermute | solution.py:475
  106.0 11.0 %collective-permute-start.29 = (bf16[64,32,128]{2,1,0:T(8,128)(2,1)S(1)}, bf16[64,32,128]{2,1,0:T(8,128)(2,1)S(1)}, u32[]{:S(2)}, u32[]{:S(2)}) collective-permute-start(bf16[64,32,128]{2,1,0:T(8,128)(2,1)S(1)} %add_up.37.refs_3_), channel_id=1, source_target_pairs={{0,2},{7,5},{2,4},{5,3},{4,6},{3,1},{8,10},{15,13},{10,12},{13,11}... | collective-permute-start | bytes 1572872 | tf_op jit(solution)/shard_map/ppermute | solution.py:475
  110.3 18.0 %collective-permute-start.25 = (bf16[64,64,128]{2,1,0:T(8,128)(2,1)S(1)}, bf16[64,64,128]{2,1,0:T(8,128)(2,1)S(1)}, u32[]{:S(2)}, u32[]{:S(2)}) collective-permute-start(bf16[64,64,128]{2,1,0:T(8,128)(2,1)S(1)} %copy-done.19), channel_id=1, source_target_pairs={{1,0},{2,3},{3,2},{4,5},{5,4},{6,7},{9,8},{10,11},{11,10},{12,13},... | collective-permute-start | bytes 3145736 | tf_op jit(solution)/shard_map/ppermute | solution.py:466
  113.0 10.5 %collective-permute-start.32 = (bf16[64,32,128]{2,1,0:T(8,128)(2,1)S(1)}, bf16[64,32,128]{2,1,0:T(8,128)(2,1)S(1)}, u32[]{:S(2)}, u32[]{:S(2)}) collective-permute-start(bf16[64,32,128]{2,1,0:T(8,128)(2,1)S(1)} %add_up.38.refs_4_.refs_2_), channel_id=1, source_target_pairs={{0,2},{7,5},{2,4},{5,3},{4,6},{3,1},{8,10},{15,13},{10,12},{13,11}... | collective-permute-start | bytes 1572872 | tf_op jit(solution)/shard_map/ppermute | solution.py:475
  117.2 11.9 %collective-permute-start.31 = (bf16[64,32,128]{2,1,0:T(8,128)(2,1)S(1)}, bf16[64,32,128]{2,1,0:T(8,128)(2,1)S(1)}, u32[]{:S(2)}, u32[]{:S(2)}) collective-permute-start(bf16[64,32,128]{2,1,0:T(8,128)(2,1)S(1)} %add_up.39.refs_4_), channel_id=1, source_target_pairs={{0,2},{7,5},{2,4},{5,3},{4,6},{3,1},{8,10},{15,13},{10,12},{13,11}... | collective-permute-start | bytes 1572872 | tf_op jit(solution)/shard_map/ppermute | solution.py:475
  123.8 11.1 %collective-permute-start.36 = (bf16[64,32,128]{2,1,0:T(8,128)(2,1)S(1)}, bf16[64,32,128]{2,1,0:T(8,128)(2,1)S(1)}, u32[]{:S(2)}, u32[]{:S(2)}) collective-permute-start(bf16[64,32,128]{2,1,0:T(8,128)(2,1)S(1)} %add_up.40.refs_3_), channel_id=1, source_target_pairs={{0,2},{7,5},{2,4},{5,3},{4,6},{3,1},{8,10},{15,13},{10,12},{13,11}... | collective-permute-start | bytes 1572872 | tf_op jit(solution)/shard_map/ppermute | solution.py:475
  128.3 18.5 %collective-permute-start.35 = (bf16[64,64,128]{2,1,0:T(8,128)(2,1)S(1)}, bf16[64,64,128]{2,1,0:T(8,128)(2,1)S(1)}, u32[]{:S(2)}, u32[]{:S(2)}) collective-permute-start(bf16[64,64,128]{2,1,0:T(8,128)(2,1)S(1)} %copy-done.15), channel_id=1, source_target_pairs={{0,1},{1,0},{2,3},{3,2},{4,5},{5,4},{6,7},{7,6},{8,9},{9,8},{10,11... | collective-permute-start | bytes 3145736 | tf_op jit(solution)/shard_map/ppermute | solution.py:466
  129.6 11.1 %collective-permute-start.33 = (bf16[64,32,128]{2,1,0:T(8,128)(2,1)S(1)}, bf16[64,32,128]{2,1,0:T(8,128)(2,1)S(1)}, u32[]{:S(2)}, u32[]{:S(2)}) collective-permute-start(bf16[64,32,128]{2,1,0:T(8,128)(2,1)S(1)} %add_up.41.refs_3_), channel_id=1, source_target_pairs={{0,2},{7,5},{2,4},{5,3},{4,6},{3,1},{8,10},{15,13},{10,12},{13,11}... | collective-permute-start | bytes 1572872 | tf_op jit(solution)/shard_map/ppermute | solution.py:475
  135.4 11.3 %collective-permute-start.37 = (bf16[64,32,128]{2,1,0:T(8,128)(2,1)S(1)}, bf16[64,32,128]{2,1,0:T(8,128)(2,1)S(1)}, u32[]{:S(2)}, u32[]{:S(2)}) collective-permute-start(bf16[64,32,128]{2,1,0:T(8,128)(2,1)S(1)} %add_up.43.refs_3_), channel_id=1, source_target_pairs={{0,2},{7,5},{2,4},{5,3},{4,6},{3,1},{8,10},{15,13},{10,12},{13,11}... | collective-permute-start | bytes 1572872 | tf_op jit(solution)/shard_map/ppermute | solution.py:475
  140.1 7.4 %collective-permute-start.42 = (bf16[64,32,128]{2,1,0:T(8,128)(2,1)}, bf16[64,32,128]{2,1,0:T(8,128)(2,1)S(1)}, u32[]{:S(2)}, u32[]{:S(2)}) collective-permute-start(bf16[64,32,128]{2,1,0:T(8,128)(2,1)} %collective-permute-done.30.refs_2_.refs_5_), channel_id=1, source_target_pairs={{0,1},{1,0},{2,3},{3,2},{4,5},{5,4},{6,7},{7,6},{8,9},{9,8},{10,11... | collective-permute-start | bytes 1572872 | tf_op jit(solution)/shard_map/ppermute | solution.py:466
  140.1 7.5 %collective-permute-start.41 = (bf16[64,32,128]{2,1,0:T(8,128)(2,1)}, bf16[64,32,128]{2,1,0:T(8,128)(2,1)S(1)}, u32[]{:S(2)}, u32[]{:S(2)}) collective-permute-start(bf16[64,32,128]{2,1,0:T(8,128)(2,1)} %collective-permute-done.28.refs_2_.refs_4_), channel_id=1, source_target_pairs={{0,1},{1,0},{2,3},{3,2},{4,5},{5,4},{6,7},{7,6},{8,9},{9,8},{10,11... | collective-permute-start | bytes 1572872 | tf_op jit(solution)/shard_map/ppermute | solution.py:466
  140.7 7.3 %collective-permute-start.34 = (bf16[64,32,128]{2,1,0:T(8,128)(2,1)S(1)}, bf16[64,32,128]{2,1,0:T(8,128)(2,1)S(1)}, u32[]{:S(2)}, u32[]{:S(2)}) collective-permute-start(bf16[64,32,128]{2,1,0:T(8,128)(2,1)S(1)} %collective-permute-done.33.refs_0_), channel_id=1, source_target_pairs={{0,1},{1,0},{2,3},{3,2},{4,5},{5,4},{6,7},{7,6},{8,9},{9,8},{10,11... | collective-permute-start | bytes 1572872 | tf_op jit(solution)/shard_map/ppermute | solution.py:466
  146.7 2.6 %collective-permute-start.38 = (bf16[64,32,128]{2,1,0:T(8,128)(2,1)S(1)}, bf16[64,32,128]{2,1,0:T(8,128)(2,1)S(1)}, u32[]{:S(2)}, u32[]{:S(2)}) collective-permute-start(bf16[64,32,128]{2,1,0:T(8,128)(2,1)S(1)} %collective-permute-done.37.refs_0_), channel_id=1, source_target_pairs={{0,1},{1,0},{2,3},{3,2},{4,5},{5,4},{6,7},{7,6},{8,9},{9,8},{10,11... | collective-permute-start | bytes 1572872 | tf_op jit(solution)/shard_map/ppermute | solution.py:466
  146.9 8.0 %collective-permute-start.44 = (bf16[64,32,128]{2,1,0:T(8,128)(2,1)S(1)}, bf16[64,32,128]{2,1,0:T(8,128)(2,1)S(1)}, u32[]{:S(2)}, u32[]{:S(2)}) collective-permute-start(bf16[64,32,128]{2,1,0:T(8,128)(2,1)S(1)} %collective-permute-done.32.refs_2_.refs_3_), channel_id=1, source_target_pairs={{0,1},{1,0},{2,3},{3,2},{4,5},{5,4},{6,7},{7,6},{8,9},{9,8},{10,11... | collective-permute-start | bytes 1572872 | tf_op jit(solution)/shard_map/ppermute | solution.py:466
  147.5 10.3 %collective-permute-start.43 = (bf16[64,32,128]{2,1,0:T(8,128)(2,1)S(1)}, bf16[64,32,128]{2,1,0:T(8,128)(2,1)S(1)}, u32[]{:S(2)}, u32[]{:S(2)}) collective-permute-start(bf16[64,32,128]{2,1,0:T(8,128)(2,1)S(1)} %collective-permute-done.29.refs_2_.refs_3_), channel_id=1, source_target_pairs={{0,1},{1,0},{2,3},{3,2},{4,5},{5,4},{6,7},{7,6},{8,9},{9,8},{10,11... | collective-permute-start | bytes 1572872 | tf_op jit(solution)/shard_map/ppermute | solution.py:466
  147.6 10.3 %collective-permute-start.46 = (bf16[64,32,128]{2,1,0:T(8,128)(2,1)S(1)}, bf16[64,32,128]{2,1,0:T(8,128)(2,1)S(1)}, u32[]{:S(2)}, u32[]{:S(2)}) collective-permute-start(bf16[64,32,128]{2,1,0:T(8,128)(2,1)S(1)} %collective-permute-done.36.refs_2_.refs_1_), channel_id=1, source_target_pairs={{0,1},{1,0},{2,3},{3,2},{4,5},{5,4},{6,7},{7,6},{8,9},{9,8},{10,11... | collective-permute-start | bytes 1572872 | tf_op jit(solution)/shard_map/ppermute | solution.py:466
  148.0 9.8 %collective-permute-start.45 = (bf16[64,32,128]{2,1,0:T(8,128)(2,1)S(1)}, bf16[64,32,128]{2,1,0:T(8,128)(2,1)S(1)}, u32[]{:S(2)}, u32[]{:S(2)}) collective-permute-start(bf16[64,32,128]{2,1,0:T(8,128)(2,1)S(1)} %collective-permute-done.31.refs_2_.refs_0_), channel_id=1, source_target_pairs={{0,1},{1,0},{2,3},{3,2},{4,5},{5,4},{6,7},{7,6},{8,9},{9,8},{10,11... | collective-permute-start | bytes 1572872 | tf_op jit(solution)/shard_map/ppermute | solution.py:466
  149.3 14.2 %collective-permute-start.40 = (bf16[64,32,128]{2,1,0:T(8,128)(2,1)S(1)}, bf16[64,32,128]{2,1,0:T(8,128)(2,1)S(1)}, u32[]{:S(2)}, u32[]{:S(2)}) collective-permute-start(bf16[64,32,128]{2,1,0:T(8,128)(2,1)S(1)} %get-tuple-element.61.refs_3_), channel_id=1, source_target_pairs={{0,2},{7,5},{2,4},{5,3},{4,6},{3,1},{8,10},{15,13},{10,12},{13,11}... | collective-permute-start | bytes 1572872 | tf_op jit(solution)/shard_map/ppermute | solution.py:475
  154.9 11.5 %collective-permute-start.39 = (bf16[64,32,128]{2,1,0:T(8,128)(2,1)S(1)}, bf16[64,32,128]{2,1,0:T(8,128)(2,1)S(1)}, u32[]{:S(2)}, u32[]{:S(2)}) collective-permute-start(bf16[64,32,128]{2,1,0:T(8,128)(2,1)S(1)} %get-tuple-element.63.refs_14_.refs_1_.refs_3_), channel_id=1, source_target_pairs={{0,2},{7,5},{2,4},{5,3},{4,6},{3,1},{8,10},{15,13},{10,12},{13,11}... | collective-permute-start | bytes 1572872 | tf_op jit(solution)/shard_map/ppermute | solution.py:475
  161.9 17.9 %collective-permute-start.49 = (bf16[64,64,128]{2,1,0:T(8,128)(2,1)S(1)}, bf16[64,64,128]{2,1,0:T(8,128)(2,1)S(1)}, u32[]{:S(2)}, u32[]{:S(2)}) collective-permute-start(bf16[64,64,128]{2,1,0:T(8,128)(2,1)S(1)} %get-tuple-element.64.refs_2_), channel_id=1, source_target_pairs={{0,8},{1,17},{2,10},{3,19},{4,12},{5,21},{6,14},{7,23},{8,0},{9,25... | collective-permute-start | bytes 3145736 | tf_op jit(solution)/shard_map/ppermute | solution.py:463
  163.7 9.4 %collective-permute-start.48 = (bf16[64,32,128]{2,1,0:T(8,128)(2,1)S(1)}, bf16[64,32,128]{2,1,0:T(8,128)(2,1)S(1)}, u32[]{:S(2)}, u32[]{:S(2)}) collective-permute-start(bf16[64,32,128]{2,1,0:T(8,128)(2,1)S(1)} %add_up.46.refs_1_), channel_id=1, source_target_pairs={{0,2},{7,5},{2,4},{5,3},{4,6},{3,1},{8,10},{15,13},{10,12},{13,11}... | collective-permute-start | bytes 1572872 | tf_op jit(solution)/shard_map/ppermute | solution.py:475
  173.2 11.1 %collective-permute-start.51 = (bf16[64,32,128]{2,1,0:T(8,128)(2,1)S(1)}, bf16[64,32,128]{2,1,0:T(8,128)(2,1)S(1)}, u32[]{:S(2)}, u32[]{:S(2)}) collective-permute-start(bf16[64,32,128]{2,1,0:T(8,128)(2,1)S(1)} %add_up.48.refs_1_), channel_id=1, source_target_pairs={{0,2},{7,5},{2,4},{5,3},{4,6},{3,1},{8,10},{15,13},{10,12},{13,11}... | collective-permute-start | bytes 1572872 | tf_op jit(solution)/shard_map/ppermute | solution.py:475
  177.6 12.3 %collective-permute-start.47 = (bf16[64,32,128]{2,1,0:T(8,128)(2,1)S(1)}, bf16[64,32,128]{2,1,0:T(8,128)(2,1)S(1)}, u32[]{:S(2)}, u32[]{:S(2)}) collective-permute-start(bf16[64,32,128]{2,1,0:T(8,128)(2,1)S(1)} %add_up.47.refs_1_), channel_id=1, source_target_pairs={{0,2},{7,5},{2,4},{5,3},{4,6},{3,1},{8,10},{15,13},{10,12},{13,11}... | collective-permute-start | bytes 1572872 | tf_op jit(solution)/shard_map/ppermute | solution.py:475
  179.7 14.7 %collective-permute-start.52 = (bf16[64,32,128]{2,1,0:T(8,128)(2,1)S(1)}, bf16[64,32,128]{2,1,0:T(8,128)(2,1)S(1)}, u32[]{:S(2)}, u32[]{:S(2)}) collective-permute-start(bf16[64,32,128]{2,1,0:T(8,128)(2,1)S(1)} %collective-permute-done.40.refs_0_.refs_2_), channel_id=1, source_target_pairs={{0,1},{1,0},{2,3},{3,2},{4,5},{5,4},{6,7},{7,6},{8,9},{9,8},{10,11... | collective-permute-start | bytes 1572872 | tf_op jit(solution)/shard_map/ppermute | solution.py:466
  179.9 14.6 %collective-permute-start.55 = (bf16[32,64,128]{2,1,0:T(8,128)(2,1)S(1)}, bf16[32,64,128]{2,1,0:T(8,128)(2,1)S(1)}, u32[]{:S(2)}, u32[]{:S(2)}) collective-permute-start(bf16[32,64,128]{2,1,0:T(8,128)(2,1)S(1)} %add_up.50), channel_id=1, source_target_pairs={{0,16},{1,9},{2,18},{3,11},{4,20},{5,13},{6,22},{7,15},{8,24},{9,1... | collective-permute-start | bytes 1572872 | tf_op jit(solution)/shard_map/ppermute | solution.py:463
  180.3 14.7 %collective-permute-start.53 = (bf16[64,32,128]{2,1,0:T(8,128)(2,1)S(1)}, bf16[64,32,128]{2,1,0:T(8,128)(2,1)S(1)}, u32[]{:S(2)}, u32[]{:S(2)}) collective-permute-start(bf16[64,32,128]{2,1,0:T(8,128)(2,1)S(1)} %collective-permute-done.48.refs_0_.refs_1_), channel_id=1, source_target_pairs={{0,1},{1,0},{2,3},{3,2},{4,5},{5,4},{6,7},{7,6},{8,9},{9,8},{10,11... | collective-permute-start | bytes 1572872 | tf_op jit(solution)/shard_map/ppermute | solution.py:466
  184.3 10.7 %collective-permute-start.54 = (bf16[64,32,128]{2,1,0:T(8,128)(2,1)S(1)}, bf16[64,32,128]{2,1,0:T(8,128)(2,1)S(1)}, u32[]{:S(2)}, u32[]{:S(2)}) collective-permute-start(bf16[64,32,128]{2,1,0:T(8,128)(2,1)S(1)} %collective-permute-done.51.refs_0_), channel_id=1, source_target_pairs={{0,1},{1,0},{2,3},{3,2},{4,5},{5,4},{6,7},{7,6},{8,9},{9,8},{10,11... | collective-permute-start | bytes 1572872 | tf_op jit(solution)/shard_map/ppermute | solution.py:466
  190.0 11.1 %collective-permute-start.50 = (bf16[64,32,128]{2,1,0:T(8,128)(2,1)S(1)}, bf16[64,32,128]{2,1,0:T(8,128)(2,1)S(1)}, u32[]{:S(2)}, u32[]{:S(2)}) collective-permute-start(bf16[64,32,128]{2,1,0:T(8,128)(2,1)S(1)} %add_up.49), channel_id=1, source_target_pairs={{0,2},{7,5},{2,4},{5,3},{4,6},{3,1},{8,10},{15,13},{10,12},{13,11}... | collective-permute-start | bytes 1572872 | tf_op jit(solution)/shard_map/ppermute | solution.py:475
  194.4 7.3 %collective-permute-start.56 = (bf16[64,32,128]{2,1,0:T(8,128)(2,1)S(1)}, bf16[64,32,128]{2,1,0:T(8,128)(2,1)S(1)}, u32[]{:S(2)}, u32[]{:S(2)}) collective-permute-start(bf16[64,32,128]{2,1,0:T(8,128)(2,1)S(1)} %collective-permute-done.39.refs_0_.refs_2_), channel_id=1, source_target_pairs={{0,1},{1,0},{2,3},{3,2},{4,5},{5,4},{6,7},{7,6},{8,9},{9,8},{10,11... | collective-permute-start | bytes 1572872 | tf_op jit(solution)/shard_map/ppermute | solution.py:466
  194.5 7.2 %collective-permute-start.57 = (bf16[64,32,128]{2,1,0:T(8,128)(2,1)S(1)}, bf16[64,32,128]{2,1,0:T(8,128)(2,1)S(1)}, u32[]{:S(2)}, u32[]{:S(2)}) collective-permute-start(bf16[64,32,128]{2,1,0:T(8,128)(2,1)S(1)} %collective-permute-done.47.refs_0_.refs_1_), channel_id=1, source_target_pairs={{0,1},{1,0},{2,3},{3,2},{4,5},{5,4},{6,7},{7,6},{8,9},{9,8},{10,11... | collective-permute-start | bytes 1572872 | tf_op jit(solution)/shard_map/ppermute | solution.py:466
  201.1 2.0 collective-permute-start.58
  201.2 9.2 %collective-permute-start.59 = (bf16[64,32,128]{2,1,0:T(8,128)(2,1)S(1)}, bf16[64,32,128]{2,1,0:T(8,128)(2,1)S(1)}, u32[]{:S(2)}, u32[]{:S(2)}) collective-permute-start(bf16[64,32,128]{2,1,0:T(8,128)(2,1)S(1)} %get-tuple-element.66.refs_1_), channel_id=1, source_target_pairs={{0,8},{1,17},{2,10},{3,19},{4,12},{5,21},{6,14},{7,23},{8,0},{9,25... | collective-permute-start | bytes 1572872 | tf_op jit(solution)/shard_map/ppermute | solution.py:463
  205.9 12.5 %collective-permute-start.61 = (bf16[64,32,128]{2,1,0:T(8,128)(2,1)S(1)}, bf16[64,32,128]{2,1,0:T(8,128)(2,1)S(1)}, u32[]{:S(2)}, u32[]{:S(2)}) collective-permute-start(bf16[64,32,128]{2,1,0:T(8,128)(2,1)S(1)} %get-tuple-element.67.refs_4_), channel_id=1, source_target_pairs={{0,8},{1,17},{2,10},{3,19},{4,12},{5,21},{6,14},{7,23},{8,0},{9,25... | collective-permute-start | bytes 1572872 | tf_op jit(solution)/shard_map/ppermute | solution.py:463
  211.3 12.6 %collective-permute-start.60 = (bf16[32,32,128]{2,1,0:T(8,128)(2,1)}, bf16[32,32,128]{2,1,0:T(8,128)(2,1)S(1)}, u32[]{:S(2)}, u32[]{:S(2)}) collective-permute-start(bf16[32,32,128]{2,1,0:T(8,128)(2,1)} %add_up.52), channel_id=1, source_target_pairs={{0,16},{1,9},{2,18},{3,11},{4,20},{5,13},{6,22},{7,15},{8,24},{9,1... | collective-permute-start | bytes 786440 | tf_op jit(solution)/shard_map/ppermute | solution.py:463
  219.4 6.7 %collective-permute-start.62 = (bf16[32,32,128]{2,1,0:T(8,128)(2,1)}, bf16[32,32,128]{2,1,0:T(8,128)(2,1)}, u32[]{:S(2)}, u32[]{:S(2)}) collective-permute-start(bf16[32,32,128]{2,1,0:T(8,128)(2,1)} %add_up.53), channel_id=1, source_target_pairs={{0,16},{1,9},{2,18},{3,11},{4,20},{5,13},{6,22},{7,15},{8,24},{9,1... | collective-permute-start | bytes 786440 | tf_op jit(solution)/shard_map/ppermute | solution.py:463
  (24 other events, 207.5 us)

commit v6 on v5

--- a/solution.py
+++ b/solution.py
@@ -167,7 +167,7 @@
         kernel,
         in_specs=[IN_VMEM] + [ANY] * len(deps),
         out_specs=IN_VMEM,
-        out_shape=jax.ShapeDtypeStruct((blocks, part, tile), BF16),
+        out_shape=pltpu.VMEM((blocks, part, tile), BF16),
         compiler_params=params(16),
         name="turn_panel",
     )(in_hbm(panel), *deps)
@@ -230,7 +230,7 @@
     slot_count = 2 * chips - 1
     n_in = len(blocks)
     chip_list = 3 * slots
-    pieces = math.gcd(slots, 5)
+    pieces = math.gcd(slots, 2 if source is None else 5)
     piece = slots // pieces
 
     def kernel(index_ref, *refs):
@@ -296,7 +296,7 @@
                 arriving(at).wait()
             over_tiles(
                 piece,
-                32,
+                80 if source is None else 32,
                 lambda n: product(at * piece + n),
                 lambda n, found: add(at * piece + n, found),
             )

time: 230 us -> 229 us (level)
  transfers between devices with their start and end apart: 63 -> 63, of which waited for: 21 -> 22; matrix products, arithmetic and copies ran while one was open for 0% -> 0% of each run, Pallas kernels for 18% -> 18%
where the time goes in v6:
time: 229 us; the launch traced here: 228 us
  starting transfers between devices  112 us (49%)
  waiting for transfers between devices  57.7 us (25%)
  Pallas kernels  54 us (24%)
  local copies, waits for them, and re-layouts  3.22 us (1%)
    ppermute x20, starting transfers between devices, along(): return lax.ppermute(x, 'col', pairs)  77.7 us
    ppermute x20, waiting for transfers between devices, along(): return lax.ppermute(x, 'col', pairs)  29.7 us
    pallas_call x2, Pallas kernels, word_products(): pl.pallas_call(kernel, in_specs=[IN_SMEM] + operand_specs + [ANY] * (n_in...  16.2 us
    pallas_call x27, Pallas kernels, add_up(): pl.pallas_call(kernel, grid_spec=pltpu.PrefetchScalarGridSpec(num_scalar_...  14.6 us
    ppermute x12, waiting for transfers between devices, row_swap(): return lax.ppermute(x, ('row', 'col'), pairs)  14.3 us
    ppermute x26, starting transfers between devices, core_swap(): lax.ppermute(x, 'col', [(i, i ^ 1) for i in range(n_col) if keep(i % 2, i...  13.7 us
    ppermute x12, starting transfers between devices, row_swap(): return lax.ppermute(x, ('row', 'col'), pairs)  12.7 us
    pallas_call x3, Pallas kernels, context_products(): pl.pallas_call(kernel, in_specs=[IN_SMEM, IN_VMEM] + [ANY] * (slot_count...  9.52 us
  transfers between devices with their start and end apart: 63, of which 22 were waited for; matrix products, arithmetic and copies ran while one was open for 0% of the time, Pallas kernels for 18%

profile of v6, /device:TPU:0, one launch (start us, length us, event | category | flops | bytes accessed | tf_op | source)
XLA Modules:
  0.0 228.4 jit_solution(7498758235734892137)
XLA Ops:
  0.6 1.5 turn_panel.2.refs_0_.refs_5_
  2.2 3.0 %collective-permute-start.8 = (bf16[32,64,128]{2,1,0:T(8,128)(2,1)S(1)}, bf16[32,64,128]{2,1,0:T(8,128)(2,1)S(1)}, u32[]{:S(2)}, u32[]{:S(2)}) collective-permute-start(bf16[32,64,128]{2,1,0:T(8,128)(2,1)S(1)} %turn_panel.2.refs_0_.refs_5_), channel_id=1, source_target_pairs={{0,8},{1,17},{2,10},{3,19},{4,12},{5,21},{6,14},{7,23},{8,0},{9,25... | collective-permute-start | bytes 1572872 | tf_op jit(solution)/shard_map/ppermute | solution.py:463
  5.2 4.8 %count_sums.1 = (f32[256,128]{1,0:T(8,128)S(1)}, f32[128,128]{1,0:T(8,128)S(1)}) custom-call(s32[160,128,128]{2,1,0:T(8,128)} %bitcast.8, s32[160]{0:T(256)} %bitcast.13, s32[160]{0:T(256)} %bitcast.10, bf16[32,64,128]{2,1,0:T(8,128)(2,1)S(1)} %turn_panel.2.refs_0_.refs_5_), custom_call_target="tpu_custom_call" | custom-call | bytes 36900 | tf_op jit(solution)/shard_map/count_sums/pallas_call | solution.py:90
  10.1 2.0 collective-permute-start.1
  12.1 1.4 collective-permute-start.2
  13.6 1.5 collective-permute-start.7
  15.6 2.5 %collective-permute-done.2.refs_3_ = f32[128,128]{1,0:T(8,128)S(1)} collective-permute-done((f32[128,128]{1,0:T(8,128)S(1)}, f32[128,128]{1,0:T(8,128)S(1)}, u32[]{:S(2)}, u32[]{:S(2)}) %collective-permute-start.2) | collective-permute-done | bytes 65568 | tf_op jit(solution)/shard_map/ppermute | solution.py:478
  19.5 1.6 collective-permute-start.4
  21.1 2.7 %collective-permute-done.4.b_ref = f32[136,128]{1,0:T(8,128)S(1)} collective-permute-done((f32[136,128]{1,0:T(8,128)S(1)}, f32[136,128]{1,0:T(8,128)S(1)}, u32[]{:S(2)}, u32[]{:S(2)}) %collective-permute-start.4) | collective-permute-done | bytes 69664 | tf_op jit(solution)/shard_map/ppermute | solution.py:481
  23.9 2.7 %collective-permute-start.5 = (f32[136,128]{1,0:T(8,128)S(1)}, f32[136,128]{1,0:T(8,128)S(1)}, u32[]{:S(2)}, u32[]{:S(2)}) collective-permute-start(f32[136,128]{1,0:T(8,128)S(1)} %plus.4.a_ref), channel_id=1, source_target_pairs={{0,4},{1,5},{2,6},{3,7},{4,0},{5,1},{6,2},{7,3},{8,12},{9,13},{10,... | collective-permute-start | bytes 208904 | tf_op jit(solution)/shard_map/ppermute | solution.py:481
  26.5 2.7 %collective-permute-done.5.b_ref = f32[136,128]{1,0:T(8,128)S(1)} collective-permute-done((f32[136,128]{1,0:T(8,128)S(1)}, f32[136,128]{1,0:T(8,128)S(1)}, u32[]{:S(2)}, u32[]{:S(2)}) %collective-permute-start.5) | collective-permute-done | bytes 69664 | tf_op jit(solution)/shard_map/ppermute | solution.py:481
  31.4 9.2 %ppmi_word_products.1 = (bf16[160,128,128]{2,1,0:T(8,128)(2,1)S(1)}, bf16[64,64,128]{2,1,0:T(8,128)(2,1)S(1)}, bf16[64,64,128]{2,1,0:T(8,128)(2,1)S(1)}, bf16[64...) custom-call(s32[487]{0:T(512)S(1)} %pad_add_fusion.index_ref, ...), custom_call_target="tpu_custom_call" | custom-call | bytes 36900 | tf_op jit(solution)/shard_map/ppmi_word_products/pallas_call | solution.py:338
  40.6 1.3 collective-permute-start.12
  41.9 1.3 collective-permute-start.11
  43.2 2.0 collective-permute-done.12.refs_1_
  45.5 1.3 collective-permute-start.13
  46.8 1.3 collective-permute-start.10
  48.5 5.0 %collective-permute-start.15 = (bf16[64,32,128]{2,1,0:T(8,128)(2,1)S(1)}, bf16[64,32,128]{2,1,0:T(8,128)(2,1)S(1)}, u32[]{:S(2)}, u32[]{:S(2)}) collective-permute-start(bf16[64,32,128]{2,1,0:T(8,128)(2,1)S(1)} %add_up.28.refs_3_.refs_2_), channel_id=1, source_target_pairs={{0,2},{7,5},{2,4},{5,3},{4,6},{3,1},{8,10},{15,13},{10,12},{13,11}... | collective-permute-start | bytes 1572872 | tf_op jit(solution)/shard_map/ppermute | solution.py:475
  53.5 1.6 turn_panel.3.refs_1_
  55.1 1.7 collective-permute-start.23
  57.2 5.1 %collective-permute-start.14 = (bf16[64,32,128]{2,1,0:T(8,128)(2,1)S(1)}, bf16[64,32,128]{2,1,0:T(8,128)(2,1)S(1)}, u32[]{:S(2)}, u32[]{:S(2)}) collective-permute-start(bf16[64,32,128]{2,1,0:T(8,128)(2,1)S(1)} %add_up.29.refs_3_), channel_id=1, source_target_pairs={{0,2},{7,5},{2,4},{5,3},{4,6},{3,1},{8,10},{15,13},{10,12},{13,11}... | collective-permute-start | bytes 1572872 | tf_op jit(solution)/shard_map/ppermute | solution.py:475
  62.8 2.9 %collective-permute-start.19 = (bf16[64,32,128]{2,1,0:T(8,128)(2,1)S(1)}, bf16[64,32,128]{2,1,0:T(8,128)(2,1)S(1)}, u32[]{:S(2)}, u32[]{:S(2)}) collective-permute-start(bf16[64,32,128]{2,1,0:T(8,128)(2,1)S(1)} %add_up.30.refs_3_.refs_1_), channel_id=1, source_target_pairs={{0,2},{7,5},{2,4},{5,3},{4,6},{3,1},{8,10},{15,13},{10,12},{13,11}... | collective-permute-start | bytes 1572872 | tf_op jit(solution)/shard_map/ppermute | solution.py:475
  66.4 1.7 collective-permute-start.24
  69.4 4.4 %collective-permute-start.16 = (bf16[64,32,128]{2,1,0:T(8,128)(2,1)S(1)}, bf16[64,32,128]{2,1,0:T(8,128)(2,1)S(1)}, u32[]{:S(2)}, u32[]{:S(2)}) collective-permute-start(bf16[64,32,128]{2,1,0:T(8,128)(2,1)S(1)} %add_up.31.refs_3_), channel_id=1, source_target_pairs={{0,2},{7,5},{2,4},{5,3},{4,6},{3,1},{8,10},{15,13},{10,12},{13,11}... | collective-permute-start | bytes 1572872 | tf_op jit(solution)/shard_map/ppermute | solution.py:475
  75.0 4.4 %collective-permute-start.20 = (bf16[64,32,128]{2,1,0:T(8,128)(2,1)S(1)}, bf16[64,32,128]{2,1,0:T(8,128)(2,1)S(1)}, u32[]{:S(2)}, u32[]{:S(2)}) collective-permute-start(bf16[64,32,128]{2,1,0:T(8,128)(2,1)S(1)} %add_up.33.refs_3_.refs_5_), channel_id=1, source_target_pairs={{0,2},{7,5},{2,4},{5,3},{4,6},{3,1},{8,10},{15,13},{10,12},{13,11}... | collective-permute-start | bytes 1572872 | tf_op jit(solution)/shard_map/ppermute | solution.py:475
  80.7 6.9 %word_products.1 = (bf16[64,64,128]{2,1,0:T(8,128)(2,1)}, bf16[64,64,128]{2,1,0:T(8,128)(2,1)}, bf16[64,64,128]{2,1,0:T(8,128)(2,1)S(1)}, bf16[64,64,128]{2,1,0:...) custom-call(s32[487]{0:T(512)S(1)} %pad_add_fusion.index_ref, ...), custom_call_target="tpu_custom_call" | custom-call | bytes 36900 | tf_op jit(solution)/shard_map/word_products/pallas_call | solution.py:338
  87.8 1.5 collective-permute-start.27
  89.2 1.9 collective-permute-start.21
  91.5 1.3 add_up.34
  92.8 3.9 %collective-permute-start.28 = (bf16[64,32,128]{2,1,0:T(8,128)(2,1)}, bf16[64,32,128]{2,1,0:T(8,128)(2,1)}, u32[]{:S(2)}, u32[]{:S(2)}) collective-permute-start(bf16[64,32,128]{2,1,0:T(8,128)(2,1)} %get-tuple-element.49.refs_3_.refs_6_), channel_id=1, source_target_pairs={{0,2},{7,5},{2,4},{5,3},{4,6},{3,1},{8,10},{15,13},{10,12},{13,11}... | collective-permute-start | bytes 1572872 | tf_op jit(solution)/shard_map/ppermute | solution.py:475
  96.7 1.3 collective-permute-start.26
  98.0 1.3 add_up.35
  99.3 3.4 %collective-permute-start.30 = (bf16[64,32,128]{2,1,0:T(8,128)(2,1)}, bf16[64,32,128]{2,1,0:T(8,128)(2,1)}, u32[]{:S(2)}, u32[]{:S(2)}) collective-permute-start(bf16[64,32,128]{2,1,0:T(8,128)(2,1)} %get-tuple-element.58.refs_3_.refs_7_), channel_id=1, source_target_pairs={{0,2},{7,5},{2,4},{5,3},{4,6},{3,1},{8,10},{15,13},{10,12},{13,11}... | collective-permute-start | bytes 1572872 | tf_op jit(solution)/shard_map/ppermute | solution.py:475
  104.1 1.5 add_up.37.refs_3_
  105.6 4.3 %collective-permute-start.29 = (bf16[64,32,128]{2,1,0:T(8,128)(2,1)S(1)}, bf16[64,32,128]{2,1,0:T(8,128)(2,1)S(1)}, u32[]{:S(2)}, u32[]{:S(2)}) collective-permute-start(bf16[64,32,128]{2,1,0:T(8,128)(2,1)S(1)} %add_up.37.refs_3_), channel_id=1, source_target_pairs={{0,2},{7,5},{2,4},{5,3},{4,6},{3,1},{8,10},{15,13},{10,12},{13,11}... | collective-permute-start | bytes 1572872 | tf_op jit(solution)/shard_map/ppermute | solution.py:475
  110.0 1.3 collective-permute-start.25
  111.3 1.4 add_up.38.refs_4_.refs_2_
  112.7 3.9 %collective-permute-start.32 = (bf16[64,32,128]{2,1,0:T(8,128)(2,1)S(1)}, bf16[64,32,128]{2,1,0:T(8,128)(2,1)S(1)}, u32[]{:S(2)}, u32[]{:S(2)}) collective-permute-start(bf16[64,32,128]{2,1,0:T(8,128)(2,1)S(1)} %add_up.38.refs_4_.refs_2_), channel_id=1, source_target_pairs={{0,2},{7,5},{2,4},{5,3},{4,6},{3,1},{8,10},{15,13},{10,12},{13,11}... | collective-permute-start | bytes 1572872 | tf_op jit(solution)/shard_map/ppermute | solution.py:475
  116.9 4.6 %collective-permute-start.31 = (bf16[64,32,128]{2,1,0:T(8,128)(2,1)S(1)}, bf16[64,32,128]{2,1,0:T(8,128)(2,1)S(1)}, u32[]{:S(2)}, u32[]{:S(2)}) collective-permute-start(bf16[64,32,128]{2,1,0:T(8,128)(2,1)S(1)} %add_up.39.refs_4_), channel_id=1, source_target_pairs={{0,2},{7,5},{2,4},{5,3},{4,6},{3,1},{8,10},{15,13},{10,12},{13,11}... | collective-permute-start | bytes 1572872 | tf_op jit(solution)/shard_map/ppermute | solution.py:475
  121.5 1.7 collective-permute-done.32.refs_2_.refs_3_
  123.5 4.4 %collective-permute-start.36 = (bf16[64,32,128]{2,1,0:T(8,128)(2,1)S(1)}, bf16[64,32,128]{2,1,0:T(8,128)(2,1)S(1)}, u32[]{:S(2)}, u32[]{:S(2)}) collective-permute-start(bf16[64,32,128]{2,1,0:T(8,128)(2,1)S(1)} %add_up.40.refs_3_), channel_id=1, source_target_pairs={{0,2},{7,5},{2,4},{5,3},{4,6},{3,1},{8,10},{15,13},{10,12},{13,11}... | collective-permute-start | bytes 1572872 | tf_op jit(solution)/shard_map/ppermute | solution.py:475
  129.3 4.4 %collective-permute-start.33 = (bf16[64,32,128]{2,1,0:T(8,128)(2,1)S(1)}, bf16[64,32,128]{2,1,0:T(8,128)(2,1)S(1)}, u32[]{:S(2)}, u32[]{:S(2)}) collective-permute-start(bf16[64,32,128]{2,1,0:T(8,128)(2,1)S(1)} %add_up.41.refs_3_), channel_id=1, source_target_pairs={{0,2},{7,5},{2,4},{5,3},{4,6},{3,1},{8,10},{15,13},{10,12},{13,11}... | collective-permute-start | bytes 1572872 | tf_op jit(solution)/shard_map/ppermute | solution.py:475
  135.1 4.7 %collective-permute-start.37 = (bf16[64,32,128]{2,1,0:T(8,128)(2,1)S(1)}, bf16[64,32,128]{2,1,0:T(8,128)(2,1)S(1)}, u32[]{:S(2)}, u32[]{:S(2)}) collective-permute-start(bf16[64,32,128]{2,1,0:T(8,128)(2,1)S(1)} %add_up.43.refs_3_), channel_id=1, source_target_pairs={{0,2},{7,5},{2,4},{5,3},{4,6},{3,1},{8,10},{15,13},{10,12},{13,11}... | collective-permute-start | bytes 1572872 | tf_op jit(solution)/shard_map/ppermute | solution.py:475
  140.6 5.8 %collective-permute-done.37.refs_0_ = bf16[64,32,128]{2,1,0:T(8,128)(2,1)S(1)} collective-permute-done((bf16[64,32,128]{2,1,0:T(8,128)(2,1)S(1)}, bf16[64,32,128]{2,1,0:T(8,128)(2,1)S(1)}, u32[]{:S(2)}, u32[]{:S(2)}) %collective-permute-start.37) | collective-permute-done | bytes 524320 | tf_op jit(solution)/shard_map/ppermute | solution.py:475
  149.0 4.4 %collective-permute-start.40 = (bf16[64,32,128]{2,1,0:T(8,128)(2,1)S(1)}, bf16[64,32,128]{2,1,0:T(8,128)(2,1)S(1)}, u32[]{:S(2)}, u32[]{:S(2)}) collective-permute-start(bf16[64,32,128]{2,1,0:T(8,128)(2,1)S(1)} %get-tuple-element.61.refs_3_), channel_id=1, source_target_pairs={{0,2},{7,5},{2,4},{5,3},{4,6},{3,1},{8,10},{15,13},{10,12},{13,11}... | collective-permute-start | bytes 1572872 | tf_op jit(solution)/shard_map/ppermute | solution.py:475
  154.6 2.9 %collective-permute-start.39 = (bf16[64,32,128]{2,1,0:T(8,128)(2,1)S(1)}, bf16[64,32,128]{2,1,0:T(8,128)(2,1)S(1)}, u32[]{:S(2)}, u32[]{:S(2)}) collective-permute-start(bf16[64,32,128]{2,1,0:T(8,128)(2,1)S(1)} %get-tuple-element.63.refs_14_.refs_1_.refs_3_), channel_id=1, source_target_pairs={{0,2},{7,5},{2,4},{5,3},{4,6},{3,1},{8,10},{15,13},{10,12},{13,11}... | collective-permute-start | bytes 1572872 | tf_op jit(solution)/shard_map/ppermute | solution.py:475
  157.6 3.9 %context_products.3 = (bf16[64,64,128]{2,1,0:T(8,128)(2,1)S(1)}, f32[64,64,128]{2,1,0:T(8,128)S(1)}) custom-call(s32[487]{0:T(512)S(1)} %pad_add_fusion.index_ref, bf16[160,128,128]{2,1,0:T(8,128)(2,1)S(1)} %bitcast.7, bf16[64,32,128]{2,1,0:T(8,128)(2,1)S(1)} %collective-permute-done.31.refs_2_.refs_0_, ...), custom_call_target="tpu_custom_call" | custom-call | bytes 36900 | tf_op jit(solution)/shard_map/context_products/pallas_call | solution.py:397
  161.5 1.7 collective-permute-start.49
  163.3 2.8 %collective-permute-start.48 = (bf16[64,32,128]{2,1,0:T(8,128)(2,1)S(1)}, bf16[64,32,128]{2,1,0:T(8,128)(2,1)S(1)}, u32[]{:S(2)}, u32[]{:S(2)}) collective-permute-start(bf16[64,32,128]{2,1,0:T(8,128)(2,1)S(1)} %add_up.46.refs_1_), channel_id=1, source_target_pairs={{0,2},{7,5},{2,4},{5,3},{4,6},{3,1},{8,10},{15,13},{10,12},{13,11}... | collective-permute-start | bytes 1572872 | tf_op jit(solution)/shard_map/ppermute | solution.py:475
  166.2 6.5 %collective-permute-done.48.refs_0_.refs_1_ = bf16[64,32,128]{2,1,0:T(8,128)(2,1)S(1)} collective-permute-done((bf16[64,32,128]{2,1,0:T(8,128)(2,1)S(1)}, bf16[64,32,128]{2,1,0:T(8,128)(2,1)S(1)}, u32[]{:S(2)}, u32[]{:S(2)}) %collective-permute-start.48) | collective-permute-done | bytes 524320 | tf_op jit(solution)/shard_map/ppermute | solution.py:475
  172.9 4.4 %collective-permute-start.51 = (bf16[64,32,128]{2,1,0:T(8,128)(2,1)S(1)}, bf16[64,32,128]{2,1,0:T(8,128)(2,1)S(1)}, u32[]{:S(2)}, u32[]{:S(2)}) collective-permute-start(bf16[64,32,128]{2,1,0:T(8,128)(2,1)S(1)} %add_up.48.refs_1_), channel_id=1, source_target_pairs={{0,2},{7,5},{2,4},{5,3},{4,6},{3,1},{8,10},{15,13},{10,12},{13,11}... | collective-permute-start | bytes 1572872 | tf_op jit(solution)/shard_map/ppermute | solution.py:475
  177.3 2.0 collective-permute-start.47
  180.9 3.1 %collective-permute-done.51.refs_0_ = bf16[64,32,128]{2,1,0:T(8,128)(2,1)S(1)} collective-permute-done((bf16[64,32,128]{2,1,0:T(8,128)(2,1)S(1)}, bf16[64,32,128]{2,1,0:T(8,128)(2,1)S(1)}, u32[]{:S(2)}, u32[]{:S(2)}) %collective-permute-start.51) | collective-permute-done | bytes 524320 | tf_op jit(solution)/shard_map/ppermute | solution.py:475
  183.9 5.6 %collective-permute-done.47.refs_0_.refs_1_ = bf16[64,32,128]{2,1,0:T(8,128)(2,1)S(1)} collective-permute-done((bf16[64,32,128]{2,1,0:T(8,128)(2,1)S(1)}, bf16[64,32,128]{2,1,0:T(8,128)(2,1)S(1)}, u32[]{:S(2)}, u32[]{:S(2)}) %collective-permute-start.47) | collective-permute-done | bytes 524320 | tf_op jit(solution)/shard_map/ppermute | solution.py:475
  189.7 4.4 %collective-permute-start.50 = (bf16[64,32,128]{2,1,0:T(8,128)(2,1)S(1)}, bf16[64,32,128]{2,1,0:T(8,128)(2,1)S(1)}, u32[]{:S(2)}, u32[]{:S(2)}) collective-permute-start(bf16[64,32,128]{2,1,0:T(8,128)(2,1)S(1)} %add_up.49), channel_id=1, source_target_pairs={{0,2},{7,5},{2,4},{5,3},{4,6},{3,1},{8,10},{15,13},{10,12},{13,11}... | collective-permute-start | bytes 1572872 | tf_op jit(solution)/shard_map/ppermute | solution.py:475
  194.7 2.8 %context_products.4 = (bf16[64,32,128]{2,1,0:T(8,128)(2,1)S(1)}, f32[64,32,128]{2,1,0:T(8,128)S(1)}) custom-call(s32[487]{0:T(512)S(1)} %pad_add_fusion.index_ref, bf16[160,128,128]{2,1,0:T(8,128)(2,1)S(1)} %bitcast.7, bf16[64,32,128]{2,1,0:T(8,128)(2,1)S(1)} %collective-permute-done.51.refs_0_, ...), custom_call_target="tpu_custom_call" | custom-call | bytes 36900 | tf_op jit(solution)/shard_map/context_products/pallas_call | solution.py:397
  197.5 3.2 %collective-permute-done.50.refs_0_ = bf16[64,32,128]{2,1,0:T(8,128)(2,1)S(1)} collective-permute-done((bf16[64,32,128]{2,1,0:T(8,128)(2,1)S(1)}, bf16[64,32,128]{2,1,0:T(8,128)(2,1)S(1)}, u32[]{:S(2)}, u32[]{:S(2)}) %collective-permute-start.50) | collective-permute-done | bytes 524320 | tf_op jit(solution)/shard_map/ppermute | solution.py:475
  201.4 1.4 collective-permute-done.58.refs_6_
  202.8 2.8 %context_products.5 = (bf16[64,32,128]{2,1,0:T(8,128)(2,1)S(1)}, f32[64,32,128]{2,1,0:T(8,128)S(1)}) custom-call(s32[487]{0:T(512)S(1)} %pad_add_fusion.index_ref, bf16[160,128,128]{2,1,0:T(8,128)(2,1)S(1)} %bitcast.7, bf16[64,32,128]{2,1,0:T(8,128)(2,1)S(1)} %add_up.51.refs_0_, bf16[64,32,128]{2,1,0:T(8,128)(2,1)S(1)} %collective-permute-done.47.refs_0_.refs_1_, ...), custom_call_target="tpu_custom_call" | custom-call | bytes 36900 | tf_op jit(solution)/shard_map/context_products/pallas_call | solution.py:397
  206.1 4.1 %collective-permute-done.59.refs_1_.refs_4_ = bf16[64,32,128]{2,1,0:T(8,128)(2,1)S(1)} collective-permute-done((bf16[64,32,128]{2,1,0:T(8,128)(2,1)S(1)}, bf16[64,32,128]{2,1,0:T(8,128)(2,1)S(1)}, u32[]{:S(2)}, u32[]{:S(2)}) %collective-permute-start.59) | collective-permute-done | bytes 524320 | tf_op jit(solution)/shard_map/ppermute | solution.py:463
  211.3 6.8 %collective-permute-done.61.refs_1_.refs_7_ = bf16[64,32,128]{2,1,0:T(8,128)(2,1)S(1)} collective-permute-done((bf16[64,32,128]{2,1,0:T(8,128)(2,1)S(1)}, bf16[64,32,128]{2,1,0:T(8,128)(2,1)S(1)}, u32[]{:S(2)}, u32[]{:S(2)}) %collective-permute-start.61) | collective-permute-done | bytes 524320 | tf_op jit(solution)/shard_map/ppermute | solution.py:463
  220.5 3.1 %turn_back.2 = f32[4096,128]{1,0:T(8,128)} custom-call(s32[1]{0:T(128)S(6)} %select_n.44.start_ref, f32[64,32,128]{2,1,0:T(8,128)} %get-tuple-element.48.refs_0_, f32[64,32,128]{2,1,0:T(8,128)} %get-tuple-element.50.refs_1_, f32[64,32,128]{2,1,0:T(8,128)} %get-tuple-element.60.refs_2_, f32[64,32,128]{2,1,0:T(8,128)} %get-tuple-element.62.refs_3_, ...), custom_call_target="tpu_custom_call" | custom-call | bytes 36900 | tf_op jit(solution)/shard_map/turn_back/pallas_call | solution.py:428
  223.5 2.2 collective-permute-done.62.refs_8_
  225.8 2.6 %turn_back.3 = f32[4096,128]{1,0:T(8,128)} custom-call(s32[1]{0:T(128)} %constant.92.clone.1.place_ref.start_ref, f32[64,64,128]{2,1,0:T(8,128)S(1)} %get-tuple-element.65.refs_0_, bf16[64,64,128]{2,1,0:T(8,128)(2,1)S(1)} %collective-permute-done.49.refs_2_.refs_1_, bf16[32,64,128]{2,1,0:T(8,128)(2,1)S(1)} %copy-done.2, f32[64,32,128]{2,1,0:T(8,128)S(1)} %copy-done.4, ...), custom_call_target="tpu_custom_call" | custom-call | bytes 36900 | tf_op jit(solution)/shard_map/turn_back/pallas_call | solution.py:428
  (157 shorter events, 26.8 us)
Async XLA Ops:
  2.2 12.9 %collective-permute-start.8 = (bf16[32,64,128]{2,1,0:T(8,128)(2,1)S(1)}, bf16[32,64,128]{2,1,0:T(8,128)(2,1)S(1)}, u32[]{:S(2)}, u32[]{:S(2)}) collective-permute-start(bf16[32,64,128]{2,1,0:T(8,128)(2,1)S(1)} %turn_panel.2.refs_0_.refs_5_), channel_id=1, source_target_pairs={{0,8},{1,17},{2,10},{3,19},{4,12},{5,21},{6,14},{7,23},{8,0},{9,25... | collective-permute-start | bytes 1572872 | tf_op jit(solution)/shard_map/ppermute | solution.py:463
  10.0 5.6 %collective-permute-start = (f32[128,128]{1,0:T(8,128)S(1)}, f32[128,128]{1,0:T(8,128)S(1)}, u32[]{:S(2)}, u32[]{:S(2)}) collective-permute-start(f32[128,128]{1,0:T(8,128)S(1)} %get-tuple-element.37.refs_0_), channel_id=1, source_target_pairs={{0,8},{8,0},{16,24},{24,16},{1,9},{9,1},{17,25},{25,17},{2,10},{10... | collective-permute-start | bytes 196616 | tf_op jit(solution)/shard_map/ppermute | solution.py:478
  10.1 5.5 %collective-permute-start.1 = (f32[128,128]{1,0:T(8,128)S(1)}, f32[128,128]{1,0:T(8,128)S(1)}, u32[]{:S(2)}, u32[]{:S(2)}) collective-permute-start(f32[128,128]{1,0:T(8,128)S(1)} %get-tuple-element.37.refs_0_), channel_id=1, source_target_pairs={{0,16},{8,24},{16,0},{24,8},{1,17},{9,25},{17,1},{25,9},{2,18},{10... | collective-permute-start | bytes 196616 | tf_op jit(solution)/shard_map/ppermute | solution.py:478
  12.1 5.9 %collective-permute-start.2 = (f32[128,128]{1,0:T(8,128)S(1)}, f32[128,128]{1,0:T(8,128)S(1)}, u32[]{:S(2)}, u32[]{:S(2)}) collective-permute-start(f32[128,128]{1,0:T(8,128)S(1)} %get-tuple-element.37.refs_0_), channel_id=1, source_target_pairs={{0,24},{8,16},{16,8},{24,0},{1,25},{9,17},{17,9},{25,1},{2,26},{10... | collective-permute-start | bytes 196616 | tf_op jit(solution)/shard_map/ppermute | solution.py:478
  13.6 17.0 %collective-permute-start.7 = (bf16[32,64,128]{2,1,0:T(8,128)(2,1)S(1)}, bf16[32,64,128]{2,1,0:T(8,128)(2,1)S(1)}, u32[]{:S(2)}, u32[]{:S(2)}) collective-permute-start(bf16[32,64,128]{2,1,0:T(8,128)(2,1)S(1)} %turn_panel.2.refs_0_.refs_5_), channel_id=1, source_target_pairs={{0,16},{1,9},{2,18},{3,11},{4,20},{5,13},{6,22},{7,15},{8,24},{9,1... | collective-permute-start | bytes 1572872 | tf_op jit(solution)/shard_map/ppermute | solution.py:463
  15.1 15.5 %collective-permute-start.9 = (bf16[32,64,128]{2,1,0:T(8,128)(2,1)S(1)}, bf16[32,64,128]{2,1,0:T(8,128)(2,1)S(1)}, u32[]{:S(2)}, u32[]{:S(2)}) collective-permute-start(bf16[32,64,128]{2,1,0:T(8,128)(2,1)S(1)} %collective-permute-done.8.refs_7_), channel_id=1, source_target_pairs={{0,16},{1,9},{2,18},{3,11},{4,20},{5,13},{6,22},{7,15},{8,24},{9,1... | collective-permute-start | bytes 1572872 | tf_op jit(solution)/shard_map/ppermute | solution.py:463
  18.1 1.3 collective-permute-start.3
  19.5 4.4 %collective-permute-start.4 = (f32[136,128]{1,0:T(8,128)S(1)}, f32[136,128]{1,0:T(8,128)S(1)}, u32[]{:S(2)}, u32[]{:S(2)}) collective-permute-start(f32[136,128]{1,0:T(8,128)S(1)} %plus.3.a_ref), channel_id=1, source_target_pairs={{0,2},{1,3},{2,0},{3,1},{4,6},{5,7},{6,4},{7,5},{8,10},{9,11},{10,... | collective-permute-start | bytes 208904 | tf_op jit(solution)/shard_map/ppermute | solution.py:481
  23.9 5.4 %collective-permute-start.5 = (f32[136,128]{1,0:T(8,128)S(1)}, f32[136,128]{1,0:T(8,128)S(1)}, u32[]{:S(2)}, u32[]{:S(2)}) collective-permute-start(f32[136,128]{1,0:T(8,128)S(1)} %plus.4.a_ref), channel_id=1, source_target_pairs={{0,4},{1,5},{2,6},{3,7},{4,0},{5,1},{6,2},{7,3},{8,12},{9,13},{10,... | collective-permute-start | bytes 208904 | tf_op jit(solution)/shard_map/ppermute | solution.py:481
  29.2 1.3 collective-permute-start.6
  40.6 40.1 %copy-start = (bf16[160,128,128]{2,1,0:T(8,128)(2,1)}, bf16[160,128,128]{2,1,0:T(8,128)(2,1)S(1)}, u32[]{:S(2)}) copy-start(bf16[160,128,128]{2,1,0:T(8,128)(2,1)S(1)} %get-tuple-element.51.refs_0_.tiles_ref) | copy-start | bytes 15728644
  40.6 4.6 %collective-permute-start.12 = (bf16[64,64,128]{2,1,0:T(8,128)(2,1)S(1)}, bf16[64,64,128]{2,1,0:T(8,128)(2,1)S(1)}, u32[]{:S(2)}, u32[]{:S(2)}) collective-permute-start(bf16[64,64,128]{2,1,0:T(8,128)(2,1)S(1)} %get-tuple-element.46), channel_id=1, source_target_pairs={{1,0},{6,7},{9,8},{14,15},{17,16},{22,23},{25,24},{30,31}} | collective-permute-start | bytes 3145736 | tf_op jit(solution)/shard_map/ppermute | solution.py:466
  41.9 14.9 %collective-permute-start.11 = (bf16[64,64,128]{2,1,0:T(8,128)(2,1)S(1)}, bf16[64,64,128]{2,1,0:T(8,128)(2,1)S(1)}, u32[]{:S(2)}, u32[]{:S(2)}) collective-permute-start(bf16[64,64,128]{2,1,0:T(8,128)(2,1)S(1)} %get-tuple-element.44), channel_id=1, source_target_pairs={{1,0},{3,2},{4,5},{6,7},{9,8},{11,10},{12,13},{14,15},{17,16},{19,... | collective-permute-start | bytes 3145736 | tf_op jit(solution)/shard_map/ppermute | solution.py:466
  45.5 11.3 %collective-permute-start.13 = (bf16[64,32,128]{2,1,0:T(8,128)(2,1)S(1)}, bf16[64,32,128]{2,1,0:T(8,128)(2,1)S(1)}, u32[]{:S(2)}, u32[]{:S(2)}) collective-permute-start(bf16[64,32,128]{2,1,0:T(8,128)(2,1)S(1)} %add_up.27.refs_2_.refs_0_), channel_id=1, source_target_pairs={{0,2},{7,5},{2,4},{5,3},{4,6},{3,1},{8,10},{15,13},{10,12},{13,11}... | collective-permute-start | bytes 1572872 | tf_op jit(solution)/shard_map/ppermute | solution.py:475
  46.8 19.6 %collective-permute-start.10 = (bf16[64,64,128]{2,1,0:T(8,128)(2,1)S(1)}, bf16[64,64,128]{2,1,0:T(8,128)(2,1)S(1)}, u32[]{:S(2)}, u32[]{:S(2)}) collective-permute-start(bf16[64,64,128]{2,1,0:T(8,128)(2,1)S(1)} %get-tuple-element.42), channel_id=1, source_target_pairs={{1,0},{2,3},{3,2},{4,5},{5,4},{6,7},{9,8},{10,11},{11,10},{12,13},... | collective-permute-start | bytes 3145736 | tf_op jit(solution)/shard_map/ppermute | solution.py:466
  48.5 13.9 %collective-permute-start.15 = (bf16[64,32,128]{2,1,0:T(8,128)(2,1)S(1)}, bf16[64,32,128]{2,1,0:T(8,128)(2,1)S(1)}, u32[]{:S(2)}, u32[]{:S(2)}) collective-permute-start(bf16[64,32,128]{2,1,0:T(8,128)(2,1)S(1)} %add_up.28.refs_3_.refs_2_), channel_id=1, source_target_pairs={{0,2},{7,5},{2,4},{5,3},{4,6},{3,1},{8,10},{15,13},{10,12},{13,11}... | collective-permute-start | bytes 1572872 | tf_op jit(solution)/shard_map/ppermute | solution.py:475
  55.1 10.7 %collective-permute-start.23 = (bf16[32,64,128]{2,1,0:T(8,128)(2,1)S(1)}, bf16[32,64,128]{2,1,0:T(8,128)(2,1)S(1)}, u32[]{:S(2)}, u32[]{:S(2)}) collective-permute-start(bf16[32,64,128]{2,1,0:T(8,128)(2,1)S(1)} %turn_panel.3.refs_1_), channel_id=1, source_target_pairs={{0,8},{1,17},{2,10},{3,19},{4,12},{5,21},{6,14},{7,23},{8,0},{9,25... | collective-permute-start | bytes 1572872 | tf_op jit(solution)/shard_map/ppermute | solution.py:463
  57.2 11.7 %collective-permute-start.14 = (bf16[64,32,128]{2,1,0:T(8,128)(2,1)S(1)}, bf16[64,32,128]{2,1,0:T(8,128)(2,1)S(1)}, u32[]{:S(2)}, u32[]{:S(2)}) collective-permute-start(bf16[64,32,128]{2,1,0:T(8,128)(2,1)S(1)} %add_up.29.refs_3_), channel_id=1, source_target_pairs={{0,2},{7,5},{2,4},{5,3},{4,6},{3,1},{8,10},{15,13},{10,12},{13,11}... | collective-permute-start | bytes 1572872 | tf_op jit(solution)/shard_map/ppermute | solution.py:475
  62.8 11.8 %collective-permute-start.19 = (bf16[64,32,128]{2,1,0:T(8,128)(2,1)S(1)}, bf16[64,32,128]{2,1,0:T(8,128)(2,1)S(1)}, u32[]{:S(2)}, u32[]{:S(2)}) collective-permute-start(bf16[64,32,128]{2,1,0:T(8,128)(2,1)S(1)} %add_up.30.refs_3_.refs_1_), channel_id=1, source_target_pairs={{0,2},{7,5},{2,4},{5,3},{4,6},{3,1},{8,10},{15,13},{10,12},{13,11}... | collective-permute-start | bytes 1572872 | tf_op jit(solution)/shard_map/ppermute | solution.py:475
  65.7 25.4 %collective-permute-start.18 = (bf16[64,64,128]{2,1,0:T(8,128)(2,1)S(1)}, bf16[64,64,128]{2,1,0:T(8,128)(2,1)S(1)}, u32[]{:S(2)}, u32[]{:S(2)}) collective-permute-start(bf16[64,64,128]{2,1,0:T(8,128)(2,1)S(1)} %get-tuple-element.47.refs_0_), channel_id=1, source_target_pairs={{0,1},{1,0},{2,3},{3,2},{4,5},{5,4},{6,7},{7,6},{8,9},{9,8},{10,11... | collective-permute-start | bytes 3145736 | tf_op jit(solution)/shard_map/ppermute | solution.py:466
  65.8 13.7 %collective-permute-start.22 = (bf16[32,64,128]{2,1,0:T(8,128)(2,1)S(1)}, bf16[32,64,128]{2,1,0:T(8,128)(2,1)S(1)}, u32[]{:S(2)}, u32[]{:S(2)}) collective-permute-start(bf16[32,64,128]{2,1,0:T(8,128)(2,1)S(1)} %turn_panel.3.refs_1_), channel_id=1, source_target_pairs={{0,16},{1,9},{2,18},{3,11},{4,20},{5,13},{6,22},{7,15},{8,24},{9,1... | collective-permute-start | bytes 1572872 | tf_op jit(solution)/shard_map/ppermute | solution.py:463
  66.4 14.3 %collective-permute-start.24 = (bf16[32,64,128]{2,1,0:T(8,128)(2,1)S(1)}, bf16[32,64,128]{2,1,0:T(8,128)(2,1)S(1)}, u32[]{:S(2)}, u32[]{:S(2)}) collective-permute-start(bf16[32,64,128]{2,1,0:T(8,128)(2,1)S(1)} %add_up.36), channel_id=1, source_target_pairs={{0,16},{1,9},{2,18},{3,11},{4,20},{5,13},{6,22},{7,15},{8,24},{9,1... | collective-permute-start | bytes 1572872 | tf_op jit(solution)/shard_map/ppermute | solution.py:463
  69.4 18.2 %collective-permute-start.16 = (bf16[64,32,128]{2,1,0:T(8,128)(2,1)S(1)}, bf16[64,32,128]{2,1,0:T(8,128)(2,1)S(1)}, u32[]{:S(2)}, u32[]{:S(2)}) collective-permute-start(bf16[64,32,128]{2,1,0:T(8,128)(2,1)S(1)} %add_up.31.refs_3_), channel_id=1, source_target_pairs={{0,2},{7,5},{2,4},{5,3},{4,6},{3,1},{8,10},{15,13},{10,12},{13,11}... | collective-permute-start | bytes 1572872 | tf_op jit(solution)/shard_map/ppermute | solution.py:475
  75.0 14.2 %collective-permute-start.20 = (bf16[64,32,128]{2,1,0:T(8,128)(2,1)S(1)}, bf16[64,32,128]{2,1,0:T(8,128)(2,1)S(1)}, u32[]{:S(2)}, u32[]{:S(2)}) collective-permute-start(bf16[64,32,128]{2,1,0:T(8,128)(2,1)S(1)} %add_up.33.refs_3_.refs_5_), channel_id=1, source_target_pairs={{0,2},{7,5},{2,4},{5,3},{4,6},{3,1},{8,10},{15,13},{10,12},{13,11}... | collective-permute-start | bytes 1572872 | tf_op jit(solution)/shard_map/ppermute | solution.py:475
  87.7 3.8 %collective-permute-start.17 = (bf16[64,32,128]{2,1,0:T(8,128)(2,1)S(1)}, bf16[64,32,128]{2,1,0:T(8,128)(2,1)S(1)}, u32[]{:S(2)}, u32[]{:S(2)}) collective-permute-start(bf16[64,32,128]{2,1,0:T(8,128)(2,1)S(1)} %collective-permute-done.16.refs_0_), channel_id=1, source_target_pairs={{0,1},{1,0},{2,3},{3,2},{4,5},{5,4},{6,7},{7,6},{8,9},{9,8},{10,11... | collective-permute-start | bytes 1572872 | tf_op jit(solution)/shard_map/ppermute | solution.py:466
  87.8 14.9 %collective-permute-start.27 = (bf16[64,64,128]{2,1,0:T(8,128)(2,1)}, bf16[64,64,128]{2,1,0:T(8,128)(2,1)}, u32[]{:S(2)}, u32[]{:S(2)}) collective-permute-start(bf16[64,64,128]{2,1,0:T(8,128)(2,1)} %get-tuple-element.57), channel_id=1, source_target_pairs={{1,0},{6,7},{9,8},{14,15},{17,16},{22,23},{25,24},{30,31}} | collective-permute-start | bytes 3145736 | tf_op jit(solution)/shard_map/ppermute | solution.py:466
  89.2 8.7 %collective-permute-start.21 = (bf16[64,32,128]{2,1,0:T(8,128)(2,1)S(1)}, bf16[64,32,128]{2,1,0:T(8,128)(2,1)S(1)}, u32[]{:S(2)}, u32[]{:S(2)}) collective-permute-start(bf16[64,32,128]{2,1,0:T(8,128)(2,1)S(1)} %collective-permute-done.20.refs_0_), channel_id=1, source_target_pairs={{0,1},{1,0},{2,3},{3,2},{4,5},{5,4},{6,7},{7,6},{8,9},{9,8},{10,11... | collective-permute-start | bytes 1572872 | tf_op jit(solution)/shard_map/ppermute | solution.py:466
  92.8 10.1 %collective-permute-start.28 = (bf16[64,32,128]{2,1,0:T(8,128)(2,1)}, bf16[64,32,128]{2,1,0:T(8,128)(2,1)}, u32[]{:S(2)}, u32[]{:S(2)}) collective-permute-start(bf16[64,32,128]{2,1,0:T(8,128)(2,1)} %get-tuple-element.49.refs_3_.refs_6_), channel_id=1, source_target_pairs={{0,2},{7,5},{2,4},{5,3},{4,6},{3,1},{8,10},{15,13},{10,12},{13,11}... | collective-permute-start | bytes 1572872 | tf_op jit(solution)/shard_map/ppermute | solution.py:475
  96.7 19.9 %collective-permute-start.26 = (bf16[64,64,128]{2,1,0:T(8,128)(2,1)}, bf16[64,64,128]{2,1,0:T(8,128)(2,1)S(1)}, u32[]{:S(2)}, u32[]{:S(2)}) collective-permute-start(bf16[64,64,128]{2,1,0:T(8,128)(2,1)} %get-tuple-element.55), channel_id=1, source_target_pairs={{1,0},{3,2},{4,5},{6,7},{9,8},{11,10},{12,13},{14,15},{17,16},{19,... | collective-permute-start | bytes 3145736 | tf_op jit(solution)/shard_map/ppermute | solution.py:466
  99.3 12.0 %collective-permute-start.30 = (bf16[64,32,128]{2,1,0:T(8,128)(2,1)}, bf16[64,32,128]{2,1,0:T(8,128)(2,1)}, u32[]{:S(2)}, u32[]{:S(2)}) collective-permute-start(bf16[64,32,128]{2,1,0:T(8,128)(2,1)} %get-tuple-element.58.refs_3_.refs_7_), channel_id=1, source_target_pairs={{0,2},{7,5},{2,4},{5,3},{4,6},{3,1},{8,10},{15,13},{10,12},{13,11}... | collective-permute-start | bytes 1572872 | tf_op jit(solution)/shard_map/ppermute | solution.py:475
  105.6 11.0 %collective-permute-start.29 = (bf16[64,32,128]{2,1,0:T(8,128)(2,1)S(1)}, bf16[64,32,128]{2,1,0:T(8,128)(2,1)S(1)}, u32[]{:S(2)}, u32[]{:S(2)}) collective-permute-start(bf16[64,32,128]{2,1,0:T(8,128)(2,1)S(1)} %add_up.37.refs_3_), channel_id=1, source_target_pairs={{0,2},{7,5},{2,4},{5,3},{4,6},{3,1},{8,10},{15,13},{10,12},{13,11}... | collective-permute-start | bytes 1572872 | tf_op jit(solution)/shard_map/ppermute | solution.py:475
  110.0 18.0 %collective-permute-start.25 = (bf16[64,64,128]{2,1,0:T(8,128)(2,1)S(1)}, bf16[64,64,128]{2,1,0:T(8,128)(2,1)S(1)}, u32[]{:S(2)}, u32[]{:S(2)}) collective-permute-start(bf16[64,64,128]{2,1,0:T(8,128)(2,1)S(1)} %copy-done.19), channel_id=1, source_target_pairs={{1,0},{2,3},{3,2},{4,5},{5,4},{6,7},{9,8},{10,11},{11,10},{12,13},... | collective-permute-start | bytes 3145736 | tf_op jit(solution)/shard_map/ppermute | solution.py:466
  112.7 10.5 %collective-permute-start.32 = (bf16[64,32,128]{2,1,0:T(8,128)(2,1)S(1)}, bf16[64,32,128]{2,1,0:T(8,128)(2,1)S(1)}, u32[]{:S(2)}, u32[]{:S(2)}) collective-permute-start(bf16[64,32,128]{2,1,0:T(8,128)(2,1)S(1)} %add_up.38.refs_4_.refs_2_), channel_id=1, source_target_pairs={{0,2},{7,5},{2,4},{5,3},{4,6},{3,1},{8,10},{15,13},{10,12},{13,11}... | collective-permute-start | bytes 1572872 | tf_op jit(solution)/shard_map/ppermute | solution.py:475
  116.9 11.9 %collective-permute-start.31 = (bf16[64,32,128]{2,1,0:T(8,128)(2,1)S(1)}, bf16[64,32,128]{2,1,0:T(8,128)(2,1)S(1)}, u32[]{:S(2)}, u32[]{:S(2)}) collective-permute-start(bf16[64,32,128]{2,1,0:T(8,128)(2,1)S(1)} %add_up.39.refs_4_), channel_id=1, source_target_pairs={{0,2},{7,5},{2,4},{5,3},{4,6},{3,1},{8,10},{15,13},{10,12},{13,11}... | collective-permute-start | bytes 1572872 | tf_op jit(solution)/shard_map/ppermute | solution.py:475
  123.5 11.1 %collective-permute-start.36 = (bf16[64,32,128]{2,1,0:T(8,128)(2,1)S(1)}, bf16[64,32,128]{2,1,0:T(8,128)(2,1)S(1)}, u32[]{:S(2)}, u32[]{:S(2)}) collective-permute-start(bf16[64,32,128]{2,1,0:T(8,128)(2,1)S(1)} %add_up.40.refs_3_), channel_id=1, source_target_pairs={{0,2},{7,5},{2,4},{5,3},{4,6},{3,1},{8,10},{15,13},{10,12},{13,11}... | collective-permute-start | bytes 1572872 | tf_op jit(solution)/shard_map/ppermute | solution.py:475
  128.0 18.5 %collective-permute-start.35 = (bf16[64,64,128]{2,1,0:T(8,128)(2,1)S(1)}, bf16[64,64,128]{2,1,0:T(8,128)(2,1)S(1)}, u32[]{:S(2)}, u32[]{:S(2)}) collective-permute-start(bf16[64,64,128]{2,1,0:T(8,128)(2,1)S(1)} %copy-done.15), channel_id=1, source_target_pairs={{0,1},{1,0},{2,3},{3,2},{4,5},{5,4},{6,7},{7,6},{8,9},{9,8},{10,11... | collective-permute-start | bytes 3145736 | tf_op jit(solution)/shard_map/ppermute | solution.py:466
  129.3 11.1 %collective-permute-start.33 = (bf16[64,32,128]{2,1,0:T(8,128)(2,1)S(1)}, bf16[64,32,128]{2,1,0:T(8,128)(2,1)S(1)}, u32[]{:S(2)}, u32[]{:S(2)}) collective-permute-start(bf16[64,32,128]{2,1,0:T(8,128)(2,1)S(1)} %add_up.41.refs_3_), channel_id=1, source_target_pairs={{0,2},{7,5},{2,4},{5,3},{4,6},{3,1},{8,10},{15,13},{10,12},{13,11}... | collective-permute-start | bytes 1572872 | tf_op jit(solution)/shard_map/ppermute | solution.py:475
  135.1 11.3 %collective-permute-start.37 = (bf16[64,32,128]{2,1,0:T(8,128)(2,1)S(1)}, bf16[64,32,128]{2,1,0:T(8,128)(2,1)S(1)}, u32[]{:S(2)}, u32[]{:S(2)}) collective-permute-start(bf16[64,32,128]{2,1,0:T(8,128)(2,1)S(1)} %add_up.43.refs_3_), channel_id=1, source_target_pairs={{0,2},{7,5},{2,4},{5,3},{4,6},{3,1},{8,10},{15,13},{10,12},{13,11}... | collective-permute-start | bytes 1572872 | tf_op jit(solution)/shard_map/ppermute | solution.py:475
  139.7 7.4 %collective-permute-start.42 = (bf16[64,32,128]{2,1,0:T(8,128)(2,1)}, bf16[64,32,128]{2,1,0:T(8,128)(2,1)S(1)}, u32[]{:S(2)}, u32[]{:S(2)}) collective-permute-start(bf16[64,32,128]{2,1,0:T(8,128)(2,1)} %collective-permute-done.30.refs_2_.refs_5_), channel_id=1, source_target_pairs={{0,1},{1,0},{2,3},{3,2},{4,5},{5,4},{6,7},{7,6},{8,9},{9,8},{10,11... | collective-permute-start | bytes 1572872 | tf_op jit(solution)/shard_map/ppermute | solution.py:466
  139.8 7.5 %collective-permute-start.41 = (bf16[64,32,128]{2,1,0:T(8,128)(2,1)}, bf16[64,32,128]{2,1,0:T(8,128)(2,1)S(1)}, u32[]{:S(2)}, u32[]{:S(2)}) collective-permute-start(bf16[64,32,128]{2,1,0:T(8,128)(2,1)} %collective-permute-done.28.refs_2_.refs_4_), channel_id=1, source_target_pairs={{0,1},{1,0},{2,3},{3,2},{4,5},{5,4},{6,7},{7,6},{8,9},{9,8},{10,11... | collective-permute-start | bytes 1572872 | tf_op jit(solution)/shard_map/ppermute | solution.py:466
  140.4 7.3 %collective-permute-start.34 = (bf16[64,32,128]{2,1,0:T(8,128)(2,1)S(1)}, bf16[64,32,128]{2,1,0:T(8,128)(2,1)S(1)}, u32[]{:S(2)}, u32[]{:S(2)}) collective-permute-start(bf16[64,32,128]{2,1,0:T(8,128)(2,1)S(1)} %collective-permute-done.33.refs_0_), channel_id=1, source_target_pairs={{0,1},{1,0},{2,3},{3,2},{4,5},{5,4},{6,7},{7,6},{8,9},{9,8},{10,11... | collective-permute-start | bytes 1572872 | tf_op jit(solution)/shard_map/ppermute | solution.py:466
  146.4 2.6 %collective-permute-start.38 = (bf16[64,32,128]{2,1,0:T(8,128)(2,1)S(1)}, bf16[64,32,128]{2,1,0:T(8,128)(2,1)S(1)}, u32[]{:S(2)}, u32[]{:S(2)}) collective-permute-start(bf16[64,32,128]{2,1,0:T(8,128)(2,1)S(1)} %collective-permute-done.37.refs_0_), channel_id=1, source_target_pairs={{0,1},{1,0},{2,3},{3,2},{4,5},{5,4},{6,7},{7,6},{8,9},{9,8},{10,11... | collective-permute-start | bytes 1572872 | tf_op jit(solution)/shard_map/ppermute | solution.py:466
  146.6 8.0 %collective-permute-start.44 = (bf16[64,32,128]{2,1,0:T(8,128)(2,1)S(1)}, bf16[64,32,128]{2,1,0:T(8,128)(2,1)S(1)}, u32[]{:S(2)}, u32[]{:S(2)}) collective-permute-start(bf16[64,32,128]{2,1,0:T(8,128)(2,1)S(1)} %collective-permute-done.32.refs_2_.refs_3_), channel_id=1, source_target_pairs={{0,1},{1,0},{2,3},{3,2},{4,5},{5,4},{6,7},{7,6},{8,9},{9,8},{10,11... | collective-permute-start | bytes 1572872 | tf_op jit(solution)/shard_map/ppermute | solution.py:466
  147.2 10.3 %collective-permute-start.43 = (bf16[64,32,128]{2,1,0:T(8,128)(2,1)S(1)}, bf16[64,32,128]{2,1,0:T(8,128)(2,1)S(1)}, u32[]{:S(2)}, u32[]{:S(2)}) collective-permute-start(bf16[64,32,128]{2,1,0:T(8,128)(2,1)S(1)} %collective-permute-done.29.refs_2_.refs_3_), channel_id=1, source_target_pairs={{0,1},{1,0},{2,3},{3,2},{4,5},{5,4},{6,7},{7,6},{8,9},{9,8},{10,11... | collective-permute-start | bytes 1572872 | tf_op jit(solution)/shard_map/ppermute | solution.py:466
  147.3 10.3 %collective-permute-start.46 = (bf16[64,32,128]{2,1,0:T(8,128)(2,1)S(1)}, bf16[64,32,128]{2,1,0:T(8,128)(2,1)S(1)}, u32[]{:S(2)}, u32[]{:S(2)}) collective-permute-start(bf16[64,32,128]{2,1,0:T(8,128)(2,1)S(1)} %collective-permute-done.36.refs_2_.refs_1_), channel_id=1, source_target_pairs={{0,1},{1,0},{2,3},{3,2},{4,5},{5,4},{6,7},{7,6},{8,9},{9,8},{10,11... | collective-permute-start | bytes 1572872 | tf_op jit(solution)/shard_map/ppermute | solution.py:466
  147.7 9.8 %collective-permute-start.45 = (bf16[64,32,128]{2,1,0:T(8,128)(2,1)S(1)}, bf16[64,32,128]{2,1,0:T(8,128)(2,1)S(1)}, u32[]{:S(2)}, u32[]{:S(2)}) collective-permute-start(bf16[64,32,128]{2,1,0:T(8,128)(2,1)S(1)} %collective-permute-done.31.refs_2_.refs_0_), channel_id=1, source_target_pairs={{0,1},{1,0},{2,3},{3,2},{4,5},{5,4},{6,7},{7,6},{8,9},{9,8},{10,11... | collective-permute-start | bytes 1572872 | tf_op jit(solution)/shard_map/ppermute | solution.py:466
  149.0 14.2 %collective-permute-start.40 = (bf16[64,32,128]{2,1,0:T(8,128)(2,1)S(1)}, bf16[64,32,128]{2,1,0:T(8,128)(2,1)S(1)}, u32[]{:S(2)}, u32[]{:S(2)}) collective-permute-start(bf16[64,32,128]{2,1,0:T(8,128)(2,1)S(1)} %get-tuple-element.61.refs_3_), channel_id=1, source_target_pairs={{0,2},{7,5},{2,4},{5,3},{4,6},{3,1},{8,10},{15,13},{10,12},{13,11}... | collective-permute-start | bytes 1572872 | tf_op jit(solution)/shard_map/ppermute | solution.py:475
  154.6 11.5 %collective-permute-start.39 = (bf16[64,32,128]{2,1,0:T(8,128)(2,1)S(1)}, bf16[64,32,128]{2,1,0:T(8,128)(2,1)S(1)}, u32[]{:S(2)}, u32[]{:S(2)}) collective-permute-start(bf16[64,32,128]{2,1,0:T(8,128)(2,1)S(1)} %get-tuple-element.63.refs_14_.refs_1_.refs_3_), channel_id=1, source_target_pairs={{0,2},{7,5},{2,4},{5,3},{4,6},{3,1},{8,10},{15,13},{10,12},{13,11}... | collective-permute-start | bytes 1572872 | tf_op jit(solution)/shard_map/ppermute | solution.py:475
  161.5 17.9 %collective-permute-start.49 = (bf16[64,64,128]{2,1,0:T(8,128)(2,1)S(1)}, bf16[64,64,128]{2,1,0:T(8,128)(2,1)S(1)}, u32[]{:S(2)}, u32[]{:S(2)}) collective-permute-start(bf16[64,64,128]{2,1,0:T(8,128)(2,1)S(1)} %get-tuple-element.64.refs_2_), channel_id=1, source_target_pairs={{0,8},{1,17},{2,10},{3,19},{4,12},{5,21},{6,14},{7,23},{8,0},{9,25... | collective-permute-start | bytes 3145736 | tf_op jit(solution)/shard_map/ppermute | solution.py:463
  163.3 9.4 %collective-permute-start.48 = (bf16[64,32,128]{2,1,0:T(8,128)(2,1)S(1)}, bf16[64,32,128]{2,1,0:T(8,128)(2,1)S(1)}, u32[]{:S(2)}, u32[]{:S(2)}) collective-permute-start(bf16[64,32,128]{2,1,0:T(8,128)(2,1)S(1)} %add_up.46.refs_1_), channel_id=1, source_target_pairs={{0,2},{7,5},{2,4},{5,3},{4,6},{3,1},{8,10},{15,13},{10,12},{13,11}... | collective-permute-start | bytes 1572872 | tf_op jit(solution)/shard_map/ppermute | solution.py:475
  172.9 11.1 %collective-permute-start.51 = (bf16[64,32,128]{2,1,0:T(8,128)(2,1)S(1)}, bf16[64,32,128]{2,1,0:T(8,128)(2,1)S(1)}, u32[]{:S(2)}, u32[]{:S(2)}) collective-permute-start(bf16[64,32,128]{2,1,0:T(8,128)(2,1)S(1)} %add_up.48.refs_1_), channel_id=1, source_target_pairs={{0,2},{7,5},{2,4},{5,3},{4,6},{3,1},{8,10},{15,13},{10,12},{13,11}... | collective-permute-start | bytes 1572872 | tf_op jit(solution)/shard_map/ppermute | solution.py:475
  177.3 12.3 %collective-permute-start.47 = (bf16[64,32,128]{2,1,0:T(8,128)(2,1)S(1)}, bf16[64,32,128]{2,1,0:T(8,128)(2,1)S(1)}, u32[]{:S(2)}, u32[]{:S(2)}) collective-permute-start(bf16[64,32,128]{2,1,0:T(8,128)(2,1)S(1)} %add_up.47.refs_1_), channel_id=1, source_target_pairs={{0,2},{7,5},{2,4},{5,3},{4,6},{3,1},{8,10},{15,13},{10,12},{13,11}... | collective-permute-start | bytes 1572872 | tf_op jit(solution)/shard_map/ppermute | solution.py:475
  179.3 14.7 %collective-permute-start.52 = (bf16[64,32,128]{2,1,0:T(8,128)(2,1)S(1)}, bf16[64,32,128]{2,1,0:T(8,128)(2,1)S(1)}, u32[]{:S(2)}, u32[]{:S(2)}) collective-permute-start(bf16[64,32,128]{2,1,0:T(8,128)(2,1)S(1)} %collective-permute-done.40.refs_0_.refs_2_), channel_id=1, source_target_pairs={{0,1},{1,0},{2,3},{3,2},{4,5},{5,4},{6,7},{7,6},{8,9},{9,8},{10,11... | collective-permute-start | bytes 1572872 | tf_op jit(solution)/shard_map/ppermute | solution.py:466
  179.5 14.6 %collective-permute-start.55 = (bf16[32,64,128]{2,1,0:T(8,128)(2,1)S(1)}, bf16[32,64,128]{2,1,0:T(8,128)(2,1)S(1)}, u32[]{:S(2)}, u32[]{:S(2)}) collective-permute-start(bf16[32,64,128]{2,1,0:T(8,128)(2,1)S(1)} %add_up.50), channel_id=1, source_target_pairs={{0,16},{1,9},{2,18},{3,11},{4,20},{5,13},{6,22},{7,15},{8,24},{9,1... | collective-permute-start | bytes 1572872 | tf_op jit(solution)/shard_map/ppermute | solution.py:463
  180.0 14.7 %collective-permute-start.53 = (bf16[64,32,128]{2,1,0:T(8,128)(2,1)S(1)}, bf16[64,32,128]{2,1,0:T(8,128)(2,1)S(1)}, u32[]{:S(2)}, u32[]{:S(2)}) collective-permute-start(bf16[64,32,128]{2,1,0:T(8,128)(2,1)S(1)} %collective-permute-done.48.refs_0_.refs_1_), channel_id=1, source_target_pairs={{0,1},{1,0},{2,3},{3,2},{4,5},{5,4},{6,7},{7,6},{8,9},{9,8},{10,11... | collective-permute-start | bytes 1572872 | tf_op jit(solution)/shard_map/ppermute | solution.py:466
  183.9 10.7 %collective-permute-start.54 = (bf16[64,32,128]{2,1,0:T(8,128)(2,1)S(1)}, bf16[64,32,128]{2,1,0:T(8,128)(2,1)S(1)}, u32[]{:S(2)}, u32[]{:S(2)}) collective-permute-start(bf16[64,32,128]{2,1,0:T(8,128)(2,1)S(1)} %collective-permute-done.51.refs_0_), channel_id=1, source_target_pairs={{0,1},{1,0},{2,3},{3,2},{4,5},{5,4},{6,7},{7,6},{8,9},{9,8},{10,11... | collective-permute-start | bytes 1572872 | tf_op jit(solution)/shard_map/ppermute | solution.py:466
  189.7 11.1 %collective-permute-start.50 = (bf16[64,32,128]{2,1,0:T(8,128)(2,1)S(1)}, bf16[64,32,128]{2,1,0:T(8,128)(2,1)S(1)}, u32[]{:S(2)}, u32[]{:S(2)}) collective-permute-start(bf16[64,32,128]{2,1,0:T(8,128)(2,1)S(1)} %add_up.49), channel_id=1, source_target_pairs={{0,2},{7,5},{2,4},{5,3},{4,6},{3,1},{8,10},{15,13},{10,12},{13,11}... | collective-permute-start | bytes 1572872 | tf_op jit(solution)/shard_map/ppermute | solution.py:475
  194.1 7.3 %collective-permute-start.56 = (bf16[64,32,128]{2,1,0:T(8,128)(2,1)S(1)}, bf16[64,32,128]{2,1,0:T(8,128)(2,1)S(1)}, u32[]{:S(2)}, u32[]{:S(2)}) collective-permute-start(bf16[64,32,128]{2,1,0:T(8,128)(2,1)S(1)} %collective-permute-done.39.refs_0_.refs_2_), channel_id=1, source_target_pairs={{0,1},{1,0},{2,3},{3,2},{4,5},{5,4},{6,7},{7,6},{8,9},{9,8},{10,11... | collective-permute-start | bytes 1572872 | tf_op jit(solution)/shard_map/ppermute | solution.py:466
  194.2 7.2 %collective-permute-start.57 = (bf16[64,32,128]{2,1,0:T(8,128)(2,1)S(1)}, bf16[64,32,128]{2,1,0:T(8,128)(2,1)S(1)}, u32[]{:S(2)}, u32[]{:S(2)}) collective-permute-start(bf16[64,32,128]{2,1,0:T(8,128)(2,1)S(1)} %collective-permute-done.47.refs_0_.refs_1_), channel_id=1, source_target_pairs={{0,1},{1,0},{2,3},{3,2},{4,5},{5,4},{6,7},{7,6},{8,9},{9,8},{10,11... | collective-permute-start | bytes 1572872 | tf_op jit(solution)/shard_map/ppermute | solution.py:466
  200.8 2.0 collective-permute-start.58
  200.9 9.2 %collective-permute-start.59 = (bf16[64,32,128]{2,1,0:T(8,128)(2,1)S(1)}, bf16[64,32,128]{2,1,0:T(8,128)(2,1)S(1)}, u32[]{:S(2)}, u32[]{:S(2)}) collective-permute-start(bf16[64,32,128]{2,1,0:T(8,128)(2,1)S(1)} %get-tuple-element.66.refs_1_), channel_id=1, source_target_pairs={{0,8},{1,17},{2,10},{3,19},{4,12},{5,21},{6,14},{7,23},{8,0},{9,25... | collective-permute-start | bytes 1572872 | tf_op jit(solution)/shard_map/ppermute | solution.py:463
  205.6 12.5 %collective-permute-start.61 = (bf16[64,32,128]{2,1,0:T(8,128)(2,1)S(1)}, bf16[64,32,128]{2,1,0:T(8,128)(2,1)S(1)}, u32[]{:S(2)}, u32[]{:S(2)}) collective-permute-start(bf16[64,32,128]{2,1,0:T(8,128)(2,1)S(1)} %get-tuple-element.67.refs_4_), channel_id=1, source_target_pairs={{0,8},{1,17},{2,10},{3,19},{4,12},{5,21},{6,14},{7,23},{8,0},{9,25... | collective-permute-start | bytes 1572872 | tf_op jit(solution)/shard_map/ppermute | solution.py:463
  211.0 12.6 %collective-permute-start.60 = (bf16[32,32,128]{2,1,0:T(8,128)(2,1)}, bf16[32,32,128]{2,1,0:T(8,128)(2,1)S(1)}, u32[]{:S(2)}, u32[]{:S(2)}) collective-permute-start(bf16[32,32,128]{2,1,0:T(8,128)(2,1)} %add_up.52), channel_id=1, source_target_pairs={{0,16},{1,9},{2,18},{3,11},{4,20},{5,13},{6,22},{7,15},{8,24},{9,1... | collective-permute-start | bytes 786440 | tf_op jit(solution)/shard_map/ppermute | solution.py:463
  219.0 6.7 %collective-permute-start.62 = (bf16[32,32,128]{2,1,0:T(8,128)(2,1)}, bf16[32,32,128]{2,1,0:T(8,128)(2,1)}, u32[]{:S(2)}, u32[]{:S(2)}) collective-permute-start(bf16[32,32,128]{2,1,0:T(8,128)(2,1)} %add_up.53), channel_id=1, source_target_pairs={{0,16},{1,9},{2,18},{3,11},{4,20},{5,13},{6,22},{7,15},{8,24},{9,1... | collective-permute-start | bytes 786440 | tf_op jit(solution)/shard_map/ppermute | solution.py:463
  (24 other events, 207.4 us)

commit v7 on v6

--- a/solution.py
+++ b/solution.py
@@ -577,7 +577,7 @@
                 (payload,) = add_up(terms, block_rows, part, [BF16], last, other)
             else:
                 payload = near[before][n][hop - 1]
-                if through and n == (0 if step == 1 else PARTS - 1):
+                if through and step > 1 and n == PARTS - 1:
                     last = (*last, through[min(step - 1, bits)])
                 (payload,) = add_up([(payload, (0, 0))], block_rows, part, [BF16], last)
             got[n] = along(payload)

time: 229 us -> 229 us (level)
  no operation moved by 1% of the time
where the time goes in v7:
time: 229 us; the launch traced here: 228 us
  starting transfers between devices  112 us (49%)
  waiting for transfers between devices  57.7 us (25%)
  Pallas kernels  54 us (24%)
  local copies, waits for them, and re-layouts  3.22 us (1%)
    ppermute x20, starting transfers between devices, along(): return lax.ppermute(x, 'col', pairs)  77.7 us
    ppermute x20, waiting for transfers between devices, along(): return lax.ppermute(x, 'col', pairs)  29.7 us
    pallas_call x2, Pallas kernels, word_products(): pl.pallas_call(kernel, in_specs=[IN_SMEM] + operand_specs + [ANY] * (n_in...  16.2 us
    pallas_call x27, Pallas kernels, add_up(): pl.pallas_call(kernel, grid_spec=pltpu.PrefetchScalarGridSpec(num_scalar_...  14.6 us
    ppermute x12, waiting for transfers between devices, row_swap(): return lax.ppermute(x, ('row', 'col'), pairs)  14.3 us
    ppermute x26, starting transfers between devices, core_swap(): lax.ppermute(x, 'col', [(i, i ^ 1) for i in range(n_col) if keep(i % 2, i...  13.7 us
    ppermute x12, starting transfers between devices, row_swap(): return lax.ppermute(x, ('row', 'col'), pairs)  12.6 us
    pallas_call x3, Pallas kernels, context_products(): pl.pallas_call(kernel, in_specs=[IN_SMEM, IN_VMEM] + [ANY] * (slot_count...  9.52 us
  transfers between devices with their start and end apart: 63, of which 22 were waited for; matrix products, arithmetic and copies ran while one was open for 0% of the time, Pallas kernels for 18%

profile of v7, /device:TPU:0, one launch (start us, length us, event | category | flops | bytes accessed | tf_op | source)
XLA Modules:
  0.0 228.4 jit_solution(3107629537373796214)
XLA Ops:
  0.6 1.5 turn_panel.2.refs_0_.refs_5_
  2.2 3.0 %collective-permute-start.8 = (bf16[32,64,128]{2,1,0:T(8,128)(2,1)S(1)}, bf16[32,64,128]{2,1,0:T(8,128)(2,1)S(1)}, u32[]{:S(2)}, u32[]{:S(2)}) collective-permute-start(bf16[32,64,128]{2,1,0:T(8,128)(2,1)S(1)} %turn_panel.2.refs_0_.refs_5_), channel_id=1, source_target_pairs={{0,8},{1,17},{2,10},{3,19},{4,12},{5,21},{6,14},{7,23},{8,0},{9,25... | collective-permute-start | bytes 1572872 | tf_op jit(solution)/shard_map/ppermute | solution.py:463
  5.2 4.8 %count_sums.1 = (f32[256,128]{1,0:T(8,128)S(1)}, f32[128,128]{1,0:T(8,128)S(1)}) custom-call(s32[160,128,128]{2,1,0:T(8,128)} %bitcast.8, s32[160]{0:T(256)} %bitcast.13, s32[160]{0:T(256)} %bitcast.10, bf16[32,64,128]{2,1,0:T(8,128)(2,1)S(1)} %turn_panel.2.refs_0_.refs_5_), custom_call_target="tpu_custom_call" | custom-call | bytes 36900 | tf_op jit(solution)/shard_map/count_sums/pallas_call | solution.py:90
  10.1 2.0 collective-permute-start.1
  12.1 1.4 collective-permute-start.2
  13.6 1.5 collective-permute-start.7
  15.6 2.5 %collective-permute-done.2.refs_3_ = f32[128,128]{1,0:T(8,128)S(1)} collective-permute-done((f32[128,128]{1,0:T(8,128)S(1)}, f32[128,128]{1,0:T(8,128)S(1)}, u32[]{:S(2)}, u32[]{:S(2)}) %collective-permute-start.2) | collective-permute-done | bytes 65568 | tf_op jit(solution)/shard_map/ppermute | solution.py:478
  19.5 1.6 collective-permute-start.4
  21.1 2.7 %collective-permute-done.4.b_ref = f32[136,128]{1,0:T(8,128)S(1)} collective-permute-done((f32[136,128]{1,0:T(8,128)S(1)}, f32[136,128]{1,0:T(8,128)S(1)}, u32[]{:S(2)}, u32[]{:S(2)}) %collective-permute-start.4) | collective-permute-done | bytes 69664 | tf_op jit(solution)/shard_map/ppermute | solution.py:481
  23.9 2.6 %collective-permute-start.5 = (f32[136,128]{1,0:T(8,128)S(1)}, f32[136,128]{1,0:T(8,128)S(1)}, u32[]{:S(2)}, u32[]{:S(2)}) collective-permute-start(f32[136,128]{1,0:T(8,128)S(1)} %plus.4.a_ref), channel_id=1, source_target_pairs={{0,4},{1,5},{2,6},{3,7},{4,0},{5,1},{6,2},{7,3},{8,12},{9,13},{10,... | collective-permute-start | bytes 208904 | tf_op jit(solution)/shard_map/ppermute | solution.py:481
  26.5 2.7 %collective-permute-done.5.b_ref = f32[136,128]{1,0:T(8,128)S(1)} collective-permute-done((f32[136,128]{1,0:T(8,128)S(1)}, f32[136,128]{1,0:T(8,128)S(1)}, u32[]{:S(2)}, u32[]{:S(2)}) %collective-permute-start.5) | collective-permute-done | bytes 69664 | tf_op jit(solution)/shard_map/ppermute | solution.py:481
  31.4 9.2 %ppmi_word_products.1 = (bf16[160,128,128]{2,1,0:T(8,128)(2,1)S(1)}, bf16[64,64,128]{2,1,0:T(8,128)(2,1)S(1)}, bf16[64,64,128]{2,1,0:T(8,128)(2,1)S(1)}, bf16[64...) custom-call(s32[487]{0:T(512)S(1)} %pad_add_fusion.index_ref, ...), custom_call_target="tpu_custom_call" | custom-call | bytes 36900 | tf_op jit(solution)/shard_map/ppmi_word_products/pallas_call | solution.py:338
  40.6 1.3 collective-permute-start.12
  41.9 1.3 collective-permute-start.11
  43.2 2.0 collective-permute-done.12.refs_1_
  45.5 1.3 collective-permute-start.13
  46.8 1.3 collective-permute-start.10
  48.5 5.0 %collective-permute-start.15 = (bf16[64,32,128]{2,1,0:T(8,128)(2,1)S(1)}, bf16[64,32,128]{2,1,0:T(8,128)(2,1)S(1)}, u32[]{:S(2)}, u32[]{:S(2)}) collective-permute-start(bf16[64,32,128]{2,1,0:T(8,128)(2,1)S(1)} %add_up.28.refs_3_.refs_2_), channel_id=1, source_target_pairs={{0,2},{7,5},{2,4},{5,3},{4,6},{3,1},{8,10},{15,13},{10,12},{13,11}... | collective-permute-start | bytes 1572872 | tf_op jit(solution)/shard_map/ppermute | solution.py:475
  53.5 1.6 turn_panel.3.refs_1_
  55.1 1.7 collective-permute-start.23
  57.2 5.1 %collective-permute-start.14 = (bf16[64,32,128]{2,1,0:T(8,128)(2,1)S(1)}, bf16[64,32,128]{2,1,0:T(8,128)(2,1)S(1)}, u32[]{:S(2)}, u32[]{:S(2)}) collective-permute-start(bf16[64,32,128]{2,1,0:T(8,128)(2,1)S(1)} %add_up.29.refs_3_), channel_id=1, source_target_pairs={{0,2},{7,5},{2,4},{5,3},{4,6},{3,1},{8,10},{15,13},{10,12},{13,11}... | collective-permute-start | bytes 1572872 | tf_op jit(solution)/shard_map/ppermute | solution.py:475
  62.8 2.9 %collective-permute-start.19 = (bf16[64,32,128]{2,1,0:T(8,128)(2,1)S(1)}, bf16[64,32,128]{2,1,0:T(8,128)(2,1)S(1)}, u32[]{:S(2)}, u32[]{:S(2)}) collective-permute-start(bf16[64,32,128]{2,1,0:T(8,128)(2,1)S(1)} %add_up.30.refs_3_.refs_1_), channel_id=1, source_target_pairs={{0,2},{7,5},{2,4},{5,3},{4,6},{3,1},{8,10},{15,13},{10,12},{13,11}... | collective-permute-start | bytes 1572872 | tf_op jit(solution)/shard_map/ppermute | solution.py:475
  66.4 1.7 collective-permute-start.24
  69.4 4.4 %collective-permute-start.16 = (bf16[64,32,128]{2,1,0:T(8,128)(2,1)S(1)}, bf16[64,32,128]{2,1,0:T(8,128)(2,1)S(1)}, u32[]{:S(2)}, u32[]{:S(2)}) collective-permute-start(bf16[64,32,128]{2,1,0:T(8,128)(2,1)S(1)} %add_up.31.refs_3_), channel_id=1, source_target_pairs={{0,2},{7,5},{2,4},{5,3},{4,6},{3,1},{8,10},{15,13},{10,12},{13,11}... | collective-permute-start | bytes 1572872 | tf_op jit(solution)/shard_map/ppermute | solution.py:475
  75.0 4.4 %collective-permute-start.20 = (bf16[64,32,128]{2,1,0:T(8,128)(2,1)S(1)}, bf16[64,32,128]{2,1,0:T(8,128)(2,1)S(1)}, u32[]{:S(2)}, u32[]{:S(2)}) collective-permute-start(bf16[64,32,128]{2,1,0:T(8,128)(2,1)S(1)} %add_up.33.refs_3_.refs_5_), channel_id=1, source_target_pairs={{0,2},{7,5},{2,4},{5,3},{4,6},{3,1},{8,10},{15,13},{10,12},{13,11}... | collective-permute-start | bytes 1572872 | tf_op jit(solution)/shard_map/ppermute | solution.py:475
  80.7 6.9 %word_products.1 = (bf16[64,64,128]{2,1,0:T(8,128)(2,1)}, bf16[64,64,128]{2,1,0:T(8,128)(2,1)}, bf16[64,64,128]{2,1,0:T(8,128)(2,1)S(1)}, bf16[64,64,128]{2,1,0:...) custom-call(s32[487]{0:T(512)S(1)} %pad_add_fusion.index_ref, ...), custom_call_target="tpu_custom_call" | custom-call | bytes 36900 | tf_op jit(solution)/shard_map/word_products/pallas_call | solution.py:338
  87.7 1.5 collective-permute-start.27
  89.2 1.9 collective-permute-start.21
  91.5 1.3 add_up.34
  92.8 3.9 %collective-permute-start.28 = (bf16[64,32,128]{2,1,0:T(8,128)(2,1)}, bf16[64,32,128]{2,1,0:T(8,128)(2,1)}, u32[]{:S(2)}, u32[]{:S(2)}) collective-permute-start(bf16[64,32,128]{2,1,0:T(8,128)(2,1)} %get-tuple-element.49.refs_3_.refs_6_), channel_id=1, source_target_pairs={{0,2},{7,5},{2,4},{5,3},{4,6},{3,1},{8,10},{15,13},{10,12},{13,11}... | collective-permute-start | bytes 1572872 | tf_op jit(solution)/shard_map/ppermute | solution.py:475
  96.7 1.3 collective-permute-start.26
  98.0 1.3 add_up.35
  99.3 3.4 %collective-permute-start.30 = (bf16[64,32,128]{2,1,0:T(8,128)(2,1)}, bf16[64,32,128]{2,1,0:T(8,128)(2,1)}, u32[]{:S(2)}, u32[]{:S(2)}) collective-permute-start(bf16[64,32,128]{2,1,0:T(8,128)(2,1)} %get-tuple-element.58.refs_3_.refs_7_), channel_id=1, source_target_pairs={{0,2},{7,5},{2,4},{5,3},{4,6},{3,1},{8,10},{15,13},{10,12},{13,11}... | collective-permute-start | bytes 1572872 | tf_op jit(solution)/shard_map/ppermute | solution.py:475
  104.1 1.5 add_up.37.refs_3_
  105.6 4.3 %collective-permute-start.29 = (bf16[64,32,128]{2,1,0:T(8,128)(2,1)S(1)}, bf16[64,32,128]{2,1,0:T(8,128)(2,1)S(1)}, u32[]{:S(2)}, u32[]{:S(2)}) collective-permute-start(bf16[64,32,128]{2,1,0:T(8,128)(2,1)S(1)} %add_up.37.refs_3_), channel_id=1, source_target_pairs={{0,2},{7,5},{2,4},{5,3},{4,6},{3,1},{8,10},{15,13},{10,12},{13,11}... | collective-permute-start | bytes 1572872 | tf_op jit(solution)/shard_map/ppermute | solution.py:475
  110.0 1.3 collective-permute-start.25
  111.3 1.4 add_up.38.refs_4_.refs_2_
  112.7 3.9 %collective-permute-start.32 = (bf16[64,32,128]{2,1,0:T(8,128)(2,1)S(1)}, bf16[64,32,128]{2,1,0:T(8,128)(2,1)S(1)}, u32[]{:S(2)}, u32[]{:S(2)}) collective-permute-start(bf16[64,32,128]{2,1,0:T(8,128)(2,1)S(1)} %add_up.38.refs_4_.refs_2_), channel_id=1, source_target_pairs={{0,2},{7,5},{2,4},{5,3},{4,6},{3,1},{8,10},{15,13},{10,12},{13,11}... | collective-permute-start | bytes 1572872 | tf_op jit(solution)/shard_map/ppermute | solution.py:475
  116.9 4.6 %collective-permute-start.31 = (bf16[64,32,128]{2,1,0:T(8,128)(2,1)S(1)}, bf16[64,32,128]{2,1,0:T(8,128)(2,1)S(1)}, u32[]{:S(2)}, u32[]{:S(2)}) collective-permute-start(bf16[64,32,128]{2,1,0:T(8,128)(2,1)S(1)} %add_up.39.refs_4_), channel_id=1, source_target_pairs={{0,2},{7,5},{2,4},{5,3},{4,6},{3,1},{8,10},{15,13},{10,12},{13,11}... | collective-permute-start | bytes 1572872 | tf_op jit(solution)/shard_map/ppermute | solution.py:475
  121.5 1.7 collective-permute-done.32.refs_2_.refs_3_
  123.5 4.4 %collective-permute-start.36 = (bf16[64,32,128]{2,1,0:T(8,128)(2,1)S(1)}, bf16[64,32,128]{2,1,0:T(8,128)(2,1)S(1)}, u32[]{:S(2)}, u32[]{:S(2)}) collective-permute-start(bf16[64,32,128]{2,1,0:T(8,128)(2,1)S(1)} %add_up.40.refs_3_), channel_id=1, source_target_pairs={{0,2},{7,5},{2,4},{5,3},{4,6},{3,1},{8,10},{15,13},{10,12},{13,11}... | collective-permute-start | bytes 1572872 | tf_op jit(solution)/shard_map/ppermute | solution.py:475
  129.3 4.4 %collective-permute-start.33 = (bf16[64,32,128]{2,1,0:T(8,128)(2,1)S(1)}, bf16[64,32,128]{2,1,0:T(8,128)(2,1)S(1)}, u32[]{:S(2)}, u32[]{:S(2)}) collective-permute-start(bf16[64,32,128]{2,1,0:T(8,128)(2,1)S(1)} %add_up.41.refs_3_), channel_id=1, source_target_pairs={{0,2},{7,5},{2,4},{5,3},{4,6},{3,1},{8,10},{15,13},{10,12},{13,11}... | collective-permute-start | bytes 1572872 | tf_op jit(solution)/shard_map/ppermute | solution.py:475
  135.0 4.7 %collective-permute-start.37 = (bf16[64,32,128]{2,1,0:T(8,128)(2,1)S(1)}, bf16[64,32,128]{2,1,0:T(8,128)(2,1)S(1)}, u32[]{:S(2)}, u32[]{:S(2)}) collective-permute-start(bf16[64,32,128]{2,1,0:T(8,128)(2,1)S(1)} %add_up.43.refs_3_), channel_id=1, source_target_pairs={{0,2},{7,5},{2,4},{5,3},{4,6},{3,1},{8,10},{15,13},{10,12},{13,11}... | collective-permute-start | bytes 1572872 | tf_op jit(solution)/shard_map/ppermute | solution.py:475
  140.6 5.8 %collective-permute-done.37.refs_0_ = bf16[64,32,128]{2,1,0:T(8,128)(2,1)S(1)} collective-permute-done((bf16[64,32,128]{2,1,0:T(8,128)(2,1)S(1)}, bf16[64,32,128]{2,1,0:T(8,128)(2,1)S(1)}, u32[]{:S(2)}, u32[]{:S(2)}) %collective-permute-start.37) | collective-permute-done | bytes 524320 | tf_op jit(solution)/shard_map/ppermute | solution.py:475
  149.0 4.4 %collective-permute-start.40 = (bf16[64,32,128]{2,1,0:T(8,128)(2,1)S(1)}, bf16[64,32,128]{2,1,0:T(8,128)(2,1)S(1)}, u32[]{:S(2)}, u32[]{:S(2)}) collective-permute-start(bf16[64,32,128]{2,1,0:T(8,128)(2,1)S(1)} %get-tuple-element.61.refs_3_), channel_id=1, source_target_pairs={{0,2},{7,5},{2,4},{5,3},{4,6},{3,1},{8,10},{15,13},{10,12},{13,11}... | collective-permute-start | bytes 1572872 | tf_op jit(solution)/shard_map/ppermute | solution.py:475
  154.6 2.9 %collective-permute-start.39 = (bf16[64,32,128]{2,1,0:T(8,128)(2,1)S(1)}, bf16[64,32,128]{2,1,0:T(8,128)(2,1)S(1)}, u32[]{:S(2)}, u32[]{:S(2)}) collective-permute-start(bf16[64,32,128]{2,1,0:T(8,128)(2,1)S(1)} %get-tuple-element.63.refs_1_.refs_14_.refs_3_), channel_id=1, source_target_pairs={{0,2},{7,5},{2,4},{5,3},{4,6},{3,1},{8,10},{15,13},{10,12},{13,11}... | collective-permute-start | bytes 1572872 | tf_op jit(solution)/shard_map/ppermute | solution.py:475
  157.6 3.9 %context_products.3 = (bf16[64,64,128]{2,1,0:T(8,128)(2,1)S(1)}, f32[64,64,128]{2,1,0:T(8,128)S(1)}) custom-call(s32[487]{0:T(512)S(1)} %pad_add_fusion.index_ref, bf16[160,128,128]{2,1,0:T(8,128)(2,1)S(1)} %bitcast.7, bf16[64,32,128]{2,1,0:T(8,128)(2,1)S(1)} %collective-permute-done.31.refs_2_.refs_0_, ...), custom_call_target="tpu_custom_call" | custom-call | bytes 36900 | tf_op jit(solution)/shard_map/context_products/pallas_call | solution.py:397
  161.5 1.7 collective-permute-start.49
  163.3 2.8 %collective-permute-start.42 = (bf16[64,32,128]{2,1,0:T(8,128)(2,1)S(1)}, bf16[64,32,128]{2,1,0:T(8,128)(2,1)S(1)}, u32[]{:S(2)}, u32[]{:S(2)}) collective-permute-start(bf16[64,32,128]{2,1,0:T(8,128)(2,1)S(1)} %add_up.46.refs_1_), channel_id=1, source_target_pairs={{0,2},{7,5},{2,4},{5,3},{4,6},{3,1},{8,10},{15,13},{10,12},{13,11}... | collective-permute-start | bytes 1572872 | tf_op jit(solution)/shard_map/ppermute | solution.py:475
  166.2 6.5 %collective-permute-done.42.refs_0_.refs_1_ = bf16[64,32,128]{2,1,0:T(8,128)(2,1)S(1)} collective-permute-done((bf16[64,32,128]{2,1,0:T(8,128)(2,1)S(1)}, bf16[64,32,128]{2,1,0:T(8,128)(2,1)S(1)}, u32[]{:S(2)}, u32[]{:S(2)}) %collective-permute-start.42) | collective-permute-done | bytes 524320 | tf_op jit(solution)/shard_map/ppermute | solution.py:475
  172.9 4.4 %collective-permute-start.51 = (bf16[64,32,128]{2,1,0:T(8,128)(2,1)S(1)}, bf16[64,32,128]{2,1,0:T(8,128)(2,1)S(1)}, u32[]{:S(2)}, u32[]{:S(2)}) collective-permute-start(bf16[64,32,128]{2,1,0:T(8,128)(2,1)S(1)} %add_up.48.refs_1_), channel_id=1, source_target_pairs={{0,2},{7,5},{2,4},{5,3},{4,6},{3,1},{8,10},{15,13},{10,12},{13,11}... | collective-permute-start | bytes 1572872 | tf_op jit(solution)/shard_map/ppermute | solution.py:475
  177.3 2.0 collective-permute-start.41
  180.9 3.1 %collective-permute-done.51.refs_0_ = bf16[64,32,128]{2,1,0:T(8,128)(2,1)S(1)} collective-permute-done((bf16[64,32,128]{2,1,0:T(8,128)(2,1)S(1)}, bf16[64,32,128]{2,1,0:T(8,128)(2,1)S(1)}, u32[]{:S(2)}, u32[]{:S(2)}) %collective-permute-start.51) | collective-permute-done | bytes 524320 | tf_op jit(solution)/shard_map/ppermute | solution.py:475
  183.9 5.6 %collective-permute-done.41.refs_0_.refs_1_ = bf16[64,32,128]{2,1,0:T(8,128)(2,1)S(1)} collective-permute-done((bf16[64,32,128]{2,1,0:T(8,128)(2,1)S(1)}, bf16[64,32,128]{2,1,0:T(8,128)(2,1)S(1)}, u32[]{:S(2)}, u32[]{:S(2)}) %collective-permute-start.41) | collective-permute-done | bytes 524320 | tf_op jit(solution)/shard_map/ppermute | solution.py:475
  189.7 4.4 %collective-permute-start.50 = (bf16[64,32,128]{2,1,0:T(8,128)(2,1)S(1)}, bf16[64,32,128]{2,1,0:T(8,128)(2,1)S(1)}, u32[]{:S(2)}, u32[]{:S(2)}) collective-permute-start(bf16[64,32,128]{2,1,0:T(8,128)(2,1)S(1)} %add_up.49), channel_id=1, source_target_pairs={{0,2},{7,5},{2,4},{5,3},{4,6},{3,1},{8,10},{15,13},{10,12},{13,11}... | collective-permute-start | bytes 1572872 | tf_op jit(solution)/shard_map/ppermute | solution.py:475
  194.7 2.8 %context_products.4 = (bf16[64,32,128]{2,1,0:T(8,128)(2,1)S(1)}, f32[64,32,128]{2,1,0:T(8,128)S(1)}) custom-call(s32[487]{0:T(512)S(1)} %pad_add_fusion.index_ref, bf16[160,128,128]{2,1,0:T(8,128)(2,1)S(1)} %bitcast.7, bf16[64,32,128]{2,1,0:T(8,128)(2,1)S(1)} %collective-permute-done.51.refs_0_, ...), custom_call_target="tpu_custom_call" | custom-call | bytes 36900 | tf_op jit(solution)/shard_map/context_products/pallas_call | solution.py:397
  197.5 3.2 %collective-permute-done.50.refs_0_ = bf16[64,32,128]{2,1,0:T(8,128)(2,1)S(1)} collective-permute-done((bf16[64,32,128]{2,1,0:T(8,128)(2,1)S(1)}, bf16[64,32,128]{2,1,0:T(8,128)(2,1)S(1)}, u32[]{:S(2)}, u32[]{:S(2)}) %collective-permute-start.50) | collective-permute-done | bytes 524320 | tf_op jit(solution)/shard_map/ppermute | solution.py:475
  201.4 1.4 collective-permute-done.58.refs_6_
  202.8 2.8 %context_products.5 = (bf16[64,32,128]{2,1,0:T(8,128)(2,1)S(1)}, f32[64,32,128]{2,1,0:T(8,128)S(1)}) custom-call(s32[487]{0:T(512)S(1)} %pad_add_fusion.index_ref, bf16[160,128,128]{2,1,0:T(8,128)(2,1)S(1)} %bitcast.7, bf16[64,32,128]{2,1,0:T(8,128)(2,1)S(1)} %add_up.51.refs_0_, bf16[64,32,128]{2,1,0:T(8,128)(2,1)S(1)} %collective-permute-done.41.refs_0_.refs_1_, ...), custom_call_target="tpu_custom_call" | custom-call | bytes 36900 | tf_op jit(solution)/shard_map/context_products/pallas_call | solution.py:397
  206.1 4.1 %collective-permute-done.59.refs_1_.refs_4_ = bf16[64,32,128]{2,1,0:T(8,128)(2,1)S(1)} collective-permute-done((bf16[64,32,128]{2,1,0:T(8,128)(2,1)S(1)}, bf16[64,32,128]{2,1,0:T(8,128)(2,1)S(1)}, u32[]{:S(2)}, u32[]{:S(2)}) %collective-permute-start.59) | collective-permute-done | bytes 524320 | tf_op jit(solution)/shard_map/ppermute | solution.py:463
  211.3 6.8 %collective-permute-done.61.refs_1_.refs_7_ = bf16[64,32,128]{2,1,0:T(8,128)(2,1)S(1)} collective-permute-done((bf16[64,32,128]{2,1,0:T(8,128)(2,1)S(1)}, bf16[64,32,128]{2,1,0:T(8,128)(2,1)S(1)}, u32[]{:S(2)}, u32[]{:S(2)}) %collective-permute-start.61) | collective-permute-done | bytes 524320 | tf_op jit(solution)/shard_map/ppermute | solution.py:463
  220.5 3.1 %turn_back.2 = f32[4096,128]{1,0:T(8,128)} custom-call(s32[1]{0:T(128)S(6)} %select_n.44.start_ref, f32[64,32,128]{2,1,0:T(8,128)} %get-tuple-element.48.refs_0_, f32[64,32,128]{2,1,0:T(8,128)} %get-tuple-element.50.refs_1_, f32[64,32,128]{2,1,0:T(8,128)} %get-tuple-element.60.refs_2_, f32[64,32,128]{2,1,0:T(8,128)} %get-tuple-element.62.refs_3_, ...), custom_call_target="tpu_custom_call" | custom-call | bytes 36900 | tf_op jit(solution)/shard_map/turn_back/pallas_call | solution.py:428
  223.5 2.2 collective-permute-done.62.refs_8_
  225.8 2.6 %turn_back.3 = f32[4096,128]{1,0:T(8,128)} custom-call(s32[1]{0:T(128)} %constant.92.clone.1.place_ref.start_ref, f32[64,64,128]{2,1,0:T(8,128)S(1)} %get-tuple-element.65.refs_0_, bf16[64,64,128]{2,1,0:T(8,128)(2,1)S(1)} %collective-permute-done.49.refs_2_.refs_1_, bf16[32,64,128]{2,1,0:T(8,128)(2,1)S(1)} %copy-done.2, f32[64,32,128]{2,1,0:T(8,128)S(1)} %copy-done.4, ...), custom_call_target="tpu_custom_call" | custom-call | bytes 36900 | tf_op jit(solution)/shard_map/turn_back/pallas_call | solution.py:428
  (157 shorter events, 26.8 us)
Async XLA Ops:
  2.2 12.9 %collective-permute-start.8 = (bf16[32,64,128]{2,1,0:T(8,128)(2,1)S(1)}, bf16[32,64,128]{2,1,0:T(8,128)(2,1)S(1)}, u32[]{:S(2)}, u32[]{:S(2)}) collective-permute-start(bf16[32,64,128]{2,1,0:T(8,128)(2,1)S(1)} %turn_panel.2.refs_0_.refs_5_), channel_id=1, source_target_pairs={{0,8},{1,17},{2,10},{3,19},{4,12},{5,21},{6,14},{7,23},{8,0},{9,25... | collective-permute-start | bytes 1572872 | tf_op jit(solution)/shard_map/ppermute | solution.py:463
  10.0 5.6 %collective-permute-start = (f32[128,128]{1,0:T(8,128)S(1)}, f32[128,128]{1,0:T(8,128)S(1)}, u32[]{:S(2)}, u32[]{:S(2)}) collective-permute-start(f32[128,128]{1,0:T(8,128)S(1)} %get-tuple-element.37.refs_0_), channel_id=1, source_target_pairs={{0,8},{8,0},{16,24},{24,16},{1,9},{9,1},{17,25},{25,17},{2,10},{10... | collective-permute-start | bytes 196616 | tf_op jit(solution)/shard_map/ppermute | solution.py:478
  10.1 5.5 %collective-permute-start.1 = (f32[128,128]{1,0:T(8,128)S(1)}, f32[128,128]{1,0:T(8,128)S(1)}, u32[]{:S(2)}, u32[]{:S(2)}) collective-permute-start(f32[128,128]{1,0:T(8,128)S(1)} %get-tuple-element.37.refs_0_), channel_id=1, source_target_pairs={{0,16},{8,24},{16,0},{24,8},{1,17},{9,25},{17,1},{25,9},{2,18},{10... | collective-permute-start | bytes 196616 | tf_op jit(solution)/shard_map/ppermute | solution.py:478
  12.1 5.9 %collective-permute-start.2 = (f32[128,128]{1,0:T(8,128)S(1)}, f32[128,128]{1,0:T(8,128)S(1)}, u32[]{:S(2)}, u32[]{:S(2)}) collective-permute-start(f32[128,128]{1,0:T(8,128)S(1)} %get-tuple-element.37.refs_0_), channel_id=1, source_target_pairs={{0,24},{8,16},{16,8},{24,0},{1,25},{9,17},{17,9},{25,1},{2,26},{10... | collective-permute-start | bytes 196616 | tf_op jit(solution)/shard_map/ppermute | solution.py:478
  13.6 17.0 %collective-permute-start.7 = (bf16[32,64,128]{2,1,0:T(8,128)(2,1)S(1)}, bf16[32,64,128]{2,1,0:T(8,128)(2,1)S(1)}, u32[]{:S(2)}, u32[]{:S(2)}) collective-permute-start(bf16[32,64,128]{2,1,0:T(8,128)(2,1)S(1)} %turn_panel.2.refs_0_.refs_5_), channel_id=1, source_target_pairs={{0,16},{1,9},{2,18},{3,11},{4,20},{5,13},{6,22},{7,15},{8,24},{9,1... | collective-permute-start | bytes 1572872 | tf_op jit(solution)/shard_map/ppermute | solution.py:463
  15.1 15.5 %collective-permute-start.9 = (bf16[32,64,128]{2,1,0:T(8,128)(2,1)S(1)}, bf16[32,64,128]{2,1,0:T(8,128)(2,1)S(1)}, u32[]{:S(2)}, u32[]{:S(2)}) collective-permute-start(bf16[32,64,128]{2,1,0:T(8,128)(2,1)S(1)} %collective-permute-done.8.refs_7_), channel_id=1, source_target_pairs={{0,16},{1,9},{2,18},{3,11},{4,20},{5,13},{6,22},{7,15},{8,24},{9,1... | collective-permute-start | bytes 1572872 | tf_op jit(solution)/shard_map/ppermute | solution.py:463
  18.1 1.3 collective-permute-start.3
  19.5 4.4 %collective-permute-start.4 = (f32[136,128]{1,0:T(8,128)S(1)}, f32[136,128]{1,0:T(8,128)S(1)}, u32[]{:S(2)}, u32[]{:S(2)}) collective-permute-start(f32[136,128]{1,0:T(8,128)S(1)} %plus.3.a_ref), channel_id=1, source_target_pairs={{0,2},{1,3},{2,0},{3,1},{4,6},{5,7},{6,4},{7,5},{8,10},{9,11},{10,... | collective-permute-start | bytes 208904 | tf_op jit(solution)/shard_map/ppermute | solution.py:481
  23.9 5.4 %collective-permute-start.5 = (f32[136,128]{1,0:T(8,128)S(1)}, f32[136,128]{1,0:T(8,128)S(1)}, u32[]{:S(2)}, u32[]{:S(2)}) collective-permute-start(f32[136,128]{1,0:T(8,128)S(1)} %plus.4.a_ref), channel_id=1, source_target_pairs={{0,4},{1,5},{2,6},{3,7},{4,0},{5,1},{6,2},{7,3},{8,12},{9,13},{10,... | collective-permute-start | bytes 208904 | tf_op jit(solution)/shard_map/ppermute | solution.py:481
  29.2 1.3 collective-permute-start.6
  40.6 40.1 %copy-start = (bf16[160,128,128]{2,1,0:T(8,128)(2,1)}, bf16[160,128,128]{2,1,0:T(8,128)(2,1)S(1)}, u32[]{:S(2)}) copy-start(bf16[160,128,128]{2,1,0:T(8,128)(2,1)S(1)} %get-tuple-element.51.refs_0_.tiles_ref) | copy-start | bytes 15728644
  40.6 4.6 %collective-permute-start.12 = (bf16[64,64,128]{2,1,0:T(8,128)(2,1)S(1)}, bf16[64,64,128]{2,1,0:T(8,128)(2,1)S(1)}, u32[]{:S(2)}, u32[]{:S(2)}) collective-permute-start(bf16[64,64,128]{2,1,0:T(8,128)(2,1)S(1)} %get-tuple-element.46), channel_id=1, source_target_pairs={{1,0},{6,7},{9,8},{14,15},{17,16},{22,23},{25,24},{30,31}} | collective-permute-start | bytes 3145736 | tf_op jit(solution)/shard_map/ppermute | solution.py:466
  41.9 14.8 %collective-permute-start.11 = (bf16[64,64,128]{2,1,0:T(8,128)(2,1)S(1)}, bf16[64,64,128]{2,1,0:T(8,128)(2,1)S(1)}, u32[]{:S(2)}, u32[]{:S(2)}) collective-permute-start(bf16[64,64,128]{2,1,0:T(8,128)(2,1)S(1)} %get-tuple-element.44), channel_id=1, source_target_pairs={{1,0},{3,2},{4,5},{6,7},{9,8},{11,10},{12,13},{14,15},{17,16},{19,... | collective-permute-start | bytes 3145736 | tf_op jit(solution)/shard_map/ppermute | solution.py:466
  45.5 11.3 %collective-permute-start.13 = (bf16[64,32,128]{2,1,0:T(8,128)(2,1)S(1)}, bf16[64,32,128]{2,1,0:T(8,128)(2,1)S(1)}, u32[]{:S(2)}, u32[]{:S(2)}) collective-permute-start(bf16[64,32,128]{2,1,0:T(8,128)(2,1)S(1)} %add_up.27.refs_2_.refs_0_), channel_id=1, source_target_pairs={{0,2},{7,5},{2,4},{5,3},{4,6},{3,1},{8,10},{15,13},{10,12},{13,11}... | collective-permute-start | bytes 1572872 | tf_op jit(solution)/shard_map/ppermute | solution.py:475
  46.8 19.6 %collective-permute-start.10 = (bf16[64,64,128]{2,1,0:T(8,128)(2,1)S(1)}, bf16[64,64,128]{2,1,0:T(8,128)(2,1)S(1)}, u32[]{:S(2)}, u32[]{:S(2)}) collective-permute-start(bf16[64,64,128]{2,1,0:T(8,128)(2,1)S(1)} %get-tuple-element.42), channel_id=1, source_target_pairs={{1,0},{2,3},{3,2},{4,5},{5,4},{6,7},{9,8},{10,11},{11,10},{12,13},... | collective-permute-start | bytes 3145736 | tf_op jit(solution)/shard_map/ppermute | solution.py:466
  48.5 13.9 %collective-permute-start.15 = (bf16[64,32,128]{2,1,0:T(8,128)(2,1)S(1)}, bf16[64,32,128]{2,1,0:T(8,128)(2,1)S(1)}, u32[]{:S(2)}, u32[]{:S(2)}) collective-permute-start(bf16[64,32,128]{2,1,0:T(8,128)(2,1)S(1)} %add_up.28.refs_3_.refs_2_), channel_id=1, source_target_pairs={{0,2},{7,5},{2,4},{5,3},{4,6},{3,1},{8,10},{15,13},{10,12},{13,11}... | collective-permute-start | bytes 1572872 | tf_op jit(solution)/shard_map/ppermute | solution.py:475
  55.1 10.7 %collective-permute-start.23 = (bf16[32,64,128]{2,1,0:T(8,128)(2,1)S(1)}, bf16[32,64,128]{2,1,0:T(8,128)(2,1)S(1)}, u32[]{:S(2)}, u32[]{:S(2)}) collective-permute-start(bf16[32,64,128]{2,1,0:T(8,128)(2,1)S(1)} %turn_panel.3.refs_1_), channel_id=1, source_target_pairs={{0,8},{1,17},{2,10},{3,19},{4,12},{5,21},{6,14},{7,23},{8,0},{9,25... | collective-permute-start | bytes 1572872 | tf_op jit(solution)/shard_map/ppermute | solution.py:463
  57.2 11.8 %collective-permute-start.14 = (bf16[64,32,128]{2,1,0:T(8,128)(2,1)S(1)}, bf16[64,32,128]{2,1,0:T(8,128)(2,1)S(1)}, u32[]{:S(2)}, u32[]{:S(2)}) collective-permute-start(bf16[64,32,128]{2,1,0:T(8,128)(2,1)S(1)} %add_up.29.refs_3_), channel_id=1, source_target_pairs={{0,2},{7,5},{2,4},{5,3},{4,6},{3,1},{8,10},{15,13},{10,12},{13,11}... | collective-permute-start | bytes 1572872 | tf_op jit(solution)/shard_map/ppermute | solution.py:475
  62.8 11.8 %collective-permute-start.19 = (bf16[64,32,128]{2,1,0:T(8,128)(2,1)S(1)}, bf16[64,32,128]{2,1,0:T(8,128)(2,1)S(1)}, u32[]{:S(2)}, u32[]{:S(2)}) collective-permute-start(bf16[64,32,128]{2,1,0:T(8,128)(2,1)S(1)} %add_up.30.refs_3_.refs_1_), channel_id=1, source_target_pairs={{0,2},{7,5},{2,4},{5,3},{4,6},{3,1},{8,10},{15,13},{10,12},{13,11}... | collective-permute-start | bytes 1572872 | tf_op jit(solution)/shard_map/ppermute | solution.py:475
  65.7 25.4 %collective-permute-start.18 = (bf16[64,64,128]{2,1,0:T(8,128)(2,1)S(1)}, bf16[64,64,128]{2,1,0:T(8,128)(2,1)S(1)}, u32[]{:S(2)}, u32[]{:S(2)}) collective-permute-start(bf16[64,64,128]{2,1,0:T(8,128)(2,1)S(1)} %get-tuple-element.47.refs_0_), channel_id=1, source_target_pairs={{0,1},{1,0},{2,3},{3,2},{4,5},{5,4},{6,7},{7,6},{8,9},{9,8},{10,11... | collective-permute-start | bytes 3145736 | tf_op jit(solution)/shard_map/ppermute | solution.py:466
  65.8 13.7 %collective-permute-start.22 = (bf16[32,64,128]{2,1,0:T(8,128)(2,1)S(1)}, bf16[32,64,128]{2,1,0:T(8,128)(2,1)S(1)}, u32[]{:S(2)}, u32[]{:S(2)}) collective-permute-start(bf16[32,64,128]{2,1,0:T(8,128)(2,1)S(1)} %turn_panel.3.refs_1_), channel_id=1, source_target_pairs={{0,16},{1,9},{2,18},{3,11},{4,20},{5,13},{6,22},{7,15},{8,24},{9,1... | collective-permute-start | bytes 1572872 | tf_op jit(solution)/shard_map/ppermute | solution.py:463
  66.4 14.3 %collective-permute-start.24 = (bf16[32,64,128]{2,1,0:T(8,128)(2,1)S(1)}, bf16[32,64,128]{2,1,0:T(8,128)(2,1)S(1)}, u32[]{:S(2)}, u32[]{:S(2)}) collective-permute-start(bf16[32,64,128]{2,1,0:T(8,128)(2,1)S(1)} %add_up.36), channel_id=1, source_target_pairs={{0,16},{1,9},{2,18},{3,11},{4,20},{5,13},{6,22},{7,15},{8,24},{9,1... | collective-permute-start | bytes 1572872 | tf_op jit(solution)/shard_map/ppermute | solution.py:463
  69.4 18.2 %collective-permute-start.16 = (bf16[64,32,128]{2,1,0:T(8,128)(2,1)S(1)}, bf16[64,32,128]{2,1,0:T(8,128)(2,1)S(1)}, u32[]{:S(2)}, u32[]{:S(2)}) collective-permute-start(bf16[64,32,128]{2,1,0:T(8,128)(2,1)S(1)} %add_up.31.refs_3_), channel_id=1, source_target_pairs={{0,2},{7,5},{2,4},{5,3},{4,6},{3,1},{8,10},{15,13},{10,12},{13,11}... | collective-permute-start | bytes 1572872 | tf_op jit(solution)/shard_map/ppermute | solution.py:475
  75.0 14.2 %collective-permute-start.20 = (bf16[64,32,128]{2,1,0:T(8,128)(2,1)S(1)}, bf16[64,32,128]{2,1,0:T(8,128)(2,1)S(1)}, u32[]{:S(2)}, u32[]{:S(2)}) collective-permute-start(bf16[64,32,128]{2,1,0:T(8,128)(2,1)S(1)} %add_up.33.refs_3_.refs_5_), channel_id=1, source_target_pairs={{0,2},{7,5},{2,4},{5,3},{4,6},{3,1},{8,10},{15,13},{10,12},{13,11}... | collective-permute-start | bytes 1572872 | tf_op jit(solution)/shard_map/ppermute | solution.py:475
  87.7 3.8 %collective-permute-start.17 = (bf16[64,32,128]{2,1,0:T(8,128)(2,1)S(1)}, bf16[64,32,128]{2,1,0:T(8,128)(2,1)S(1)}, u32[]{:S(2)}, u32[]{:S(2)}) collective-permute-start(bf16[64,32,128]{2,1,0:T(8,128)(2,1)S(1)} %collective-permute-done.16.refs_0_), channel_id=1, source_target_pairs={{0,1},{1,0},{2,3},{3,2},{4,5},{5,4},{6,7},{7,6},{8,9},{9,8},{10,11... | collective-permute-start | bytes 1572872 | tf_op jit(solution)/shard_map/ppermute | solution.py:466
  87.7 14.9 %collective-permute-start.27 = (bf16[64,64,128]{2,1,0:T(8,128)(2,1)}, bf16[64,64,128]{2,1,0:T(8,128)(2,1)}, u32[]{:S(2)}, u32[]{:S(2)}) collective-permute-start(bf16[64,64,128]{2,1,0:T(8,128)(2,1)} %get-tuple-element.57), channel_id=1, source_target_pairs={{1,0},{6,7},{9,8},{14,15},{17,16},{22,23},{25,24},{30,31}} | collective-permute-start | bytes 3145736 | tf_op jit(solution)/shard_map/ppermute | solution.py:466
  89.2 8.7 %collective-permute-start.21 = (bf16[64,32,128]{2,1,0:T(8,128)(2,1)S(1)}, bf16[64,32,128]{2,1,0:T(8,128)(2,1)S(1)}, u32[]{:S(2)}, u32[]{:S(2)}) collective-permute-start(bf16[64,32,128]{2,1,0:T(8,128)(2,1)S(1)} %collective-permute-done.20.refs_0_), channel_id=1, source_target_pairs={{0,1},{1,0},{2,3},{3,2},{4,5},{5,4},{6,7},{7,6},{8,9},{9,8},{10,11... | collective-permute-start | bytes 1572872 | tf_op jit(solution)/shard_map/ppermute | solution.py:466
  92.8 10.1 %collective-permute-start.28 = (bf16[64,32,128]{2,1,0:T(8,128)(2,1)}, bf16[64,32,128]{2,1,0:T(8,128)(2,1)}, u32[]{:S(2)}, u32[]{:S(2)}) collective-permute-start(bf16[64,32,128]{2,1,0:T(8,128)(2,1)} %get-tuple-element.49.refs_3_.refs_6_), channel_id=1, source_target_pairs={{0,2},{7,5},{2,4},{5,3},{4,6},{3,1},{8,10},{15,13},{10,12},{13,11}... | collective-permute-start | bytes 1572872 | tf_op jit(solution)/shard_map/ppermute | solution.py:475
  96.7 19.9 %collective-permute-start.26 = (bf16[64,64,128]{2,1,0:T(8,128)(2,1)}, bf16[64,64,128]{2,1,0:T(8,128)(2,1)S(1)}, u32[]{:S(2)}, u32[]{:S(2)}) collective-permute-start(bf16[64,64,128]{2,1,0:T(8,128)(2,1)} %get-tuple-element.55), channel_id=1, source_target_pairs={{1,0},{3,2},{4,5},{6,7},{9,8},{11,10},{12,13},{14,15},{17,16},{19,... | collective-permute-start | bytes 3145736 | tf_op jit(solution)/shard_map/ppermute | solution.py:466
  99.3 12.0 %collective-permute-start.30 = (bf16[64,32,128]{2,1,0:T(8,128)(2,1)}, bf16[64,32,128]{2,1,0:T(8,128)(2,1)}, u32[]{:S(2)}, u32[]{:S(2)}) collective-permute-start(bf16[64,32,128]{2,1,0:T(8,128)(2,1)} %get-tuple-element.58.refs_3_.refs_7_), channel_id=1, source_target_pairs={{0,2},{7,5},{2,4},{5,3},{4,6},{3,1},{8,10},{15,13},{10,12},{13,11}... | collective-permute-start | bytes 1572872 | tf_op jit(solution)/shard_map/ppermute | solution.py:475
  105.6 11.0 %collective-permute-start.29 = (bf16[64,32,128]{2,1,0:T(8,128)(2,1)S(1)}, bf16[64,32,128]{2,1,0:T(8,128)(2,1)S(1)}, u32[]{:S(2)}, u32[]{:S(2)}) collective-permute-start(bf16[64,32,128]{2,1,0:T(8,128)(2,1)S(1)} %add_up.37.refs_3_), channel_id=1, source_target_pairs={{0,2},{7,5},{2,4},{5,3},{4,6},{3,1},{8,10},{15,13},{10,12},{13,11}... | collective-permute-start | bytes 1572872 | tf_op jit(solution)/shard_map/ppermute | solution.py:475
  110.0 18.0 %collective-permute-start.25 = (bf16[64,64,128]{2,1,0:T(8,128)(2,1)S(1)}, bf16[64,64,128]{2,1,0:T(8,128)(2,1)S(1)}, u32[]{:S(2)}, u32[]{:S(2)}) collective-permute-start(bf16[64,64,128]{2,1,0:T(8,128)(2,1)S(1)} %copy-done.19), channel_id=1, source_target_pairs={{1,0},{2,3},{3,2},{4,5},{5,4},{6,7},{9,8},{10,11},{11,10},{12,13},... | collective-permute-start | bytes 3145736 | tf_op jit(solution)/shard_map/ppermute | solution.py:466
  112.7 10.5 %collective-permute-start.32 = (bf16[64,32,128]{2,1,0:T(8,128)(2,1)S(1)}, bf16[64,32,128]{2,1,0:T(8,128)(2,1)S(1)}, u32[]{:S(2)}, u32[]{:S(2)}) collective-permute-start(bf16[64,32,128]{2,1,0:T(8,128)(2,1)S(1)} %add_up.38.refs_4_.refs_2_), channel_id=1, source_target_pairs={{0,2},{7,5},{2,4},{5,3},{4,6},{3,1},{8,10},{15,13},{10,12},{13,11}... | collective-permute-start | bytes 1572872 | tf_op jit(solution)/shard_map/ppermute | solution.py:475
  116.9 11.9 %collective-permute-start.31 = (bf16[64,32,128]{2,1,0:T(8,128)(2,1)S(1)}, bf16[64,32,128]{2,1,0:T(8,128)(2,1)S(1)}, u32[]{:S(2)}, u32[]{:S(2)}) collective-permute-start(bf16[64,32,128]{2,1,0:T(8,128)(2,1)S(1)} %add_up.39.refs_4_), channel_id=1, source_target_pairs={{0,2},{7,5},{2,4},{5,3},{4,6},{3,1},{8,10},{15,13},{10,12},{13,11}... | collective-permute-start | bytes 1572872 | tf_op jit(solution)/shard_map/ppermute | solution.py:475
  123.5 11.1 %collective-permute-start.36 = (bf16[64,32,128]{2,1,0:T(8,128)(2,1)S(1)}, bf16[64,32,128]{2,1,0:T(8,128)(2,1)S(1)}, u32[]{:S(2)}, u32[]{:S(2)}) collective-permute-start(bf16[64,32,128]{2,1,0:T(8,128)(2,1)S(1)} %add_up.40.refs_3_), channel_id=1, source_target_pairs={{0,2},{7,5},{2,4},{5,3},{4,6},{3,1},{8,10},{15,13},{10,12},{13,11}... | collective-permute-start | bytes 1572872 | tf_op jit(solution)/shard_map/ppermute | solution.py:475
  127.9 18.5 %collective-permute-start.35 = (bf16[64,64,128]{2,1,0:T(8,128)(2,1)S(1)}, bf16[64,64,128]{2,1,0:T(8,128)(2,1)S(1)}, u32[]{:S(2)}, u32[]{:S(2)}) collective-permute-start(bf16[64,64,128]{2,1,0:T(8,128)(2,1)S(1)} %copy-done.15), channel_id=1, source_target_pairs={{0,1},{1,0},{2,3},{3,2},{4,5},{5,4},{6,7},{7,6},{8,9},{9,8},{10,11... | collective-permute-start | bytes 3145736 | tf_op jit(solution)/shard_map/ppermute | solution.py:466
  129.3 11.1 %collective-permute-start.33 = (bf16[64,32,128]{2,1,0:T(8,128)(2,1)S(1)}, bf16[64,32,128]{2,1,0:T(8,128)(2,1)S(1)}, u32[]{:S(2)}, u32[]{:S(2)}) collective-permute-start(bf16[64,32,128]{2,1,0:T(8,128)(2,1)S(1)} %add_up.41.refs_3_), channel_id=1, source_target_pairs={{0,2},{7,5},{2,4},{5,3},{4,6},{3,1},{8,10},{15,13},{10,12},{13,11}... | collective-permute-start | bytes 1572872 | tf_op jit(solution)/shard_map/ppermute | solution.py:475
  135.0 11.3 %collective-permute-start.37 = (bf16[64,32,128]{2,1,0:T(8,128)(2,1)S(1)}, bf16[64,32,128]{2,1,0:T(8,128)(2,1)S(1)}, u32[]{:S(2)}, u32[]{:S(2)}) collective-permute-start(bf16[64,32,128]{2,1,0:T(8,128)(2,1)S(1)} %add_up.43.refs_3_), channel_id=1, source_target_pairs={{0,2},{7,5},{2,4},{5,3},{4,6},{3,1},{8,10},{15,13},{10,12},{13,11}... | collective-permute-start | bytes 1572872 | tf_op jit(solution)/shard_map/ppermute | solution.py:475
  139.7 7.4 %collective-permute-start.44 = (bf16[64,32,128]{2,1,0:T(8,128)(2,1)}, bf16[64,32,128]{2,1,0:T(8,128)(2,1)S(1)}, u32[]{:S(2)}, u32[]{:S(2)}) collective-permute-start(bf16[64,32,128]{2,1,0:T(8,128)(2,1)} %collective-permute-done.30.refs_2_.refs_5_), channel_id=1, source_target_pairs={{0,1},{1,0},{2,3},{3,2},{4,5},{5,4},{6,7},{7,6},{8,9},{9,8},{10,11... | collective-permute-start | bytes 1572872 | tf_op jit(solution)/shard_map/ppermute | solution.py:466
  139.8 7.5 %collective-permute-start.43 = (bf16[64,32,128]{2,1,0:T(8,128)(2,1)}, bf16[64,32,128]{2,1,0:T(8,128)(2,1)S(1)}, u32[]{:S(2)}, u32[]{:S(2)}) collective-permute-start(bf16[64,32,128]{2,1,0:T(8,128)(2,1)} %collective-permute-done.28.refs_2_.refs_4_), channel_id=1, source_target_pairs={{0,1},{1,0},{2,3},{3,2},{4,5},{5,4},{6,7},{7,6},{8,9},{9,8},{10,11... | collective-permute-start | bytes 1572872 | tf_op jit(solution)/shard_map/ppermute | solution.py:466
  140.4 7.3 %collective-permute-start.34 = (bf16[64,32,128]{2,1,0:T(8,128)(2,1)S(1)}, bf16[64,32,128]{2,1,0:T(8,128)(2,1)S(1)}, u32[]{:S(2)}, u32[]{:S(2)}) collective-permute-start(bf16[64,32,128]{2,1,0:T(8,128)(2,1)S(1)} %collective-permute-done.33.refs_0_), channel_id=1, source_target_pairs={{0,1},{1,0},{2,3},{3,2},{4,5},{5,4},{6,7},{7,6},{8,9},{9,8},{10,11... | collective-permute-start | bytes 1572872 | tf_op jit(solution)/shard_map/ppermute | solution.py:466
  146.4 2.6 %collective-permute-start.38 = (bf16[64,32,128]{2,1,0:T(8,128)(2,1)S(1)}, bf16[64,32,128]{2,1,0:T(8,128)(2,1)S(1)}, u32[]{:S(2)}, u32[]{:S(2)}) collective-permute-start(bf16[64,32,128]{2,1,0:T(8,128)(2,1)S(1)} %collective-permute-done.37.refs_0_), channel_id=1, source_target_pairs={{0,1},{1,0},{2,3},{3,2},{4,5},{5,4},{6,7},{7,6},{8,9},{9,8},{10,11... | collective-permute-start | bytes 1572872 | tf_op jit(solution)/shard_map/ppermute | solution.py:466
  146.6 8.0 %collective-permute-start.46 = (bf16[64,32,128]{2,1,0:T(8,128)(2,1)S(1)}, bf16[64,32,128]{2,1,0:T(8,128)(2,1)S(1)}, u32[]{:S(2)}, u32[]{:S(2)}) collective-permute-start(bf16[64,32,128]{2,1,0:T(8,128)(2,1)S(1)} %collective-permute-done.32.refs_2_.refs_3_), channel_id=1, source_target_pairs={{0,1},{1,0},{2,3},{3,2},{4,5},{5,4},{6,7},{7,6},{8,9},{9,8},{10,11... | collective-permute-start | bytes 1572872 | tf_op jit(solution)/shard_map/ppermute | solution.py:466
  147.2 10.3 %collective-permute-start.45 = (bf16[64,32,128]{2,1,0:T(8,128)(2,1)S(1)}, bf16[64,32,128]{2,1,0:T(8,128)(2,1)S(1)}, u32[]{:S(2)}, u32[]{:S(2)}) collective-permute-start(bf16[64,32,128]{2,1,0:T(8,128)(2,1)S(1)} %collective-permute-done.29.refs_2_.refs_3_), channel_id=1, source_target_pairs={{0,1},{1,0},{2,3},{3,2},{4,5},{5,4},{6,7},{7,6},{8,9},{9,8},{10,11... | collective-permute-start | bytes 1572872 | tf_op jit(solution)/shard_map/ppermute | solution.py:466
  147.3 10.3 %collective-permute-start.48 = (bf16[64,32,128]{2,1,0:T(8,128)(2,1)S(1)}, bf16[64,32,128]{2,1,0:T(8,128)(2,1)S(1)}, u32[]{:S(2)}, u32[]{:S(2)}) collective-permute-start(bf16[64,32,128]{2,1,0:T(8,128)(2,1)S(1)} %collective-permute-done.36.refs_2_.refs_1_), channel_id=1, source_target_pairs={{0,1},{1,0},{2,3},{3,2},{4,5},{5,4},{6,7},{7,6},{8,9},{9,8},{10,11... | collective-permute-start | bytes 1572872 | tf_op jit(solution)/shard_map/ppermute | solution.py:466
  147.7 9.8 %collective-permute-start.47 = (bf16[64,32,128]{2,1,0:T(8,128)(2,1)S(1)}, bf16[64,32,128]{2,1,0:T(8,128)(2,1)S(1)}, u32[]{:S(2)}, u32[]{:S(2)}) collective-permute-start(bf16[64,32,128]{2,1,0:T(8,128)(2,1)S(1)} %collective-permute-done.31.refs_2_.refs_0_), channel_id=1, source_target_pairs={{0,1},{1,0},{2,3},{3,2},{4,5},{5,4},{6,7},{7,6},{8,9},{9,8},{10,11... | collective-permute-start | bytes 1572872 | tf_op jit(solution)/shard_map/ppermute | solution.py:466
  149.0 14.2 %collective-permute-start.40 = (bf16[64,32,128]{2,1,0:T(8,128)(2,1)S(1)}, bf16[64,32,128]{2,1,0:T(8,128)(2,1)S(1)}, u32[]{:S(2)}, u32[]{:S(2)}) collective-permute-start(bf16[64,32,128]{2,1,0:T(8,128)(2,1)S(1)} %get-tuple-element.61.refs_3_), channel_id=1, source_target_pairs={{0,2},{7,5},{2,4},{5,3},{4,6},{3,1},{8,10},{15,13},{10,12},{13,11}... | collective-permute-start | bytes 1572872 | tf_op jit(solution)/shard_map/ppermute | solution.py:475
  154.6 11.5 %collective-permute-start.39 = (bf16[64,32,128]{2,1,0:T(8,128)(2,1)S(1)}, bf16[64,32,128]{2,1,0:T(8,128)(2,1)S(1)}, u32[]{:S(2)}, u32[]{:S(2)}) collective-permute-start(bf16[64,32,128]{2,1,0:T(8,128)(2,1)S(1)} %get-tuple-element.63.refs_1_.refs_14_.refs_3_), channel_id=1, source_target_pairs={{0,2},{7,5},{2,4},{5,3},{4,6},{3,1},{8,10},{15,13},{10,12},{13,11}... | collective-permute-start | bytes 1572872 | tf_op jit(solution)/shard_map/ppermute | solution.py:475
  161.5 17.9 %collective-permute-start.49 = (bf16[64,64,128]{2,1,0:T(8,128)(2,1)S(1)}, bf16[64,64,128]{2,1,0:T(8,128)(2,1)S(1)}, u32[]{:S(2)}, u32[]{:S(2)}) collective-permute-start(bf16[64,64,128]{2,1,0:T(8,128)(2,1)S(1)} %get-tuple-element.64), channel_id=1, source_target_pairs={{0,8},{1,17},{2,10},{3,19},{4,12},{5,21},{6,14},{7,23},{8,0},{9,25... | collective-permute-start | bytes 3145736 | tf_op jit(solution)/shard_map/ppermute | solution.py:463
  163.3 9.4 %collective-permute-start.42 = (bf16[64,32,128]{2,1,0:T(8,128)(2,1)S(1)}, bf16[64,32,128]{2,1,0:T(8,128)(2,1)S(1)}, u32[]{:S(2)}, u32[]{:S(2)}) collective-permute-start(bf16[64,32,128]{2,1,0:T(8,128)(2,1)S(1)} %add_up.46.refs_1_), channel_id=1, source_target_pairs={{0,2},{7,5},{2,4},{5,3},{4,6},{3,1},{8,10},{15,13},{10,12},{13,11}... | collective-permute-start | bytes 1572872 | tf_op jit(solution)/shard_map/ppermute | solution.py:475
  172.9 11.1 %collective-permute-start.51 = (bf16[64,32,128]{2,1,0:T(8,128)(2,1)S(1)}, bf16[64,32,128]{2,1,0:T(8,128)(2,1)S(1)}, u32[]{:S(2)}, u32[]{:S(2)}) collective-permute-start(bf16[64,32,128]{2,1,0:T(8,128)(2,1)S(1)} %add_up.48.refs_1_), channel_id=1, source_target_pairs={{0,2},{7,5},{2,4},{5,3},{4,6},{3,1},{8,10},{15,13},{10,12},{13,11}... | collective-permute-start | bytes 1572872 | tf_op jit(solution)/shard_map/ppermute | solution.py:475
  177.3 12.3 %collective-permute-start.41 = (bf16[64,32,128]{2,1,0:T(8,128)(2,1)S(1)}, bf16[64,32,128]{2,1,0:T(8,128)(2,1)S(1)}, u32[]{:S(2)}, u32[]{:S(2)}) collective-permute-start(bf16[64,32,128]{2,1,0:T(8,128)(2,1)S(1)} %add_up.47.refs_1_), channel_id=1, source_target_pairs={{0,2},{7,5},{2,4},{5,3},{4,6},{3,1},{8,10},{15,13},{10,12},{13,11}... | collective-permute-start | bytes 1572872 | tf_op jit(solution)/shard_map/ppermute | solution.py:475
  179.3 14.7 %collective-permute-start.52 = (bf16[64,32,128]{2,1,0:T(8,128)(2,1)S(1)}, bf16[64,32,128]{2,1,0:T(8,128)(2,1)S(1)}, u32[]{:S(2)}, u32[]{:S(2)}) collective-permute-start(bf16[64,32,128]{2,1,0:T(8,128)(2,1)S(1)} %collective-permute-done.40.refs_0_.refs_2_), channel_id=1, source_target_pairs={{0,1},{1,0},{2,3},{3,2},{4,5},{5,4},{6,7},{7,6},{8,9},{9,8},{10,11... | collective-permute-start | bytes 1572872 | tf_op jit(solution)/shard_map/ppermute | solution.py:466
  179.5 14.6 %collective-permute-start.55 = (bf16[32,64,128]{2,1,0:T(8,128)(2,1)S(1)}, bf16[32,64,128]{2,1,0:T(8,128)(2,1)S(1)}, u32[]{:S(2)}, u32[]{:S(2)}) collective-permute-start(bf16[32,64,128]{2,1,0:T(8,128)(2,1)S(1)} %add_up.50), channel_id=1, source_target_pairs={{0,16},{1,9},{2,18},{3,11},{4,20},{5,13},{6,22},{7,15},{8,24},{9,1... | collective-permute-start | bytes 1572872 | tf_op jit(solution)/shard_map/ppermute | solution.py:463
  180.0 14.7 %collective-permute-start.53 = (bf16[64,32,128]{2,1,0:T(8,128)(2,1)S(1)}, bf16[64,32,128]{2,1,0:T(8,128)(2,1)S(1)}, u32[]{:S(2)}, u32[]{:S(2)}) collective-permute-start(bf16[64,32,128]{2,1,0:T(8,128)(2,1)S(1)} %collective-permute-done.42.refs_0_.refs_1_), channel_id=1, source_target_pairs={{0,1},{1,0},{2,3},{3,2},{4,5},{5,4},{6,7},{7,6},{8,9},{9,8},{10,11... | collective-permute-start | bytes 1572872 | tf_op jit(solution)/shard_map/ppermute | solution.py:466
  183.9 10.7 %collective-permute-start.54 = (bf16[64,32,128]{2,1,0:T(8,128)(2,1)S(1)}, bf16[64,32,128]{2,1,0:T(8,128)(2,1)S(1)}, u32[]{:S(2)}, u32[]{:S(2)}) collective-permute-start(bf16[64,32,128]{2,1,0:T(8,128)(2,1)S(1)} %collective-permute-done.51.refs_0_), channel_id=1, source_target_pairs={{0,1},{1,0},{2,3},{3,2},{4,5},{5,4},{6,7},{7,6},{8,9},{9,8},{10,11... | collective-permute-start | bytes 1572872 | tf_op jit(solution)/shard_map/ppermute | solution.py:466
  189.7 11.1 %collective-permute-start.50 = (bf16[64,32,128]{2,1,0:T(8,128)(2,1)S(1)}, bf16[64,32,128]{2,1,0:T(8,128)(2,1)S(1)}, u32[]{:S(2)}, u32[]{:S(2)}) collective-permute-start(bf16[64,32,128]{2,1,0:T(8,128)(2,1)S(1)} %add_up.49), channel_id=1, source_target_pairs={{0,2},{7,5},{2,4},{5,3},{4,6},{3,1},{8,10},{15,13},{10,12},{13,11}... | collective-permute-start | bytes 1572872 | tf_op jit(solution)/shard_map/ppermute | solution.py:475
  194.1 7.3 %collective-permute-start.56 = (bf16[64,32,128]{2,1,0:T(8,128)(2,1)S(1)}, bf16[64,32,128]{2,1,0:T(8,128)(2,1)S(1)}, u32[]{:S(2)}, u32[]{:S(2)}) collective-permute-start(bf16[64,32,128]{2,1,0:T(8,128)(2,1)S(1)} %collective-permute-done.39.refs_0_.refs_2_), channel_id=1, source_target_pairs={{0,1},{1,0},{2,3},{3,2},{4,5},{5,4},{6,7},{7,6},{8,9},{9,8},{10,11... | collective-permute-start | bytes 1572872 | tf_op jit(solution)/shard_map/ppermute | solution.py:466
  194.2 7.2 %collective-permute-start.57 = (bf16[64,32,128]{2,1,0:T(8,128)(2,1)S(1)}, bf16[64,32,128]{2,1,0:T(8,128)(2,1)S(1)}, u32[]{:S(2)}, u32[]{:S(2)}) collective-permute-start(bf16[64,32,128]{2,1,0:T(8,128)(2,1)S(1)} %collective-permute-done.41.refs_0_.refs_1_), channel_id=1, source_target_pairs={{0,1},{1,0},{2,3},{3,2},{4,5},{5,4},{6,7},{7,6},{8,9},{9,8},{10,11... | collective-permute-start | bytes 1572872 | tf_op jit(solution)/shard_map/ppermute | solution.py:466
  200.8 2.0 collective-permute-start.58
  200.9 9.2 %collective-permute-start.59 = (bf16[64,32,128]{2,1,0:T(8,128)(2,1)S(1)}, bf16[64,32,128]{2,1,0:T(8,128)(2,1)S(1)}, u32[]{:S(2)}, u32[]{:S(2)}) collective-permute-start(bf16[64,32,128]{2,1,0:T(8,128)(2,1)S(1)} %get-tuple-element.66.refs_1_), channel_id=1, source_target_pairs={{0,8},{1,17},{2,10},{3,19},{4,12},{5,21},{6,14},{7,23},{8,0},{9,25... | collective-permute-start | bytes 1572872 | tf_op jit(solution)/shard_map/ppermute | solution.py:463
  205.6 12.5 %collective-permute-start.61 = (bf16[64,32,128]{2,1,0:T(8,128)(2,1)S(1)}, bf16[64,32,128]{2,1,0:T(8,128)(2,1)S(1)}, u32[]{:S(2)}, u32[]{:S(2)}) collective-permute-start(bf16[64,32,128]{2,1,0:T(8,128)(2,1)S(1)} %get-tuple-element.67.refs_4_), channel_id=1, source_target_pairs={{0,8},{1,17},{2,10},{3,19},{4,12},{5,21},{6,14},{7,23},{8,0},{9,25... | collective-permute-start | bytes 1572872 | tf_op jit(solution)/shard_map/ppermute | solution.py:463
  211.0 12.6 %collective-permute-start.60 = (bf16[32,32,128]{2,1,0:T(8,128)(2,1)}, bf16[32,32,128]{2,1,0:T(8,128)(2,1)S(1)}, u32[]{:S(2)}, u32[]{:S(2)}) collective-permute-start(bf16[32,32,128]{2,1,0:T(8,128)(2,1)} %add_up.52), channel_id=1, source_target_pairs={{0,16},{1,9},{2,18},{3,11},{4,20},{5,13},{6,22},{7,15},{8,24},{9,1... | collective-permute-start | bytes 786440 | tf_op jit(solution)/shard_map/ppermute | solution.py:463
  219.0 6.7 %collective-permute-start.62 = (bf16[32,32,128]{2,1,0:T(8,128)(2,1)}, bf16[32,32,128]{2,1,0:T(8,128)(2,1)}, u32[]{:S(2)}, u32[]{:S(2)}) collective-permute-start(bf16[32,32,128]{2,1,0:T(8,128)(2,1)} %add_up.53), channel_id=1, source_target_pairs={{0,16},{1,9},{2,18},{3,11},{4,20},{5,13},{6,22},{7,15},{8,24},{9,1... | collective-permute-start | bytes 786440 | tf_op jit(solution)/shard_map/ppermute | solution.py:463
  (24 other events, 207.4 us)
